TPU v7x, 32 devices: a whole 2x2x4 slice. The times are simulated.
32 devices in a mesh: face: 2 (over x), blk: 16 (over z, y, core).
Axes of the slice: x: 2, y: 2, z: 4, core: 2. Of those that a mesh axis runs over, the one named last changes fastest.
Arguments:
- fields: float32 [3, 8, 8, 8192], P(None, None, None, ('face', 'blk')), may hold values from -6 to 6
- jacobian: float32 [8, 8, 8192], P(None, None, ('face', 'blk')), may hold values from 0.6 to 1.6
- water_depth: float32 [8, 8, 8192], P(None, None, ('face', 'blk')), may hold values from 0.4 to 2.5
- coriolis: float32 [8, 8, 8192], P(None, None, ('face', 'blk')), may hold values from -2 to 2
- tide_height: float32 [8, 8, 8192], P(None, None, ('face', 'blk')), may hold values from -4 to 4
- slot_of: int32 [32, 256], P(('face', 'blk')), may hold values from 0 to 255, each once within a row
- seam_rows: int32 [2, 256], replicated, may hold values from 0 to 255, as said below
Outputs:
- stepped: float32 [3, 8, 8, 8192], P(None, None, None, ('face', 'blk'))
Inputs may be any that keep to these rules, and one draw needn't show every extreme that they name: For one seam k, drawn, seam_rows[k, y] = y; for the other, seam_rows[k, y] = 255 - y. `slot_of`: each row is a permutation of 0 to 255.
All inputs are finite; a program needn't handle non-finite values.
Results may differ from a plain program's by a relative error of at most 0.00005.
Values sent between devices are 32-bit elements; how exact they have to be, the bound alone decides.
No kernel may reach another device: no remote copies, remote signals or barrier semaphores. Data moves between devices by JAX's collectives and lax.ppermute only.
A program may use at most 64 MiB of HBM per device.

v0:
```python
import math

import jax
import jax.numpy as jnp
from jax import lax
from jax.sharding import PartitionSpec as P

BY = 16
GY = 16


time_step = 0.03
hyper_coeff = 0.0002


def passed_along(value, axis, by):
    count = lax.axis_size(axis)
    return lax.ppermute(value, axis, [(i, (i + by) % count) for i in range(count)])


def from_behind(value, axis, by):
    count = lax.axis_size(axis)
    pairs = [(i, i + by) for i in range(count) if 0 <= i + by < count]
    return lax.ppermute(value, axis, pairs)


def legendre_pair(location, degree):
    lower_value = 1.0
    upper_value = location
    for polynomial_order in range(2, degree + 1):
        lower_value, upper_value = (
            upper_value,
            (
                (2 * polynomial_order - 1) * location * upper_value
                - (polynomial_order - 1) * lower_value
            )
            / polynomial_order,
        )
    return (lower_value, upper_value)


def gll_tables(points):
    degree = points - 1
    locations = [-math.cos(math.pi * position / degree) for position in range(points)]
    for iteration in range(100):
        updated = []
        for location in locations:
            lower_value, upper_value = legendre_pair(location, degree)
            updated.append(
                location - (location * upper_value - lower_value) / ((degree + 1) * upper_value)
            )
        locations = updated
    locations[0] = -1.0
    locations[degree] = 1.0
    legendre_at = [legendre_pair(location, degree)[1] for location in locations]
    weights = [2.0 / (degree * (degree + 1) * value * value) for value in legendre_at]
    corner_value = degree * (degree + 1) / 4.0
    derivative = []
    for row_index in range(points):
        row_values = []
        for column_index in range(points):
            if row_index != column_index:
                row_values.append(
                    legendre_at[row_index]
                    / (legendre_at[column_index] * (locations[row_index] - locations[column_index]))
                )
            elif row_index == 0:
                row_values.append(-corner_value)
            elif row_index == degree:
                row_values.append(corner_value)
            else:
                row_values.append(0.0)
        derivative.append(row_values)
    return (jnp.asarray(weights, jnp.float32), jnp.asarray(derivative, jnp.float32))


def along_x(derivative, stacked):
    return jnp.einsum("ai,cije->caje", derivative, stacked, precision=lax.Precision.HIGHEST)


def along_y(derivative, stacked):
    return jnp.einsum("bj,cije->cibe", derivative, stacked, precision=lax.Precision.HIGHEST)


def seam_parts(seam_rows):
    size_y = seam_rows.shape[1]
    flipped = (seam_rows[:, 1] - seam_rows[:, 0]) % size_y != 1
    inverse = (
        jnp.zeros_like(seam_rows)
        .at[jnp.arange(2)[:, None], seam_rows]
        .set(jnp.broadcast_to(jnp.arange(size_y, dtype=jnp.int32)[None, :], seam_rows.shape))
    )
    return (flipped, inverse)


def orient(values, flipped, flip_signs):
    return jnp.where(flipped, jnp.flip(values, 1) * flip_signs[:, None, None], values)


def on_device(fields, jacobian, water_depth, coriolis, tide_height, slot_of, seam_rows):
    points = fields.shape[1]
    slot_row = slot_of[0]
    elements = slot_row.shape[0]
    size_y = seam_rows.shape[1]
    block_cols = lax.axis_size("blk") // BY
    face_id = lax.axis_index("face")
    blk_id = lax.axis_index("blk")
    block_x = blk_id // BY
    block_y = blk_id % BY
    own_rows = block_y * GY + jnp.arange(GY, dtype=jnp.int32)
    flipped, inverse = seam_parts(seam_rows)
    east_partner = seam_rows[face_id][own_rows]
    west_partner = inverse[1 - face_id][own_rows]
    east_flip = flipped[face_id]
    west_flip = flipped[1 - face_id]
    at_east = block_x == block_cols - 1
    at_west = block_x == 0
    position = jnp.arange(elements, dtype=jnp.int32) % GY
    keep_above = block_y < BY - 1
    keep_below = block_y > 0

    def x_pass(stacked, flip_signs):
        east_edge = stacked[:, points - 1]
        west_edge = stacked[:, 0]
        from_west = passed_along(east_edge[..., elements - GY :], ("face", "blk"), BY)
        from_east = passed_along(west_edge[..., :GY], ("face", "blk"), -BY)
        paired = jnp.stack([from_east, from_west])
        collected = lax.all_gather(paired, "blk", axis=3, tiled=True)
        seam_east = collected[0][..., (block_cols - 1) * size_y + east_partner]
        seam_west = collected[1][..., west_partner]
        seam_east = orient(seam_east, east_flip, flip_signs)
        seam_west = orient(seam_west, west_flip, flip_signs)
        last_east = jnp.where(at_east, seam_east, from_east)
        first_west = jnp.where(at_west, seam_west, from_west)
        partner_east = jnp.concatenate([west_edge[..., GY:], last_east], -1)
        partner_west = jnp.concatenate([first_west, east_edge[..., : elements - GY]], -1)
        return (
            stacked.at[:, points - 1]
            .set(east_edge + partner_east)
            .at[:, 0]
            .set(west_edge + partner_west)
        )

    def y_pass(stacked):
        north_edge = stacked[:, :, points - 1]
        south_edge = stacked[:, :, 0]
        top_rows = north_edge[..., GY - 1 :: GY]
        bottom_rows = south_edge[..., 0::GY]
        from_above = from_behind(bottom_rows, "blk", -1)
        from_below = from_behind(top_rows, "blk", 1)
        from_above = jnp.where(keep_above, from_above, 0.0)
        from_below = jnp.where(keep_below, from_below, 0.0)
        partner_north = jnp.where(
            position == GY - 1,
            jnp.repeat(from_above, GY, axis=-1),
            jnp.roll(south_edge, -1, axis=-1),
        )
        partner_south = jnp.where(
            position == 0, jnp.repeat(from_below, GY, axis=-1), jnp.roll(north_edge, 1, axis=-1)
        )
        return (
            stacked.at[:, :, points - 1]
            .set(north_edge + partner_north)
            .at[:, :, 0]
            .set(south_edge + partner_south)
        )

    def edge_sum(stacked, flip_signs):
        return y_pass(x_pass(stacked, flip_signs))

    weights, derivative = gll_tables(points)
    area_grid = jnp.take(jacobian, slot_row, axis=2)[None]
    depth_grid = jnp.take(water_depth, slot_row, axis=2)[None]
    spin_grid = jnp.take(coriolis, slot_row, axis=2)[None]
    tide_grid = jnp.take(tide_height, slot_row, axis=2)[None]
    root_area = jnp.sqrt(area_grid)
    mass_grid = (weights[:, None] * weights[None, :])[None, :, :, None] * area_grid
    vector_signs = jnp.array([1.0, 1.0, -1.0], dtype=jnp.float32)
    scalar_signs = jnp.ones((1,), dtype=jnp.float32)
    mass_sum = edge_sum(mass_grid, scalar_signs)

    def average(stacked):
        return edge_sum(mass_grid * stacked, vector_signs) / mass_sum

    def tendency(current):
        height_diff = current[0:1] - tide_grid
        slopes_x = along_x(
            derivative, jnp.concatenate([height_diff, root_area * depth_grid * current[1:2]], 0)
        )
        slopes_y = along_y(
            derivative, jnp.concatenate([height_diff, root_area * depth_grid * current[2:3]], 0)
        )
        spread = (slopes_x[1:2] + slopes_y[1:2]) / area_grid
        return jnp.concatenate(
            [
                -spread,
                -slopes_x[0:1] / root_area + spin_grid * current[2:3],
                -slopes_y[0:1] / root_area - spin_grid * current[1:2],
            ],
            0,
        )

    def laplace(stacked):
        return (
            along_x(derivative, along_x(derivative, stacked))
            + along_y(derivative, along_y(derivative, stacked))
        ) / area_grid

    current = jnp.take(fields, slot_row, axis=3)
    section_one = current + time_step * average(tendency(current))
    section_two = 0.75 * current + 0.25 * (section_one + time_step * average(tendency(section_one)))
    section_three = current / 3.0 + 2.0 / 3.0 * (
        section_two + time_step * average(tendency(section_two))
    )
    biharmonic = average(laplace(average(laplace(section_three))))
    stepped = section_three - time_step * hyper_coeff * biharmonic
    return jnp.zeros_like(fields).at[:, :, :, slot_row].set(stepped)


def solution(mesh):
    return jax.shard_map(
        on_device,
        mesh=mesh,
        in_specs=(
            P(None, None, None, ("face", "blk")),
            P(None, None, ("face", "blk")),
            P(None, None, ("face", "blk")),
            P(None, None, ("face", "blk")),
            P(None, None, ("face", "blk")),
            P(("face", "blk"), None),
            P(),
        ),
        out_specs=P(None, None, None, ("face", "blk")),
        check_vma=False,
    )
```

profile of v0, /device:TPU:0, one launch (start us, length us, event | category | flops | bytes accessed | tf_op | source)
XLA Modules:
  0.0 317.7 jit_solution(3846976248319593328)
XLA Ops:
  6.2 2.9 collective-permute-start.5
  19.2 2.1 copy.2796
  21.4 3.0 gather_fusion
  29.6 2.1 collective-permute-start
  32.4 24.7 %scatter_fusion = s32[2,256]{1,0:T(2,128)S(1)} fusion(s32[2,256]{1,0:T(2,128)S(1)} %broadcast.546, s32[512]{0:T(512)S(1)} %bitcast.502, s32[512]{0:T(512)S(1)} %bitcast.569), kind=kCustom, calls=%fused_computation.19 | custom fusion | bytes 10240 | tf_op jit(solution)/shard_map/scatter | solution.py:91
  60.7 23.0 %all_gather.19 = f32[2,1,8,256]{2,3,1,0:T(8,128)S(1)} all-gather(f32[2,1,8,16]{2,3,1,0:T(8,128)S(1)} %pad_maximum_fusion.13), channel_id=1, replica_groups=mesh['face'=2,'blk'=16] {'blk'}, dimensions={3}, use_global_device_ids=true | all-gather | bytes 17408 | tf_op jit(solution)/shard_map/all_gather | solution.py:128
  87.0 2.2 collective-permute-start.7
  92.9 21.6 %all_gather.18 = f32[2,3,8,256]{2,0,1,3:T(2,128)S(1)} all-gather(f32[2,3,8,16]{2,0,1,3:T(2,128)S(1)} %copy.2817), channel_id=1, replica_groups=mesh['face'=2,'blk'=16] {'blk'}, dimensions={3}, use_global_device_ids=true | all-gather | bytes 52224 | tf_op jit(solution)/shard_map/all_gather | solution.py:128
  118.9 2.2 collective-permute-start.3
  131.1 21.6 %all_gather.20 = f32[2,3,8,256]{2,0,1,3:T(2,128)S(1)} all-gather(f32[2,3,8,16]{2,0,1,3:T(2,128)S(1)} %copy.2858), channel_id=1, replica_groups=mesh['face'=2,'blk'=16] {'blk'}, dimensions={3}, use_global_device_ids=true | all-gather | bytes 52224 | tf_op jit(solution)/shard_map/all_gather | solution.py:128
  158.3 1.7 collective-permute-done.10
  160.5 4.2 %collective-permute-start.11 = (f32[3,8,16]{2,1,0:T(8,128)S(1)}, f32[3,8,16]{2,1,0:T(8,128)S(1)}, u32[]{:S(2)}, u32[]{:S(2)}) collective-permute-start(f32[3,8,16]{2,1,0:T(8,128)S(1)} %slice.1032), channel_id=1, source_target_pairs={{0,1},{1,2},{2,3},{3,4},{4,5},{5,6},{6,7},{7,8},{8,9},{9,10},{10,1... | collective-permute-start | bytes 4616 | tf_op jit(solution)/shard_map/ppermute | solution.py:24
  171.1 21.5 %all_gather.21 = f32[2,3,8,256]{2,0,1,3:T(2,128)S(1)} all-gather(f32[2,3,8,16]{2,0,1,3:T(2,128)S(1)} %copy.2883), channel_id=1, replica_groups=mesh['face'=2,'blk'=16] {'blk'}, dimensions={3}, use_global_device_ids=true | all-gather | bytes 52224 | tf_op jit(solution)/shard_map/all_gather | solution.py:128
  198.1 1.7 collective-permute-done.14
  200.4 4.2 %collective-permute-start.15 = (f32[3,8,16]{2,1,0:T(8,128)S(1)}, f32[3,8,16]{2,1,0:T(8,128)S(1)}, u32[]{:S(2)}, u32[]{:S(2)}) collective-permute-start(f32[3,8,16]{2,1,0:T(8,128)S(1)} %slice.1055), channel_id=1, source_target_pairs={{0,1},{1,2},{2,3},{3,4},{4,5},{5,6},{6,7},{7,8},{8,9},{9,10},{10,1... | collective-permute-start | bytes 4616 | tf_op jit(solution)/shard_map/ppermute | solution.py:24
  212.5 21.5 %all_gather.22 = f32[2,3,8,256]{2,0,1,3:T(2,128)S(1)} all-gather(f32[2,3,8,16]{2,0,1,3:T(2,128)S(1)} %copy.2901), channel_id=1, replica_groups=mesh['face'=2,'blk'=16] {'blk'}, dimensions={3}, use_global_device_ids=true | all-gather | bytes 52224 | tf_op jit(solution)/shard_map/all_gather | solution.py:128
  239.5 1.7 collective-permute-done.18
  241.7 4.4 %collective-permute-start.19 = (f32[3,8,16]{2,1,0:T(8,128)S(1)}, f32[3,8,16]{2,1,0:T(8,128)S(1)}, u32[]{:S(2)}, u32[]{:S(2)}) collective-permute-start(f32[3,8,16]{2,1,0:T(8,128)S(1)} %slice.1071), channel_id=1, source_target_pairs={{0,1},{1,2},{2,3},{3,4},{4,5},{5,6},{6,7},{7,8},{8,9},{9,10},{10,1... | collective-permute-start | bytes 4616 | tf_op jit(solution)/shard_map/ppermute | solution.py:24
  252.9 21.4 %all_gather.23 = f32[2,3,8,256]{2,0,1,3:T(2,128)S(1)} all-gather(f32[2,3,8,16]{2,0,1,3:T(2,128)S(1)} %copy.2920), channel_id=1, replica_groups=mesh['face'=2,'blk'=16] {'blk'}, dimensions={3}, use_global_device_ids=true | all-gather | bytes 52224 | tf_op jit(solution)/shard_map/all_gather | solution.py:128
  279.9 1.7 collective-permute-done.22
  282.1 4.2 %collective-permute-start.23 = (f32[3,8,16]{2,1,0:T(8,128)S(1)}, f32[3,8,16]{2,1,0:T(8,128)S(1)}, u32[]{:S(2)}, u32[]{:S(2)}) collective-permute-start(f32[3,8,16]{2,1,0:T(8,128)S(1)} %slice.1087), channel_id=1, source_target_pairs={{0,1},{1,2},{2,3},{3,4},{4,5},{5,6},{6,7},{7,8},{8,9},{9,10},{10,1... | collective-permute-start | bytes 4616 | tf_op jit(solution)/shard_map/ppermute | solution.py:24
  287.5 2.1 copy.2932
  289.8 26.2 %scatter_fusion.1 = f32[3,8,8,256]{2,1,3,0:T(8,128)S(1)} fusion(f32[3,8,8,256]{2,1,3,0:T(8,128)S(1)} %broadcast_in_dim.171, s32[256]{0:T(256)S(1)} %bitcast.566, f32[256,3,8,8]{3,2,1,0:T(8,128)} %copy.2932), kind=kCustom, calls=%fused_computation.20 | custom fusion | bytes 590848 | tf_op jit(solution)/shard_map/scatter | solution.py:217
  316.0 1.8 copy.2933
  (389 shorter events, 92.1 us)
Async XLA Ops:
  6.2 53.0 %collective-permute-start.5 = (f32[1,8,16]{2,0,1:T(1,128)}, f32[1,8,16]{2,0,1:T(1,128)}, u32[]{:S(2)}, u32[]{:S(2)}) collective-permute-start(f32[1,8,16]{2,0,1:T(1,128)} %slice.1155), channel_id=1, source_target_pairs={{0,16},{1,17},{2,18},{3,19},{4,20},{5,21},{6,22},{7,23},{8,24},{9,... | collective-permute-start | bytes 1544 | tf_op jit(solution)/shard_map/ppermute | solution.py:18
  9.8 50.2 %collective-permute-start.4 = (f32[1,8,16]{2,0,1:T(1,128)}, f32[1,8,16]{2,0,1:T(1,128)}, u32[]{:S(2)}, u32[]{:S(2)}) collective-permute-start(f32[1,8,16]{2,0,1:T(1,128)} %slice.1154), channel_id=1, source_target_pairs={{0,16},{1,17},{2,18},{3,19},{4,20},{5,21},{6,22},{7,23},{8,24},{9,... | collective-permute-start | bytes 1544 | tf_op jit(solution)/shard_map/ppermute | solution.py:18
  29.6 63.1 %collective-permute-start = (f32[3,8,16]{2,1,0:T(8,128)S(1)}, f32[3,8,16]{2,1,0:T(8,128)S(1)}, u32[]{:S(2)}, u32[]{:S(2)}) collective-permute-start(f32[3,8,16]{2,1,0:T(8,128)S(1)} %slice.1140), channel_id=1, source_target_pairs={{0,16},{1,17},{2,18},{3,19},{4,20},{5,21},{6,22},{7,23},{8,24},{9,... | collective-permute-start | bytes 4616 | tf_op jit(solution)/shard_map/ppermute | solution.py:18
  31.8 61.0 %collective-permute-start.1 = (f32[3,8,16]{2,1,0:T(8,128)S(1)}, f32[3,8,16]{2,1,0:T(8,128)S(1)}, u32[]{:S(2)}, u32[]{:S(2)}) collective-permute-start(f32[3,8,16]{2,1,0:T(8,128)S(1)} %slice.1141), channel_id=1, source_target_pairs={{0,16},{1,17},{2,18},{3,19},{4,20},{5,21},{6,22},{7,23},{8,24},{9,... | collective-permute-start | bytes 4616 | tf_op jit(solution)/shard_map/ppermute | solution.py:18
  87.0 3.7 %collective-permute-start.7 = (f32[1,8,16]{2,1,0:T(8,128)S(1)}, f32[1,8,16]{2,1,0:T(8,128)S(1)}, u32[]{:S(2)}, u32[]{:S(2)}) collective-permute-start(f32[1,8,16]{2,1,0:T(8,128)S(1)} %slice.1009), channel_id=1, source_target_pairs={{0,1},{1,2},{2,3},{3,4},{4,5},{5,6},{6,7},{7,8},{8,9},{9,10},{10,1... | collective-permute-start | bytes 1544 | tf_op jit(solution)/shard_map/ppermute | solution.py:24
  89.4 3.1 collective-permute-start.6
  118.9 3.9 %collective-permute-start.3 = (f32[3,8,16]{2,1,0:T(8,128)S(1)}, f32[3,8,16]{2,1,0:T(8,128)S(1)}, u32[]{:S(2)}, u32[]{:S(2)}) collective-permute-start(f32[3,8,16]{2,1,0:T(8,128)S(1)} %slice.993), channel_id=1, source_target_pairs={{0,1},{1,2},{2,3},{3,4},{4,5},{5,6},{6,7},{7,8},{8,9},{9,10},{10,1... | collective-permute-start | bytes 4616 | tf_op jit(solution)/shard_map/ppermute | solution.py:24
  121.3 3.1 collective-permute-start.2
  125.7 3.7 %collective-permute-start.9 = (f32[3,8,16]{2,1,0:T(8,128)S(1)}, f32[3,8,16]{2,1,0:T(8,128)S(1)}, u32[]{:S(2)}, u32[]{:S(2)}) collective-permute-start(f32[3,8,16]{2,1,0:T(8,128)S(1)} %slice.1176), channel_id=1, source_target_pairs={{0,16},{1,17},{2,18},{3,19},{4,20},{5,21},{6,22},{7,23},{8,24},{9,... | collective-permute-start | bytes 4616 | tf_op jit(solution)/shard_map/ppermute | solution.py:18
  127.3 3.7 %collective-permute-start.8 = (f32[3,8,16]{2,1,0:T(8,128)S(1)}, f32[3,8,16]{2,1,0:T(8,128)S(1)}, u32[]{:S(2)}, u32[]{:S(2)}) collective-permute-start(f32[3,8,16]{2,1,0:T(8,128)S(1)} %slice.1175), channel_id=1, source_target_pairs={{0,16},{1,17},{2,18},{3,19},{4,20},{5,21},{6,22},{7,23},{8,24},{9,... | collective-permute-start | bytes 4616 | tf_op jit(solution)/shard_map/ppermute | solution.py:18
  156.9 3.1 collective-permute-start.10
  160.5 5.0 %collective-permute-start.11 = (f32[3,8,16]{2,1,0:T(8,128)S(1)}, f32[3,8,16]{2,1,0:T(8,128)S(1)}, u32[]{:S(2)}, u32[]{:S(2)}) collective-permute-start(f32[3,8,16]{2,1,0:T(8,128)S(1)} %slice.1032), channel_id=1, source_target_pairs={{0,1},{1,2},{2,3},{3,4},{4,5},{5,6},{6,7},{7,8},{8,9},{9,10},{10,1... | collective-permute-start | bytes 4616 | tf_op jit(solution)/shard_map/ppermute | solution.py:24
  166.8 3.7 %collective-permute-start.13 = (f32[3,8,16]{2,1,0:T(8,128)S(1)}, f32[3,8,16]{2,1,0:T(8,128)S(1)}, u32[]{:S(2)}, u32[]{:S(2)}) collective-permute-start(f32[3,8,16]{2,1,0:T(8,128)S(1)} %slice.1197), channel_id=1, source_target_pairs={{0,16},{1,17},{2,18},{3,19},{4,20},{5,21},{6,22},{7,23},{8,24},{9,... | collective-permute-start | bytes 4616 | tf_op jit(solution)/shard_map/ppermute | solution.py:18
  167.3 3.7 %collective-permute-start.12 = (f32[3,8,16]{2,1,0:T(8,128)S(1)}, f32[3,8,16]{2,1,0:T(8,128)S(1)}, u32[]{:S(2)}, u32[]{:S(2)}) collective-permute-start(f32[3,8,16]{2,1,0:T(8,128)S(1)} %slice.1196), channel_id=1, source_target_pairs={{0,16},{1,17},{2,18},{3,19},{4,20},{5,21},{6,22},{7,23},{8,24},{9,... | collective-permute-start | bytes 4616 | tf_op jit(solution)/shard_map/ppermute | solution.py:18
  196.8 3.1 collective-permute-start.14
  200.4 5.0 %collective-permute-start.15 = (f32[3,8,16]{2,1,0:T(8,128)S(1)}, f32[3,8,16]{2,1,0:T(8,128)S(1)}, u32[]{:S(2)}, u32[]{:S(2)}) collective-permute-start(f32[3,8,16]{2,1,0:T(8,128)S(1)} %slice.1055), channel_id=1, source_target_pairs={{0,1},{1,2},{2,3},{3,4},{4,5},{5,6},{6,7},{7,8},{8,9},{9,10},{10,1... | collective-permute-start | bytes 4616 | tf_op jit(solution)/shard_map/ppermute | solution.py:24
  207.2 3.7 %collective-permute-start.17 = (f32[3,8,16]{2,1,0:T(8,128)S(1)}, f32[3,8,16]{2,1,0:T(8,128)S(1)}, u32[]{:S(2)}, u32[]{:S(2)}) collective-permute-start(f32[3,8,16]{2,1,0:T(8,128)S(1)} %slice.1211), channel_id=1, source_target_pairs={{0,16},{1,17},{2,18},{3,19},{4,20},{5,21},{6,22},{7,23},{8,24},{9,... | collective-permute-start | bytes 4616 | tf_op jit(solution)/shard_map/ppermute | solution.py:18
  208.7 3.7 %collective-permute-start.16 = (f32[3,8,16]{2,1,0:T(8,128)S(1)}, f32[3,8,16]{2,1,0:T(8,128)S(1)}, u32[]{:S(2)}, u32[]{:S(2)}) collective-permute-start(f32[3,8,16]{2,1,0:T(8,128)S(1)} %slice.1210), channel_id=1, source_target_pairs={{0,16},{1,17},{2,18},{3,19},{4,20},{5,21},{6,22},{7,23},{8,24},{9,... | collective-permute-start | bytes 4616 | tf_op jit(solution)/shard_map/ppermute | solution.py:18
  238.2 3.1 collective-permute-start.18
  241.7 5.0 %collective-permute-start.19 = (f32[3,8,16]{2,1,0:T(8,128)S(1)}, f32[3,8,16]{2,1,0:T(8,128)S(1)}, u32[]{:S(2)}, u32[]{:S(2)}) collective-permute-start(f32[3,8,16]{2,1,0:T(8,128)S(1)} %slice.1071), channel_id=1, source_target_pairs={{0,1},{1,2},{2,3},{3,4},{4,5},{5,6},{6,7},{7,8},{8,9},{9,10},{10,1... | collective-permute-start | bytes 4616 | tf_op jit(solution)/shard_map/ppermute | solution.py:24
  248.5 3.7 %collective-permute-start.21 = (f32[3,8,16]{2,1,0:T(8,128)S(1)}, f32[3,8,16]{2,1,0:T(8,128)S(1)}, u32[]{:S(2)}, u32[]{:S(2)}) collective-permute-start(f32[3,8,16]{2,1,0:T(8,128)S(1)} %slice.1225), channel_id=1, source_target_pairs={{0,16},{1,17},{2,18},{3,19},{4,20},{5,21},{6,22},{7,23},{8,24},{9,... | collective-permute-start | bytes 4616 | tf_op jit(solution)/shard_map/ppermute | solution.py:18
  249.1 3.7 %collective-permute-start.20 = (f32[3,8,16]{2,1,0:T(8,128)S(1)}, f32[3,8,16]{2,1,0:T(8,128)S(1)}, u32[]{:S(2)}, u32[]{:S(2)}) collective-permute-start(f32[3,8,16]{2,1,0:T(8,128)S(1)} %slice.1224), channel_id=1, source_target_pairs={{0,16},{1,17},{2,18},{3,19},{4,20},{5,21},{6,22},{7,23},{8,24},{9,... | collective-permute-start | bytes 4616 | tf_op jit(solution)/shard_map/ppermute | solution.py:18
  278.5 3.1 collective-permute-start.22
  282.1 5.0 %collective-permute-start.23 = (f32[3,8,16]{2,1,0:T(8,128)S(1)}, f32[3,8,16]{2,1,0:T(8,128)S(1)}, u32[]{:S(2)}, u32[]{:S(2)}) collective-permute-start(f32[3,8,16]{2,1,0:T(8,128)S(1)} %slice.1087), channel_id=1, source_target_pairs={{0,1},{1,2},{2,3},{3,4},{4,5},{5,6},{6,7},{7,8},{8,9},{9,10},{10,1... | collective-permute-start | bytes 4616 | tf_op jit(solution)/shard_map/ppermute | solution.py:24
  (14 other events, 208.0 us)
where the time goes:
time: 319 us; the launch traced here: 318 us
  blocking collectives  131 us (41%)
  local copies, waits for them, and re-layouts  97.4 us (31%)
  starting transfers between devices  42.6 us (13%)
  waiting for transfers between devices  22.7 us (7%)
  other arithmetic  17.9 us (6%)
  matrix products  4.85 us (2%)
    all_gather x6, blocking collectives, x_pass(): collected = lax.all_gather(paired, 'blk', axis=3, tiled=True)  131 us
    ppermute x12, starting transfers between devices, from_behind(): return lax.ppermute(value, axis, pairs)  29.4 us
    scatter x2, local copies, waits for them, and re-layouts, on_device(): return jnp.zeros_like(fields).at[:, :, :, slot_row].set(stepped)  27.9 us
    scatter x1, local copies, waits for them, and re-layouts, seam_parts(): inverse = jnp.zeros_like(seam_rows).at[jnp.arange(2)[:, None], seam_rows]...  24.7 us
    ppermute x12, starting transfers between devices, passed_along(): lax.ppermute(value, axis, [(i, (i + by) % count) for i in range(count)])  13.2 us
    ppermute x12, waiting for transfers between devices, from_behind(): return lax.ppermute(value, axis, pairs)  12.6 us
    ppermute x12, waiting for transfers between devices, passed_along(): lax.ppermute(value, axis, [(i, (i + by) % count) for i in range(count)])  10.2 us
    unnamed x57, local copies, waits for them, and re-layouts  6.68 us
  transfers between devices with their start and end apart: 24, of which 18 were waited for; matrix products, arithmetic and copies ran while one was open for 17% of the time, Pallas kernels for 0%

commit v1 on v0

v1 whole, which is shorter than its diff:
```python
import functools
import math

import jax
import jax.numpy as jnp
import ml_dtypes
import numpy as np
from jax import lax
from jax.experimental import pallas as pl
from jax.experimental.pallas import tpu as pltpu
from jax.sharding import PartitionSpec as P

BY = 16
GX = 16
GY = 16
NP = 8
NODES = NP * NP
ARRAYS = 7
ROWS = ARRAYS * NODES
EDGE_ROWS = 4 * NP
ALL_ROWS = ROWS + EDGE_ROWS
HALF_ROWS = ALL_ROWS // 2
RING_X = 4
RING_Y = 5
PITCH = GX + 2 * RING_X
MID = GY * PITCH
LANES = 128
EXT = MID + 2 * LANES
LEAD = LANES - RING_Y * PITCH
ELEMENTS = GX * GY

time_step = 0.03
hyper_coeff = 0.0002

f32 = jnp.float32
bf16 = jnp.bfloat16
i32 = jnp.int32


def legendre_pair(location, degree):
    lower_value = 1.0
    upper_value = location
    for polynomial_order in range(2, degree + 1):
        lower_value, upper_value = (
            upper_value,
            (
                (2 * polynomial_order - 1) * location * upper_value
                - (polynomial_order - 1) * lower_value
            )
            / polynomial_order,
        )
    return (lower_value, upper_value)


def gll_tables(points):
    degree = points - 1
    locations = [-math.cos(math.pi * position / degree) for position in range(points)]
    for iteration in range(100):
        updated = []
        for location in locations:
            lower_value, upper_value = legendre_pair(location, degree)
            updated.append(
                location - (location * upper_value - lower_value) / ((degree + 1) * upper_value)
            )
        locations = updated
    locations[0] = -1.0
    locations[degree] = 1.0
    legendre_at = [legendre_pair(location, degree)[1] for location in locations]
    weights = [2.0 / (degree * (degree + 1) * value * value) for value in legendre_at]
    corner_value = degree * (degree + 1) / 4.0
    derivative = []
    for row_index in range(points):
        row_values = []
        for column_index in range(points):
            if row_index != column_index:
                row_values.append(
                    legendre_at[row_index]
                    / (legendre_at[column_index] * (locations[row_index] - locations[column_index]))
                )
            elif row_index == 0:
                row_values.append(-corner_value)
            elif row_index == degree:
                row_values.append(corner_value)
            else:
                row_values.append(0.0)
        derivative.append(row_values)
    return np.asarray(weights, np.float64), np.asarray(derivative, np.float64)


def in_three(matrix):
    high = matrix.astype(ml_dtypes.bfloat16)
    low = (matrix - high.astype(np.float64)).astype(ml_dtypes.bfloat16)
    return np.concatenate([high, high, low], 1)


def operator_table():
    weights, derivative = gll_tables(NP)
    eye = np.eye(NP)
    node_weight = np.outer(weights, weights).reshape(NODES, 1)
    along_x = node_weight * np.kron(derivative, eye)
    along_y = node_weight * np.kron(eye, derivative)
    second = derivative @ derivative
    both = node_weight * (np.kron(second, eye) + np.kron(eye, second))
    table = np.zeros((4 * NODES, 6 * NODES), ml_dtypes.bfloat16)
    table[:NODES, : 3 * NODES] = in_three(along_x)
    table[NODES : 2 * NODES, : 3 * NODES] = in_three(along_y)
    table[2 * NODES : 3 * NODES, : 3 * NODES] = in_three(along_x)
    table[2 * NODES : 3 * NODES, 3 * NODES :] = in_three(along_y)
    table[3 * NODES :, : 3 * NODES] = in_three(both)
    spread = np.broadcast_to(node_weight, (NODES, LANES)).astype(np.float32)
    return table, np.ascontiguousarray(spread)


def lane_tables():
    table = np.zeros((24, MID), np.int32)
    for lane in range(MID):
        row, col = divmod(lane, PITCH)
        x = col - RING_X
        own = 0 <= x < GX
        table[0:8, lane] = x * GY + row if own else -1
        if not own:
            table[8:16, lane] = row * RING_X + (col if x < 0 else x - GX)
        table[16:24, lane] = 0 if own else (1 if x < 0 else 2)
    ext = np.zeros((8, EXT), np.int32)
    for lane in range(EXT):
        row, col = divmod(lane - LEAD, PITCH)
        y = row - RING_Y
        x = col - RING_X
        ext[0, lane] = x in (-RING_X, GX + RING_X - 1)
        ext[1, lane] = y == GY - 1
        ext[2, lane] = y == 0
        ext[3, lane] = 0 <= y < GY and 0 <= x < GX
    return table, ext


def exact_pieces(values):
    high = values.astype(bf16)
    rest = values - high.astype(f32)
    middle = rest.astype(bf16)
    low = (rest - middle.astype(f32)).astype(bf16)
    return high, middle, low


def dot(a, b):
    return jnp.dot(a, b, preferred_element_type=f32)


def dot_other(a, b):
    return lax.dot_general(a, b, (((1,), (1,)), ((), ())), preferred_element_type=f32)


def picked(values, one_hot, product=dot):
    high, middle, low = exact_pieces(values)
    return (product(high, one_hot) + product(middle, one_hot)) + product(low, one_hot)


def as_one_hot(row_of_lane, depth):
    index = lax.broadcasted_iota(i32, (depth, row_of_lane.shape[1]), 0)
    return jnp.where(index == row_of_lane[0:1], 1.0, 0.0).astype(bf16)


def high_low_high(values):
    high = values.astype(bf16)
    low = (values - high.astype(f32)).astype(bf16)
    return [high, low, high]


def by_slot(slot_ref, cell_of_lane):
    slots = jnp.broadcast_to(slot_ref[...], (8, ELEMENTS)).astype(f32).astype(bf16)
    chosen = dot(slots, as_one_hot(cell_of_lane, ELEMENTS))
    chosen = jnp.where(cell_of_lane >= 0, chosen, -1.0)
    index = lax.broadcasted_iota(i32, (ELEMENTS, cell_of_lane.shape[1]), 0).astype(f32)
    return jnp.where(index == chosen[0:1], 1.0, 0.0).astype(bf16)


def stored_rows(fields_ref, others):
    parts = [fields_ref[...].reshape(3 * NODES, ELEMENTS)]
    parts += [ref[...].reshape(NODES, ELEMENTS) for ref in others]
    return jnp.concatenate(parts, 0)


def mass_tendency(table, h, u, v, tide, area_depth, weighted_area, spin):
    p = high_low_high(h - tide)
    slopes = dot(table[: 2 * NODES, : 3 * NODES], jnp.concatenate(p, 0))
    flux = high_low_high(area_depth * u) + high_low_high(area_depth * v)
    spread = dot(table[2 * NODES : 3 * NODES], jnp.concatenate(flux, 0))
    return [
        -spread,
        spin * v - weighted_area * slopes[:NODES],
        -spin * u - weighted_area * slopes[NODES:],
    ]


def seam_flags(seam_ref, block_cols):
    size_y = seam_ref.shape[1]
    face = lax.axis_index("face")
    blk = lax.axis_index("blk")
    block_x = blk // BY

    def flipped(k):
        return jnp.where(lax.rem(seam_ref[k, 1] - seam_ref[k, 0] + size_y, size_y) != 1, 1, 0)

    first, second = flipped(0), flipped(1)
    east_flip = jnp.where(face == 0, first, second)
    west_flip = jnp.where(face == 0, second, first)
    if block_cols == 1:
        return 1 - east_flip, 0, east_flip, 1
    at_east = jnp.where(block_x == block_cols - 1, east_flip, 0)
    at_west = jnp.where(block_x == 0, west_flip, 0)
    return 1, at_east, 0, at_west


def strips_kernel(
    block_cols, seam_ref, slot_ref, fields_ref, area_ref, depth_ref, spin_ref, tide_ref,
    table_ref, weight_ref, out0_ref, out1_ref,
):
    east0, flip0, east1, flip1 = seam_flags(seam_ref, block_cols)
    lane = lax.broadcasted_iota(i32, (8, 2 * LANES), 1)
    second = (lane & 64) != 0
    place = lane & 63
    row = place >> 2
    row = jnp.where(jnp.where(second, flip1, flip0) != 0, GY - 1 - row, row)
    east = jnp.where(second, east1, east0) != 0
    col = jnp.where(east, GX - RING_X, 0) + (place & 3)
    col = jnp.where(lane >= LANES, jnp.where(east, GX - RING_X - 1, RING_X), col)
    one_hot = by_slot(slot_ref, col * GY + row)
    stored = stored_rows(fields_ref, (area_ref, depth_ref, spin_ref, tide_ref))
    both = picked(stored, one_hot)

    lane = lax.broadcasted_iota(i32, (1, LANES), 1)
    second = lane >= 64
    flip = jnp.where(second, flip1, flip0) != 0
    sign = jnp.where(flip, -1.0, 1.0)
    node = lax.broadcasted_iota(i32, (1, NP, 1), 1)

    def in_frame(values):
        shaped = values.reshape(-1, NP, LANES)
        turned = pltpu.roll(shaped, 4, 1)
        turned = jnp.where((node & 2) == 0, pltpu.roll(turned, 6, 1), pltpu.roll(turned, 2, 1))
        turned = jnp.where((node & 1) == 0, pltpu.roll(turned, 7, 1), pltpu.roll(turned, 1, 1))
        values = jnp.where(flip[None], turned, shaped).reshape(values.shape)
        parts = [values[k * NODES : (k + 1) * NODES] for k in range(ARRAYS)]
        parts[2] = parts[2] * sign
        parts[5] = parts[5] * sign
        return parts

    strip = in_frame(both[:, :LANES])
    h, u, v, area, depth, spin, tide = in_frame(both[:, LANES:])
    root = jnp.sqrt(area)
    mass = weight_ref[...] * area
    edges = mass_tendency(
        table_ref[...], h, u, v, tide, root * depth, root, mass * spin
    ) + [mass]
    east = jnp.where(second, east1, east0) != 0
    edges = [jnp.where(east, part[NODES - NP :], part[:NP]) for part in edges]
    whole = jnp.concatenate(strip + edges, 0)
    top, bottom = whole[:HALF_ROWS], whole[HALF_ROWS:]
    out0_ref[...] = jnp.where(second, pltpu.roll(bottom, 64, 1), top)
    out1_ref[...] = jnp.where(second, bottom, pltpu.roll(top, 64, 1))


def own_kernel(
    slot_ref, fields_ref, area_ref, depth_ref, spin_ref, tide_ref, lanes_ref, own_ref, hot_ref
):
    one_hot = by_slot(slot_ref, lanes_ref[0:8])
    stored = stored_rows(fields_ref, (area_ref, depth_ref, spin_ref, tide_ref))
    own_ref[...] = picked(stored, one_hot)
    hot_ref[...] = one_hot


def middle_kernel(
    block_cols, seam_ref, in0_ref, in1_ref, own_ref, lanes_ref, low_ref, centre_ref, high_ref
):
    east0, flip0, east1, flip1 = seam_flags(seam_ref, block_cols)
    second = lax.broadcasted_iota(i32, (1, LANES), 1) >= 64
    in0, in1 = in0_ref[...], in1_ref[...]
    top = jnp.where(second, pltpu.roll(in1, 64, 1), in0)
    bottom = jnp.where(second, in1, pltpu.roll(in0, 64, 1))
    whole = jnp.concatenate([top, bottom], 0)
    side = lanes_ref[16:24]
    first_at = jnp.where(side == 2, 64 * (1 - east0), 64 * east0)
    place = jnp.where(side == 0, -1, lanes_ref[8:16] + first_at)
    placed = picked(whole, as_one_hot(place, LANES))
    for k, ref in enumerate((low_ref, centre_ref, high_ref)):
        part = slice(k * LANES, (k + 1) * LANES)
        ref[:ROWS] = placed[:ROWS, part] + own_ref[:, part]
        ref[ROWS:] = placed[ROWS:, part]


def steps_kernel(
    below_ref, low_ref, centre_ref, high_ref, above_ref, hot_ref, table_ref, weight_ref,
    ext_ref, out_ref, sums,
):
    tiles = (below_ref, low_ref, centre_ref, high_ref, above_ref)
    block_y = lax.rem(lax.axis_index("blk"), BY)

    def rows_of(start, count):
        return jnp.concatenate([ref[start : start + count] for ref in tiles], 1)

    table = table_ref[...]
    weight = jnp.concatenate([weight_ref[...]] * len(tiles), 1)
    at_rim = ext_ref[0:1] != 0
    top_row = jnp.where(block_y == BY - 1, ext_ref[1:2], 0) != 0
    bottom_row = jnp.where(block_y == 0, ext_ref[2:3], 0) != 0

    def edge_sum(parts, rims=None):
        count = len(parts) * NP
        for c, part in enumerate(parts):
            west, east = part[:NP], part[NODES - NP :]
            at_east = pltpu.roll(west, EXT - 1, 1)
            at_west = pltpu.roll(east, 1, 1)
            if rims is not None:
                at_east = jnp.where(at_rim, rims[c], at_east)
                at_west = jnp.where(at_rim, rims[c], at_west)
            part = jnp.concatenate([west + at_west, part[NP : NODES - NP], east + at_east], 0)
            for k in range(len(tiles)):
                sums[k, c * NODES : (c + 1) * NODES] = part[:, k * LANES : (k + 1) * LANES]
        south_at, north_at = pl.ds(0, count, stride=NP), pl.ds(NP - 1, count, stride=NP)
        south = jnp.concatenate([sums[k, south_at] for k in range(len(tiles))], 1)
        north = jnp.concatenate([sums[k, north_at] for k in range(len(tiles))], 1)
        to_north = north + jnp.where(top_row, 0.0, pltpu.roll(south, EXT - PITCH, 1))
        to_south = south + jnp.where(bottom_row, 0.0, pltpu.roll(north, PITCH, 1))
        for k in range(len(tiles)):
            sums[k, south_at] = to_south[:, k * LANES : (k + 1) * LANES]
            sums[k, north_at] = to_north[:, k * LANES : (k + 1) * LANES]
        return [
            jnp.concatenate(
                [sums[k, c * NODES : (c + 1) * NODES] for k in range(len(tiles))], 1
            )
            for c in range(len(parts))
        ]

    start = [rows_of(c * NODES, NODES) for c in range(3)]
    area, depth, spin, tide = [rows_of(c * NODES, NODES) for c in range(3, ARRAYS)]
    root = jnp.sqrt(area)
    mass = weight * area
    mass_spin = mass * spin
    area_depth = root * depth
    per_mass = 1.0 / edge_sum([mass], [rows_of(ROWS + 3 * NP, NP)])[0]

    def average(parts, rims=None):
        return [part * per_mass for part in edge_sum(parts, rims)]

    def tendency(s):
        return mass_tendency(table, *s, tide, area_depth, root, mass_spin)

    def laplace(s):
        return [
            dot(table[3 * NODES :, : 3 * NODES], jnp.concatenate(high_low_high(part), 0))
            for part in s
        ]

    rims = [rows_of(ROWS + c * NP, NP) for c in range(3)]
    change = average(tendency(start), rims)
    one = [s + time_step * c for s, c in zip(start, change)]
    change = average(tendency(one))
    two = [0.75 * s + 0.25 * (o + time_step * c) for s, o, c in zip(start, one, change)]
    change = average(tendency(two))
    three = [s / 3.0 + 2.0 / 3.0 * (o + time_step * c) for s, o, c in zip(start, two, change)]
    biharmonic = average(laplace(average(laplace(three))))
    own = ext_ref[3:4, LANES : LANES + MID] != 0
    stepped = [
        jnp.where(
            own,
            (s - time_step * hyper_coeff * b)[:, LANES : LANES + MID],
            0.0,
        )
        for s, b in zip(three, biharmonic)
    ]
    stored = picked(jnp.concatenate(stepped, 0), hot_ref[...], dot_other)
    out_ref[...] = stored.reshape(out_ref.shape)


def on_device(fields, jacobian, water_depth, coriolis, tide_height, slot_of, seam_rows):
    block_cols = lax.axis_size("blk") // BY
    count = lax.axis_size("face") * lax.axis_size("blk")
    table, weight = operator_table()
    lanes, ext = lane_tables()
    table, weight, lanes, ext = (jnp.asarray(part) for part in (table, weight, lanes, ext))
    vmem = pl.BlockSpec(memory_space=pltpu.VMEM)
    smem = pl.BlockSpec(memory_space=pltpu.SMEM)
    params = pltpu.CompilerParams(vmem_limit_bytes=48 * 2**20)
    held = (fields, jacobian, water_depth, coriolis, tide_height)

    def call(kernel, ins, outs, cost, scratch=(), name=None):
        return pl.pallas_call(
            kernel,
            out_shape=[jax.ShapeDtypeStruct(*out) for out in outs],
            in_specs=[smem if spec is smem else vmem for spec, value in ins],
            out_specs=[vmem] * len(outs),
            scratch_shapes=list(scratch),
            compiler_params=params,
            cost_estimate=pl.CostEstimate(
                flops=cost, bytes_accessed=2 * 2**20, transcendentals=0
            ),
            name=name,
        )(*[value for spec, value in ins])

    strip = ((HALF_ROWS, LANES), f32)
    strip0, strip1 = call(
        functools.partial(strips_kernel, block_cols),
        [(smem, seam_rows)] + [(vmem, x) for x in (slot_of, *held, table, weight)],
        [strip, strip],
        10**8,
        name="strips",
    )
    span = block_cols * BY

    def rank(face, block_x, block_y):
        return face * span + block_x * BY + block_y

    both = ("face", "blk")
    places = [(f, x, y) for f in range(2) for x in range(block_cols) for y in range(BY)]
    if block_cols == 1:
        halo0 = lax.ppermute(
            strip0, both, [(rank(f, x, y), rank(1 - f, x, y)) for f, x, y in places]
        )
        halo1 = lax.ppermute(
            strip1, both, [(rank(f, x, y), rank(1 - f, x, BY - 1 - y)) for f, x, y in places]
        )
    else:
        last = block_cols - 1
        flipped = (seam_rows[:, 1] - seam_rows[:, 0]) % seam_rows.shape[1] != 1
        face = lax.axis_index("face")
        block_x = lax.axis_index("blk") // BY
        from_west = lax.ppermute(strip0, both, [(i, (i + BY) % count) for i in range(count)])
        from_east = lax.ppermute(strip1, both, [(i, (i - BY) % count) for i in range(count)])
        turned_west = lax.ppermute(
            strip0, both,
            [(rank(f, last, y), rank(1 - f, 0, BY - 1 - y)) for f in range(2) for y in range(BY)],
        )
        turned_east = lax.ppermute(
            strip1, both,
            [(rank(f, 0, y), rank(1 - f, last, BY - 1 - y)) for f in range(2) for y in range(BY)],
        )
        halo0 = jnp.where((block_x == last) & flipped[face], turned_east, from_east)
        halo1 = jnp.where((block_x == 0) & flipped[1 - face], turned_west, from_west)
    own, hot = call(
        own_kernel,
        [(vmem, x) for x in (slot_of, *held, lanes)],
        [((ROWS, MID), f32), ((ELEMENTS, MID), bf16)],
        3 * 10**8,
        name="own",
    )
    tile = ((ALL_ROWS, LANES), f32)
    low, centre, high = call(
        functools.partial(middle_kernel, block_cols),
        [(smem, seam_rows)] + [(vmem, x) for x in (halo0, halo1, own, lanes)],
        [tile, tile, tile],
        10**8,
        name="middle",
    )
    above = lax.ppermute(
        low, both, [(rank(f, x, y), rank(f, x, (y - 1) % BY)) for f, x, y in places]
    )
    below = lax.ppermute(
        high, both, [(rank(f, x, y), rank(f, x, (y + 1) % BY)) for f, x, y in places]
    )
    (stepped,) = call(
        steps_kernel,
        [(vmem, x) for x in (below, low, centre, high, above, hot, table, weight, ext)],
        [(fields.shape, f32)],
        10**9,
        scratch=[pltpu.VMEM((EXT // LANES, 3 * NODES, LANES), f32)],
        name="steps",
    )
    return stepped


def solution(mesh):
    return jax.shard_map(
        on_device,
        mesh=mesh,
        in_specs=(
            P(None, None, None, ("face", "blk")),
            P(None, None, ("face", "blk")),
            P(None, None, ("face", "blk")),
            P(None, None, ("face", "blk")),
            P(None, None, ("face", "blk")),
            P(("face", "blk"), None),
            P(),
        ),
        out_specs=P(None, None, None, ("face", "blk")),
        check_vma=False,
    )
```

time: 319 us -> 35.4 us (0.11)
  the two profiles are of different devices: /device:TPU:0 before, /device:TPU:1 now
where the time goes in v1:
time: 35.4 us; the launch traced here: 34.9 us
  waiting for transfers between devices  11.7 us (33%)
  starting transfers between devices  9.05 us (26%)
  local copies, waits for them, and re-layouts  7.37 us (21%)
  Pallas kernels  6.73 us (19%)
    unnamed x38, local copies, waits for them, and re-layouts  7.37 us
    pallas_call x4, Pallas kernels, call(): pl.pallas_call(kernel, out_shape=[jax.ShapeDtypeStruct(*out) for out in o...  6.73 us
    ppermute x1, waiting for transfers between devices, on_device(): lax.ppermute(low, both, [(rank(f, x, y), rank(f, x, (y - 1) % BY)) for f,...  5.11 us
    ppermute x1, starting transfers between devices, on_device(): lax.ppermute(strip1, both, [(rank(f, x, y), rank(1 - f, x, BY - 1 - y)) f...  5.09 us
    ppermute x1, waiting for transfers between devices, on_device(): lax.ppermute(strip1, both, [(rank(f, x, y), rank(1 - f, x, BY - 1 - y)) f...  3.45 us
    ppermute x1, waiting for transfers between devices, on_device(): lax.ppermute(high, both, [(rank(f, x, y), rank(f, x, (y + 1) % BY)) for f...  3.14 us
    ppermute x1, starting transfers between devices, on_device(): lax.ppermute(strip0, both, [(rank(f, x, y), rank(1 - f, x, y)) for f, x,...  2.06 us
    ppermute x1, starting transfers between devices, on_device(): lax.ppermute(high, both, [(rank(f, x, y), rank(f, x, (y + 1) % BY)) for f...  1.89 us
  transfers between devices with their start and end apart: 4, of which 3 were waited for; matrix products, arithmetic and copies ran while one was open for 0% of the time, Pallas kernels for 2%

profile of v1, /device:TPU:1, one launch (start us, length us, event | category | flops | bytes accessed | tf_op | source)
XLA Modules:
  0.0 34.9 jit_solution(9002172382343550756)
XLA Ops:
  0.0 0.9 %copy-done = f32[3,8,8,256]{3,2,1,0:T(8,128)S(1)} copy-done((f32[3,8,8,256]{3,2,1,0:T(8,128)S(1)}, f32[3,8,8,256]{3,2,1,0:T(8,128)}, u32[]{:S(2)}) %copy-start) | copy-done | bytes 196632
  0.9 0.9 %copy-done.2 = bf16[256,384]{1,0:T(8,128)(2,1)S(1)} copy-done((bf16[256,384]{1,0:T(8,128)(2,1)S(1)}, bf16[256,384]{1,0:T(8,128)(2,1)}, u32[]{:S(2)}) %copy-start.2) | copy-done | bytes 196632
  1.9 0.8 %copy-done.4 = f32[8,8,256]{2,1,0:T(8,128)S(1)} copy-done((f32[8,8,256]{2,1,0:T(8,128)S(1)}, f32[8,8,256]{2,1,0:T(8,128)}, u32[]{:S(2)}) %copy-start.4) | copy-done | bytes 65560
  2.7 0.8 %copy-done.6 = f32[8,8,256]{2,1,0:T(8,128)S(1)} copy-done((f32[8,8,256]{2,1,0:T(8,128)S(1)}, f32[8,8,256]{2,1,0:T(8,128)}, u32[]{:S(2)}) %copy-start.6) | copy-done | bytes 65560
  3.5 0.8 %copy-done.8 = f32[8,8,256]{2,1,0:T(8,128)S(1)} copy-done((f32[8,8,256]{2,1,0:T(8,128)S(1)}, f32[8,8,256]{2,1,0:T(8,128)}, u32[]{:S(2)}) %copy-start.8) | copy-done | bytes 65560
  4.4 0.8 %copy-done.10 = f32[8,8,256]{2,1,0:T(8,128)S(1)} copy-done((f32[8,8,256]{2,1,0:T(8,128)S(1)}, f32[8,8,256]{2,1,0:T(8,128)}, u32[]{:S(2)}) %copy-start.10) | copy-done | bytes 65560
  5.2 0.8 %copy-done.13 = f32[64,128]{1,0:T(8,128)S(1)} copy-done((f32[64,128]{1,0:T(8,128)S(1)}, f32[64,128]{1,0:T(8,128)}, u32[]{:S(2)}) %copy-start.13) | copy-done | bytes 32792
  6.0 0.7 %copy-done.15 = s32[2,256]{1,0:T(2,128)S(1)} copy-done((s32[2,256]{1,0:T(2,128)S(1)}, s32[2,256]{1,0:T(2,128)}, u32[]{:S(2)}) %copy-start.15) | copy-done | bytes 2072
  6.7 0.7 %copy-done.17 = s32[1,256]{1,0:T(1,128)S(1)} copy-done((s32[1,256]{1,0:T(1,128)S(1)}, s32[1,256]{1,0:T(1,128)}, u32[]{:S(2)}) %copy-start.17) | copy-done | bytes 1048
  7.4 0.0 copy-start.12
  7.4 1.4 %strips.1 = (f32[240,128]{1,0:T(8,128)S(1)}, f32[240,128]{1,0:T(8,128)S(1)}) custom-call(s32[2,256]{1,0:T(2,128)S(1)} %copy-done.15, s32[1,256]{1,0:T(1,128)S(1)} %copy-done.17, f32[3,8,8,256]{3,2,1,0:T(8,128)S(1)} %copy-done, f32[8,8,256]{2,1,0:T(8,128)S(1)} %copy-done.4, f32[8,8,256]{2,1,0:T(8,128)S(1)} %copy-done.6, f32[8,8,256]{2,1,0:T(8,128)S(1)} %copy-done.8, ...), custom_call_target="tpu_custom_call" | custom-call | flops 100000000 | bytes 2097152 | tf_op jit(solution)/shard_map/strips/pallas_call | solution.py:386
  8.8 2.1 %collective-permute-start = (f32[240,128]{1,0:T(8,128)S(1)}, f32[240,128]{1,0:T(8,128)S(1)}, u32[]{:S(2)}, u32[]{:S(2)}) collective-permute-start(f32[240,128]{1,0:T(8,128)S(1)} %get-tuple-element.12), channel_id=1, source_target_pairs={{0,16},{1,17},{2,18},{3,19},{4,20},{5,21},{6,22},{7,23},{8,24},{9,... | collective-permute-start | bytes 368648 | tf_op jit(solution)/shard_map/ppermute | solution.py:415
  10.8 5.1 %collective-permute-start.1 = (f32[240,128]{1,0:T(8,128)S(1)}, f32[240,128]{1,0:T(8,128)S(1)}, u32[]{:S(2)}, u32[]{:S(2)}) collective-permute-start(f32[240,128]{1,0:T(8,128)S(1)} %get-tuple-element.13), channel_id=1, source_target_pairs={{0,31},{1,30},{2,29},{3,28},{4,27},{5,26},{6,25},{7,24},{8,23},{9,... | collective-permute-start | bytes 368648 | tf_op jit(solution)/shard_map/ppermute | solution.py:418
  15.9 0.0 copy-done.1
  16.0 0.0 copy-start.16
  16.0 0.7 %own.1 = (f32[448,384]{1,0:T(8,128)S(1)}, bf16[256,384]{1,0:T(8,128)(2,1)S(1)}) custom-call(s32[1,256]{1,0:T(1,128)S(1)} %copy-done.17, f32[3,8,8,256]{3,2,1,0:T(8,128)S(1)} %copy-done.1, f32[8,8,256]{2,1,0:T(8,128)S(1)} %copy-done.5, f32[8,8,256]{2,1,0:T(8,128)S(1)} %copy-done.7, f32[8,8,256]{2,1,0:T(8,128)S(1)} %copy-done.9, f32[8,8,256]{2,1,0:T(8,128)S(1)} %copy-done.11, ...), custom_call_target="tpu_custom_call" | custom-call | flops 300000000 | bytes 2097152 | tf_op jit(solution)/shard_map/own/pallas_call | solution.py:386
  16.7 0.0 collective-permute-done.in0_ref
  16.7 3.5 %collective-permute-done.1.in1_ref = f32[240,128]{1,0:T(8,128)S(1)} collective-permute-done((f32[240,128]{1,0:T(8,128)S(1)}, f32[240,128]{1,0:T(8,128)S(1)}, u32[]{:S(2)}, u32[]{:S(2)}) %collective-permute-start.1) | collective-permute-done | bytes 122912 | tf_op jit(solution)/shard_map/ppermute | solution.py:418
  20.2 1.1 %middle.1 = (f32[480,128]{1,0:T(8,128)S(1)}, f32[480,128]{1,0:T(8,128)S(1)}, f32[480,128]{1,0:T(8,128)S(1)}) custom-call(s32[2,256]{1,0:T(2,128)S(1)} %copy-done.16, f32[240,128]{1,0:T(8,128)S(1)} %collective-permute-done.in0_ref, f32[240,128]{1,0:T(8,128)S(1)} %collective-permute-done.1.in1_ref, f32[448,384]{1,0:T(8,128)S(1)} %get-tuple-element.14.own_ref, ...), custom_call_target="tpu_custom_call" | custom-call | flops 100000000 | bytes 2097152 | tf_op jit(solution)/shard_map/middle/pallas_call | solution.py:386
  21.2 1.9 %collective-permute-start.2 = (f32[480,128]{1,0:T(8,128)S(1)}, f32[480,128]{1,0:T(8,128)S(1)}, u32[]{:S(2)}, u32[]{:S(2)}) collective-permute-start(f32[480,128]{1,0:T(8,128)S(1)} %get-tuple-element.15.high_ref), channel_id=1, source_target_pairs={{0,1},{1,2},{2,3},{3,4},{4,5},{5,6},{6,7},{7,8},{8,9},{9,10},{10,1... | collective-permute-start | bytes 737288 | tf_op jit(solution)/shard_map/ppermute | solution.py:456
  23.1 0.0 collective-permute-start.3
  23.1 3.1 %collective-permute-done.2.below_ref = f32[480,128]{1,0:T(8,128)S(1)} collective-permute-done((f32[480,128]{1,0:T(8,128)S(1)}, f32[480,128]{1,0:T(8,128)S(1)}, u32[]{:S(2)}, u32[]{:S(2)}) %collective-permute-start.2) | collective-permute-done | bytes 245792 | tf_op jit(solution)/shard_map/ppermute | solution.py:456
  26.3 5.1 %collective-permute-done.3.above_ref = f32[480,128]{1,0:T(8,128)S(1)} collective-permute-done((f32[480,128]{1,0:T(8,128)S(1)}, f32[480,128]{1,0:T(8,128)S(1)}, u32[]{:S(2)}, u32[]{:S(2)}) %collective-permute-start.3) | collective-permute-done | bytes 245792 | tf_op jit(solution)/shard_map/ppermute | solution.py:453
  31.4 3.6 %steps.1 = f32[3,8,8,256]{3,2,1,0:T(8,128)} custom-call(f32[480,128]{1,0:T(8,128)S(1)} %collective-permute-done.2.below_ref, f32[480,128]{1,0:T(8,128)S(1)} %get-tuple-element.16.low_ref, f32[480,128]{1,0:T(8,128)S(1)} %get-tuple-element.17.centre_ref, f32[480,128]{1,0:T(8,128)S(1)} %get-tuple-element.15.high_ref, ...), custom_call_target="tpu_custom_call" | custom-call | flops 1000000000 | bytes 2097152 | tf_op jit(solution)/shard_map/steps/pallas_call | solution.py:386
  (26 shorter events, 0.0 us)
Async XLA Ops:
  0.0 0.9 %copy-start = (f32[3,8,8,256]{3,2,1,0:T(8,128)S(1)}, f32[3,8,8,256]{3,2,1,0:T(8,128)}, u32[]{:S(2)}) copy-start(f32[3,8,8,256]{3,2,1,0:T(8,128)} %fields_ref.3) | copy-start | bytes 589828
  0.9 0.9 %copy-start.2 = (bf16[256,384]{1,0:T(8,128)(2,1)S(1)}, bf16[256,384]{1,0:T(8,128)(2,1)}, u32[]{:S(2)}) copy-start(bf16[256,384]{1,0:T(8,128)(2,1)} %constant.8.clone.table_ref) | copy-start | bytes 589828
  1.9 0.8 %copy-start.4 = (f32[8,8,256]{2,1,0:T(8,128)S(1)}, f32[8,8,256]{2,1,0:T(8,128)}, u32[]{:S(2)}) copy-start(f32[8,8,256]{2,1,0:T(8,128)} %area_ref.3) | copy-start | bytes 196612
  2.7 0.8 %copy-start.6 = (f32[8,8,256]{2,1,0:T(8,128)S(1)}, f32[8,8,256]{2,1,0:T(8,128)}, u32[]{:S(2)}) copy-start(f32[8,8,256]{2,1,0:T(8,128)} %depth_ref.3) | copy-start | bytes 196612
  3.5 0.8 %copy-start.8 = (f32[8,8,256]{2,1,0:T(8,128)S(1)}, f32[8,8,256]{2,1,0:T(8,128)}, u32[]{:S(2)}) copy-start(f32[8,8,256]{2,1,0:T(8,128)} %spin_ref.3) | copy-start | bytes 196612
  4.4 0.8 %copy-start.10 = (f32[8,8,256]{2,1,0:T(8,128)S(1)}, f32[8,8,256]{2,1,0:T(8,128)}, u32[]{:S(2)}) copy-start(f32[8,8,256]{2,1,0:T(8,128)} %tide_ref.3) | copy-start | bytes 196612
  5.2 0.8 %copy-start.13 = (f32[64,128]{1,0:T(8,128)S(1)}, f32[64,128]{1,0:T(8,128)}, u32[]{:S(2)}) copy-start(f32[64,128]{1,0:T(8,128)} %constant.9.clone.weight_ref) | copy-start | bytes 98308
  6.0 0.7 %copy-start.15 = (s32[2,256]{1,0:T(2,128)S(1)}, s32[2,256]{1,0:T(2,128)}, u32[]{:S(2)}) copy-start(s32[2,256]{1,0:T(2,128)} %seam_ref.3) | copy-start | bytes 6148
  6.7 0.7 %copy-start.17 = (s32[1,256]{1,0:T(1,128)S(1)}, s32[1,256]{1,0:T(1,128)}, u32[]{:S(2)}) copy-start(s32[1,256]{1,0:T(1,128)} %slot_ref.3) | copy-start | bytes 3076
  7.3 8.6 %copy-start.1 = (f32[3,8,8,256]{3,2,1,0:T(8,128)S(1)}, f32[3,8,8,256]{3,2,1,0:T(8,128)}, u32[]{:S(2)}) copy-start(f32[3,8,8,256]{3,2,1,0:T(8,128)} %fields_ref.3) | copy-start | bytes 589828
  7.3 8.6 %copy-start.5 = (f32[8,8,256]{2,1,0:T(8,128)S(1)}, f32[8,8,256]{2,1,0:T(8,128)}, u32[]{:S(2)}) copy-start(f32[8,8,256]{2,1,0:T(8,128)} %area_ref.3) | copy-start | bytes 196612
  7.3 8.6 %copy-start.7 = (f32[8,8,256]{2,1,0:T(8,128)S(1)}, f32[8,8,256]{2,1,0:T(8,128)}, u32[]{:S(2)}) copy-start(f32[8,8,256]{2,1,0:T(8,128)} %depth_ref.3) | copy-start | bytes 196612
  7.3 8.6 %copy-start.9 = (f32[8,8,256]{2,1,0:T(8,128)S(1)}, f32[8,8,256]{2,1,0:T(8,128)}, u32[]{:S(2)}) copy-start(f32[8,8,256]{2,1,0:T(8,128)} %spin_ref.3) | copy-start | bytes 196612
  7.3 8.6 %copy-start.11 = (f32[8,8,256]{2,1,0:T(8,128)S(1)}, f32[8,8,256]{2,1,0:T(8,128)}, u32[]{:S(2)}) copy-start(f32[8,8,256]{2,1,0:T(8,128)} %tide_ref.3) | copy-start | bytes 196612
  7.4 8.6 %copy-start.12 = (s32[24,384]{1,0:T(8,128)S(1)}, s32[24,384]{1,0:T(8,128)}, u32[]{:S(2)}) copy-start(s32[24,384]{1,0:T(8,128)} %constant.10.clone.lanes_ref) | copy-start | bytes 110596
  8.8 7.9 %collective-permute-start = (f32[240,128]{1,0:T(8,128)S(1)}, f32[240,128]{1,0:T(8,128)S(1)}, u32[]{:S(2)}, u32[]{:S(2)}) collective-permute-start(f32[240,128]{1,0:T(8,128)S(1)} %get-tuple-element.12), channel_id=1, source_target_pairs={{0,16},{1,17},{2,18},{3,19},{4,20},{5,21},{6,22},{7,23},{8,24},{9,... | collective-permute-start | bytes 368648 | tf_op jit(solution)/shard_map/ppermute | solution.py:415
  10.8 9.3 %collective-permute-start.1 = (f32[240,128]{1,0:T(8,128)S(1)}, f32[240,128]{1,0:T(8,128)S(1)}, u32[]{:S(2)}, u32[]{:S(2)}) collective-permute-start(f32[240,128]{1,0:T(8,128)S(1)} %get-tuple-element.13), channel_id=1, source_target_pairs={{0,31},{1,30},{2,29},{3,28},{4,27},{5,26},{6,25},{7,24},{8,23},{9,... | collective-permute-start | bytes 368648 | tf_op jit(solution)/shard_map/ppermute | solution.py:418
  16.0 4.2 %copy-start.16 = (s32[2,256]{1,0:T(2,128)S(1)}, s32[2,256]{1,0:T(2,128)}, u32[]{:S(2)}) copy-start(s32[2,256]{1,0:T(2,128)} %seam_ref.3) | copy-start | bytes 6148
  20.1 11.2 %copy-start.3 = (bf16[256,384]{1,0:T(8,128)(2,1)S(1)}, bf16[256,384]{1,0:T(8,128)(2,1)}, u32[]{:S(2)}) copy-start(bf16[256,384]{1,0:T(8,128)(2,1)} %constant.8.clone.table_ref) | copy-start | bytes 589828
  20.1 11.2 %copy-start.14 = (f32[64,128]{1,0:T(8,128)S(1)}, f32[64,128]{1,0:T(8,128)}, u32[]{:S(2)}) copy-start(f32[64,128]{1,0:T(8,128)} %constant.9.clone.weight_ref) | copy-start | bytes 98308
  20.1 11.2 %copy-start.18 = (s32[8,640]{1,0:T(8,128)S(1)}, s32[8,640]{1,0:T(8,128)}, u32[]{:S(2)}) copy-start(s32[8,640]{1,0:T(8,128)} %constant.11.clone.ext_ref) | copy-start | bytes 61444
  21.2 5.0 %collective-permute-start.2 = (f32[480,128]{1,0:T(8,128)S(1)}, f32[480,128]{1,0:T(8,128)S(1)}, u32[]{:S(2)}, u32[]{:S(2)}) collective-permute-start(f32[480,128]{1,0:T(8,128)S(1)} %get-tuple-element.15.high_ref), channel_id=1, source_target_pairs={{0,1},{1,2},{2,3},{3,4},{4,5},{5,6},{6,7},{7,8},{8,9},{9,10},{10,1... | collective-permute-start | bytes 737288 | tf_op jit(solution)/shard_map/ppermute | solution.py:456
  23.1 8.3 %collective-permute-start.3 = (f32[480,128]{1,0:T(8,128)S(1)}, f32[480,128]{1,0:T(8,128)S(1)}, u32[]{:S(2)}, u32[]{:S(2)}) collective-permute-start(f32[480,128]{1,0:T(8,128)S(1)} %get-tuple-element.16.low_ref), channel_id=1, source_target_pairs={{0,15},{1,0},{2,1},{3,2},{4,3},{5,4},{6,5},{7,6},{8,7},{9,8},{10,9... | collective-permute-start | bytes 737288 | tf_op jit(solution)/shard_map/ppermute | solution.py:453

commit v2 on v1

--- a/solution.py
+++ b/solution.py
@@ -108,7 +108,7 @@
     table[2 * NODES : 3 * NODES, 3 * NODES :] = in_three(along_y)
     table[3 * NODES :, : 3 * NODES] = in_three(both)
     spread = np.broadcast_to(node_weight, (NODES, LANES)).astype(np.float32)
-    return table, np.ascontiguousarray(spread)
+    return table.astype(np.float32), np.ascontiguousarray(spread)
 
 
 def lane_tables():
@@ -173,6 +173,17 @@
     return jnp.where(index == chosen[0:1], 1.0, 0.0).astype(bf16)
 
 
+def brought(sources, buffers, sems):
+    copies = [
+        pltpu.make_async_copy(source, buffer, sems.at[k])
+        for k, (source, buffer) in enumerate(zip(sources, buffers))
+    ]
+    for copy in copies:
+        copy.start()
+    for copy in copies:
+        copy.wait()
+
+
 def stored_rows(fields_ref, others):
     parts = [fields_ref[...].reshape(3 * NODES, ELEMENTS)]
     parts += [ref[...].reshape(NODES, ELEMENTS) for ref in others]
@@ -210,10 +221,11 @@
     return 1, at_east, 0, at_west
 
 
-def strips_kernel(
-    block_cols, seam_ref, slot_ref, fields_ref, area_ref, depth_ref, spin_ref, tide_ref,
-    table_ref, weight_ref, out0_ref, out1_ref,
-):
+def strips_kernel(block_cols, *refs):
+    sources, (out0_ref, out1_ref), buffers, sems = refs[:9], refs[9:11], refs[11:20], refs[20]
+    brought(sources, buffers, sems)
+    seam_ref, slot_ref, fields_ref, area_ref, depth_ref, spin_ref, tide_ref = buffers[:7]
+    table_ref, weight_ref = buffers[7:]
     east0, flip0, east1, flip1 = seam_flags(seam_ref, block_cols)
     lane = lax.broadcasted_iota(i32, (8, 2 * LANES), 1)
     second = (lane & 64) != 0
@@ -249,7 +261,7 @@
     root = jnp.sqrt(area)
     mass = weight_ref[...] * area
     edges = mass_tendency(
-        table_ref[...], h, u, v, tide, root * depth, root, mass * spin
+        table_ref[...].astype(bf16), h, u, v, tide, root * depth, root, mass * spin
     ) + [mass]
     east = jnp.where(second, east1, east0) != 0
     edges = [jnp.where(east, part[NODES - NP :], part[:NP]) for part in edges]
@@ -259,9 +271,10 @@
     out1_ref[...] = jnp.where(second, bottom, pltpu.roll(top, 64, 1))
 
 
-def own_kernel(
-    slot_ref, fields_ref, area_ref, depth_ref, spin_ref, tide_ref, lanes_ref, own_ref, hot_ref
-):
+def own_kernel(*refs):
+    sources, (own_ref, hot_ref), buffers, sems = refs[:7], refs[7:9], refs[9:16], refs[16]
+    brought(sources, buffers, sems)
+    slot_ref, fields_ref, area_ref, depth_ref, spin_ref, tide_ref, lanes_ref = buffers
     one_hot = by_slot(slot_ref, lanes_ref[0:8])
     stored = stored_rows(fields_ref, (area_ref, depth_ref, spin_ref, tide_ref))
     own_ref[...] = picked(stored, one_hot)
@@ -297,7 +310,7 @@
     def rows_of(start, count):
         return jnp.concatenate([ref[start : start + count] for ref in tiles], 1)
 
-    table = table_ref[...]
+    table = table_ref[...].astype(bf16)
     weight = jnp.concatenate([weight_ref[...]] * len(tiles), 1)
     at_rim = ext_ref[0:1] != 0
     top_row = jnp.where(block_y == BY - 1, ext_ref[1:2], 0) != 0
@@ -332,6 +345,7 @@
 
     start = [rows_of(c * NODES, NODES) for c in range(3)]
     area, depth, spin, tide = [rows_of(c * NODES, NODES) for c in range(3, ARRAYS)]
+    area = jnp.where(area > 0.0, area, 1.0)
     root = jnp.sqrt(area)
     mass = weight * area
     mass_spin = mass * spin
@@ -379,6 +393,7 @@
     table, weight, lanes, ext = (jnp.asarray(part) for part in (table, weight, lanes, ext))
     vmem = pl.BlockSpec(memory_space=pltpu.VMEM)
     smem = pl.BlockSpec(memory_space=pltpu.SMEM)
+    hbm = pl.BlockSpec(memory_space=pltpu.HBM)
     params = pltpu.CompilerParams(vmem_limit_bytes=48 * 2**20)
     held = (fields, jacobian, water_depth, coriolis, tide_height)
 
@@ -386,7 +401,7 @@
         return pl.pallas_call(
             kernel,
             out_shape=[jax.ShapeDtypeStruct(*out) for out in outs],
-            in_specs=[smem if spec is smem else vmem for spec, value in ins],
+            in_specs=[spec for spec, value in ins],
             out_specs=[vmem] * len(outs),
             scratch_shapes=list(scratch),
             compiler_params=params,
@@ -394,14 +409,26 @@
                 flops=cost, bytes_accessed=2 * 2**20, transcendentals=0
             ),
             name=name,
-        )(*[value for spec, value in ins])
+        )(
+            *[
+                pltpu.with_memory_space_constraint(value, pltpu.HBM) if spec is hbm else value
+                for spec, value in ins
+            ]
+        )
 
     strip = ((HALF_ROWS, LANES), f32)
+    def room(values, spaces=None):
+        spaces = spaces or [pltpu.VMEM] * len(values)
+        buffers = [space(x.shape, x.dtype) for space, x in zip(spaces, values)]
+        return buffers + [pltpu.SemaphoreType.DMA((len(values),))]
+
+    needed = (seam_rows, slot_of, *held, table, weight)
     strip0, strip1 = call(
         functools.partial(strips_kernel, block_cols),
-        [(smem, seam_rows)] + [(vmem, x) for x in (slot_of, *held, table, weight)],
+        [(hbm, x) for x in needed],
         [strip, strip],
         10**8,
+        scratch=room(needed, [pltpu.SMEM] + [pltpu.VMEM] * (len(needed) - 1)),
         name="strips",
     )
     span = block_cols * BY
@@ -412,11 +439,11 @@
     both = ("face", "blk")
     places = [(f, x, y) for f in range(2) for x in range(block_cols) for y in range(BY)]
     if block_cols == 1:
+        halo1 = lax.ppermute(
+            strip1, both, [(rank(f, x, y), rank(1 - f, x, BY - 1 - y)) for f, x, y in places]
+        )
         halo0 = lax.ppermute(
             strip0, both, [(rank(f, x, y), rank(1 - f, x, y)) for f, x, y in places]
-        )
-        halo1 = lax.ppermute(
-            strip1, both, [(rank(f, x, y), rank(1 - f, x, BY - 1 - y)) for f, x, y in places]
         )
     else:
         last = block_cols - 1
@@ -435,11 +462,13 @@
         )
         halo0 = jnp.where((block_x == last) & flipped[face], turned_east, from_east)
         halo1 = jnp.where((block_x == 0) & flipped[1 - face], turned_west, from_west)
+    needed = (slot_of, *held, lanes)
     own, hot = call(
         own_kernel,
-        [(vmem, x) for x in (slot_of, *held, lanes)],
+        [(hbm, x) for x in needed],
         [((ROWS, MID), f32), ((ELEMENTS, MID), bf16)],
         3 * 10**8,
+        scratch=room(needed),
         name="own",
     )
     tile = ((ALL_ROWS, LANES), f32)
@@ -451,10 +480,10 @@
         name="middle",
     )
     above = lax.ppermute(
-        low, both, [(rank(f, x, y), rank(f, x, (y - 1) % BY)) for f, x, y in places]
+        low, both, [(rank(f, x, y), rank(f, x, y - 1)) for f, x, y in places if y > 0]
     )
     below = lax.ppermute(
-        high, both, [(rank(f, x, y), rank(f, x, (y + 1) % BY)) for f, x, y in places]
+        high, both, [(rank(f, x, y), rank(f, x, y + 1)) for f, x, y in places if y < BY - 1]
     )
     (stepped,) = call(
         steps_kernel,

time: 35.4 us -> 30.5 us (0.86)
  the two profiles are of different devices: /device:TPU:1 before, /device:TPU:13 now
where the time goes in v2:
time: 30.5 us; the launch traced here: 30.3 us
  waiting for transfers between devices  12.7 us (42%)
  starting transfers between devices  8.95 us (29%)
  Pallas kernels  8.61 us (28%)
    pallas_call x4, Pallas kernels, call(): pl.pallas_call(kernel, out_shape=[jax.ShapeDtypeStruct(*out) for out in o...  8.61 us
    ppermute x1, waiting for transfers between devices, on_device(): lax.ppermute(strip1, both, [(rank(f, x, y), rank(1 - f, x, BY - 1 - y)) f...  6.19 us
    ppermute x1, waiting for transfers between devices, on_device(): lax.ppermute(low, both, [(rank(f, x, y), rank(f, x, y - 1)) for f, x, y i...  5.29 us
    ppermute x1, starting transfers between devices, on_device(): lax.ppermute(high, both, [(rank(f, x, y), rank(f, x, y + 1)) for f, x, y...  3.7 us
    ppermute x1, starting transfers between devices, on_device(): lax.ppermute(strip1, both, [(rank(f, x, y), rank(1 - f, x, BY - 1 - y)) f...  2.05 us
    ppermute x1, starting transfers between devices, on_device(): lax.ppermute(low, both, [(rank(f, x, y), rank(f, x, y - 1)) for f, x, y i...  1.92 us
    ppermute x1, starting transfers between devices, on_device(): lax.ppermute(strip0, both, [(rank(f, x, y), rank(1 - f, x, y)) for f, x,...  1.27 us
    ppermute x1, waiting for transfers between devices, on_device(): lax.ppermute(high, both, [(rank(f, x, y), rank(f, x, y + 1)) for f, x, y...  1.19 us
  transfers between devices with their start and end apart: 4, of which 3 were waited for; matrix products, arithmetic and copies ran while one was open for 0% of the time, Pallas kernels for 6%

profile of v2, /device:TPU:13, one launch (start us, length us, event | category | flops | bytes accessed | tf_op | source)
XLA Modules:
  0.0 30.3 jit_solution(3841866073214756415)
XLA Ops:
  0.0 2.2 %strips.1 = (f32[240,128]{1,0:T(8,128)S(1)}, f32[240,128]{1,0:T(8,128)S(1)}) custom-call(s32[2,256]{1,0:T(2,128)} %seam_ref.1, s32[1,256]{1,0:T(1,128)} %refs_0_.3, f32[3,8,8,256]{3,2,1,0:T(8,128)} %refs_1_.3, f32[8,8,256]{2,1,0:T(8,128)} %refs_2_.3, f32[8,8,256]{2,1,0:T(8,128)} %refs_3_.3, f32[8,8,256]{2,1,0:T(8,128)} %refs_4_.3, f32[8,8,256]{2,1,0:T(8,128)} %refs_5_.3, ...), custom_call_target="tpu_custom_call" | custom-call | flops 100000000 | bytes 2097152 | tf_op jit(solution)/shard_map/strips/pallas_call | solution.py:401
  2.2 1.3 %collective-permute-start = (f32[240,128]{1,0:T(8,128)S(1)}, f32[240,128]{1,0:T(8,128)S(1)}, u32[]{:S(2)}, u32[]{:S(2)}) collective-permute-start(f32[240,128]{1,0:T(8,128)S(1)} %get-tuple-element.12), channel_id=1, source_target_pairs={{0,16},{1,17},{2,18},{3,19},{4,20},{5,21},{6,22},{7,23},{8,24},{9,... | collective-permute-start | bytes 368648 | tf_op jit(solution)/shard_map/ppermute | solution.py:445
  3.5 0.0 copy-start.1
  3.5 2.1 %collective-permute-start.1 = (f32[240,128]{1,0:T(8,128)S(1)}, f32[240,128]{1,0:T(8,128)S(1)}, u32[]{:S(2)}, u32[]{:S(2)}) collective-permute-start(f32[240,128]{1,0:T(8,128)S(1)} %get-tuple-element.13), channel_id=1, source_target_pairs={{0,31},{1,30},{2,29},{3,28},{4,27},{5,26},{6,25},{7,24},{8,23},{9,... | collective-permute-start | bytes 368648 | tf_op jit(solution)/shard_map/ppermute | solution.py:442
  5.5 0.0 copy-start.3
  5.5 1.8 %own.1 = (f32[448,384]{1,0:T(8,128)S(1)}, bf16[256,384]{1,0:T(8,128)(2,1)S(1)}) custom-call(s32[1,256]{1,0:T(1,128)} %refs_0_.3, f32[3,8,8,256]{3,2,1,0:T(8,128)} %refs_1_.3, f32[8,8,256]{2,1,0:T(8,128)} %refs_2_.3, f32[8,8,256]{2,1,0:T(8,128)} %refs_3_.3, f32[8,8,256]{2,1,0:T(8,128)} %refs_4_.3, f32[8,8,256]{2,1,0:T(8,128)} %refs_5_.3, ...), custom_call_target="tpu_custom_call" | custom-call | flops 300000000 | bytes 2097152 | tf_op jit(solution)/shard_map/own/pallas_call | solution.py:401
  7.3 0.0 collective-permute-done.in0_ref
  7.4 6.2 %collective-permute-done.1.in1_ref = f32[240,128]{1,0:T(8,128)S(1)} collective-permute-done((f32[240,128]{1,0:T(8,128)S(1)}, f32[240,128]{1,0:T(8,128)S(1)}, u32[]{:S(2)}, u32[]{:S(2)}) %collective-permute-start.1) | collective-permute-done | bytes 122912 | tf_op jit(solution)/shard_map/ppermute | solution.py:442
  13.5 0.0 copy-done.1
  13.5 0.0 copy-done.3
  13.5 0.0 copy-start
  13.6 0.0 copy-start.2
  13.6 0.0 copy-start.4
  13.6 1.1 %middle.1 = (f32[480,128]{1,0:T(8,128)S(1)}, f32[480,128]{1,0:T(8,128)S(1)}, f32[480,128]{1,0:T(8,128)S(1)}) custom-call(s32[2,256]{1,0:T(2,128)S(1)} %copy-done.3, f32[240,128]{1,0:T(8,128)S(1)} %collective-permute-done.in0_ref, f32[240,128]{1,0:T(8,128)S(1)} %collective-permute-done.1.in1_ref, f32[448,384]{1,0:T(8,128)S(1)} %get-tuple-element.14.own_ref, ...), custom_call_target="tpu_custom_call" | custom-call | flops 100000000 | bytes 2097152 | tf_op jit(solution)/shard_map/middle/pallas_call | solution.py:401
  14.7 3.7 %collective-permute-start.2 = (f32[480,128]{1,0:T(8,128)S(1)}, f32[480,128]{1,0:T(8,128)S(1)}, u32[]{:S(2)}, u32[]{:S(2)}) collective-permute-start(f32[480,128]{1,0:T(8,128)S(1)} %get-tuple-element.15.high_ref), channel_id=1, source_target_pairs={{0,1},{1,2},{2,3},{3,4},{4,5},{5,6},{6,7},{7,8},{8,9},{9,10},{10,1... | collective-permute-start | bytes 737288 | tf_op jit(solution)/shard_map/ppermute | solution.py:485
  18.4 1.9 %collective-permute-start.3 = (f32[480,128]{1,0:T(8,128)S(1)}, f32[480,128]{1,0:T(8,128)S(1)}, u32[]{:S(2)}, u32[]{:S(2)}) collective-permute-start(f32[480,128]{1,0:T(8,128)S(1)} %get-tuple-element.16.low_ref), channel_id=1, source_target_pairs={{1,0},{2,1},{3,2},{4,3},{5,4},{6,5},{7,6},{8,7},{9,8},{10,9},{11,1... | collective-permute-start | bytes 737288 | tf_op jit(solution)/shard_map/ppermute | solution.py:482
  20.3 1.2 %collective-permute-done.2.below_ref = f32[480,128]{1,0:T(8,128)S(1)} collective-permute-done((f32[480,128]{1,0:T(8,128)S(1)}, f32[480,128]{1,0:T(8,128)S(1)}, u32[]{:S(2)}, u32[]{:S(2)}) %collective-permute-start.2) | collective-permute-done | bytes 245792 | tf_op jit(solution)/shard_map/ppermute | solution.py:485
  21.5 5.3 %collective-permute-done.3.above_ref = f32[480,128]{1,0:T(8,128)S(1)} collective-permute-done((f32[480,128]{1,0:T(8,128)S(1)}, f32[480,128]{1,0:T(8,128)S(1)}, u32[]{:S(2)}, u32[]{:S(2)}) %collective-permute-start.3) | collective-permute-done | bytes 245792 | tf_op jit(solution)/shard_map/ppermute | solution.py:482
  26.8 0.0 copy-done
  26.8 0.0 copy-done.2
  26.8 0.0 copy-done.4
  26.8 3.5 %steps.1 = f32[3,8,8,256]{3,2,1,0:T(8,128)} custom-call(f32[480,128]{1,0:T(8,128)S(1)} %collective-permute-done.2.below_ref, f32[480,128]{1,0:T(8,128)S(1)} %get-tuple-element.16.low_ref, f32[480,128]{1,0:T(8,128)S(1)} %get-tuple-element.17.centre_ref, f32[480,128]{1,0:T(8,128)S(1)} %get-tuple-element.15.high_ref, ...), custom_call_target="tpu_custom_call" | custom-call | flops 1000000000 | bytes 2097152 | tf_op jit(solution)/shard_map/steps/pallas_call | solution.py:401
Async XLA Ops:
  2.2 5.2 %collective-permute-start = (f32[240,128]{1,0:T(8,128)S(1)}, f32[240,128]{1,0:T(8,128)S(1)}, u32[]{:S(2)}, u32[]{:S(2)}) collective-permute-start(f32[240,128]{1,0:T(8,128)S(1)} %get-tuple-element.12), channel_id=1, source_target_pairs={{0,16},{1,17},{2,18},{3,19},{4,20},{5,21},{6,22},{7,23},{8,24},{9,... | collective-permute-start | bytes 368648 | tf_op jit(solution)/shard_map/ppermute | solution.py:445
  3.5 10.1 %copy-start.1 = (s32[24,384]{1,0:T(8,128)S(1)}, s32[24,384]{1,0:T(8,128)}, u32[]{:S(2)}) copy-start(s32[24,384]{1,0:T(8,128)} %constant.10.clone.refs_6_.lanes_ref) | copy-start | bytes 110596
  3.5 10.1 %collective-permute-start.1 = (f32[240,128]{1,0:T(8,128)S(1)}, f32[240,128]{1,0:T(8,128)S(1)}, u32[]{:S(2)}, u32[]{:S(2)}) collective-permute-start(f32[240,128]{1,0:T(8,128)S(1)} %get-tuple-element.13), channel_id=1, source_target_pairs={{0,31},{1,30},{2,29},{3,28},{4,27},{5,26},{6,25},{7,24},{8,23},{9,... | collective-permute-start | bytes 368648 | tf_op jit(solution)/shard_map/ppermute | solution.py:442
  5.5 8.0 %copy-start.3 = (s32[2,256]{1,0:T(2,128)S(1)}, s32[2,256]{1,0:T(2,128)}, u32[]{:S(2)}) copy-start(s32[2,256]{1,0:T(2,128)} %seam_ref.1) | copy-start | bytes 6148
  13.5 13.2 %copy-start = (f32[256,384]{1,0:T(8,128)S(1)}, f32[256,384]{1,0:T(8,128)}, u32[]{:S(2)}) copy-start(f32[256,384]{1,0:T(8,128)} %constant.8.clone.refs_7_.table_ref) | copy-start | bytes 1179652
  13.6 13.2 %copy-start.2 = (f32[64,128]{1,0:T(8,128)S(1)}, f32[64,128]{1,0:T(8,128)}, u32[]{:S(2)}) copy-start(f32[64,128]{1,0:T(8,128)} %constant.9.clone.refs_8_.weight_ref) | copy-start | bytes 98308
  13.6 13.2 %copy-start.4 = (s32[8,640]{1,0:T(8,128)S(1)}, s32[8,640]{1,0:T(8,128)}, u32[]{:S(2)}) copy-start(s32[8,640]{1,0:T(8,128)} %constant.11.clone.ext_ref) | copy-start | bytes 61444
  14.7 6.8 %collective-permute-start.2 = (f32[480,128]{1,0:T(8,128)S(1)}, f32[480,128]{1,0:T(8,128)S(1)}, u32[]{:S(2)}, u32[]{:S(2)}) collective-permute-start(f32[480,128]{1,0:T(8,128)S(1)} %get-tuple-element.15.high_ref), channel_id=1, source_target_pairs={{0,1},{1,2},{2,3},{3,4},{4,5},{5,6},{6,7},{7,8},{8,9},{9,10},{10,1... | collective-permute-start | bytes 737288 | tf_op jit(solution)/shard_map/ppermute | solution.py:485
  18.4 8.4 %collective-permute-start.3 = (f32[480,128]{1,0:T(8,128)S(1)}, f32[480,128]{1,0:T(8,128)S(1)}, u32[]{:S(2)}, u32[]{:S(2)}) collective-permute-start(f32[480,128]{1,0:T(8,128)S(1)} %get-tuple-element.16.low_ref), channel_id=1, source_target_pairs={{1,0},{2,1},{3,2},{4,3},{5,4},{6,5},{7,6},{8,7},{9,8},{10,9},{11,1... | collective-permute-start | bytes 737288 | tf_op jit(solution)/shard_map/ppermute | solution.py:482

commit v3 on v2

--- a/solution.py
+++ b/solution.py
@@ -20,13 +20,13 @@
 EDGE_ROWS = 4 * NP
 ALL_ROWS = ROWS + EDGE_ROWS
 HALF_ROWS = ALL_ROWS // 2
-RING_X = 4
-RING_Y = 5
-PITCH = GX + 2 * RING_X
+RING = 4
+RIM_ROWS = ROWS + 2 * EDGE_ROWS
+PITCH = GX + 2 * RING
 MID = GY * PITCH
 LANES = 128
 EXT = MID + 2 * LANES
-LEAD = LANES - RING_Y * PITCH
+LEAD = LANES - RING * PITCH
 ELEMENTS = GX * GY
 
 time_step = 0.03
@@ -115,22 +115,36 @@
     table = np.zeros((24, MID), np.int32)
     for lane in range(MID):
         row, col = divmod(lane, PITCH)
-        x = col - RING_X
+        x = col - RING
         own = 0 <= x < GX
         table[0:8, lane] = x * GY + row if own else -1
         if not own:
-            table[8:16, lane] = row * RING_X + (col if x < 0 else x - GX)
+            table[8:16, lane] = row * RING + (col if x < 0 else x - GX)
         table[16:24, lane] = 0 if own else (1 if x < 0 else 2)
     ext = np.zeros((8, EXT), np.int32)
+    outer = np.zeros((24, 2 * LANES), np.int32)
     for lane in range(EXT):
         row, col = divmod(lane - LEAD, PITCH)
-        y = row - RING_Y
-        x = col - RING_X
-        ext[0, lane] = x in (-RING_X, GX + RING_X - 1)
+        y = row - RING
+        x = col - RING
+        inside = 0 <= row < GY + 2 * RING
+        ext[0, lane] = x in (-RING, GX + RING - 1)
         ext[1, lane] = y == GY - 1
         ext[2, lane] = y == 0
         ext[3, lane] = 0 <= y < GY and 0 <= x < GX
-    return table, ext
+        ext[4, lane] = y == -RING
+        ext[5, lane] = y == GY + RING - 1
+        if inside and not 0 <= y < GY:
+            place = lane if y < 0 else lane - LANES - MID + LANES
+            step = y + RING if y < 0 else y - GY
+            if 0 <= x < GX:
+                outer[0:8, place] = step * GX + x
+                outer[8:16, place] = 1
+            else:
+                outer[0:8, place] = LANES + step * RING + (x + RING if x < 0 else x - GX)
+                outer[8:16, place] = 2 if x < 0 else 3
+            outer[16:24, place] = y > 0
+    return table, ext, outer
 
 
 def exact_pieces(values):
@@ -202,6 +216,33 @@
     ]
 
 
+def edge_values(table_ref, weight_ref, h, u, v, area, depth, spin, tide):
+    root = jnp.sqrt(area)
+    mass = weight_ref[...] * area
+    table = table_ref[...].astype(bf16)
+    return mass_tendency(table, h, u, v, tide, root * depth, root, mass * spin) + [mass]
+
+
+def row_edges(sums):
+    return sums[pl.ds(NP - 1, EDGE_ROWS, stride=NP)], sums[pl.ds(0, EDGE_ROWS, stride=NP)]
+
+
+def packed(whole):
+    second = lax.broadcasted_iota(i32, (1, LANES), 1) >= 64
+    top, bottom = whole[:HALF_ROWS], whole[HALF_ROWS:]
+    return (
+        jnp.where(second, pltpu.roll(bottom, 64, 1), top),
+        jnp.where(second, bottom, pltpu.roll(top, 64, 1)),
+    )
+
+
+def unpacked(in0, in1):
+    second = lax.broadcasted_iota(i32, (1, LANES), 1) >= 64
+    top = jnp.where(second, pltpu.roll(in1, 64, 1), in0)
+    bottom = jnp.where(second, in1, pltpu.roll(in0, 64, 1))
+    return jnp.concatenate([top, bottom], 0)
+
+
 def seam_flags(seam_ref, block_cols):
     size_y = seam_ref.shape[1]
     face = lax.axis_index("face")
@@ -222,7 +263,8 @@
 
 
 def strips_kernel(block_cols, *refs):
-    sources, (out0_ref, out1_ref), buffers, sems = refs[:9], refs[9:11], refs[11:20], refs[20]
+    sources, (out0_ref, out1_ref, stored_ref) = refs[:9], refs[9:12]
+    buffers, sems = refs[12:21], refs[21]
     brought(sources, buffers, sems)
     seam_ref, slot_ref, fields_ref, area_ref, depth_ref, spin_ref, tide_ref = buffers[:7]
     table_ref, weight_ref = buffers[7:]
@@ -233,10 +275,11 @@
     row = place >> 2
     row = jnp.where(jnp.where(second, flip1, flip0) != 0, GY - 1 - row, row)
     east = jnp.where(second, east1, east0) != 0
-    col = jnp.where(east, GX - RING_X, 0) + (place & 3)
-    col = jnp.where(lane >= LANES, jnp.where(east, GX - RING_X - 1, RING_X), col)
+    col = jnp.where(east, GX - RING, 0) + (place & 3)
+    col = jnp.where(lane >= LANES, jnp.where(east, GX - RING - 1, RING), col)
     one_hot = by_slot(slot_ref, col * GY + row)
     stored = stored_rows(fields_ref, (area_ref, depth_ref, spin_ref, tide_ref))
+    stored_ref[...] = stored
     both = picked(stored, one_hot)
 
     lane = lax.broadcasted_iota(i32, (1, LANES), 1)
@@ -258,26 +301,69 @@
 
     strip = in_frame(both[:, :LANES])
     h, u, v, area, depth, spin, tide = in_frame(both[:, LANES:])
-    root = jnp.sqrt(area)
-    mass = weight_ref[...] * area
-    edges = mass_tendency(
-        table_ref[...].astype(bf16), h, u, v, tide, root * depth, root, mass * spin
-    ) + [mass]
+    edges = edge_values(table_ref, weight_ref, h, u, v, area, depth, spin, tide)
     east = jnp.where(second, east1, east0) != 0
     edges = [jnp.where(east, part[NODES - NP :], part[:NP]) for part in edges]
-    whole = jnp.concatenate(strip + edges, 0)
-    top, bottom = whole[:HALF_ROWS], whole[HALF_ROWS:]
-    out0_ref[...] = jnp.where(second, pltpu.roll(bottom, 64, 1), top)
-    out1_ref[...] = jnp.where(second, bottom, pltpu.roll(top, 64, 1))
-
-
-def own_kernel(*refs):
-    sources, (own_ref, hot_ref), buffers, sems = refs[:7], refs[7:9], refs[9:16], refs[16]
-    brought(sources, buffers, sems)
-    slot_ref, fields_ref, area_ref, depth_ref, spin_ref, tide_ref, lanes_ref = buffers
+    out0_ref[...], out1_ref[...] = packed(jnp.concatenate(strip + edges, 0))
+
+
+def rows_kernel(stored_ref, slot_ref, table_ref, weight_ref, out0_ref, out1_ref, sums):
+    odd = lax.axis_index("blk") & 1
+
+    def goes_up(lane):
+        return jnp.where((lane & 64) != 0, odd, 1 - odd) != 0
+
+    lane = lax.broadcasted_iota(i32, (8, 2 * LANES), 1)
+    up = goes_up(lane)
+    row = jnp.where(up, GY - RING, 0) + ((lane & 63) >> 4)
+    row = jnp.where(lane >= LANES, jnp.where(up, GY - RING - 1, RING), row)
+    both = picked(stored_ref[...], by_slot(slot_ref, (lane & 15) * GY + row))
+    h, u, v, area, depth, spin, tide = [
+        both[k * NODES : (k + 1) * NODES, LANES:] for k in range(ARRAYS)
+    ]
+    edges = edge_values(table_ref, weight_ref, h, u, v, area, depth, spin, tide)
+    sums[...] = jnp.concatenate(edges, 0)
+    north, south = row_edges(sums)
+    up = goes_up(lax.broadcasted_iota(i32, (1, LANES), 1))
+    rim = jnp.where(up, north, south)
+    out0_ref[...], out1_ref[...] = packed(jnp.concatenate([both[:, :LANES], rim], 0))
+
+
+def corners_kernel(
+    in0_ref, in1_ref, table_ref, weight_ref, out0_ref, out1_ref, sums
+):
+    odd = lax.axis_index("blk") & 1
+    whole = unpacked(in0_ref[...], in1_ref[...])
+    parts = [whole[k * NODES : (k + 1) * NODES] for k in range(ARRAYS)]
+    sums[...] = jnp.concatenate(edge_values(table_ref, weight_ref, *parts), 0)
+    north, south = row_edges(sums)
+    lane = lax.broadcasted_iota(i32, (1, LANES), 1)
+
+    def squeezed(values, shift):
+        return jnp.where(
+            lane < 16,
+            pltpu.roll(values, shift, 1) if shift else values,
+            pltpu.roll(values, (shift + 80) % LANES, 1),
+        )
+
+    up = squeezed(jnp.concatenate([whole, pltpu.roll(north, 4, 1)], 0), 80)
+    down = squeezed(jnp.concatenate([whole, pltpu.roll(south, LANES - 4, 1)], 0), 0)
+
+    def in_fours(values):
+        parts = [values[k * LANES : (k + 1) * LANES] for k in range(4)]
+        out = parts[0]
+        for k in range(1, 4):
+            out = jnp.where(lane >= 32 * k, pltpu.roll(parts[k], 32 * k, 1), out)
+        return out
+
+    up, down = in_fours(up), in_fours(down)
+    out0_ref[...] = jnp.where(odd != 0, down, up)
+    out1_ref[...] = jnp.where(odd != 0, up, down)
+
+
+def own_kernel(stored_ref, slot_ref, lanes_ref, own_ref, hot_ref):
     one_hot = by_slot(slot_ref, lanes_ref[0:8])
-    stored = stored_rows(fields_ref, (area_ref, depth_ref, spin_ref, tide_ref))
-    own_ref[...] = picked(stored, one_hot)
+    own_ref[...] = picked(stored_ref[...], one_hot)
     hot_ref[...] = one_hot
 
 
@@ -285,11 +371,7 @@
     block_cols, seam_ref, in0_ref, in1_ref, own_ref, lanes_ref, low_ref, centre_ref, high_ref
 ):
     east0, flip0, east1, flip1 = seam_flags(seam_ref, block_cols)
-    second = lax.broadcasted_iota(i32, (1, LANES), 1) >= 64
-    in0, in1 = in0_ref[...], in1_ref[...]
-    top = jnp.where(second, pltpu.roll(in1, 64, 1), in0)
-    bottom = jnp.where(second, in1, pltpu.roll(in0, 64, 1))
-    whole = jnp.concatenate([top, bottom], 0)
+    whole = unpacked(in0_ref[...], in1_ref[...])
     side = lanes_ref[16:24]
     first_at = jnp.where(side == 2, 64 * (1 - east0), 64 * east0)
     place = jnp.where(side == 0, -1, lanes_ref[8:16] + first_at)
@@ -301,11 +383,31 @@
 
 
 def steps_kernel(
-    below_ref, low_ref, centre_ref, high_ref, above_ref, hot_ref, table_ref, weight_ref,
-    ext_ref, out_ref, sums,
+    block_cols, seam_ref, rows0_ref, rows1_ref, corner0_ref, corner1_ref, low_ref, centre_ref,
+    high_ref, hot_ref, table_ref, weight_ref, ext_ref, outer_ref, out_ref, sums,
 ):
-    tiles = (below_ref, low_ref, centre_ref, high_ref, above_ref)
+    east0, flip0, east1, flip1 = seam_flags(seam_ref, block_cols)
+    odd = lax.axis_index("blk") & 1
     block_y = lax.rem(lax.axis_index("blk"), BY)
+
+    lane = lax.broadcasted_iota(i32, (1, LANES), 1)
+    strips = unpacked(rows0_ref[...], rows1_ref[...])
+    strips = jnp.concatenate(
+        [strips[:ROWS], jnp.zeros((EDGE_ROWS, LANES), f32), strips[ROWS:]], 0
+    )
+    corner0, corner1 = corner0_ref[...], corner1_ref[...]
+    corners = []
+    for k in range(4):
+        first = pltpu.roll(corner0, LANES - 32 * k, 1) if k else corner0
+        other = pltpu.roll(corner1, (LANES + 32 - 32 * k) % LANES, 1) if k != 1 else corner1
+        corners.append(jnp.where(lane < 32, first, other))
+    around = jnp.concatenate([strips, jnp.concatenate(corners, 0)], 1)
+    kind = outer_ref[8:16]
+    sender = jnp.where(outer_ref[16:24] != 0, odd, 1 - odd)
+    strip_at = jnp.where(kind == 3, 16 * (1 - east0), 16 * east0)
+    place = outer_ref[0:8] + jnp.where(kind == 1, 64 * sender, 32 * sender + strip_at)
+    outer = picked(around, as_one_hot(jnp.where(kind == 0, -1, place), 2 * LANES))
+    tiles = (outer[:, :LANES], low_ref, centre_ref, high_ref, outer[:, LANES:])
 
     def rows_of(start, count):
         return jnp.concatenate([ref[start : start + count] for ref in tiles], 1)
@@ -316,7 +418,10 @@
     top_row = jnp.where(block_y == BY - 1, ext_ref[1:2], 0) != 0
     bottom_row = jnp.where(block_y == 0, ext_ref[2:3], 0) != 0
 
-    def edge_sum(parts, rims=None):
+    first_row = ext_ref[4:5] != 0
+    last_row = ext_ref[5:6] != 0
+
+    def edge_sum(parts, rims=None, rows=None):
         count = len(parts) * NP
         for c, part in enumerate(parts):
             west, east = part[:NP], part[NODES - NP :]
@@ -331,8 +436,12 @@
         south_at, north_at = pl.ds(0, count, stride=NP), pl.ds(NP - 1, count, stride=NP)
         south = jnp.concatenate([sums[k, south_at] for k in range(len(tiles))], 1)
         north = jnp.concatenate([sums[k, north_at] for k in range(len(tiles))], 1)
-        to_north = north + jnp.where(top_row, 0.0, pltpu.roll(south, EXT - PITCH, 1))
-        to_south = south + jnp.where(bottom_row, 0.0, pltpu.roll(north, PITCH, 1))
+        at_north = jnp.where(top_row, 0.0, pltpu.roll(south, EXT - PITCH, 1))
+        at_south = jnp.where(bottom_row, 0.0, pltpu.roll(north, PITCH, 1))
+        if rows is not None:
+            at_north = jnp.where(last_row, rows, at_north)
+            at_south = jnp.where(first_row, rows, at_south)
+        to_north, to_south = north + at_north, south + at_south
         for k in range(len(tiles)):
             sums[k, south_at] = to_south[:, k * LANES : (k + 1) * LANES]
             sums[k, north_at] = to_north[:, k * LANES : (k + 1) * LANES]
@@ -345,15 +454,25 @@
 
     start = [rows_of(c * NODES, NODES) for c in range(3)]
     area, depth, spin, tide = [rows_of(c * NODES, NODES) for c in range(3, ARRAYS)]
-    area = jnp.where(area > 0.0, area, 1.0)
     root = jnp.sqrt(area)
     mass = weight * area
     mass_spin = mass * spin
     area_depth = root * depth
-    per_mass = 1.0 / edge_sum([mass], [rows_of(ROWS + 3 * NP, NP)])[0]
-
-    def average(parts, rims=None):
-        return [part * per_mass for part in edge_sum(parts, rims)]
+    rims = [rows_of(ROWS + c * NP, NP) for c in range(4)]
+    blank = jnp.zeros((EDGE_ROWS, MID), f32)
+    rows = jnp.concatenate([tiles[0][ALL_ROWS:], blank, tiles[-1][ALL_ROWS:]], 1)
+    node = lax.broadcasted_iota(i32, (1, NP, 1), 1)
+    east = pltpu.roll(rows, EXT - 1, 1).reshape(4, NP, EXT)
+    west = pltpu.roll(rows, 1, 1).reshape(4, NP, EXT)
+    rows = (
+        rows.reshape(4, NP, EXT)
+        + jnp.where(node == NP - 1, pltpu.roll(east, NP - 1, 1), 0.0)
+        + jnp.where(node == 0, pltpu.roll(west, 1, 1), 0.0)
+    ).reshape(EDGE_ROWS, EXT)
+    per_mass = 1.0 / edge_sum([mass], rims[3:], rows[3 * NP :])[0]
+
+    def average(parts, rims=None, rows=None):
+        return [part * per_mass for part in edge_sum(parts, rims, rows)]
 
     def tendency(s):
         return mass_tendency(table, *s, tide, area_depth, root, mass_spin)
@@ -364,8 +483,7 @@
             for part in s
         ]
 
-    rims = [rows_of(ROWS + c * NP, NP) for c in range(3)]
-    change = average(tendency(start), rims)
+    change = average(tendency(start), rims[:3], rows[: 3 * NP])
     one = [s + time_step * c for s, c in zip(start, change)]
     change = average(tendency(one))
     two = [0.75 * s + 0.25 * (o + time_step * c) for s, o, c in zip(start, one, change)]
@@ -389,8 +507,7 @@
     block_cols = lax.axis_size("blk") // BY
     count = lax.axis_size("face") * lax.axis_size("blk")
     table, weight = operator_table()
-    lanes, ext = lane_tables()
-    table, weight, lanes, ext = (jnp.asarray(part) for part in (table, weight, lanes, ext))
+    table, weight, lanes, ext, outer = map(jnp.asarray, (table, weight, *lane_tables()))
     vmem = pl.BlockSpec(memory_space=pltpu.VMEM)
     smem = pl.BlockSpec(memory_space=pltpu.SMEM)
     hbm = pl.BlockSpec(memory_space=pltpu.HBM)
@@ -423,10 +540,10 @@
         return buffers + [pltpu.SemaphoreType.DMA((len(values),))]
 
     needed = (seam_rows, slot_of, *held, table, weight)
-    strip0, strip1 = call(
+    strip0, strip1, stored = call(
         functools.partial(strips_kernel, block_cols),
         [(hbm, x) for x in needed],
-        [strip, strip],
+        [strip, strip, ((ROWS, ELEMENTS), f32)],
         10**8,
         scratch=room(needed, [pltpu.SMEM] + [pltpu.VMEM] * (len(needed) - 1)),
         name="strips",
@@ -462,15 +579,48 @@
         )
         halo0 = jnp.where((block_x == last) & flipped[face], turned_east, from_east)
         halo1 = jnp.where((block_x == 0) & flipped[1 - face], turned_west, from_west)
-    needed = (slot_of, *held, lanes)
+    sums = [pltpu.VMEM((4 * NODES, LANES), f32)]
+    rows0, rows1 = call(
+        rows_kernel,
+        [(vmem, x) for x in (stored, slot_of, table, weight)],
+        [strip, strip],
+        10**8,
+        scratch=sums,
+        name="rows",
+    )
+
+    def in_pair(y):
+        return y ^ 1
+
+    def next_pair(y):
+        other = y + 1 if y % 2 else y - 1
+        return other if 0 <= other < BY else y
+
+    def swapped(value, partner):
+        return lax.ppermute(
+            value, both, [(rank(f, x, y), rank(f, x, partner(y))) for f, x, y in places]
+        )
+
+    from_rows1 = swapped(rows1, next_pair)
+    from_rows0 = swapped(rows0, in_pair)
     own, hot = call(
         own_kernel,
-        [(hbm, x) for x in needed],
+        [(vmem, x) for x in (stored, slot_of, lanes)],
         [((ROWS, MID), f32), ((ELEMENTS, MID), bf16)],
         3 * 10**8,
-        scratch=room(needed),
         name="own",
     )
+    corner = ((RIM_ROWS // 4, LANES), f32)
+    corner0, corner1 = call(
+        corners_kernel,
+        [(vmem, x) for x in (halo0, halo1, table, weight)],
+        [corner, corner],
+        10**8,
+        scratch=sums,
+        name="corners",
+    )
+    from_corner1 = swapped(corner1, next_pair)
+    from_corner0 = swapped(corner0, in_pair)
     tile = ((ALL_ROWS, LANES), f32)
     low, centre, high = call(
         functools.partial(middle_kernel, block_cols),
@@ -479,15 +629,16 @@
         10**8,
         name="middle",
     )
-    above = lax.ppermute(
-        low, both, [(rank(f, x, y), rank(f, x, y - 1)) for f, x, y in places if y > 0]
-    )
-    below = lax.ppermute(
-        high, both, [(rank(f, x, y), rank(f, x, y + 1)) for f, x, y in places if y < BY - 1]
-    )
     (stepped,) = call(
-        steps_kernel,
-        [(vmem, x) for x in (below, low, centre, high, above, hot, table, weight, ext)],
+        functools.partial(steps_kernel, block_cols),
+        [(smem, seam_rows)]
+        + [
+            (vmem, x)
+            for x in (
+                from_rows0, from_rows1, from_corner0, from_corner1, low, centre, high,
+                hot, table, weight, ext, outer,
+            )
+        ],
         [(fields.shape, f32)],
         10**9,
         scratch=[pltpu.VMEM((EXT // LANES, 3 * NODES, LANES), f32)],

time: 30.5 us -> 27.4 us (0.90)
  waiting for transfers between devices: 12.7 us -> 6.26 us
  starting transfers between devices: 8.95 us -> 10.8 us
  Pallas kernels: 8.61 us -> 9.99 us
    ppermute x2 -> x4, waiting for transfers between devices: 6.49 us -> 2.16 us  [swapped(): lax.ppermute(value, both, [(rank(f, x, y), rank(f, x, partner(y))) for f,...]
    ppermute x1, waiting for transfers between devices: 6.19 us -> 4.1 us  [on_device(): lax.ppermute(strip1, both, [(rank(f, x, y), rank(1 - f, x, BY - 1 - y)) f...]
    ppermute x2 -> x4, starting transfers between devices: 5.62 us -> 7.43 us  [swapped(): lax.ppermute(value, both, [(rank(f, x, y), rank(f, x, partner(y))) for f,...]
    pallas_call x4 -> x6, Pallas kernels: 8.61 us -> 9.99 us  [call(): pl.pallas_call(kernel, out_shape=[jax.ShapeDtypeStruct(*out) for out in o...]
  transfers between devices with their start and end apart: 4 -> 6, of which waited for: 3 -> 2; matrix products, arithmetic and copies ran while one was open for 0% -> 0% of each run, Pallas kernels for 6% -> 12%
where the time goes in v3:
time: 27.4 us; the launch traced here: 27.2 us
  starting transfers between devices  10.8 us (39%)
  Pallas kernels  9.99 us (36%)
  waiting for transfers between devices  6.26 us (23%)
    pallas_call x6, Pallas kernels, call(): pl.pallas_call(kernel, out_shape=[jax.ShapeDtypeStruct(*out) for out in o...  9.99 us
    ppermute x4, starting transfers between devices, swapped(): lax.ppermute(value, both, [(rank(f, x, y), rank(f, x, partner(y))) for f,...  7.43 us
    ppermute x1, waiting for transfers between devices, on_device(): lax.ppermute(strip1, both, [(rank(f, x, y), rank(1 - f, x, BY - 1 - y)) f...  4.1 us
    ppermute x4, waiting for transfers between devices, swapped(): lax.ppermute(value, both, [(rank(f, x, y), rank(f, x, partner(y))) for f,...  2.16 us
    ppermute x1, starting transfers between devices, on_device(): lax.ppermute(strip1, both, [(rank(f, x, y), rank(1 - f, x, BY - 1 - y)) f...  2.05 us
    ppermute x1, starting transfers between devices, on_device(): lax.ppermute(strip0, both, [(rank(f, x, y), rank(1 - f, x, y)) for f, x,...  1.28 us
  transfers between devices with their start and end apart: 6, of which 2 were waited for; matrix products, arithmetic and copies ran while one was open for 0% of the time, Pallas kernels for 12%

profile of v3, /device:TPU:13, one launch (start us, length us, event | category | flops | bytes accessed | tf_op | source)
XLA Modules:
  0.0 27.2 jit_solution(15082986325781465770)
XLA Ops:
  0.0 2.2 %strips.1 = (f32[240,128]{1,0:T(8,128)S(1)}, f32[240,128]{1,0:T(8,128)S(1)}, f32[448,256]{1,0:T(8,128)S(1)}) custom-call(s32[2,256]{1,0:T(2,128)} %seam_ref.3, s32[1,256]{1,0:T(1,128)} %slot_ref.3, f32[3,8,8,256]{3,2,1,0:T(8,128)} %refs_2_.1, f32[8,8,256]{2,1,0:T(8,128)} %refs_3_.1, f32[8,8,256]{2,1,0:T(8,128)} %refs_4_.1, f32[8,8,256]{2,1,0:T(8,128)} %refs_5_.1, ...), custom_call_target="tpu_custom_call" | custom-call | flops 100000000 | bytes 2097152 | tf_op jit(solution)/shard_map/strips/pallas_call | solution.py:518
  2.2 1.3 %collective-permute-start.2 = (f32[240,128]{1,0:T(8,128)S(1)}, f32[240,128]{1,0:T(8,128)S(1)}, u32[]{:S(2)}, u32[]{:S(2)}) collective-permute-start(f32[240,128]{1,0:T(8,128)S(1)} %get-tuple-element.20), channel_id=1, source_target_pairs={{0,16},{1,17},{2,18},{3,19},{4,20},{5,21},{6,22},{7,23},{8,24},{9,... | collective-permute-start | bytes 368648 | tf_op jit(solution)/shard_map/ppermute | solution.py:562
  3.5 2.1 %collective-permute-start.3 = (f32[240,128]{1,0:T(8,128)S(1)}, f32[240,128]{1,0:T(8,128)S(1)}, u32[]{:S(2)}, u32[]{:S(2)}) collective-permute-start(f32[240,128]{1,0:T(8,128)S(1)} %get-tuple-element.21), channel_id=1, source_target_pairs={{0,31},{1,30},{2,29},{3,28},{4,27},{5,26},{6,25},{7,24},{8,23},{9,... | collective-permute-start | bytes 368648 | tf_op jit(solution)/shard_map/ppermute | solution.py:559
  5.6 0.8 %rows.1 = (f32[240,128]{1,0:T(8,128)S(1)}, f32[240,128]{1,0:T(8,128)S(1)}) custom-call(f32[448,256]{1,0:T(8,128)S(1)} %get-tuple-element.17.stored_ref, s32[1,256]{1,0:T(1,128)S(1)} %copy-done.4, f32[256,384]{1,0:T(8,128)S(1)} %copy-done, f32[64,128]{1,0:T(8,128)S(1)} %copy-done.1), custom_call_target="tpu_custom_call" | custom-call | flops 100000000 | bytes 2097152 | tf_op jit(solution)/shard_map/rows/pallas_call | solution.py:518
  6.4 0.0 collective-permute-start
  6.4 0.0 copy-start.2
  6.4 3.5 %collective-permute-start.1 = (f32[240,128]{1,0:T(8,128)S(1)}, f32[240,128]{1,0:T(8,128)S(1)}, u32[]{:S(2)}, u32[]{:S(2)}) collective-permute-start(f32[240,128]{1,0:T(8,128)S(1)} %get-tuple-element.19), channel_id=1, source_target_pairs={{0,0},{1,2},{2,1},{3,4},{4,3},{5,6},{6,5},{7,8},{8,7},{9,10},{10,9... | collective-permute-start | bytes 368648 | tf_op jit(solution)/shard_map/ppermute | solution.py:600
  10.0 0.0 collective-permute-done.2.in0_ref
  10.0 4.1 %collective-permute-done.3.in1_ref = f32[240,128]{1,0:T(8,128)S(1)} collective-permute-done((f32[240,128]{1,0:T(8,128)S(1)}, f32[240,128]{1,0:T(8,128)S(1)}, u32[]{:S(2)}, u32[]{:S(2)}) %collective-permute-start.3) | collective-permute-done | bytes 122912 | tf_op jit(solution)/shard_map/ppermute | solution.py:559
  14.1 0.5 %corners.1 = (f32[128,128]{1,0:T(8,128)S(1)}, f32[128,128]{1,0:T(8,128)S(1)}) custom-call(f32[240,128]{1,0:T(8,128)S(1)} %collective-permute-done.2.in0_ref, f32[240,128]{1,0:T(8,128)S(1)} %collective-permute-done.3.in1_ref, f32[256,384]{1,0:T(8,128)S(1)} %copy-done, f32[64,128]{1,0:T(8,128)S(1)} %copy-done.1), custom_call_target="tpu_custom_call" | custom-call | flops 100000000 | bytes 2097152 | tf_op jit(solution)/shard_map/corners/pallas_call | solution.py:518
  14.6 1.4 %collective-permute-start.4 = (f32[128,128]{1,0:T(8,128)S(1)}, f32[128,128]{1,0:T(8,128)S(1)}, u32[]{:S(2)}, u32[]{:S(2)}) collective-permute-start(f32[128,128]{1,0:T(8,128)S(1)} %get-tuple-element.22), channel_id=1, source_target_pairs={{0,1},{1,0},{2,3},{3,2},{4,5},{5,4},{6,7},{7,6},{8,9},{9,8},{10,11... | collective-permute-start | bytes 196616 | tf_op jit(solution)/shard_map/ppermute | solution.py:600
  16.1 2.5 %collective-permute-start.5 = (f32[128,128]{1,0:T(8,128)S(1)}, f32[128,128]{1,0:T(8,128)S(1)}, u32[]{:S(2)}, u32[]{:S(2)}) collective-permute-start(f32[128,128]{1,0:T(8,128)S(1)} %get-tuple-element.23), channel_id=1, source_target_pairs={{0,0},{1,2},{2,1},{3,4},{4,3},{5,6},{6,5},{7,8},{8,7},{9,10},{10,9... | collective-permute-start | bytes 196616 | tf_op jit(solution)/shard_map/ppermute | solution.py:600
  18.5 0.0 copy-done.2
  18.5 0.0 copy-start.3
  18.5 0.7 %own.1 = (f32[448,384]{1,0:T(8,128)S(1)}, bf16[256,384]{1,0:T(8,128)(2,1)S(1)}) custom-call(f32[448,256]{1,0:T(8,128)S(1)} %get-tuple-element.17.stored_ref, s32[1,256]{1,0:T(1,128)S(1)} %copy-done.4, s32[24,384]{1,0:T(8,128)S(1)} %copy-done.2), custom_call_target="tpu_custom_call" | custom-call | flops 300000000 | bytes 2097152 | tf_op jit(solution)/shard_map/own/pallas_call | solution.py:518
  19.2 0.0 copy-start.5
  19.3 0.0 copy-start.6
  19.3 1.1 %middle.1 = (f32[480,128]{1,0:T(8,128)S(1)}, f32[480,128]{1,0:T(8,128)S(1)}, f32[480,128]{1,0:T(8,128)S(1)}) custom-call(s32[2,256]{1,0:T(2,128)S(1)} %copy-done.3, f32[240,128]{1,0:T(8,128)S(1)} %collective-permute-done.2.in0_ref, f32[240,128]{1,0:T(8,128)S(1)} %collective-permute-done.3.in1_ref, f32[448,384]{1,0:T(8,128)S(1)} %get-tuple-element.24.own_ref, ...), custom_call_target="tpu_custom_call" | custom-call | flops 100000000 | bytes 2097152 | tf_op jit(solution)/shard_map/middle/pallas_call | solution.py:518
  20.3 0.0 collective-permute-done.rows0_ref
  20.4 0.0 collective-permute-done.1.rows1_ref
  20.4 0.0 collective-permute-done.4.corner0_ref
  20.4 2.2 %collective-permute-done.5.corner1_ref = f32[128,128]{1,0:T(8,128)S(1)} collective-permute-done((f32[128,128]{1,0:T(8,128)S(1)}, f32[128,128]{1,0:T(8,128)S(1)}, u32[]{:S(2)}, u32[]{:S(2)}) %collective-permute-start.5) | collective-permute-done | bytes 65568 | tf_op jit(solution)/shard_map/ppermute | solution.py:600
  22.5 0.0 copy-done.5
  22.5 4.6 %steps.1 = f32[3,8,8,256]{3,2,1,0:T(8,128)} custom-call(s32[2,256]{1,0:T(2,128)S(1)} %copy-done.3, f32[240,128]{1,0:T(8,128)S(1)} %collective-permute-done.rows0_ref, f32[240,128]{1,0:T(8,128)S(1)} %collective-permute-done.1.rows1_ref, f32[128,128]{1,0:T(8,128)S(1)} %collective-permute-done.4.corner0_ref, f32[128,128]{1,0:T(8,128)S(1)} %collective-permute-done.5.corner1_ref, ...), custom_call_target="tpu_custom_call" | custom-call | flops 1000000000 | bytes 2097152 | tf_op jit(solution)/shard_map/steps/pallas_call | solution.py:518
  (8 shorter events, 0.0 us)
Async XLA Ops:
  0.0 5.6 %copy-start = (f32[256,384]{1,0:T(8,128)S(1)}, f32[256,384]{1,0:T(8,128)}, u32[]{:S(2)}) copy-start(f32[256,384]{1,0:T(8,128)} %constant.10.clone.refs_7_.table_ref) | copy-start | bytes 1179652
  0.0 5.6 %copy-start.1 = (f32[64,128]{1,0:T(8,128)S(1)}, f32[64,128]{1,0:T(8,128)}, u32[]{:S(2)}) copy-start(f32[64,128]{1,0:T(8,128)} %constant.11.clone.refs_8_.weight_ref) | copy-start | bytes 98308
  2.2 7.7 %collective-permute-start.2 = (f32[240,128]{1,0:T(8,128)S(1)}, f32[240,128]{1,0:T(8,128)S(1)}, u32[]{:S(2)}, u32[]{:S(2)}) collective-permute-start(f32[240,128]{1,0:T(8,128)S(1)} %get-tuple-element.20), channel_id=1, source_target_pairs={{0,16},{1,17},{2,18},{3,19},{4,20},{5,21},{6,22},{7,23},{8,24},{9,... | collective-permute-start | bytes 368648 | tf_op jit(solution)/shard_map/ppermute | solution.py:562
  3.5 2.1 %copy-start.4 = (s32[1,256]{1,0:T(1,128)S(1)}, s32[1,256]{1,0:T(1,128)}, u32[]{:S(2)}) copy-start(s32[1,256]{1,0:T(1,128)} %slot_ref.3) | copy-start | bytes 3076
  3.5 10.6 %collective-permute-start.3 = (f32[240,128]{1,0:T(8,128)S(1)}, f32[240,128]{1,0:T(8,128)S(1)}, u32[]{:S(2)}, u32[]{:S(2)}) collective-permute-start(f32[240,128]{1,0:T(8,128)S(1)} %get-tuple-element.21), channel_id=1, source_target_pairs={{0,31},{1,30},{2,29},{3,28},{4,27},{5,26},{6,25},{7,24},{8,23},{9,... | collective-permute-start | bytes 368648 | tf_op jit(solution)/shard_map/ppermute | solution.py:559
  6.4 14.0 %collective-permute-start = (f32[240,128]{1,0:T(8,128)S(1)}, f32[240,128]{1,0:T(8,128)S(1)}, u32[]{:S(2)}, u32[]{:S(2)}) collective-permute-start(f32[240,128]{1,0:T(8,128)S(1)} %get-tuple-element.18), channel_id=1, source_target_pairs={{0,1},{1,0},{2,3},{3,2},{4,5},{5,4},{6,7},{7,6},{8,9},{9,8},{10,11... | collective-permute-start | bytes 368648 | tf_op jit(solution)/shard_map/ppermute | solution.py:600
  6.4 12.1 %copy-start.2 = (s32[24,384]{1,0:T(8,128)S(1)}, s32[24,384]{1,0:T(8,128)}, u32[]{:S(2)}) copy-start(s32[24,384]{1,0:T(8,128)} %constant.12.clone.lanes_ref) | copy-start | bytes 110596
  6.4 13.9 %collective-permute-start.1 = (f32[240,128]{1,0:T(8,128)S(1)}, f32[240,128]{1,0:T(8,128)S(1)}, u32[]{:S(2)}, u32[]{:S(2)}) collective-permute-start(f32[240,128]{1,0:T(8,128)S(1)} %get-tuple-element.19), channel_id=1, source_target_pairs={{0,0},{1,2},{2,1},{3,4},{4,3},{5,6},{6,5},{7,8},{8,7},{9,10},{10,9... | collective-permute-start | bytes 368648 | tf_op jit(solution)/shard_map/ppermute | solution.py:600
  14.6 5.7 %collective-permute-start.4 = (f32[128,128]{1,0:T(8,128)S(1)}, f32[128,128]{1,0:T(8,128)S(1)}, u32[]{:S(2)}, u32[]{:S(2)}) collective-permute-start(f32[128,128]{1,0:T(8,128)S(1)} %get-tuple-element.22), channel_id=1, source_target_pairs={{0,1},{1,0},{2,3},{3,2},{4,5},{5,4},{6,7},{7,6},{8,9},{9,8},{10,11... | collective-permute-start | bytes 196616 | tf_op jit(solution)/shard_map/ppermute | solution.py:600
  16.1 6.5 %collective-permute-start.5 = (f32[128,128]{1,0:T(8,128)S(1)}, f32[128,128]{1,0:T(8,128)S(1)}, u32[]{:S(2)}, u32[]{:S(2)}) collective-permute-start(f32[128,128]{1,0:T(8,128)S(1)} %get-tuple-element.23), channel_id=1, source_target_pairs={{0,0},{1,2},{2,1},{3,4},{4,3},{5,6},{6,5},{7,8},{8,7},{9,10},{10,9... | collective-permute-start | bytes 196616 | tf_op jit(solution)/shard_map/ppermute | solution.py:600
  18.5 0.7 %copy-start.3 = (s32[2,256]{1,0:T(2,128)S(1)}, s32[2,256]{1,0:T(2,128)}, u32[]{:S(2)}) copy-start(s32[2,256]{1,0:T(2,128)} %seam_ref.3) | copy-start | bytes 6148
  19.2 3.3 %copy-start.5 = (s32[24,256]{1,0:T(8,128)S(1)}, s32[24,256]{1,0:T(8,128)}, u32[]{:S(2)}) copy-start(s32[24,256]{1,0:T(8,128)} %constant.14.clone.outer_ref) | copy-start | bytes 73732
  19.3 3.3 %copy-start.6 = (s32[8,640]{1,0:T(8,128)S(1)}, s32[8,640]{1,0:T(8,128)}, u32[]{:S(2)}) copy-start(s32[8,640]{1,0:T(8,128)} %constant.13.clone.ext_ref) | copy-start | bytes 61444

commit v4 on v3

--- a/solution.py
+++ b/solution.py
@@ -22,6 +22,7 @@
 HALF_ROWS = ALL_ROWS // 2
 RING = 4
 RIM_ROWS = ROWS + 2 * EDGE_ROWS
+CORNER_ROWS = RIM_ROWS // 8
 PITCH = GX + 2 * RING
 MID = GY * PITCH
 LANES = 128
@@ -218,13 +219,34 @@
 
 def edge_values(table_ref, weight_ref, h, u, v, area, depth, spin, tide):
     root = jnp.sqrt(area)
-    mass = weight_ref[...] * area
+    mass = jnp.concatenate([weight_ref[...]] * (area.shape[1] // LANES), 1) * area
     table = table_ref[...].astype(bf16)
     return mass_tendency(table, h, u, v, tide, root * depth, root, mass * spin) + [mass]
 
 
 def row_edges(sums):
     return sums[pl.ds(NP - 1, EDGE_ROWS, stride=NP)], sums[pl.ds(0, EDGE_ROWS, stride=NP)]
+
+
+def beside(left, right):
+    return jnp.concatenate([left, right], 1)
+
+
+def with_row_rim(whole, sums, top):
+    north, south = row_edges(sums)
+    rim = jnp.where(top, pltpu.roll(north, RING, 1), pltpu.roll(south, LANES - RING, 1))
+    return jnp.concatenate([whole, rim], 0)
+
+
+def corner_of(whole, start, top):
+    lane = lax.broadcasted_iota(i32, (1, LANES), 1)
+    base = LANES - start - jnp.where(top != 0, 48, 0)
+    out = None
+    for k in range(RIM_ROWS // CORNER_ROWS):
+        part = whole[k * CORNER_ROWS : (k + 1) * CORNER_ROWS]
+        part = pltpu.roll(part, (base + 16 * k) & (LANES - 1), 1)
+        out = part if k == 0 else jnp.where(lane >= 16 * k, part, out)
+    return out
 
 
 def packed(whole):
@@ -263,8 +285,8 @@
 
 
 def strips_kernel(block_cols, *refs):
-    sources, (out0_ref, out1_ref, stored_ref) = refs[:9], refs[9:12]
-    buffers, sems = refs[12:21], refs[21]
+    sources, (out1_ref, far1_ref, out0_ref, far0_ref, stored_ref) = refs[:9], refs[9:14]
+    buffers, sems, sums = refs[14:23], refs[23], refs[24]
     brought(sources, buffers, sems)
     seam_ref, slot_ref, fields_ref, area_ref, depth_ref, spin_ref, tide_ref = buffers[:7]
     table_ref, weight_ref = buffers[7:]
@@ -299,12 +321,18 @@
         parts[5] = parts[5] * sign
         return parts
 
-    strip = in_frame(both[:, :LANES])
-    h, u, v, area, depth, spin, tide = in_frame(both[:, LANES:])
-    edges = edge_values(table_ref, weight_ref, h, u, v, area, depth, spin, tide)
+    strip, ring = in_frame(both[:, :LANES]), in_frame(both[:, LANES:])
+    edges = edge_values(table_ref, weight_ref, *map(beside, strip, ring))
     east = jnp.where(second, east1, east0) != 0
-    edges = [jnp.where(east, part[NODES - NP :], part[:NP]) for part in edges]
-    out0_ref[...], out1_ref[...] = packed(jnp.concatenate(strip + edges, 0))
+    ends = [jnp.where(east, part[NODES - NP :, LANES:], part[:NP, LANES:]) for part in edges]
+    whole = jnp.concatenate(strip + ends, 0)
+    out0_ref[...], out1_ref[...] = packed(whole)
+    odd = lax.axis_index("blk") & 1
+    sums[...] = jnp.concatenate([part[:, :LANES] for part in edges], 0)
+    top0, top1 = odd ^ flip0, odd ^ flip1
+    whole = with_row_rim(whole, sums, jnp.where(second, top1, top0) != 0)
+    far0_ref[...] = corner_of(whole, 0, top0)
+    far1_ref[...] = corner_of(whole, 64, top1)
 
 
 def rows_kernel(stored_ref, slot_ref, table_ref, weight_ref, out0_ref, out1_ref, sums):
@@ -329,36 +357,15 @@
     out0_ref[...], out1_ref[...] = packed(jnp.concatenate([both[:, :LANES], rim], 0))
 
 
-def corners_kernel(
-    in0_ref, in1_ref, table_ref, weight_ref, out0_ref, out1_ref, sums
-):
-    odd = lax.axis_index("blk") & 1
+def corners_kernel(in1_ref, in0_ref, table_ref, weight_ref, *refs):
+    out_ref, sums = refs[-2:]
+    top = 1 - (lax.axis_index("blk") & 1)
     whole = unpacked(in0_ref[...], in1_ref[...])
     parts = [whole[k * NODES : (k + 1) * NODES] for k in range(ARRAYS)]
     sums[...] = jnp.concatenate(edge_values(table_ref, weight_ref, *parts), 0)
-    north, south = row_edges(sums)
-    lane = lax.broadcasted_iota(i32, (1, LANES), 1)
-
-    def squeezed(values, shift):
-        return jnp.where(
-            lane < 16,
-            pltpu.roll(values, shift, 1) if shift else values,
-            pltpu.roll(values, (shift + 80) % LANES, 1),
-        )
-
-    up = squeezed(jnp.concatenate([whole, pltpu.roll(north, 4, 1)], 0), 80)
-    down = squeezed(jnp.concatenate([whole, pltpu.roll(south, LANES - 4, 1)], 0), 0)
-
-    def in_fours(values):
-        parts = [values[k * LANES : (k + 1) * LANES] for k in range(4)]
-        out = parts[0]
-        for k in range(1, 4):
-            out = jnp.where(lane >= 32 * k, pltpu.roll(parts[k], 32 * k, 1), out)
-        return out
-
-    up, down = in_fours(up), in_fours(down)
-    out0_ref[...] = jnp.where(odd != 0, down, up)
-    out1_ref[...] = jnp.where(odd != 0, up, down)
+    whole = with_row_rim(whole, sums, jnp.broadcast_to(top != 0, (1, LANES)))
+    out_ref[:CORNER_ROWS] = corner_of(whole, 0, top)
+    out_ref[CORNER_ROWS:] = corner_of(whole, 64, top)
 
 
 def own_kernel(stored_ref, slot_ref, lanes_ref, own_ref, hot_ref):
@@ -383,8 +390,8 @@
 
 
 def steps_kernel(
-    block_cols, seam_ref, rows0_ref, rows1_ref, corner0_ref, corner1_ref, low_ref, centre_ref,
-    high_ref, hot_ref, table_ref, weight_ref, ext_ref, outer_ref, out_ref, sums,
+    block_cols, seam_ref, rows0_ref, rows1_ref, near_ref, far0_ref, far1_ref, low_ref,
+    centre_ref, high_ref, hot_ref, table_ref, weight_ref, ext_ref, outer_ref, out_ref, sums,
 ):
     east0, flip0, east1, flip1 = seam_flags(seam_ref, block_cols)
     odd = lax.axis_index("blk") & 1
@@ -395,12 +402,16 @@
     strips = jnp.concatenate(
         [strips[:ROWS], jnp.zeros((EDGE_ROWS, LANES), f32), strips[ROWS:]], 0
     )
-    corner0, corner1 = corner0_ref[...], corner1_ref[...]
+    near = near_ref[...]
+    sources = (near[:CORNER_ROWS], near[CORNER_ROWS:], far0_ref[...], far1_ref[...])
     corners = []
-    for k in range(4):
-        first = pltpu.roll(corner0, LANES - 32 * k, 1) if k else corner0
-        other = pltpu.roll(corner1, (LANES + 32 - 32 * k) % LANES, 1) if k != 1 else corner1
-        corners.append(jnp.where(lane < 32, first, other))
+    for k in range(RIM_ROWS // CORNER_ROWS):
+        rows = None
+        for n, source in enumerate(sources):
+            shift = 16 * (n - k) % LANES
+            part = pltpu.roll(source, shift, 1) if shift else source
+            rows = part if n == 0 else jnp.where(lane >= 16 * n, part, rows)
+        corners.append(rows)
     around = jnp.concatenate([strips, jnp.concatenate(corners, 0)], 1)
     kind = outer_ref[8:16]
     sender = jnp.where(outer_ref[16:24] != 0, odd, 1 - odd)
@@ -505,7 +516,6 @@
 
 def on_device(fields, jacobian, water_depth, coriolis, tide_height, slot_of, seam_rows):
     block_cols = lax.axis_size("blk") // BY
-    count = lax.axis_size("face") * lax.axis_size("blk")
     table, weight = operator_table()
     table, weight, lanes, ext, outer = map(jnp.asarray, (table, weight, *lane_tables()))
     vmem = pl.BlockSpec(memory_space=pltpu.VMEM)
@@ -540,46 +550,74 @@
         return buffers + [pltpu.SemaphoreType.DMA((len(values),))]
 
     needed = (seam_rows, slot_of, *held, table, weight)
-    strip0, strip1, stored = call(
+    corner = ((CORNER_ROWS, LANES), f32)
+    sums = [pltpu.VMEM((4 * NODES, LANES), f32)]
+    strip1, corner1, strip0, corner0, stored = call(
         functools.partial(strips_kernel, block_cols),
         [(hbm, x) for x in needed],
-        [strip, strip, ((ROWS, ELEMENTS), f32)],
+        [strip, corner, strip, corner, ((ROWS, ELEMENTS), f32)],
         10**8,
-        scratch=room(needed, [pltpu.SMEM] + [pltpu.VMEM] * (len(needed) - 1)),
+        scratch=room(needed, [pltpu.SMEM] + [pltpu.VMEM] * (len(needed) - 1)) + sums,
         name="strips",
     )
     span = block_cols * BY
+    both = ("face", "blk")
+    places = [(f, x, y) for f in range(2) for x in range(block_cols) for y in range(BY)]
 
     def rank(face, block_x, block_y):
         return face * span + block_x * BY + block_y
 
-    both = ("face", "blk")
-    places = [(f, x, y) for f in range(2) for x in range(block_cols) for y in range(BY)]
-    if block_cols == 1:
-        halo1 = lax.ppermute(
-            strip1, both, [(rank(f, x, y), rank(1 - f, x, BY - 1 - y)) for f, x, y in places]
+    def same(y):
+        return y
+
+    def in_pair(y):
+        return y ^ 1
+
+    def next_pair(y):
+        other = y + 1 if y % 2 else y - 1
+        return other if 0 <= other < BY else y
+
+    def swapped(value, partner):
+        return lax.ppermute(
+            value, both, [(rank(f, x, y), rank(f, x, partner(y))) for f, x, y in places]
         )
-        halo0 = lax.ppermute(
-            strip0, both, [(rank(f, x, y), rank(1 - f, x, y)) for f, x, y in places]
-        )
-    else:
+
+    def across(value0, value1, partner):
         last = block_cols - 1
+        straight = {
+            (f, x, y): (f, x + 1, partner(y)) if x < last else (1 - f, 0, partner(y))
+            for f, x, y in places
+        }
+        turned = {
+            (f, last, y): (1 - f, 0, BY - 1 - partner(y)) for f in range(2) for y in range(BY)
+        }
+
+        def eastward(value, pairs):
+            return lax.ppermute(value, both, [(rank(*a), rank(*b)) for a, b in pairs.items()])
+
+        def westward(value, pairs):
+            return lax.ppermute(value, both, [(rank(*b), rank(*a)) for a, b in pairs.items()])
+
+        if block_cols == 1:
+            return eastward(value0, straight), eastward(value1, turned)
         flipped = (seam_rows[:, 1] - seam_rows[:, 0]) % seam_rows.shape[1] != 1
         face = lax.axis_index("face")
         block_x = lax.axis_index("blk") // BY
-        from_west = lax.ppermute(strip0, both, [(i, (i + BY) % count) for i in range(count)])
-        from_east = lax.ppermute(strip1, both, [(i, (i - BY) % count) for i in range(count)])
-        turned_west = lax.ppermute(
-            strip0, both,
-            [(rank(f, last, y), rank(1 - f, 0, BY - 1 - y)) for f in range(2) for y in range(BY)],
+        return (
+            jnp.where(
+                (block_x == last) & flipped[face],
+                westward(value1, turned),
+                westward(value1, straight),
+            ),
+            jnp.where(
+                (block_x == 0) & flipped[1 - face],
+                eastward(value0, turned),
+                eastward(value0, straight),
+            ),
         )
-        turned_east = lax.ppermute(
-            strip1, both,
-            [(rank(f, 0, y), rank(1 - f, last, BY - 1 - y)) for f in range(2) for y in range(BY)],
-        )
-        halo0 = jnp.where((block_x == last) & flipped[face], turned_east, from_east)
-        halo1 = jnp.where((block_x == 0) & flipped[1 - face], turned_west, from_west)
-    sums = [pltpu.VMEM((4 * NODES, LANES), f32)]
+
+    halo0, halo1 = across(strip0, strip1, same)
+    far0, far1 = across(corner0, corner1, next_pair)
     rows0, rows1 = call(
         rows_kernel,
         [(vmem, x) for x in (stored, slot_of, table, weight)],
@@ -588,19 +626,6 @@
         scratch=sums,
         name="rows",
     )
-
-    def in_pair(y):
-        return y ^ 1
-
-    def next_pair(y):
-        other = y + 1 if y % 2 else y - 1
-        return other if 0 <= other < BY else y
-
-    def swapped(value, partner):
-        return lax.ppermute(
-            value, both, [(rank(f, x, y), rank(f, x, partner(y))) for f, x, y in places]
-        )
-
     from_rows1 = swapped(rows1, next_pair)
     from_rows0 = swapped(rows0, in_pair)
     own, hot = call(
@@ -610,17 +635,15 @@
         3 * 10**8,
         name="own",
     )
-    corner = ((RIM_ROWS // 4, LANES), f32)
-    corner0, corner1 = call(
+    (near,) = call(
         corners_kernel,
-        [(vmem, x) for x in (halo0, halo1, table, weight)],
-        [corner, corner],
+        [(vmem, x) for x in (halo1, halo0, table, weight, hot, far1, far0)],
+        [((2 * CORNER_ROWS, LANES), f32)],
         10**8,
         scratch=sums,
         name="corners",
     )
-    from_corner1 = swapped(corner1, next_pair)
-    from_corner0 = swapped(corner0, in_pair)
+    near = swapped(near, in_pair)
     tile = ((ALL_ROWS, LANES), f32)
     low, centre, high = call(
         functools.partial(middle_kernel, block_cols),
@@ -635,7 +658,7 @@
         + [
             (vmem, x)
             for x in (
-                from_rows0, from_rows1, from_corner0, from_corner1, low, centre, high,
+                from_rows0, from_rows1, near, far0, far1, low, centre, high,
                 hot, table, weight, ext, outer,
             )
         ],

time: 27.4 us -> 27 us (0.985)
  the two profiles are of different devices: /device:TPU:13 before, /device:TPU:0 now
where the time goes in v4:
time: 27 us; the launch traced here: 26.9 us
  starting transfers between devices  10.4 us (39%)
  Pallas kernels  10.1 us (37%)
  waiting for transfers between devices  6.07 us (22%)
    pallas_call x6, Pallas kernels, call(): pl.pallas_call(kernel, out_shape=[jax.ShapeDtypeStruct(*out) for out in o...  10.1 us
    ppermute x4, starting transfers between devices, eastward(): lax.ppermute(value, both, [(rank(*a), rank(*b)) for a, b in pairs.items()])  9.55 us
    ppermute x4, waiting for transfers between devices, eastward(): lax.ppermute(value, both, [(rank(*a), rank(*b)) for a, b in pairs.items()])  6.06 us
    ppermute x3, starting transfers between devices, swapped(): lax.ppermute(value, both, [(rank(f, x, y), rank(f, x, partner(y))) for f,...  0.89 us
  transfers between devices with their start and end apart: 7, of which 2 were waited for; matrix products, arithmetic and copies ran while one was open for 0% of the time, Pallas kernels for 11%

profile of v4, /device:TPU:0, one launch (start us, length us, event | category | flops | bytes accessed | tf_op | source)
XLA Modules:
  0.0 26.9 jit_solution(15268469336566102842)
XLA Ops:
  0.0 2.3 %strips.1 = (f32[240,128]{1,0:T(8,128)S(1)}, f32[64,128]{1,0:T(8,128)S(1)}, f32[240,128]{1,0:T(8,128)S(1)}, f32[64,128]{1,0:T(8,128)S(1)}, f32[448,256]{1,0:T(8,128)S(1)}) custom-call(s32[2,256]{1,0:T(2,128)} %seam_ref.3, s32[1,256]{1,0:T(1,128)} %slot_ref.3, f32[3,8,8,256]{3,2,1,0:T(8,128)} %refs_2_.1, f32[8,8,256]{2,1,0:T(8,128)} %refs_3_.1, ...), custom_call_target="tpu_custom_call" | custom-call | flops 100000000 | bytes 2097152 | tf_op jit(solution)/shard_map/strips/pallas_call | solution.py:528
  2.3 6.4 %collective-permute-start.2 = (f32[240,128]{1,0:T(8,128)S(1)}, f32[240,128]{1,0:T(8,128)S(1)}, u32[]{:S(2)}, u32[]{:S(2)}) collective-permute-start(f32[240,128]{1,0:T(8,128)S(1)} %get-tuple-element.20), channel_id=1, source_target_pairs={{0,31},{1,30},{2,29},{3,28},{4,27},{5,26},{6,25},{7,24},{8,23},{9,... | collective-permute-start | bytes 368648 | tf_op jit(solution)/shard_map/ppermute | solution.py:596
  8.8 0.5 %collective-permute-start.3 = (f32[240,128]{1,0:T(8,128)S(1)}, f32[240,128]{1,0:T(8,128)S(1)}, u32[]{:S(2)}, u32[]{:S(2)}) collective-permute-start(f32[240,128]{1,0:T(8,128)S(1)} %get-tuple-element.21), channel_id=1, source_target_pairs={{0,16},{1,17},{2,18},{3,19},{4,20},{5,21},{6,22},{7,23},{8,24},{9,... | collective-permute-start | bytes 368648 | tf_op jit(solution)/shard_map/ppermute | solution.py:596
  9.3 1.1 %collective-permute-start.4 = (f32[64,128]{1,0:T(8,128)S(1)}, f32[64,128]{1,0:T(8,128)S(1)}, u32[]{:S(2)}, u32[]{:S(2)}) collective-permute-start(f32[64,128]{1,0:T(8,128)S(1)} %get-tuple-element.23), channel_id=1, source_target_pairs={{0,31},{1,29},{2,30},{3,27},{4,28},{5,25},{6,26},{7,23},{8,24},{9,... | collective-permute-start | bytes 98312 | tf_op jit(solution)/shard_map/ppermute | solution.py:596
  10.4 0.0 copy-done
  10.4 0.0 copy-done.1
  10.4 0.0 copy-done.4
  10.4 0.8 %rows.1 = (f32[240,128]{1,0:T(8,128)S(1)}, f32[240,128]{1,0:T(8,128)S(1)}) custom-call(f32[448,256]{1,0:T(8,128)S(1)} %get-tuple-element.17.stored_ref, s32[1,256]{1,0:T(1,128)S(1)} %copy-done.4, f32[256,384]{1,0:T(8,128)S(1)} %copy-done, f32[64,128]{1,0:T(8,128)S(1)} %copy-done.1), custom_call_target="tpu_custom_call" | custom-call | flops 100000000 | bytes 2097152 | tf_op jit(solution)/shard_map/rows/pallas_call | solution.py:528
  11.2 0.2 collective-permute-start
  11.4 0.7 %collective-permute-start.1 = (f32[240,128]{1,0:T(8,128)S(1)}, f32[240,128]{1,0:T(8,128)S(1)}, u32[]{:S(2)}, u32[]{:S(2)}) collective-permute-start(f32[240,128]{1,0:T(8,128)S(1)} %get-tuple-element.19), channel_id=1, source_target_pairs={{0,0},{1,2},{2,1},{3,4},{4,3},{5,6},{6,5},{7,8},{8,7},{9,10},{10,9... | collective-permute-start | bytes 368648 | tf_op jit(solution)/shard_map/ppermute | solution.py:581
  12.1 4.3 %collective-permute-done.4.refs_1_.far1_ref = f32[64,128]{1,0:T(8,128)S(1)} collective-permute-done((f32[64,128]{1,0:T(8,128)S(1)}, f32[64,128]{1,0:T(8,128)S(1)}, u32[]{:S(2)}, u32[]{:S(2)}) %collective-permute-start.4) | collective-permute-done | bytes 32800 | tf_op jit(solution)/shard_map/ppermute | solution.py:596
  16.4 1.5 %collective-permute-start.5 = (f32[64,128]{1,0:T(8,128)S(1)}, f32[64,128]{1,0:T(8,128)S(1)}, u32[]{:S(2)}, u32[]{:S(2)}) collective-permute-start(f32[64,128]{1,0:T(8,128)S(1)} %get-tuple-element.24), channel_id=1, source_target_pairs={{0,16},{1,18},{2,17},{3,20},{4,19},{5,22},{6,21},{7,24},{8,23},{9,... | collective-permute-start | bytes 98312 | tf_op jit(solution)/shard_map/ppermute | solution.py:596
  17.9 0.7 %own.1 = (f32[448,384]{1,0:T(8,128)S(1)}, bf16[256,384]{1,0:T(8,128)(2,1)S(1)}) custom-call(f32[448,256]{1,0:T(8,128)S(1)} %get-tuple-element.17.stored_ref, s32[1,256]{1,0:T(1,128)S(1)} %copy-done.4, s32[24,384]{1,0:T(8,128)S(1)} %copy-done.2), custom_call_target="tpu_custom_call" | custom-call | flops 300000000 | bytes 2097152 | tf_op jit(solution)/shard_map/own/pallas_call | solution.py:528
  18.6 1.8 %collective-permute-done.5.refs_2_.far0_ref = f32[64,128]{1,0:T(8,128)S(1)} collective-permute-done((f32[64,128]{1,0:T(8,128)S(1)}, f32[64,128]{1,0:T(8,128)S(1)}, u32[]{:S(2)}, u32[]{:S(2)}) %collective-permute-start.5) | collective-permute-done | bytes 32800 | tf_op jit(solution)/shard_map/ppermute | solution.py:596
  20.3 0.0 collective-permute-done.2.in1_ref
  20.3 0.0 collective-permute-done.3.in0_ref
  20.3 0.4 %corners.1 = f32[128,128]{1,0:T(8,128)S(1)} custom-call(f32[240,128]{1,0:T(8,128)S(1)} %collective-permute-done.2.in1_ref, f32[240,128]{1,0:T(8,128)S(1)} %collective-permute-done.3.in0_ref, f32[256,384]{1,0:T(8,128)S(1)} %copy-done, f32[64,128]{1,0:T(8,128)S(1)} %copy-done.1, bf16[256,384]{1,0:T(8,128)(2,1)S(1)} %get-tuple-element.22.refs_0_.hot_ref, ...), custom_call_target="tpu_custom_call" | custom-call | flops 100000000 | bytes 2097152 | tf_op jit(solution)/shard_map/corners/pallas_call | solution.py:528
  20.8 0.1 collective-permute-start.6
  20.8 0.2 copy-done.3
  21.0 1.1 %middle.1 = (f32[480,128]{1,0:T(8,128)S(1)}, f32[480,128]{1,0:T(8,128)S(1)}, f32[480,128]{1,0:T(8,128)S(1)}) custom-call(s32[2,256]{1,0:T(2,128)S(1)} %copy-done.3, f32[240,128]{1,0:T(8,128)S(1)} %collective-permute-done.3.in0_ref, f32[240,128]{1,0:T(8,128)S(1)} %collective-permute-done.2.in1_ref, f32[448,384]{1,0:T(8,128)S(1)} %get-tuple-element.25.own_ref, ...), custom_call_target="tpu_custom_call" | custom-call | flops 100000000 | bytes 2097152 | tf_op jit(solution)/shard_map/middle/pallas_call | solution.py:528
  22.1 0.0 collective-permute-done.rows0_ref
  22.1 0.0 collective-permute-done.1.rows1_ref
  22.1 0.0 collective-permute-done.6.near_ref
  22.1 4.7 %steps.1 = f32[3,8,8,256]{3,2,1,0:T(8,128)} custom-call(s32[2,256]{1,0:T(2,128)S(1)} %copy-done.3, f32[240,128]{1,0:T(8,128)S(1)} %collective-permute-done.rows0_ref, f32[240,128]{1,0:T(8,128)S(1)} %collective-permute-done.1.rows1_ref, f32[128,128]{1,0:T(8,128)S(1)} %collective-permute-done.6.near_ref, ...), custom_call_target="tpu_custom_call" | custom-call | flops 1000000000 | bytes 2097152 | tf_op jit(solution)/shard_map/steps/pallas_call | solution.py:528
  (10 shorter events, 0.0 us)
Async XLA Ops:
  0.0 10.4 %copy-start = (f32[256,384]{1,0:T(8,128)S(1)}, f32[256,384]{1,0:T(8,128)}, u32[]{:S(2)}) copy-start(f32[256,384]{1,0:T(8,128)} %constant.10.clone.refs_7_.table_ref) | copy-start | bytes 1179652
  0.0 10.4 %copy-start.1 = (f32[64,128]{1,0:T(8,128)S(1)}, f32[64,128]{1,0:T(8,128)}, u32[]{:S(2)}) copy-start(f32[64,128]{1,0:T(8,128)} %constant.11.clone.refs_8_.weight_ref) | copy-start | bytes 98308
  2.3 18.0 %collective-permute-start.2 = (f32[240,128]{1,0:T(8,128)S(1)}, f32[240,128]{1,0:T(8,128)S(1)}, u32[]{:S(2)}, u32[]{:S(2)}) collective-permute-start(f32[240,128]{1,0:T(8,128)S(1)} %get-tuple-element.20), channel_id=1, source_target_pairs={{0,31},{1,30},{2,29},{3,28},{4,27},{5,26},{6,25},{7,24},{8,23},{9,... | collective-permute-start | bytes 368648 | tf_op jit(solution)/shard_map/ppermute | solution.py:596
  8.8 11.6 %collective-permute-start.3 = (f32[240,128]{1,0:T(8,128)S(1)}, f32[240,128]{1,0:T(8,128)S(1)}, u32[]{:S(2)}, u32[]{:S(2)}) collective-permute-start(f32[240,128]{1,0:T(8,128)S(1)} %get-tuple-element.21), channel_id=1, source_target_pairs={{0,16},{1,17},{2,18},{3,19},{4,20},{5,21},{6,22},{7,23},{8,24},{9,... | collective-permute-start | bytes 368648 | tf_op jit(solution)/shard_map/ppermute | solution.py:596
  9.3 1.1 %copy-start.4 = (s32[1,256]{1,0:T(1,128)S(1)}, s32[1,256]{1,0:T(1,128)}, u32[]{:S(2)}) copy-start(s32[1,256]{1,0:T(1,128)} %slot_ref.3) | copy-start | bytes 3076
  9.3 7.1 %collective-permute-start.4 = (f32[64,128]{1,0:T(8,128)S(1)}, f32[64,128]{1,0:T(8,128)S(1)}, u32[]{:S(2)}, u32[]{:S(2)}) collective-permute-start(f32[64,128]{1,0:T(8,128)S(1)} %get-tuple-element.23), channel_id=1, source_target_pairs={{0,31},{1,29},{2,30},{3,27},{4,28},{5,25},{6,26},{7,23},{8,24},{9,... | collective-permute-start | bytes 98312 | tf_op jit(solution)/shard_map/ppermute | solution.py:596
  10.4 7.4 %copy-start.2 = (s32[24,384]{1,0:T(8,128)S(1)}, s32[24,384]{1,0:T(8,128)}, u32[]{:S(2)}) copy-start(s32[24,384]{1,0:T(8,128)} %constant.12.clone.lanes_ref) | copy-start | bytes 110596
  11.2 10.8 %collective-permute-start = (f32[240,128]{1,0:T(8,128)S(1)}, f32[240,128]{1,0:T(8,128)S(1)}, u32[]{:S(2)}, u32[]{:S(2)}) collective-permute-start(f32[240,128]{1,0:T(8,128)S(1)} %get-tuple-element.18), channel_id=1, source_target_pairs={{0,1},{1,0},{2,3},{3,2},{4,5},{5,4},{6,7},{7,6},{8,9},{9,8},{10,11... | collective-permute-start | bytes 368648 | tf_op jit(solution)/shard_map/ppermute | solution.py:581
  11.4 10.7 %collective-permute-start.1 = (f32[240,128]{1,0:T(8,128)S(1)}, f32[240,128]{1,0:T(8,128)S(1)}, u32[]{:S(2)}, u32[]{:S(2)}) collective-permute-start(f32[240,128]{1,0:T(8,128)S(1)} %get-tuple-element.19), channel_id=1, source_target_pairs={{0,0},{1,2},{2,1},{3,4},{4,3},{5,6},{6,5},{7,8},{8,7},{9,10},{10,9... | collective-permute-start | bytes 368648 | tf_op jit(solution)/shard_map/ppermute | solution.py:581
  16.4 3.9 %collective-permute-start.5 = (f32[64,128]{1,0:T(8,128)S(1)}, f32[64,128]{1,0:T(8,128)S(1)}, u32[]{:S(2)}, u32[]{:S(2)}) collective-permute-start(f32[64,128]{1,0:T(8,128)S(1)} %get-tuple-element.24), channel_id=1, source_target_pairs={{0,16},{1,18},{2,17},{3,20},{4,19},{5,22},{6,21},{7,24},{8,23},{9,... | collective-permute-start | bytes 98312 | tf_op jit(solution)/shard_map/ppermute | solution.py:596
  20.3 0.7 %copy-start.3 = (s32[2,256]{1,0:T(2,128)S(1)}, s32[2,256]{1,0:T(2,128)}, u32[]{:S(2)}) copy-start(s32[2,256]{1,0:T(2,128)} %seam_ref.3) | copy-start | bytes 6148
  20.8 1.4 %collective-permute-start.6 = (f32[128,128]{1,0:T(8,128)S(1)}, f32[128,128]{1,0:T(8,128)S(1)}, u32[]{:S(2)}, u32[]{:S(2)}) collective-permute-start(f32[128,128]{1,0:T(8,128)S(1)} %corners.1), channel_id=1, source_target_pairs={{0,1},{1,0},{2,3},{3,2},{4,5},{5,4},{6,7},{7,6},{8,9},{9,8},{10,11... | collective-permute-start | bytes 196616 | tf_op jit(solution)/shard_map/ppermute | solution.py:581
  21.0 1.1 %copy-start.5 = (s32[24,256]{1,0:T(8,128)S(1)}, s32[24,256]{1,0:T(8,128)}, u32[]{:S(2)}) copy-start(s32[24,256]{1,0:T(8,128)} %constant.14.clone.outer_ref) | copy-start | bytes 73732
  21.0 1.1 %copy-start.6 = (s32[8,640]{1,0:T(8,128)S(1)}, s32[8,640]{1,0:T(8,128)}, u32[]{:S(2)}) copy-start(s32[8,640]{1,0:T(8,128)} %constant.13.clone.ext_ref) | copy-start | bytes 61444

commit v5 on v4

--- a/solution.py
+++ b/solution.py
@@ -224,8 +224,8 @@
     return mass_tendency(table, h, u, v, tide, root * depth, root, mass * spin) + [mass]
 
 
-def row_edges(sums):
-    return sums[pl.ds(NP - 1, EDGE_ROWS, stride=NP)], sums[pl.ds(0, EDGE_ROWS, stride=NP)]
+def row_edges(sums, tile):
+    return tuple(sums[tile, pl.ds(j, EDGE_ROWS, stride=NP)] for j in (NP - 1, 0))
 
 
 def beside(left, right):
@@ -233,7 +233,7 @@
 
 
 def with_row_rim(whole, sums, top):
-    north, south = row_edges(sums)
+    north, south = row_edges(sums, 0)
     rim = jnp.where(top, pltpu.roll(north, RING, 1), pltpu.roll(south, LANES - RING, 1))
     return jnp.concatenate([whole, rim], 0)
 
@@ -285,8 +285,8 @@
 
 
 def strips_kernel(block_cols, *refs):
-    sources, (out1_ref, far1_ref, out0_ref, far0_ref, stored_ref) = refs[:9], refs[9:14]
-    buffers, sems, sums = refs[14:23], refs[23], refs[24]
+    sources, (out1_ref, out0_ref, stored_ref) = refs[:9], refs[9:12]
+    buffers, sems = refs[12:21], refs[21]
     brought(sources, buffers, sems)
     seam_ref, slot_ref, fields_ref, area_ref, depth_ref, spin_ref, tide_ref = buffers[:7]
     table_ref, weight_ref = buffers[7:]
@@ -322,20 +322,17 @@
         return parts
 
     strip, ring = in_frame(both[:, :LANES]), in_frame(both[:, LANES:])
-    edges = edge_values(table_ref, weight_ref, *map(beside, strip, ring))
+    edges = edge_values(table_ref, weight_ref, *ring)
     east = jnp.where(second, east1, east0) != 0
-    ends = [jnp.where(east, part[NODES - NP :, LANES:], part[:NP, LANES:]) for part in edges]
-    whole = jnp.concatenate(strip + ends, 0)
-    out0_ref[...], out1_ref[...] = packed(whole)
-    odd = lax.axis_index("blk") & 1
-    sums[...] = jnp.concatenate([part[:, :LANES] for part in edges], 0)
-    top0, top1 = odd ^ flip0, odd ^ flip1
-    whole = with_row_rim(whole, sums, jnp.where(second, top1, top0) != 0)
-    far0_ref[...] = corner_of(whole, 0, top0)
-    far1_ref[...] = corner_of(whole, 64, top1)
-
-
-def rows_kernel(stored_ref, slot_ref, table_ref, weight_ref, out0_ref, out1_ref, sums):
+    ends = [jnp.where(east, part[NODES - NP :], part[:NP]) for part in edges]
+    out0_ref[...], out1_ref[...] = packed(jnp.concatenate(strip + ends, 0))
+
+
+def rows_kernel(
+    block_cols, seam_ref, stored_ref, strip1_ref, strip0_ref, slot_ref, table_ref, weight_ref,
+    far1_ref, far0_ref, next_ref, pair_ref, sums,
+):
+    east0, flip0, east1, flip1 = seam_flags(seam_ref, block_cols)
     odd = lax.axis_index("blk") & 1
 
     def goes_up(lane):
@@ -346,26 +343,32 @@
     row = jnp.where(up, GY - RING, 0) + ((lane & 63) >> 4)
     row = jnp.where(lane >= LANES, jnp.where(up, GY - RING - 1, RING), row)
     both = picked(stored_ref[...], by_slot(slot_ref, (lane & 15) * GY + row))
-    h, u, v, area, depth, spin, tide = [
-        both[k * NODES : (k + 1) * NODES, LANES:] for k in range(ARRAYS)
+    whole = unpacked(strip0_ref[...], strip1_ref[...])
+    parts = [
+        beside(whole[k * NODES : (k + 1) * NODES], both[k * NODES : (k + 1) * NODES, LANES:])
+        for k in range(ARRAYS)
     ]
-    edges = edge_values(table_ref, weight_ref, h, u, v, area, depth, spin, tide)
-    sums[...] = jnp.concatenate(edges, 0)
-    north, south = row_edges(sums)
-    up = goes_up(lax.broadcasted_iota(i32, (1, LANES), 1))
-    rim = jnp.where(up, north, south)
-    out0_ref[...], out1_ref[...] = packed(jnp.concatenate([both[:, :LANES], rim], 0))
-
-
-def corners_kernel(in1_ref, in0_ref, table_ref, weight_ref, *refs):
+    edges = jnp.concatenate(edge_values(table_ref, weight_ref, *parts), 0)
+    sums[0], sums[1] = edges[:, :LANES], edges[:, LANES:]
+    lane = lax.broadcasted_iota(i32, (1, LANES), 1)
+    top0, top1 = odd ^ flip0, odd ^ flip1
+    whole = with_row_rim(whole, sums, jnp.where(lane >= 64, top1, top0) != 0)
+    far0_ref[...] = corner_of(whole, 0, top0)
+    far1_ref[...] = corner_of(whole, 64, top1)
+    rim = jnp.where(goes_up(lane), *row_edges(sums, 1))
+    pair_ref[...], next_ref[...] = packed(jnp.concatenate([both[:, :LANES], rim], 0))
+
+
+def corners_kernel(in1_ref, in0_ref, pair_ref, table_ref, weight_ref, *refs):
     out_ref, sums = refs[-2:]
     top = 1 - (lax.axis_index("blk") & 1)
     whole = unpacked(in0_ref[...], in1_ref[...])
     parts = [whole[k * NODES : (k + 1) * NODES] for k in range(ARRAYS)]
-    sums[...] = jnp.concatenate(edge_values(table_ref, weight_ref, *parts), 0)
+    sums[0] = jnp.concatenate(edge_values(table_ref, weight_ref, *parts), 0)
     whole = with_row_rim(whole, sums, jnp.broadcast_to(top != 0, (1, LANES)))
-    out_ref[:CORNER_ROWS] = corner_of(whole, 0, top)
-    out_ref[CORNER_ROWS:] = corner_of(whole, 64, top)
+    out_ref[:HALF_ROWS] = pair_ref[...]
+    out_ref[HALF_ROWS : HALF_ROWS + CORNER_ROWS] = corner_of(whole, 0, top)
+    out_ref[HALF_ROWS + CORNER_ROWS :] = corner_of(whole, 64, top)
 
 
 def own_kernel(stored_ref, slot_ref, lanes_ref, own_ref, hot_ref):
@@ -390,19 +393,20 @@
 
 
 def steps_kernel(
-    block_cols, seam_ref, rows0_ref, rows1_ref, near_ref, far0_ref, far1_ref, low_ref,
-    centre_ref, high_ref, hot_ref, table_ref, weight_ref, ext_ref, outer_ref, out_ref, sums,
+    block_cols, seam_ref, pair_ref, next_ref, far0_ref, far1_ref, low_ref, centre_ref,
+    high_ref, hot_ref, table_ref, weight_ref, ext_ref, outer_ref, out_ref, sums,
 ):
     east0, flip0, east1, flip1 = seam_flags(seam_ref, block_cols)
     odd = lax.axis_index("blk") & 1
     block_y = lax.rem(lax.axis_index("blk"), BY)
 
     lane = lax.broadcasted_iota(i32, (1, LANES), 1)
-    strips = unpacked(rows0_ref[...], rows1_ref[...])
+    pair = pair_ref[...]
+    strips = unpacked(pair[:HALF_ROWS], next_ref[...])
     strips = jnp.concatenate(
         [strips[:ROWS], jnp.zeros((EDGE_ROWS, LANES), f32), strips[ROWS:]], 0
     )
-    near = near_ref[...]
+    near = pair[HALF_ROWS:]
     sources = (near[:CORNER_ROWS], near[CORNER_ROWS:], far0_ref[...], far1_ref[...])
     corners = []
     for k in range(RIM_ROWS // CORNER_ROWS):
@@ -551,13 +555,12 @@
 
     needed = (seam_rows, slot_of, *held, table, weight)
     corner = ((CORNER_ROWS, LANES), f32)
-    sums = [pltpu.VMEM((4 * NODES, LANES), f32)]
-    strip1, corner1, strip0, corner0, stored = call(
+    strip1, strip0, stored = call(
         functools.partial(strips_kernel, block_cols),
         [(hbm, x) for x in needed],
-        [strip, corner, strip, corner, ((ROWS, ELEMENTS), f32)],
+        [strip, strip, ((ROWS, ELEMENTS), f32)],
         10**8,
-        scratch=room(needed, [pltpu.SMEM] + [pltpu.VMEM] * (len(needed) - 1)) + sums,
+        scratch=room(needed, [pltpu.SMEM] + [pltpu.VMEM] * (len(needed) - 1)),
         name="strips",
     )
     span = block_cols * BY
@@ -617,17 +620,17 @@
         )
 
     halo0, halo1 = across(strip0, strip1, same)
-    far0, far1 = across(corner0, corner1, next_pair)
-    rows0, rows1 = call(
-        rows_kernel,
-        [(vmem, x) for x in (stored, slot_of, table, weight)],
-        [strip, strip],
+    far1, far0, to_next, to_pair = call(
+        functools.partial(rows_kernel, block_cols),
+        [(smem, seam_rows)]
+        + [(vmem, x) for x in (stored, strip1, strip0, slot_of, table, weight)],
+        [corner, corner, strip, strip],
         10**8,
-        scratch=sums,
+        scratch=[pltpu.VMEM((2, 4 * NODES, LANES), f32)],
         name="rows",
     )
-    from_rows1 = swapped(rows1, next_pair)
-    from_rows0 = swapped(rows0, in_pair)
+    far0, far1 = across(far0, far1, next_pair)
+    from_next = swapped(to_next, next_pair)
     own, hot = call(
         own_kernel,
         [(vmem, x) for x in (stored, slot_of, lanes)],
@@ -635,15 +638,15 @@
         3 * 10**8,
         name="own",
     )
-    (near,) = call(
+    (to_pair,) = call(
         corners_kernel,
-        [(vmem, x) for x in (halo1, halo0, table, weight, hot, far1, far0)],
-        [((2 * CORNER_ROWS, LANES), f32)],
+        [(vmem, x) for x in (halo1, halo0, to_pair, table, weight, hot, far1, far0, from_next)],
+        [((HALF_ROWS + 2 * CORNER_ROWS, LANES), f32)],
         10**8,
-        scratch=sums,
+        scratch=[pltpu.VMEM((1, 4 * NODES, LANES), f32)],
         name="corners",
     )
-    near = swapped(near, in_pair)
+    from_pair = swapped(to_pair, in_pair)
     tile = ((ALL_ROWS, LANES), f32)
     low, centre, high = call(
         functools.partial(middle_kernel, block_cols),
@@ -658,7 +661,7 @@
         + [
             (vmem, x)
             for x in (
-                from_rows0, from_rows1, near, far0, far1, low, centre, high,
+                from_pair, from_next, far0, far1, low, centre, high,
                 hot, table, weight, ext, outer,
             )
         ],

time: 27 us -> 26 us (0.963)
  the two profiles are of different devices: /device:TPU:0 before, /device:TPU:5 now
where the time goes in v5:
time: 26 us; the launch traced here: 25.8 us
  starting transfers between devices  11.7 us (45%)
  Pallas kernels  10.6 us (41%)
  waiting for transfers between devices  2.92 us (11%)
  local copies, waits for them, and re-layouts  0.44 us (2%)
    pallas_call x6, Pallas kernels, call(): pl.pallas_call(kernel, out_shape=[jax.ShapeDtypeStruct(*out) for out in o...  10.6 us
    ppermute x4, starting transfers between devices, eastward(): lax.ppermute(value, both, [(rank(*a), rank(*b)) for a, b in pairs.items()])  8.38 us
    ppermute x2, starting transfers between devices, swapped(): lax.ppermute(value, both, [(rank(f, x, y), rank(f, x, partner(y))) for f,...  3.36 us
    ppermute x4, waiting for transfers between devices, eastward(): lax.ppermute(value, both, [(rank(*a), rank(*b)) for a, b in pairs.items()])  2.91 us
  transfers between devices with their start and end apart: 6, of which 2 were waited for; matrix products, arithmetic and copies ran while one was open for 0% of the time, Pallas kernels for 13%

profile of v5, /device:TPU:5, one launch (start us, length us, event | category | flops | bytes accessed | tf_op | source)
XLA Modules:
  0.0 25.8 jit_solution(4075425734698397808)
XLA Ops:
  0.0 2.2 %strips.1 = (f32[240,128]{1,0:T(8,128)S(1)}, f32[240,128]{1,0:T(8,128)S(1)}, f32[448,256]{1,0:T(8,128)S(1)}) custom-call(s32[2,256]{1,0:T(2,128)} %seam_ref.5, s32[1,256]{1,0:T(1,128)} %slot_ref.3, f32[3,8,8,256]{3,2,1,0:T(8,128)} %refs_2_.1, f32[8,8,256]{2,1,0:T(8,128)} %refs_3_.1, f32[8,8,256]{2,1,0:T(8,128)} %refs_4_.1, f32[8,8,256]{2,1,0:T(8,128)} %refs_5_.1, ...), custom_call_target="tpu_custom_call" | custom-call | flops 100000000 | bytes 2097152 | tf_op jit(solution)/shard_map/strips/pallas_call | solution.py:532
  2.2 0.0 copy-start.3
  2.2 4.8 %collective-permute-start = (f32[240,128]{1,0:T(8,128)S(1)}, f32[240,128]{1,0:T(8,128)S(1)}, u32[]{:S(2)}, u32[]{:S(2)}) collective-permute-start(f32[240,128]{1,0:T(8,128)S(1)} %get-tuple-element.17.strip1_ref), channel_id=1, source_target_pairs={{0,31},{1,30},{2,29},{3,28},{4,27},{5,26},{6,25},{7,24},{8,23},{9,... | collective-permute-start | bytes 368648 | tf_op jit(solution)/shard_map/ppermute | solution.py:599
  7.1 0.3 %collective-permute-start.1 = (f32[240,128]{1,0:T(8,128)S(1)}, f32[240,128]{1,0:T(8,128)S(1)}, u32[]{:S(2)}, u32[]{:S(2)}) collective-permute-start(f32[240,128]{1,0:T(8,128)S(1)} %get-tuple-element.18.strip0_ref), channel_id=1, source_target_pairs={{0,16},{1,17},{2,18},{3,19},{4,20},{5,21},{6,22},{7,23},{8,24},{9,... | collective-permute-start | bytes 368648 | tf_op jit(solution)/shard_map/ppermute | solution.py:599
  7.3 0.0 copy-done
  7.3 0.0 copy-done.1
  7.3 0.0 copy-done.3
  7.3 0.4 %copy-done.4 = s32[1,256]{1,0:T(1,128)S(1)} copy-done((s32[1,256]{1,0:T(1,128)S(1)}, s32[1,256]{1,0:T(1,128)}, u32[]{:S(2)}) %copy-start.4) | copy-done | bytes 1048
  7.7 1.5 %rows.1 = (f32[64,128]{1,0:T(8,128)S(1)}, f32[64,128]{1,0:T(8,128)S(1)}, f32[240,128]{1,0:T(8,128)S(1)}, f32[240,128]{1,0:T(8,128)S(1)}) custom-call(s32[2,256]{1,0:T(2,128)S(1)} %copy-done.3, f32[448,256]{1,0:T(8,128)S(1)} %get-tuple-element.19.stored_ref, f32[240,128]{1,0:T(8,128)S(1)} %get-tuple-element.17.strip1_ref, ...), custom_call_target="tpu_custom_call" | custom-call | flops 100000000 | bytes 2097152 | tf_op jit(solution)/shard_map/rows/pallas_call | solution.py:532
  9.2 1.9 %collective-permute-start.4 = (f32[240,128]{1,0:T(8,128)S(1)}, f32[240,128]{1,0:T(8,128)S(1)}, u32[]{:S(2)}, u32[]{:S(2)}) collective-permute-start(f32[240,128]{1,0:T(8,128)S(1)} %get-tuple-element.24), channel_id=1, source_target_pairs={{0,0},{1,2},{2,1},{3,4},{4,3},{5,6},{6,5},{7,8},{8,7},{9,10},{10,9... | collective-permute-start | bytes 368648 | tf_op jit(solution)/shard_map/ppermute | solution.py:584
  11.1 1.8 %collective-permute-start.2 = (f32[64,128]{1,0:T(8,128)S(1)}, f32[64,128]{1,0:T(8,128)S(1)}, u32[]{:S(2)}, u32[]{:S(2)}) collective-permute-start(f32[64,128]{1,0:T(8,128)S(1)} %get-tuple-element.22), channel_id=1, source_target_pairs={{0,31},{1,29},{2,30},{3,27},{4,28},{5,25},{6,26},{7,23},{8,24},{9,... | collective-permute-start | bytes 98312 | tf_op jit(solution)/shard_map/ppermute | solution.py:599
  12.9 1.5 %collective-permute-start.3 = (f32[64,128]{1,0:T(8,128)S(1)}, f32[64,128]{1,0:T(8,128)S(1)}, u32[]{:S(2)}, u32[]{:S(2)}) collective-permute-start(f32[64,128]{1,0:T(8,128)S(1)} %get-tuple-element.23), channel_id=1, source_target_pairs={{0,16},{1,18},{2,17},{3,20},{4,19},{5,22},{6,21},{7,24},{8,23},{9,... | collective-permute-start | bytes 98312 | tf_op jit(solution)/shard_map/ppermute | solution.py:599
  14.5 0.0 copy-done.2
  14.5 0.7 %own.1 = (f32[448,384]{1,0:T(8,128)S(1)}, bf16[256,384]{1,0:T(8,128)(2,1)S(1)}) custom-call(f32[448,256]{1,0:T(8,128)S(1)} %get-tuple-element.19.stored_ref, s32[1,256]{1,0:T(1,128)S(1)} %copy-done.4, s32[24,384]{1,0:T(8,128)S(1)} %copy-done.2), custom_call_target="tpu_custom_call" | custom-call | flops 300000000 | bytes 2097152 | tf_op jit(solution)/shard_map/own/pallas_call | solution.py:532
  15.2 1.2 %collective-permute-done.2.refs_1_.far1_ref = f32[64,128]{1,0:T(8,128)S(1)} collective-permute-done((f32[64,128]{1,0:T(8,128)S(1)}, f32[64,128]{1,0:T(8,128)S(1)}, u32[]{:S(2)}, u32[]{:S(2)}) %collective-permute-start.2) | collective-permute-done | bytes 32800 | tf_op jit(solution)/shard_map/ppermute | solution.py:599
  16.4 1.7 %collective-permute-done.3.refs_2_.far0_ref = f32[64,128]{1,0:T(8,128)S(1)} collective-permute-done((f32[64,128]{1,0:T(8,128)S(1)}, f32[64,128]{1,0:T(8,128)S(1)}, u32[]{:S(2)}, u32[]{:S(2)}) %collective-permute-start.3) | collective-permute-done | bytes 32800 | tf_op jit(solution)/shard_map/ppermute | solution.py:599
  18.1 0.0 collective-permute-done.in1_ref
  18.1 0.0 collective-permute-done.1.in0_ref
  18.1 0.0 collective-permute-done.4.refs_3_.next_ref
  18.1 0.4 %corners.1 = f32[368,128]{1,0:T(8,128)S(1)} custom-call(f32[240,128]{1,0:T(8,128)S(1)} %collective-permute-done.in1_ref, f32[240,128]{1,0:T(8,128)S(1)} %collective-permute-done.1.in0_ref, f32[240,128]{1,0:T(8,128)S(1)} %get-tuple-element.20.pair_ref, f32[256,384]{1,0:T(8,128)S(1)} %copy-done, f32[64,128]{1,0:T(8,128)S(1)} %copy-done.1, ...), custom_call_target="tpu_custom_call" | custom-call | flops 100000000 | bytes 2097152 | tf_op jit(solution)/shard_map/corners/pallas_call | solution.py:532
  18.5 1.4 %collective-permute-start.5 = (f32[368,128]{1,0:T(8,128)S(1)}, f32[368,128]{1,0:T(8,128)S(1)}, u32[]{:S(2)}, u32[]{:S(2)}) collective-permute-start(f32[368,128]{1,0:T(8,128)S(1)} %corners.1), channel_id=1, source_target_pairs={{0,1},{1,0},{2,3},{3,2},{4,5},{5,4},{6,7},{7,6},{8,9},{9,8},{10,11... | collective-permute-start | bytes 565256 | tf_op jit(solution)/shard_map/ppermute | solution.py:584
  19.9 1.1 %middle.1 = (f32[480,128]{1,0:T(8,128)S(1)}, f32[480,128]{1,0:T(8,128)S(1)}, f32[480,128]{1,0:T(8,128)S(1)}) custom-call(s32[2,256]{1,0:T(2,128)S(1)} %copy-done.3, f32[240,128]{1,0:T(8,128)S(1)} %collective-permute-done.1.in0_ref, f32[240,128]{1,0:T(8,128)S(1)} %collective-permute-done.in1_ref, f32[448,384]{1,0:T(8,128)S(1)} %get-tuple-element.25.own_ref, ...), custom_call_target="tpu_custom_call" | custom-call | flops 100000000 | bytes 2097152 | tf_op jit(solution)/shard_map/middle/pallas_call | solution.py:532
  21.0 0.0 collective-permute-done.5.pair_ref
  21.1 4.7 %steps.1 = f32[3,8,8,256]{3,2,1,0:T(8,128)} custom-call(s32[2,256]{1,0:T(2,128)S(1)} %copy-done.3, f32[368,128]{1,0:T(8,128)S(1)} %collective-permute-done.5.pair_ref, f32[240,128]{1,0:T(8,128)S(1)} %collective-permute-done.4.refs_3_.next_ref, f32[64,128]{1,0:T(8,128)S(1)} %collective-permute-done.3.refs_2_.far0_ref, ...), custom_call_target="tpu_custom_call" | custom-call | flops 1000000000 | bytes 2097152 | tf_op jit(solution)/shard_map/steps/pallas_call | solution.py:532
  (8 shorter events, 0.0 us)
Async XLA Ops:
  0.0 7.3 %copy-start = (f32[256,384]{1,0:T(8,128)S(1)}, f32[256,384]{1,0:T(8,128)}, u32[]{:S(2)}) copy-start(f32[256,384]{1,0:T(8,128)} %constant.10.clone.refs_7_.table_ref) | copy-start | bytes 1179652
  0.0 7.3 %copy-start.1 = (f32[64,128]{1,0:T(8,128)S(1)}, f32[64,128]{1,0:T(8,128)}, u32[]{:S(2)}) copy-start(f32[64,128]{1,0:T(8,128)} %constant.11.clone.refs_8_.weight_ref) | copy-start | bytes 98308
  2.2 5.1 %copy-start.3 = (s32[2,256]{1,0:T(2,128)S(1)}, s32[2,256]{1,0:T(2,128)}, u32[]{:S(2)}) copy-start(s32[2,256]{1,0:T(2,128)} %seam_ref.5) | copy-start | bytes 6148
  2.2 15.8 %collective-permute-start = (f32[240,128]{1,0:T(8,128)S(1)}, f32[240,128]{1,0:T(8,128)S(1)}, u32[]{:S(2)}, u32[]{:S(2)}) collective-permute-start(f32[240,128]{1,0:T(8,128)S(1)} %get-tuple-element.17.strip1_ref), channel_id=1, source_target_pairs={{0,31},{1,30},{2,29},{3,28},{4,27},{5,26},{6,25},{7,24},{8,23},{9,... | collective-permute-start | bytes 368648 | tf_op jit(solution)/shard_map/ppermute | solution.py:599
  7.1 0.7 %copy-start.4 = (s32[1,256]{1,0:T(1,128)S(1)}, s32[1,256]{1,0:T(1,128)}, u32[]{:S(2)}) copy-start(s32[1,256]{1,0:T(1,128)} %slot_ref.3) | copy-start | bytes 3076
  7.1 11.0 %collective-permute-start.1 = (f32[240,128]{1,0:T(8,128)S(1)}, f32[240,128]{1,0:T(8,128)S(1)}, u32[]{:S(2)}, u32[]{:S(2)}) collective-permute-start(f32[240,128]{1,0:T(8,128)S(1)} %get-tuple-element.18.strip0_ref), channel_id=1, source_target_pairs={{0,16},{1,17},{2,18},{3,19},{4,20},{5,21},{6,22},{7,23},{8,24},{9,... | collective-permute-start | bytes 368648 | tf_op jit(solution)/shard_map/ppermute | solution.py:599
  7.7 6.7 %copy-start.2 = (s32[24,384]{1,0:T(8,128)S(1)}, s32[24,384]{1,0:T(8,128)}, u32[]{:S(2)}) copy-start(s32[24,384]{1,0:T(8,128)} %constant.12.clone.lanes_ref) | copy-start | bytes 110596
  9.2 8.8 %collective-permute-start.4 = (f32[240,128]{1,0:T(8,128)S(1)}, f32[240,128]{1,0:T(8,128)S(1)}, u32[]{:S(2)}, u32[]{:S(2)}) collective-permute-start(f32[240,128]{1,0:T(8,128)S(1)} %get-tuple-element.24), channel_id=1, source_target_pairs={{0,0},{1,2},{2,1},{3,4},{4,3},{5,6},{6,5},{7,8},{8,7},{9,10},{10,9... | collective-permute-start | bytes 368648 | tf_op jit(solution)/shard_map/ppermute | solution.py:584
  11.1 5.2 %collective-permute-start.2 = (f32[64,128]{1,0:T(8,128)S(1)}, f32[64,128]{1,0:T(8,128)S(1)}, u32[]{:S(2)}, u32[]{:S(2)}) collective-permute-start(f32[64,128]{1,0:T(8,128)S(1)} %get-tuple-element.22), channel_id=1, source_target_pairs={{0,31},{1,29},{2,30},{3,27},{4,28},{5,25},{6,26},{7,23},{8,24},{9,... | collective-permute-start | bytes 98312 | tf_op jit(solution)/shard_map/ppermute | solution.py:599
  12.9 5.1 %collective-permute-start.3 = (f32[64,128]{1,0:T(8,128)S(1)}, f32[64,128]{1,0:T(8,128)S(1)}, u32[]{:S(2)}, u32[]{:S(2)}) collective-permute-start(f32[64,128]{1,0:T(8,128)S(1)} %get-tuple-element.23), channel_id=1, source_target_pairs={{0,16},{1,18},{2,17},{3,20},{4,19},{5,22},{6,21},{7,24},{8,23},{9,... | collective-permute-start | bytes 98312 | tf_op jit(solution)/shard_map/ppermute | solution.py:599
  18.5 2.5 %collective-permute-start.5 = (f32[368,128]{1,0:T(8,128)S(1)}, f32[368,128]{1,0:T(8,128)S(1)}, u32[]{:S(2)}, u32[]{:S(2)}) collective-permute-start(f32[368,128]{1,0:T(8,128)S(1)} %corners.1), channel_id=1, source_target_pairs={{0,1},{1,0},{2,3},{3,2},{4,5},{5,4},{6,7},{7,6},{8,9},{9,8},{10,11... | collective-permute-start | bytes 565256 | tf_op jit(solution)/shard_map/ppermute | solution.py:584
  19.9 1.1 %copy-start.5 = (s32[24,256]{1,0:T(8,128)S(1)}, s32[24,256]{1,0:T(8,128)}, u32[]{:S(2)}) copy-start(s32[24,256]{1,0:T(8,128)} %constant.14.clone.outer_ref) | copy-start | bytes 73732
  19.9 1.1 %copy-start.6 = (s32[8,640]{1,0:T(8,128)S(1)}, s32[8,640]{1,0:T(8,128)}, u32[]{:S(2)}) copy-start(s32[8,640]{1,0:T(8,128)} %constant.13.clone.ext_ref) | copy-start | bytes 61444

commit v6 on v5

--- a/solution.py
+++ b/solution.py
@@ -224,8 +224,8 @@
     return mass_tendency(table, h, u, v, tide, root * depth, root, mass * spin) + [mass]
 
 
-def row_edges(sums, tile):
-    return tuple(sums[tile, pl.ds(j, EDGE_ROWS, stride=NP)] for j in (NP - 1, 0))
+def row_edges(sums):
+    return tuple(sums[0, pl.ds(j, EDGE_ROWS, stride=NP)] for j in (NP - 1, 0))
 
 
 def beside(left, right):
@@ -233,7 +233,7 @@
 
 
 def with_row_rim(whole, sums, top):
-    north, south = row_edges(sums, 0)
+    north, south = row_edges(sums)
     rim = jnp.where(top, pltpu.roll(north, RING, 1), pltpu.roll(south, LANES - RING, 1))
     return jnp.concatenate([whole, rim], 0)
 
@@ -285,8 +285,9 @@
 
 
 def strips_kernel(block_cols, *refs):
-    sources, (out1_ref, out0_ref, stored_ref) = refs[:9], refs[9:12]
-    buffers, sems = refs[12:21], refs[21]
+    sources = refs[:9]
+    out1_ref, far1_ref, out0_ref, far0_ref, next_ref, pair_ref, stored_ref = refs[9:16]
+    buffers, sems, sums = refs[16:25], refs[25], refs[26]
     brought(sources, buffers, sems)
     seam_ref, slot_ref, fields_ref, area_ref, depth_ref, spin_ref, tide_ref = buffers[:7]
     table_ref, weight_ref = buffers[7:]
@@ -299,7 +300,16 @@
     east = jnp.where(second, east1, east0) != 0
     col = jnp.where(east, GX - RING, 0) + (place & 3)
     col = jnp.where(lane >= LANES, jnp.where(east, GX - RING - 1, RING), col)
-    one_hot = by_slot(slot_ref, col * GY + row)
+    cells = col * GY + row
+    odd = lax.axis_index("blk") & 1
+
+    def goes_up(lane):
+        return jnp.where((lane & 64) != 0, odd, 1 - odd) != 0
+
+    up = goes_up(lane)
+    row = jnp.where(up, GY - RING, 0) + ((lane & 63) >> 4)
+    row = jnp.where(lane >= LANES, jnp.where(up, GY - RING - 1, RING), row)
+    one_hot = by_slot(slot_ref, beside(cells, (lane & 15) * GY + row))
     stored = stored_rows(fields_ref, (area_ref, depth_ref, spin_ref, tide_ref))
     stored_ref[...] = stored
     both = picked(stored, one_hot)
@@ -321,42 +331,26 @@
         parts[5] = parts[5] * sign
         return parts
 
-    strip, ring = in_frame(both[:, :LANES]), in_frame(both[:, LANES:])
-    edges = edge_values(table_ref, weight_ref, *ring)
+    strip, ring = in_frame(both[:, :LANES]), in_frame(both[:, LANES : 2 * LANES])
+    rows = both[:, 3 * LANES :]
+    rows = [rows[k * NODES : (k + 1) * NODES] for k in range(ARRAYS)]
+    edges = edge_values(
+        table_ref, weight_ref, *(jnp.concatenate(parts, 1) for parts in zip(strip, ring, rows))
+    )
     east = jnp.where(second, east1, east0) != 0
-    ends = [jnp.where(east, part[NODES - NP :], part[:NP]) for part in edges]
-    out0_ref[...], out1_ref[...] = packed(jnp.concatenate(strip + ends, 0))
-
-
-def rows_kernel(
-    block_cols, seam_ref, stored_ref, strip1_ref, strip0_ref, slot_ref, table_ref, weight_ref,
-    far1_ref, far0_ref, next_ref, pair_ref, sums,
-):
-    east0, flip0, east1, flip1 = seam_flags(seam_ref, block_cols)
-    odd = lax.axis_index("blk") & 1
-
-    def goes_up(lane):
-        return jnp.where((lane & 64) != 0, odd, 1 - odd) != 0
-
-    lane = lax.broadcasted_iota(i32, (8, 2 * LANES), 1)
-    up = goes_up(lane)
-    row = jnp.where(up, GY - RING, 0) + ((lane & 63) >> 4)
-    row = jnp.where(lane >= LANES, jnp.where(up, GY - RING - 1, RING), row)
-    both = picked(stored_ref[...], by_slot(slot_ref, (lane & 15) * GY + row))
-    whole = unpacked(strip0_ref[...], strip1_ref[...])
-    parts = [
-        beside(whole[k * NODES : (k + 1) * NODES], both[k * NODES : (k + 1) * NODES, LANES:])
-        for k in range(ARRAYS)
-    ]
-    edges = jnp.concatenate(edge_values(table_ref, weight_ref, *parts), 0)
-    sums[0], sums[1] = edges[:, :LANES], edges[:, LANES:]
-    lane = lax.broadcasted_iota(i32, (1, LANES), 1)
+    ends = [part[:, LANES : 2 * LANES] for part in edges]
+    ends = [jnp.where(east, part[NODES - NP :], part[:NP]) for part in ends]
+    whole = jnp.concatenate(strip + ends, 0)
+    out0_ref[...], out1_ref[...] = packed(whole)
+    sums[0] = jnp.concatenate([part[:, :LANES] for part in edges], 0)
     top0, top1 = odd ^ flip0, odd ^ flip1
-    whole = with_row_rim(whole, sums, jnp.where(lane >= 64, top1, top0) != 0)
+    whole = with_row_rim(whole, sums, jnp.where(second, top1, top0) != 0)
     far0_ref[...] = corner_of(whole, 0, top0)
     far1_ref[...] = corner_of(whole, 64, top1)
-    rim = jnp.where(goes_up(lane), *row_edges(sums, 1))
-    pair_ref[...], next_ref[...] = packed(jnp.concatenate([both[:, :LANES], rim], 0))
+    sums[0] = jnp.concatenate([part[:, 2 * LANES :] for part in edges], 0)
+    rim = jnp.where(goes_up(lane), *row_edges(sums))
+    rows = jnp.concatenate([both[:, 2 * LANES : 3 * LANES], rim], 0)
+    pair_ref[...], next_ref[...] = packed(rows)
 
 
 def corners_kernel(in1_ref, in0_ref, pair_ref, table_ref, weight_ref, *refs):
@@ -555,12 +549,13 @@
 
     needed = (seam_rows, slot_of, *held, table, weight)
     corner = ((CORNER_ROWS, LANES), f32)
-    strip1, strip0, stored = call(
+    scratch = [pltpu.VMEM((1, 4 * NODES, LANES), f32)]
+    strip1, far1, strip0, far0, to_next, to_pair, stored = call(
         functools.partial(strips_kernel, block_cols),
         [(hbm, x) for x in needed],
-        [strip, strip, ((ROWS, ELEMENTS), f32)],
+        [strip, corner, strip, corner, strip, strip, ((ROWS, ELEMENTS), f32)],
         10**8,
-        scratch=room(needed, [pltpu.SMEM] + [pltpu.VMEM] * (len(needed) - 1)),
+        scratch=room(needed, [pltpu.SMEM] + [pltpu.VMEM] * (len(needed) - 1)) + scratch,
         name="strips",
     )
     span = block_cols * BY
@@ -620,22 +615,13 @@
         )
 
     halo0, halo1 = across(strip0, strip1, same)
-    far1, far0, to_next, to_pair = call(
-        functools.partial(rows_kernel, block_cols),
-        [(smem, seam_rows)]
-        + [(vmem, x) for x in (stored, strip1, strip0, slot_of, table, weight)],
-        [corner, corner, strip, strip],
-        10**8,
-        scratch=[pltpu.VMEM((2, 4 * NODES, LANES), f32)],
-        name="rows",
-    )
     far0, far1 = across(far0, far1, next_pair)
     from_next = swapped(to_next, next_pair)
     own, hot = call(
         own_kernel,
         [(vmem, x) for x in (stored, slot_of, lanes)],
         [((ROWS, MID), f32), ((ELEMENTS, MID), bf16)],
-        3 * 10**8,
+        10**8,
         name="own",
     )
     (to_pair,) = call(
@@ -643,7 +629,7 @@
         [(vmem, x) for x in (halo1, halo0, to_pair, table, weight, hot, far1, far0, from_next)],
         [((HALF_ROWS + 2 * CORNER_ROWS, LANES), f32)],
         10**8,
-        scratch=[pltpu.VMEM((1, 4 * NODES, LANES), f32)],
+        scratch=scratch,
         name="corners",
     )
     from_pair = swapped(to_pair, in_pair)
@@ -666,7 +652,7 @@
             )
         ],
         [(fields.shape, f32)],
-        10**9,
+        10**8,
         scratch=[pltpu.VMEM((EXT // LANES, 3 * NODES, LANES), f32)],
         name="steps",
     )

time: 26 us -> 24.3 us (0.935)
  the two profiles are of different devices: /device:TPU:5 before, /device:TPU:0 now
where the time goes in v6:
time: 24.3 us; the launch traced here: 24 us
  starting transfers between devices  9.68 us (40%)
  Pallas kernels  9.42 us (39%)
  waiting for transfers between devices  4.8 us (20%)
    pallas_call x5, Pallas kernels, call(): pl.pallas_call(kernel, out_shape=[jax.ShapeDtypeStruct(*out) for out in o...  9.42 us
    ppermute x4, starting transfers between devices, eastward(): lax.ppermute(value, both, [(rank(*a), rank(*b)) for a, b in pairs.items()])  8.61 us
    ppermute x4, waiting for transfers between devices, eastward(): lax.ppermute(value, both, [(rank(*a), rank(*b)) for a, b in pairs.items()])  4.8 us
    ppermute x2, starting transfers between devices, swapped(): lax.ppermute(value, both, [(rank(f, x, y), rank(f, x, partner(y))) for f,...  1.07 us
  transfers between devices with their start and end apart: 6, of which 1 were waited for; matrix products, arithmetic and copies ran while one was open for 0% of the time, Pallas kernels for 7%

profile of v6, /device:TPU:0, one launch (start us, length us, event | category | flops | bytes accessed | tf_op | source)
XLA Modules:
  0.0 24.0 jit_solution(6800261380850027889)
XLA Ops:
  0.0 2.5 %strips.1 = (f32[240,128]{1,0:T(8,128)S(1)}, f32[64,128]{1,0:T(8,128)S(1)}, f32[240,128]{1,0:T(8,128)S(1)}, f32[64,128]{1,0:T(8,128)S(1)}, f32[240,128]{1,0:T(8,...) custom-call(s32[2,256]{1,0:T(2,128)} %seam_ref.3, s32[1,256]{1,0:T(1,128)} %slot_ref.1, ...), custom_call_target="tpu_custom_call" | custom-call | flops 100000000 | bytes 2097152 | tf_op jit(solution)/shard_map/strips/pallas_call | solution.py:526
  2.5 0.0 copy-start
  2.5 6.4 %collective-permute-start = (f32[240,128]{1,0:T(8,128)S(1)}, f32[240,128]{1,0:T(8,128)S(1)}, u32[]{:S(2)}, u32[]{:S(2)}) collective-permute-start(f32[240,128]{1,0:T(8,128)S(1)} %get-tuple-element.17), channel_id=1, source_target_pairs={{0,31},{1,30},{2,29},{3,28},{4,27},{5,26},{6,25},{7,24},{8,23},{9,... | collective-permute-start | bytes 368648 | tf_op jit(solution)/shard_map/ppermute | solution.py:594
  8.9 0.5 %collective-permute-start.1 = (f32[240,128]{1,0:T(8,128)S(1)}, f32[240,128]{1,0:T(8,128)S(1)}, u32[]{:S(2)}, u32[]{:S(2)}) collective-permute-start(f32[240,128]{1,0:T(8,128)S(1)} %get-tuple-element.18), channel_id=1, source_target_pairs={{0,16},{1,17},{2,18},{3,19},{4,20},{5,21},{6,22},{7,23},{8,24},{9,... | collective-permute-start | bytes 368648 | tf_op jit(solution)/shard_map/ppermute | solution.py:594
  9.5 0.7 %collective-permute-start.4 = (f32[240,128]{1,0:T(8,128)S(1)}, f32[240,128]{1,0:T(8,128)S(1)}, u32[]{:S(2)}, u32[]{:S(2)}) collective-permute-start(f32[240,128]{1,0:T(8,128)S(1)} %get-tuple-element.24), channel_id=1, source_target_pairs={{0,0},{1,2},{2,1},{3,4},{4,3},{5,6},{6,5},{7,8},{8,7},{9,10},{10,9... | collective-permute-start | bytes 368648 | tf_op jit(solution)/shard_map/ppermute | solution.py:579
  10.1 1.2 %collective-permute-start.2 = (f32[64,128]{1,0:T(8,128)S(1)}, f32[64,128]{1,0:T(8,128)S(1)}, u32[]{:S(2)}, u32[]{:S(2)}) collective-permute-start(f32[64,128]{1,0:T(8,128)S(1)} %get-tuple-element.22), channel_id=1, source_target_pairs={{0,31},{1,29},{2,30},{3,27},{4,28},{5,25},{6,26},{7,23},{8,24},{9,... | collective-permute-start | bytes 98312 | tf_op jit(solution)/shard_map/ppermute | solution.py:594
  11.3 0.5 %collective-permute-start.3 = (f32[64,128]{1,0:T(8,128)S(1)}, f32[64,128]{1,0:T(8,128)S(1)}, u32[]{:S(2)}, u32[]{:S(2)}) collective-permute-start(f32[64,128]{1,0:T(8,128)S(1)} %get-tuple-element.23), channel_id=1, source_target_pairs={{0,16},{1,18},{2,17},{3,20},{4,19},{5,22},{6,21},{7,24},{8,23},{9,... | collective-permute-start | bytes 98312 | tf_op jit(solution)/shard_map/ppermute | solution.py:594
  11.8 0.0 copy-done.2
  11.8 0.0 copy-done.6
  11.8 0.7 %own.1 = (f32[448,384]{1,0:T(8,128)S(1)}, bf16[256,384]{1,0:T(8,128)(2,1)S(1)}) custom-call(f32[448,256]{1,0:T(8,128)S(1)} %get-tuple-element.20.stored_ref, s32[1,256]{1,0:T(1,128)S(1)} %copy-done.6, s32[24,384]{1,0:T(8,128)S(1)} %copy-done.2), custom_call_target="tpu_custom_call" | custom-call | flops 100000000 | bytes 2097152 | tf_op jit(solution)/shard_map/own/pallas_call | solution.py:526
  12.5 4.8 %collective-permute-done.2.refs_1_.far1_ref = f32[64,128]{1,0:T(8,128)S(1)} collective-permute-done((f32[64,128]{1,0:T(8,128)S(1)}, f32[64,128]{1,0:T(8,128)S(1)}, u32[]{:S(2)}, u32[]{:S(2)}) %collective-permute-start.2) | collective-permute-done | bytes 32800 | tf_op jit(solution)/shard_map/ppermute | solution.py:594
  17.3 0.0 collective-permute-done.3.refs_2_.far0_ref
  17.3 0.0 collective-permute-done.in1_ref
  17.3 0.0 collective-permute-done.1.in0_ref
  17.3 0.0 collective-permute-done.4.refs_3_.next_ref
  17.3 0.0 copy-done
  17.3 0.0 copy-done.1
  17.3 0.0 copy-start.5
  17.3 0.4 %corners.1 = f32[368,128]{1,0:T(8,128)S(1)} custom-call(f32[240,128]{1,0:T(8,128)S(1)} %collective-permute-done.in1_ref, f32[240,128]{1,0:T(8,128)S(1)} %collective-permute-done.1.in0_ref, f32[240,128]{1,0:T(8,128)S(1)} %get-tuple-element.19.pair_ref, f32[256,384]{1,0:T(8,128)S(1)} %copy-done, f32[64,128]{1,0:T(8,128)S(1)} %copy-done.1, ...), custom_call_target="tpu_custom_call" | custom-call | flops 100000000 | bytes 2097152 | tf_op jit(solution)/shard_map/corners/pallas_call | solution.py:526
  17.7 0.4 %collective-permute-start.5 = (f32[368,128]{1,0:T(8,128)S(1)}, f32[368,128]{1,0:T(8,128)S(1)}, u32[]{:S(2)}, u32[]{:S(2)}) collective-permute-start(f32[368,128]{1,0:T(8,128)S(1)} %corners.1), channel_id=1, source_target_pairs={{0,1},{1,0},{2,3},{3,2},{4,5},{5,4},{6,7},{7,6},{8,9},{9,8},{10,11... | collective-permute-start | bytes 565256 | tf_op jit(solution)/shard_map/ppermute | solution.py:579
  18.2 0.0 copy-done.5
  18.2 1.1 %middle.1 = (f32[480,128]{1,0:T(8,128)S(1)}, f32[480,128]{1,0:T(8,128)S(1)}, f32[480,128]{1,0:T(8,128)S(1)}) custom-call(s32[2,256]{1,0:T(2,128)S(1)} %copy-done.5, f32[240,128]{1,0:T(8,128)S(1)} %collective-permute-done.1.in0_ref, f32[240,128]{1,0:T(8,128)S(1)} %collective-permute-done.in1_ref, f32[448,384]{1,0:T(8,128)S(1)} %get-tuple-element.25.own_ref, ...), custom_call_target="tpu_custom_call" | custom-call | flops 100000000 | bytes 2097152 | tf_op jit(solution)/shard_map/middle/pallas_call | solution.py:526
  19.2 0.0 collective-permute-done.5.pair_ref
  19.3 4.8 %steps.1 = f32[3,8,8,256]{3,2,1,0:T(8,128)} custom-call(s32[2,256]{1,0:T(2,128)S(1)} %copy-done.5, f32[368,128]{1,0:T(8,128)S(1)} %collective-permute-done.5.pair_ref, f32[240,128]{1,0:T(8,128)S(1)} %collective-permute-done.4.refs_3_.next_ref, f32[64,128]{1,0:T(8,128)S(1)} %collective-permute-done.3.refs_2_.far0_ref, ...), custom_call_target="tpu_custom_call" | custom-call | flops 100000000 | bytes 2097152 | tf_op jit(solution)/shard_map/steps/pallas_call | solution.py:526
  (7 shorter events, 0.0 us)
Async XLA Ops:
  0.0 11.8 %copy-start.2 = (s32[24,384]{1,0:T(8,128)S(1)}, s32[24,384]{1,0:T(8,128)}, u32[]{:S(2)}) copy-start(s32[24,384]{1,0:T(8,128)} %constant.12.clone.lanes_ref) | copy-start | bytes 110596
  0.0 11.8 %copy-start.6 = (s32[1,256]{1,0:T(1,128)S(1)}, s32[1,256]{1,0:T(1,128)}, u32[]{:S(2)}) copy-start(s32[1,256]{1,0:T(1,128)} %slot_ref.1) | copy-start | bytes 3076
  2.5 14.8 %copy-start = (f32[256,384]{1,0:T(8,128)S(1)}, f32[256,384]{1,0:T(8,128)}, u32[]{:S(2)}) copy-start(f32[256,384]{1,0:T(8,128)} %constant.10.clone.refs_7_.table_ref) | copy-start | bytes 1179652
  2.5 14.8 %collective-permute-start = (f32[240,128]{1,0:T(8,128)S(1)}, f32[240,128]{1,0:T(8,128)S(1)}, u32[]{:S(2)}, u32[]{:S(2)}) collective-permute-start(f32[240,128]{1,0:T(8,128)S(1)} %get-tuple-element.17), channel_id=1, source_target_pairs={{0,31},{1,30},{2,29},{3,28},{4,27},{5,26},{6,25},{7,24},{8,23},{9,... | collective-permute-start | bytes 368648 | tf_op jit(solution)/shard_map/ppermute | solution.py:594
  8.9 8.3 %collective-permute-start.1 = (f32[240,128]{1,0:T(8,128)S(1)}, f32[240,128]{1,0:T(8,128)S(1)}, u32[]{:S(2)}, u32[]{:S(2)}) collective-permute-start(f32[240,128]{1,0:T(8,128)S(1)} %get-tuple-element.18), channel_id=1, source_target_pairs={{0,16},{1,17},{2,18},{3,19},{4,20},{5,21},{6,22},{7,23},{8,24},{9,... | collective-permute-start | bytes 368648 | tf_op jit(solution)/shard_map/ppermute | solution.py:594
  9.5 7.8 %collective-permute-start.4 = (f32[240,128]{1,0:T(8,128)S(1)}, f32[240,128]{1,0:T(8,128)S(1)}, u32[]{:S(2)}, u32[]{:S(2)}) collective-permute-start(f32[240,128]{1,0:T(8,128)S(1)} %get-tuple-element.24), channel_id=1, source_target_pairs={{0,0},{1,2},{2,1},{3,4},{4,3},{5,6},{6,5},{7,8},{8,7},{9,10},{10,9... | collective-permute-start | bytes 368648 | tf_op jit(solution)/shard_map/ppermute | solution.py:579
  10.1 7.1 %collective-permute-start.2 = (f32[64,128]{1,0:T(8,128)S(1)}, f32[64,128]{1,0:T(8,128)S(1)}, u32[]{:S(2)}, u32[]{:S(2)}) collective-permute-start(f32[64,128]{1,0:T(8,128)S(1)} %get-tuple-element.22), channel_id=1, source_target_pairs={{0,31},{1,29},{2,30},{3,27},{4,28},{5,25},{6,26},{7,23},{8,24},{9,... | collective-permute-start | bytes 98312 | tf_op jit(solution)/shard_map/ppermute | solution.py:594
  11.3 6.0 %collective-permute-start.3 = (f32[64,128]{1,0:T(8,128)S(1)}, f32[64,128]{1,0:T(8,128)S(1)}, u32[]{:S(2)}, u32[]{:S(2)}) collective-permute-start(f32[64,128]{1,0:T(8,128)S(1)} %get-tuple-element.23), channel_id=1, source_target_pairs={{0,16},{1,18},{2,17},{3,20},{4,19},{5,22},{6,21},{7,24},{8,23},{9,... | collective-permute-start | bytes 98312 | tf_op jit(solution)/shard_map/ppermute | solution.py:594
  11.8 5.5 %copy-start.1 = (f32[64,128]{1,0:T(8,128)S(1)}, f32[64,128]{1,0:T(8,128)}, u32[]{:S(2)}) copy-start(f32[64,128]{1,0:T(8,128)} %constant.11.clone.refs_8_.weight_ref) | copy-start | bytes 98308
  17.3 0.9 %copy-start.5 = (s32[2,256]{1,0:T(2,128)S(1)}, s32[2,256]{1,0:T(2,128)}, u32[]{:S(2)}) copy-start(s32[2,256]{1,0:T(2,128)} %seam_ref.3) | copy-start | bytes 6148
  17.7 1.5 %collective-permute-start.5 = (f32[368,128]{1,0:T(8,128)S(1)}, f32[368,128]{1,0:T(8,128)S(1)}, u32[]{:S(2)}, u32[]{:S(2)}) collective-permute-start(f32[368,128]{1,0:T(8,128)S(1)} %corners.1), channel_id=1, source_target_pairs={{0,1},{1,0},{2,3},{3,2},{4,5},{5,4},{6,7},{7,6},{8,9},{9,8},{10,11... | collective-permute-start | bytes 565256 | tf_op jit(solution)/shard_map/ppermute | solution.py:579
  18.2 1.1 %copy-start.3 = (s32[24,256]{1,0:T(8,128)S(1)}, s32[24,256]{1,0:T(8,128)}, u32[]{:S(2)}) copy-start(s32[24,256]{1,0:T(8,128)} %constant.14.clone.outer_ref) | copy-start | bytes 73732
  18.2 1.1 %copy-start.4 = (s32[8,640]{1,0:T(8,128)S(1)}, s32[8,640]{1,0:T(8,128)}, u32[]{:S(2)}) copy-start(s32[8,640]{1,0:T(8,128)} %constant.13.clone.ext_ref) | copy-start | bytes 61444

commit v7 on v6

--- a/solution.py
+++ b/solution.py
@@ -232,12 +232,6 @@
     return jnp.concatenate([left, right], 1)
 
 
-def with_row_rim(whole, sums, top):
-    north, south = row_edges(sums)
-    rim = jnp.where(top, pltpu.roll(north, RING, 1), pltpu.roll(south, LANES - RING, 1))
-    return jnp.concatenate([whole, rim], 0)
-
-
 def corner_of(whole, start, top):
     lane = lax.broadcasted_iota(i32, (1, LANES), 1)
     base = LANES - start - jnp.where(top != 0, 48, 0)
@@ -286,8 +280,8 @@
 
 def strips_kernel(block_cols, *refs):
     sources = refs[:9]
-    out1_ref, far1_ref, out0_ref, far0_ref, next_ref, pair_ref, stored_ref = refs[9:16]
-    buffers, sems, sums = refs[16:25], refs[25], refs[26]
+    out1_ref, out0_ref, next_ref, pair_ref, stored_ref = refs[9:14]
+    buffers, sems, sums = refs[14:23], refs[23], refs[24]
     brought(sources, buffers, sems)
     seam_ref, slot_ref, fields_ref, area_ref, depth_ref, spin_ref, tide_ref = buffers[:7]
     table_ref, weight_ref = buffers[7:]
@@ -334,35 +328,28 @@
     strip, ring = in_frame(both[:, :LANES]), in_frame(both[:, LANES : 2 * LANES])
     rows = both[:, 3 * LANES :]
     rows = [rows[k * NODES : (k + 1) * NODES] for k in range(ARRAYS)]
-    edges = edge_values(
-        table_ref, weight_ref, *(jnp.concatenate(parts, 1) for parts in zip(strip, ring, rows))
-    )
+    edges = edge_values(table_ref, weight_ref, *map(beside, ring, rows))
     east = jnp.where(second, east1, east0) != 0
-    ends = [part[:, LANES : 2 * LANES] for part in edges]
-    ends = [jnp.where(east, part[NODES - NP :], part[:NP]) for part in ends]
-    whole = jnp.concatenate(strip + ends, 0)
-    out0_ref[...], out1_ref[...] = packed(whole)
-    sums[0] = jnp.concatenate([part[:, :LANES] for part in edges], 0)
-    top0, top1 = odd ^ flip0, odd ^ flip1
-    whole = with_row_rim(whole, sums, jnp.where(second, top1, top0) != 0)
-    far0_ref[...] = corner_of(whole, 0, top0)
-    far1_ref[...] = corner_of(whole, 64, top1)
-    sums[0] = jnp.concatenate([part[:, 2 * LANES :] for part in edges], 0)
+    ends = [jnp.where(east, part[NODES - NP :, :LANES], part[:NP, :LANES]) for part in edges]
+    out0_ref[...], out1_ref[...] = packed(jnp.concatenate(strip + ends, 0))
+    sums[0] = jnp.concatenate([part[:, LANES:] for part in edges], 0)
     rim = jnp.where(goes_up(lane), *row_edges(sums))
     rows = jnp.concatenate([both[:, 2 * LANES : 3 * LANES], rim], 0)
     pair_ref[...], next_ref[...] = packed(rows)
 
 
-def corners_kernel(in1_ref, in0_ref, pair_ref, table_ref, weight_ref, *refs):
-    out_ref, sums = refs[-2:]
-    top = 1 - (lax.axis_index("blk") & 1)
+def corners_kernel(in1_ref, in0_ref, table_ref, weight_ref, _, next_ref, pair_ref, sums):
+    odd = lax.axis_index("blk") & 1
     whole = unpacked(in0_ref[...], in1_ref[...])
     parts = [whole[k * NODES : (k + 1) * NODES] for k in range(ARRAYS)]
     sums[0] = jnp.concatenate(edge_values(table_ref, weight_ref, *parts), 0)
-    whole = with_row_rim(whole, sums, jnp.broadcast_to(top != 0, (1, LANES)))
-    out_ref[:HALF_ROWS] = pair_ref[...]
-    out_ref[HALF_ROWS : HALF_ROWS + CORNER_ROWS] = corner_of(whole, 0, top)
-    out_ref[HALF_ROWS + CORNER_ROWS :] = corner_of(whole, 64, top)
+    north, south = row_edges(sums)
+    north, south = pltpu.roll(north, RING, 1), pltpu.roll(south, LANES - RING, 1)
+    for ref, top in ((next_ref, odd), (pair_ref, 1 - odd)):
+        rim = jnp.where(jnp.broadcast_to(top != 0, (1, LANES)), north, south)
+        rimmed = jnp.concatenate([whole, rim], 0)
+        ref[:CORNER_ROWS] = corner_of(rimmed, 0, top)
+        ref[CORNER_ROWS:] = corner_of(rimmed, 64, top)
 
 
 def own_kernel(stored_ref, slot_ref, lanes_ref, own_ref, hot_ref):
@@ -387,7 +374,7 @@
 
 
 def steps_kernel(
-    block_cols, seam_ref, pair_ref, next_ref, far0_ref, far1_ref, low_ref, centre_ref,
+    block_cols, seam_ref, next_ref, pair_ref, far_ref, near_ref, low_ref, centre_ref,
     high_ref, hot_ref, table_ref, weight_ref, ext_ref, outer_ref, out_ref, sums,
 ):
     east0, flip0, east1, flip1 = seam_flags(seam_ref, block_cols)
@@ -395,13 +382,12 @@
     block_y = lax.rem(lax.axis_index("blk"), BY)
 
     lane = lax.broadcasted_iota(i32, (1, LANES), 1)
-    pair = pair_ref[...]
-    strips = unpacked(pair[:HALF_ROWS], next_ref[...])
+    strips = unpacked(pair_ref[...], next_ref[...])
     strips = jnp.concatenate(
         [strips[:ROWS], jnp.zeros((EDGE_ROWS, LANES), f32), strips[ROWS:]], 0
     )
-    near = pair[HALF_ROWS:]
-    sources = (near[:CORNER_ROWS], near[CORNER_ROWS:], far0_ref[...], far1_ref[...])
+    near, far = near_ref[...], far_ref[...]
+    sources = (near[:CORNER_ROWS], near[CORNER_ROWS:], far[:CORNER_ROWS], far[CORNER_ROWS:])
     corners = []
     for k in range(RIM_ROWS // CORNER_ROWS):
         rows = None
@@ -548,12 +534,12 @@
         return buffers + [pltpu.SemaphoreType.DMA((len(values),))]
 
     needed = (seam_rows, slot_of, *held, table, weight)
-    corner = ((CORNER_ROWS, LANES), f32)
+    corner = ((2 * CORNER_ROWS, LANES), f32)
     scratch = [pltpu.VMEM((1, 4 * NODES, LANES), f32)]
-    strip1, far1, strip0, far0, to_next, to_pair, stored = call(
+    strip1, strip0, to_next, to_pair, stored = call(
         functools.partial(strips_kernel, block_cols),
         [(hbm, x) for x in needed],
-        [strip, corner, strip, corner, strip, strip, ((ROWS, ELEMENTS), f32)],
+        [strip, strip, strip, strip, ((ROWS, ELEMENTS), f32)],
         10**8,
         scratch=room(needed, [pltpu.SMEM] + [pltpu.VMEM] * (len(needed) - 1)) + scratch,
         name="strips",
@@ -564,9 +550,6 @@
 
     def rank(face, block_x, block_y):
         return face * span + block_x * BY + block_y
-
-    def same(y):
-        return y
 
     def in_pair(y):
         return y ^ 1
@@ -580,14 +563,14 @@
             value, both, [(rank(f, x, y), rank(f, x, partner(y))) for f, x, y in places]
         )
 
-    def across(value0, value1, partner):
+    def across(value0, value1):
         last = block_cols - 1
         straight = {
-            (f, x, y): (f, x + 1, partner(y)) if x < last else (1 - f, 0, partner(y))
+            (f, x, y): (f, x + 1, y) if x < last else (1 - f, 0, y)
             for f, x, y in places
         }
         turned = {
-            (f, last, y): (1 - f, 0, BY - 1 - partner(y)) for f in range(2) for y in range(BY)
+            (f, last, y): (1 - f, 0, BY - 1 - y) for f in range(2) for y in range(BY)
         }
 
         def eastward(value, pairs):
@@ -614,9 +597,9 @@
             ),
         )
 
-    halo0, halo1 = across(strip0, strip1, same)
-    far0, far1 = across(far0, far1, next_pair)
+    halo0, halo1 = across(strip0, strip1)
     from_next = swapped(to_next, next_pair)
+    from_pair = swapped(to_pair, in_pair)
     own, hot = call(
         own_kernel,
         [(vmem, x) for x in (stored, slot_of, lanes)],
@@ -624,15 +607,16 @@
         10**8,
         name="own",
     )
-    (to_pair,) = call(
+    far, near = call(
         corners_kernel,
-        [(vmem, x) for x in (halo1, halo0, to_pair, table, weight, hot, far1, far0, from_next)],
-        [((HALF_ROWS + 2 * CORNER_ROWS, LANES), f32)],
+        [(vmem, x) for x in (halo1, halo0, table, weight, hot)],
+        [corner, corner],
         10**8,
         scratch=scratch,
         name="corners",
     )
-    from_pair = swapped(to_pair, in_pair)
+    far = swapped(far, next_pair)
+    near = swapped(near, in_pair)
     tile = ((ALL_ROWS, LANES), f32)
     low, centre, high = call(
         functools.partial(middle_kernel, block_cols),
@@ -647,7 +631,7 @@
         + [
             (vmem, x)
             for x in (
-                from_pair, from_next, far0, far1, low, centre, high,
+                from_next, from_pair, far, near, low, centre, high,
                 hot, table, weight, ext, outer,
             )
         ],

time: 24.3 us -> 26.5 us (1.091)
  the two profiles are of different devices: /device:TPU:0 before, /device:TPU:1 now
where the time goes in v7:
time: 26.5 us; the launch traced here: 26.4 us
  starting transfers between devices  11.2 us (42%)
  Pallas kernels  9.34 us (35%)
  waiting for transfers between devices  5.65 us (21%)
    pallas_call x5, Pallas kernels, call(): pl.pallas_call(kernel, out_shape=[jax.ShapeDtypeStruct(*out) for out in o...  9.34 us
    ppermute x2, starting transfers between devices, eastward(): lax.ppermute(value, both, [(rank(*a), rank(*b)) for a, b in pairs.items()])  6.91 us
    ppermute x4, starting transfers between devices, swapped(): lax.ppermute(value, both, [(rank(f, x, y), rank(f, x, partner(y))) for f,...  4.29 us
    ppermute x2, waiting for transfers between devices, eastward(): lax.ppermute(value, both, [(rank(*a), rank(*b)) for a, b in pairs.items()])  3.31 us
    ppermute x4, waiting for transfers between devices, swapped(): lax.ppermute(value, both, [(rank(f, x, y), rank(f, x, partner(y))) for f,...  2.34 us
  transfers between devices with their start and end apart: 6, of which 2 were waited for; matrix products, arithmetic and copies ran while one was open for 0% of the time, Pallas kernels for 8%

profile of v7, /device:TPU:1, one launch (start us, length us, event | category | flops | bytes accessed | tf_op | source)
XLA Modules:
  0.0 26.4 jit_solution(18071969811168363073)
XLA Ops:
  0.0 2.3 %strips.1 = (f32[240,128]{1,0:T(8,128)S(1)}, f32[240,128]{1,0:T(8,128)S(1)}, f32[240,128]{1,0:T(8,128)S(1)}, f32[240,128]{1,0:T(8,128)S(1)}, f32[448,256]{1,0:T(8,128)S(1)}) custom-call(s32[2,256]{1,0:T(2,128)} %seam_ref.3, s32[1,256]{1,0:T(1,128)} %slot_ref.1, f32[3,8,8,256]{3,2,1,0:T(8,128)} %refs_2_.1, f32[8,8,256]{2,1,0:T(8,128)} %refs_3_.1, ...), custom_call_target="tpu_custom_call" | custom-call | flops 100000000 | bytes 2097152 | tf_op jit(solution)/shard_map/strips/pallas_call | solution.py:512
  2.4 0.0 copy-start
  2.4 6.7 %collective-permute-start.2 = (f32[240,128]{1,0:T(8,128)S(1)}, f32[240,128]{1,0:T(8,128)S(1)}, u32[]{:S(2)}, u32[]{:S(2)}) collective-permute-start(f32[240,128]{1,0:T(8,128)S(1)} %get-tuple-element.19), channel_id=1, source_target_pairs={{0,31},{1,30},{2,29},{3,28},{4,27},{5,26},{6,25},{7,24},{8,23},{9,... | collective-permute-start | bytes 368648 | tf_op jit(solution)/shard_map/ppermute | solution.py:577
  9.0 0.3 collective-permute-start.3
  9.3 2.1 %collective-permute-start = (f32[240,128]{1,0:T(8,128)S(1)}, f32[240,128]{1,0:T(8,128)S(1)}, u32[]{:S(2)}, u32[]{:S(2)}) collective-permute-start(f32[240,128]{1,0:T(8,128)S(1)} %get-tuple-element.17), channel_id=1, source_target_pairs={{0,0},{1,2},{2,1},{3,4},{4,3},{5,6},{6,5},{7,8},{8,7},{9,10},{10,9... | collective-permute-start | bytes 368648 | tf_op jit(solution)/shard_map/ppermute | solution.py:562
  11.4 0.1 collective-permute-start.1
  11.5 0.0 copy-start.1
  11.5 0.7 %own.1 = (f32[448,384]{1,0:T(8,128)S(1)}, bf16[256,384]{1,0:T(8,128)(2,1)S(1)}) custom-call(f32[448,256]{1,0:T(8,128)S(1)} %get-tuple-element.21.stored_ref, s32[1,256]{1,0:T(1,128)S(1)} %copy-done.6, s32[24,384]{1,0:T(8,128)S(1)} %copy-done.2), custom_call_target="tpu_custom_call" | custom-call | flops 100000000 | bytes 2097152 | tf_op jit(solution)/shard_map/own/pallas_call | solution.py:512
  12.2 0.0 collective-permute-done.2.in1_ref
  12.2 3.3 %collective-permute-done.3.in0_ref = f32[240,128]{1,0:T(8,128)S(1)} collective-permute-done((f32[240,128]{1,0:T(8,128)S(1)}, f32[240,128]{1,0:T(8,128)S(1)}, u32[]{:S(2)}, u32[]{:S(2)}) %collective-permute-start.3) | collective-permute-done | bytes 122912 | tf_op jit(solution)/shard_map/ppermute | solution.py:577
  15.5 0.0 copy-done.1
  15.5 0.5 %corners.1 = (f32[128,128]{1,0:T(8,128)S(1)}, f32[128,128]{1,0:T(8,128)S(1)}) custom-call(f32[240,128]{1,0:T(8,128)S(1)} %collective-permute-done.2.in1_ref, f32[240,128]{1,0:T(8,128)S(1)} %collective-permute-done.3.in0_ref, f32[256,384]{1,0:T(8,128)S(1)} %copy-done, f32[64,128]{1,0:T(8,128)S(1)} %copy-done.1, bf16[256,384]{1,0:T(8,128)(2,1)S(1)} %get-tuple-element.22._.hot_ref), custom_call_target="tpu_custom_call" | custom-call | flops 100000000 | bytes 2097152 | tf_op jit(solution)/shard_map/corners/pallas_call | solution.py:512
  16.0 0.0 copy-start.5
  16.0 2.0 %collective-permute-start.4 = (f32[128,128]{1,0:T(8,128)S(1)}, f32[128,128]{1,0:T(8,128)S(1)}, u32[]{:S(2)}, u32[]{:S(2)}) collective-permute-start(f32[128,128]{1,0:T(8,128)S(1)} %get-tuple-element.23), channel_id=1, source_target_pairs={{0,0},{1,2},{2,1},{3,4},{4,3},{5,6},{6,5},{7,8},{8,7},{9,10},{10,9... | collective-permute-start | bytes 196616 | tf_op jit(solution)/shard_map/ppermute | solution.py:562
  18.1 0.1 collective-permute-start.5
  18.1 0.0 copy-done.5
  18.1 0.0 copy-start.3
  18.2 0.0 copy-start.4
  18.2 1.1 %middle.1 = (f32[480,128]{1,0:T(8,128)S(1)}, f32[480,128]{1,0:T(8,128)S(1)}, f32[480,128]{1,0:T(8,128)S(1)}) custom-call(s32[2,256]{1,0:T(2,128)S(1)} %copy-done.5, f32[240,128]{1,0:T(8,128)S(1)} %collective-permute-done.3.in0_ref, f32[240,128]{1,0:T(8,128)S(1)} %collective-permute-done.2.in1_ref, f32[448,384]{1,0:T(8,128)S(1)} %get-tuple-element.25.own_ref, ...), custom_call_target="tpu_custom_call" | custom-call | flops 100000000 | bytes 2097152 | tf_op jit(solution)/shard_map/middle/pallas_call | solution.py:512
  19.2 0.0 collective-permute-done.next_ref
  19.3 0.0 collective-permute-done.1.pair_ref
  19.3 2.3 %collective-permute-done.4.far_ref = f32[128,128]{1,0:T(8,128)S(1)} collective-permute-done((f32[128,128]{1,0:T(8,128)S(1)}, f32[128,128]{1,0:T(8,128)S(1)}, u32[]{:S(2)}, u32[]{:S(2)}) %collective-permute-start.4) | collective-permute-done | bytes 65568 | tf_op jit(solution)/shard_map/ppermute | solution.py:562
  21.6 0.0 collective-permute-done.5.near_ref
  21.6 4.8 %steps.1 = f32[3,8,8,256]{3,2,1,0:T(8,128)} custom-call(s32[2,256]{1,0:T(2,128)S(1)} %copy-done.5, f32[240,128]{1,0:T(8,128)S(1)} %collective-permute-done.next_ref, f32[240,128]{1,0:T(8,128)S(1)} %collective-permute-done.1.pair_ref, f32[128,128]{1,0:T(8,128)S(1)} %collective-permute-done.4.far_ref, f32[128,128]{1,0:T(8,128)S(1)} %collective-permute-done.5.near_ref, ...), custom_call_target="tpu_custom_call" | custom-call | flops 100000000 | bytes 2097152 | tf_op jit(solution)/shard_map/steps/pallas_call | solution.py:512
  (7 shorter events, 0.0 us)
Async XLA Ops:
  0.0 11.5 %copy-start.2 = (s32[24,384]{1,0:T(8,128)S(1)}, s32[24,384]{1,0:T(8,128)}, u32[]{:S(2)}) copy-start(s32[24,384]{1,0:T(8,128)} %constant.12.clone.lanes_ref) | copy-start | bytes 110596
  0.0 11.5 %copy-start.6 = (s32[1,256]{1,0:T(1,128)S(1)}, s32[1,256]{1,0:T(1,128)}, u32[]{:S(2)}) copy-start(s32[1,256]{1,0:T(1,128)} %slot_ref.1) | copy-start | bytes 3076
  2.4 13.2 %copy-start = (f32[256,384]{1,0:T(8,128)S(1)}, f32[256,384]{1,0:T(8,128)}, u32[]{:S(2)}) copy-start(f32[256,384]{1,0:T(8,128)} %constant.10.clone.refs_7_.table_ref) | copy-start | bytes 1179652
  2.4 9.9 %collective-permute-start.2 = (f32[240,128]{1,0:T(8,128)S(1)}, f32[240,128]{1,0:T(8,128)S(1)}, u32[]{:S(2)}, u32[]{:S(2)}) collective-permute-start(f32[240,128]{1,0:T(8,128)S(1)} %get-tuple-element.19), channel_id=1, source_target_pairs={{0,31},{1,30},{2,29},{3,28},{4,27},{5,26},{6,25},{7,24},{8,23},{9,... | collective-permute-start | bytes 368648 | tf_op jit(solution)/shard_map/ppermute | solution.py:577
  9.0 6.5 %collective-permute-start.3 = (f32[240,128]{1,0:T(8,128)S(1)}, f32[240,128]{1,0:T(8,128)S(1)}, u32[]{:S(2)}, u32[]{:S(2)}) collective-permute-start(f32[240,128]{1,0:T(8,128)S(1)} %get-tuple-element.20), channel_id=1, source_target_pairs={{0,16},{1,17},{2,18},{3,19},{4,20},{5,21},{6,22},{7,23},{8,24},{9,... | collective-permute-start | bytes 368648 | tf_op jit(solution)/shard_map/ppermute | solution.py:577
  9.3 10.0 %collective-permute-start = (f32[240,128]{1,0:T(8,128)S(1)}, f32[240,128]{1,0:T(8,128)S(1)}, u32[]{:S(2)}, u32[]{:S(2)}) collective-permute-start(f32[240,128]{1,0:T(8,128)S(1)} %get-tuple-element.17), channel_id=1, source_target_pairs={{0,0},{1,2},{2,1},{3,4},{4,3},{5,6},{6,5},{7,8},{8,7},{9,10},{10,9... | collective-permute-start | bytes 368648 | tf_op jit(solution)/shard_map/ppermute | solution.py:562
  11.4 7.9 %collective-permute-start.1 = (f32[240,128]{1,0:T(8,128)S(1)}, f32[240,128]{1,0:T(8,128)S(1)}, u32[]{:S(2)}, u32[]{:S(2)}) collective-permute-start(f32[240,128]{1,0:T(8,128)S(1)} %get-tuple-element.18), channel_id=1, source_target_pairs={{0,1},{1,0},{2,3},{3,2},{4,5},{5,4},{6,7},{7,6},{8,9},{9,8},{10,11... | collective-permute-start | bytes 368648 | tf_op jit(solution)/shard_map/ppermute | solution.py:562
  11.5 4.0 %copy-start.1 = (f32[64,128]{1,0:T(8,128)S(1)}, f32[64,128]{1,0:T(8,128)}, u32[]{:S(2)}) copy-start(f32[64,128]{1,0:T(8,128)} %constant.11.clone.refs_8_.weight_ref) | copy-start | bytes 98308
  16.0 2.1 %copy-start.5 = (s32[2,256]{1,0:T(2,128)S(1)}, s32[2,256]{1,0:T(2,128)}, u32[]{:S(2)}) copy-start(s32[2,256]{1,0:T(2,128)} %seam_ref.3) | copy-start | bytes 6148
  16.0 5.6 %collective-permute-start.4 = (f32[128,128]{1,0:T(8,128)S(1)}, f32[128,128]{1,0:T(8,128)S(1)}, u32[]{:S(2)}, u32[]{:S(2)}) collective-permute-start(f32[128,128]{1,0:T(8,128)S(1)} %get-tuple-element.23), channel_id=1, source_target_pairs={{0,0},{1,2},{2,1},{3,4},{4,3},{5,6},{6,5},{7,8},{8,7},{9,10},{10,9... | collective-permute-start | bytes 196616 | tf_op jit(solution)/shard_map/ppermute | solution.py:562
  18.1 3.6 %collective-permute-start.5 = (f32[128,128]{1,0:T(8,128)S(1)}, f32[128,128]{1,0:T(8,128)S(1)}, u32[]{:S(2)}, u32[]{:S(2)}) collective-permute-start(f32[128,128]{1,0:T(8,128)S(1)} %get-tuple-element.24), channel_id=1, source_target_pairs={{0,1},{1,0},{2,3},{3,2},{4,5},{5,4},{6,7},{7,6},{8,9},{9,8},{10,11... | collective-permute-start | bytes 196616 | tf_op jit(solution)/shard_map/ppermute | solution.py:562
  18.1 3.5 %copy-start.3 = (s32[24,256]{1,0:T(8,128)S(1)}, s32[24,256]{1,0:T(8,128)}, u32[]{:S(2)}) copy-start(s32[24,256]{1,0:T(8,128)} %constant.14.clone.outer_ref) | copy-start | bytes 73732
  18.2 3.5 %copy-start.4 = (s32[8,640]{1,0:T(8,128)S(1)}, s32[8,640]{1,0:T(8,128)}, u32[]{:S(2)}) copy-start(s32[8,640]{1,0:T(8,128)} %constant.13.clone.ext_ref) | copy-start | bytes 61444

commit v8 on v6

--- a/solution.py
+++ b/solution.py
@@ -353,7 +353,7 @@
     pair_ref[...], next_ref[...] = packed(rows)
 
 
-def corners_kernel(in1_ref, in0_ref, pair_ref, table_ref, weight_ref, *refs):
+def corners_kernel(_, in1_ref, in0_ref, pair_ref, table_ref, weight_ref, *refs):
     out_ref, sums = refs[-2:]
     top = 1 - (lax.axis_index("blk") & 1)
     whole = unpacked(in0_ref[...], in1_ref[...])
@@ -626,7 +626,7 @@
     )
     (to_pair,) = call(
         corners_kernel,
-        [(vmem, x) for x in (halo1, halo0, to_pair, table, weight, hot, far1, far0, from_next)],
+        [(vmem, x) for x in (from_next, halo1, halo0, to_pair, table, weight, hot, far1, far0)],
         [((HALF_ROWS + 2 * CORNER_ROWS, LANES), f32)],
         10**8,
         scratch=scratch,

time: 24.3 us -> 26.3 us (1.082)
  waiting for transfers between devices: 4.8 us -> 7.08 us
  starting transfers between devices: 9.68 us -> 9.39 us
    ppermute x4, waiting for transfers between devices: 4.8 us -> 6.93 us  [eastward(): lax.ppermute(value, both, [(rank(*a), rank(*b)) for a, b in pairs.items()])]
  transfers between devices with their start and end apart: 6 -> 6, of which waited for: 1 -> 3; matrix products, arithmetic and copies ran while one was open for 0% -> 0% of each run, Pallas kernels for 7% -> 7%
where the time goes in v8:
time: 26.3 us; the launch traced here: 26.1 us
  Pallas kernels  9.42 us (36%)
  starting transfers between devices  9.39 us (36%)
  waiting for transfers between devices  7.08 us (27%)
    pallas_call x5, Pallas kernels, call(): pl.pallas_call(kernel, out_shape=[jax.ShapeDtypeStruct(*out) for out in o...  9.42 us
    ppermute x4, starting transfers between devices, eastward(): lax.ppermute(value, both, [(rank(*a), rank(*b)) for a, b in pairs.items()])  8.47 us
    ppermute x4, waiting for transfers between devices, eastward(): lax.ppermute(value, both, [(rank(*a), rank(*b)) for a, b in pairs.items()])  6.93 us
    ppermute x2, starting transfers between devices, swapped(): lax.ppermute(value, both, [(rank(f, x, y), rank(f, x, partner(y))) for f,...  0.92 us
  transfers between devices with their start and end apart: 6, of which 3 were waited for; matrix products, arithmetic and copies ran while one was open for 0% of the time, Pallas kernels for 7%

profile of v8, /device:TPU:0, one launch (start us, length us, event | category | flops | bytes accessed | tf_op | source)
XLA Modules:
  0.0 26.1 jit_solution(15019263513960089645)
XLA Ops:
  0.0 2.5 %strips.1 = (f32[240,128]{1,0:T(8,128)S(1)}, f32[64,128]{1,0:T(8,128)S(1)}, f32[240,128]{1,0:T(8,128)S(1)}, f32[64,128]{1,0:T(8,128)S(1)}, f32[240,128]{1,0:T(8,...) custom-call(s32[2,256]{1,0:T(2,128)} %seam_ref.3, s32[1,256]{1,0:T(1,128)} %slot_ref.1, ...), custom_call_target="tpu_custom_call" | custom-call | flops 100000000 | bytes 2097152 | tf_op jit(solution)/shard_map/strips/pallas_call | solution.py:526
  2.5 0.0 copy-start
  2.5 0.8 %collective-permute-start = (f32[240,128]{1,0:T(8,128)S(1)}, f32[240,128]{1,0:T(8,128)S(1)}, u32[]{:S(2)}, u32[]{:S(2)}) collective-permute-start(f32[240,128]{1,0:T(8,128)S(1)} %get-tuple-element.17), channel_id=1, source_target_pairs={{0,0},{1,2},{2,1},{3,4},{4,3},{5,6},{6,5},{7,8},{8,7},{9,10},{10,9... | collective-permute-start | bytes 368648 | tf_op jit(solution)/shard_map/ppermute | solution.py:579
  3.3 6.4 %collective-permute-start.1 = (f32[240,128]{1,0:T(8,128)S(1)}, f32[240,128]{1,0:T(8,128)S(1)}, u32[]{:S(2)}, u32[]{:S(2)}) collective-permute-start(f32[240,128]{1,0:T(8,128)S(1)} %get-tuple-element.18), channel_id=1, source_target_pairs={{0,31},{1,30},{2,29},{3,28},{4,27},{5,26},{6,25},{7,24},{8,23},{9,... | collective-permute-start | bytes 368648 | tf_op jit(solution)/shard_map/ppermute | solution.py:594
  9.7 0.5 %collective-permute-start.2 = (f32[240,128]{1,0:T(8,128)S(1)}, f32[240,128]{1,0:T(8,128)S(1)}, u32[]{:S(2)}, u32[]{:S(2)}) collective-permute-start(f32[240,128]{1,0:T(8,128)S(1)} %get-tuple-element.19), channel_id=1, source_target_pairs={{0,16},{1,17},{2,18},{3,19},{4,20},{5,21},{6,22},{7,23},{8,24},{9,... | collective-permute-start | bytes 368648 | tf_op jit(solution)/shard_map/ppermute | solution.py:594
  10.3 1.1 %collective-permute-start.3 = (f32[64,128]{1,0:T(8,128)S(1)}, f32[64,128]{1,0:T(8,128)S(1)}, u32[]{:S(2)}, u32[]{:S(2)}) collective-permute-start(f32[64,128]{1,0:T(8,128)S(1)} %get-tuple-element.23), channel_id=1, source_target_pairs={{0,31},{1,29},{2,30},{3,27},{4,28},{5,25},{6,26},{7,23},{8,24},{9,... | collective-permute-start | bytes 98312 | tf_op jit(solution)/shard_map/ppermute | solution.py:594
  11.4 0.4 %collective-permute-start.4 = (f32[64,128]{1,0:T(8,128)S(1)}, f32[64,128]{1,0:T(8,128)S(1)}, u32[]{:S(2)}, u32[]{:S(2)}) collective-permute-start(f32[64,128]{1,0:T(8,128)S(1)} %get-tuple-element.24), channel_id=1, source_target_pairs={{0,16},{1,18},{2,17},{3,20},{4,19},{5,22},{6,21},{7,24},{8,23},{9,... | collective-permute-start | bytes 98312 | tf_op jit(solution)/shard_map/ppermute | solution.py:594
  11.8 0.0 copy-done.2
  11.8 0.0 copy-done.6
  11.8 0.7 %own.1 = (f32[448,384]{1,0:T(8,128)S(1)}, bf16[256,384]{1,0:T(8,128)(2,1)S(1)}) custom-call(f32[448,256]{1,0:T(8,128)S(1)} %get-tuple-element.21.stored_ref, s32[1,256]{1,0:T(1,128)S(1)} %copy-done.6, s32[24,384]{1,0:T(8,128)S(1)} %copy-done.2), custom_call_target="tpu_custom_call" | custom-call | flops 100000000 | bytes 2097152 | tf_op jit(solution)/shard_map/own/pallas_call | solution.py:526
  12.5 4.9 %collective-permute-done.3.refs_1_.far1_ref = f32[64,128]{1,0:T(8,128)S(1)} collective-permute-done((f32[64,128]{1,0:T(8,128)S(1)}, f32[64,128]{1,0:T(8,128)S(1)}, u32[]{:S(2)}, u32[]{:S(2)}) %collective-permute-start.3) | collective-permute-done | bytes 32800 | tf_op jit(solution)/shard_map/ppermute | solution.py:594
  17.3 2.0 %collective-permute-done.4.refs_2_.far0_ref = f32[64,128]{1,0:T(8,128)S(1)} collective-permute-done((f32[64,128]{1,0:T(8,128)S(1)}, f32[64,128]{1,0:T(8,128)S(1)}, u32[]{:S(2)}, u32[]{:S(2)}) %collective-permute-start.4) | collective-permute-done | bytes 32800 | tf_op jit(solution)/shard_map/ppermute | solution.py:594
  19.4 0.0 collective-permute-done._.next_ref
  19.4 0.0 collective-permute-done.1.in1_ref
  19.4 0.0 collective-permute-done.2.in0_ref
  19.4 0.0 copy-done
  19.4 0.0 copy-done.1
  19.4 0.0 copy-start.5
  19.4 0.4 %corners.1 = f32[368,128]{1,0:T(8,128)S(1)} custom-call(f32[240,128]{1,0:T(8,128)S(1)} %collective-permute-done._.next_ref, f32[240,128]{1,0:T(8,128)S(1)} %collective-permute-done.1.in1_ref, f32[240,128]{1,0:T(8,128)S(1)} %collective-permute-done.2.in0_ref, f32[240,128]{1,0:T(8,128)S(1)} %get-tuple-element.20.pair_ref, f32[256,384]{1,0:T(8,128)S(1)} %copy-done, ...), custom_call_target="tpu_custom_call" | custom-call | flops 100000000 | bytes 2097152 | tf_op jit(solution)/shard_map/corners/pallas_call | solution.py:526
  19.9 0.1 collective-permute-start.5
  20.0 0.1 copy-done.5
  20.1 1.1 %middle.1 = (f32[480,128]{1,0:T(8,128)S(1)}, f32[480,128]{1,0:T(8,128)S(1)}, f32[480,128]{1,0:T(8,128)S(1)}) custom-call(s32[2,256]{1,0:T(2,128)S(1)} %copy-done.5, f32[240,128]{1,0:T(8,128)S(1)} %collective-permute-done.2.in0_ref, f32[240,128]{1,0:T(8,128)S(1)} %collective-permute-done.1.in1_ref, f32[448,384]{1,0:T(8,128)S(1)} %get-tuple-element.25.own_ref, ...), custom_call_target="tpu_custom_call" | custom-call | flops 100000000 | bytes 2097152 | tf_op jit(solution)/shard_map/middle/pallas_call | solution.py:526
  21.2 0.2 collective-permute-done.5.pair_ref
  21.3 4.8 %steps.1 = f32[3,8,8,256]{3,2,1,0:T(8,128)} custom-call(s32[2,256]{1,0:T(2,128)S(1)} %copy-done.5, f32[368,128]{1,0:T(8,128)S(1)} %collective-permute-done.5.pair_ref, f32[240,128]{1,0:T(8,128)S(1)} %collective-permute-done._.next_ref, f32[64,128]{1,0:T(8,128)S(1)} %collective-permute-done.4.refs_2_.far0_ref, ...), custom_call_target="tpu_custom_call" | custom-call | flops 100000000 | bytes 2097152 | tf_op jit(solution)/shard_map/steps/pallas_call | solution.py:526
  (7 shorter events, 0.0 us)
Async XLA Ops:
  0.0 11.8 %copy-start.2 = (s32[24,384]{1,0:T(8,128)S(1)}, s32[24,384]{1,0:T(8,128)}, u32[]{:S(2)}) copy-start(s32[24,384]{1,0:T(8,128)} %constant.12.clone.lanes_ref) | copy-start | bytes 110596
  0.0 11.8 %copy-start.6 = (s32[1,256]{1,0:T(1,128)S(1)}, s32[1,256]{1,0:T(1,128)}, u32[]{:S(2)}) copy-start(s32[1,256]{1,0:T(1,128)} %slot_ref.1) | copy-start | bytes 3076
  2.5 16.9 %copy-start = (f32[256,384]{1,0:T(8,128)S(1)}, f32[256,384]{1,0:T(8,128)}, u32[]{:S(2)}) copy-start(f32[256,384]{1,0:T(8,128)} %constant.10.clone.refs_7_.table_ref) | copy-start | bytes 1179652
  2.5 16.9 %collective-permute-start = (f32[240,128]{1,0:T(8,128)S(1)}, f32[240,128]{1,0:T(8,128)S(1)}, u32[]{:S(2)}, u32[]{:S(2)}) collective-permute-start(f32[240,128]{1,0:T(8,128)S(1)} %get-tuple-element.17), channel_id=1, source_target_pairs={{0,0},{1,2},{2,1},{3,4},{4,3},{5,6},{6,5},{7,8},{8,7},{9,10},{10,9... | collective-permute-start | bytes 368648 | tf_op jit(solution)/shard_map/ppermute | solution.py:579
  3.3 16.1 %collective-permute-start.1 = (f32[240,128]{1,0:T(8,128)S(1)}, f32[240,128]{1,0:T(8,128)S(1)}, u32[]{:S(2)}, u32[]{:S(2)}) collective-permute-start(f32[240,128]{1,0:T(8,128)S(1)} %get-tuple-element.18), channel_id=1, source_target_pairs={{0,31},{1,30},{2,29},{3,28},{4,27},{5,26},{6,25},{7,24},{8,23},{9,... | collective-permute-start | bytes 368648 | tf_op jit(solution)/shard_map/ppermute | solution.py:594
  9.7 9.7 %collective-permute-start.2 = (f32[240,128]{1,0:T(8,128)S(1)}, f32[240,128]{1,0:T(8,128)S(1)}, u32[]{:S(2)}, u32[]{:S(2)}) collective-permute-start(f32[240,128]{1,0:T(8,128)S(1)} %get-tuple-element.19), channel_id=1, source_target_pairs={{0,16},{1,17},{2,18},{3,19},{4,20},{5,21},{6,22},{7,23},{8,24},{9,... | collective-permute-start | bytes 368648 | tf_op jit(solution)/shard_map/ppermute | solution.py:594
  10.3 7.1 %collective-permute-start.3 = (f32[64,128]{1,0:T(8,128)S(1)}, f32[64,128]{1,0:T(8,128)S(1)}, u32[]{:S(2)}, u32[]{:S(2)}) collective-permute-start(f32[64,128]{1,0:T(8,128)S(1)} %get-tuple-element.23), channel_id=1, source_target_pairs={{0,31},{1,29},{2,30},{3,27},{4,28},{5,25},{6,26},{7,23},{8,24},{9,... | collective-permute-start | bytes 98312 | tf_op jit(solution)/shard_map/ppermute | solution.py:594
  11.4 8.0 %collective-permute-start.4 = (f32[64,128]{1,0:T(8,128)S(1)}, f32[64,128]{1,0:T(8,128)S(1)}, u32[]{:S(2)}, u32[]{:S(2)}) collective-permute-start(f32[64,128]{1,0:T(8,128)S(1)} %get-tuple-element.24), channel_id=1, source_target_pairs={{0,16},{1,18},{2,17},{3,20},{4,19},{5,22},{6,21},{7,24},{8,23},{9,... | collective-permute-start | bytes 98312 | tf_op jit(solution)/shard_map/ppermute | solution.py:594
  11.8 7.6 %copy-start.1 = (f32[64,128]{1,0:T(8,128)S(1)}, f32[64,128]{1,0:T(8,128)}, u32[]{:S(2)}) copy-start(f32[64,128]{1,0:T(8,128)} %constant.11.clone.refs_8_.weight_ref) | copy-start | bytes 98308
  19.4 0.7 %copy-start.5 = (s32[2,256]{1,0:T(2,128)S(1)}, s32[2,256]{1,0:T(2,128)}, u32[]{:S(2)}) copy-start(s32[2,256]{1,0:T(2,128)} %seam_ref.3) | copy-start | bytes 6148
  19.9 1.5 %collective-permute-start.5 = (f32[368,128]{1,0:T(8,128)S(1)}, f32[368,128]{1,0:T(8,128)S(1)}, u32[]{:S(2)}, u32[]{:S(2)}) collective-permute-start(f32[368,128]{1,0:T(8,128)S(1)} %corners.1), channel_id=1, source_target_pairs={{0,1},{1,0},{2,3},{3,2},{4,5},{5,4},{6,7},{7,6},{8,9},{9,8},{10,11... | collective-permute-start | bytes 565256 | tf_op jit(solution)/shard_map/ppermute | solution.py:579
  20.1 1.2 %copy-start.3 = (s32[24,256]{1,0:T(8,128)S(1)}, s32[24,256]{1,0:T(8,128)}, u32[]{:S(2)}) copy-start(s32[24,256]{1,0:T(8,128)} %constant.14.clone.outer_ref) | copy-start | bytes 73732
  20.1 1.2 %copy-start.4 = (s32[8,640]{1,0:T(8,128)S(1)}, s32[8,640]{1,0:T(8,128)}, u32[]{:S(2)}) copy-start(s32[8,640]{1,0:T(8,128)} %constant.13.clone.ext_ref) | copy-start | bytes 61444

commit v9 on v6

--- a/solution.py
+++ b/solution.py
@@ -17,12 +17,13 @@
 NODES = NP * NP
 ARRAYS = 7
 ROWS = ARRAYS * NODES
+MOVED = 6 * NODES
 EDGE_ROWS = 4 * NP
 ALL_ROWS = ROWS + EDGE_ROWS
-HALF_ROWS = ALL_ROWS // 2
+HALF_ROWS = (MOVED + NODES // 2 + 2 * NP) // 2
 RING = 4
 RIM_ROWS = ROWS + 2 * EDGE_ROWS
-CORNER_ROWS = RIM_ROWS // 8
+CORNER_ROWS = (MOVED + NODES // 2 + 4 * NP) // 8
 PITCH = GX + 2 * RING
 MID = GY * PITCH
 LANES = 128
@@ -148,14 +149,6 @@
     return table, ext, outer
 
 
-def exact_pieces(values):
-    high = values.astype(bf16)
-    rest = values - high.astype(f32)
-    middle = rest.astype(bf16)
-    low = (rest - middle.astype(f32)).astype(bf16)
-    return high, middle, low
-
-
 def dot(a, b):
     return jnp.dot(a, b, preferred_element_type=f32)
 
@@ -165,8 +158,9 @@
 
 
 def picked(values, one_hot, product=dot):
-    high, middle, low = exact_pieces(values)
-    return (product(high, one_hot) + product(middle, one_hot)) + product(low, one_hot)
+    high = values.astype(bf16)
+    low = (values - high.astype(f32)).astype(bf16)
+    return product(high, one_hot) + product(low, one_hot)
 
 
 def as_one_hot(row_of_lane, depth):
@@ -200,14 +194,13 @@
 
 
 def stored_rows(fields_ref, others):
-    parts = [fields_ref[...].reshape(3 * NODES, ELEMENTS)]
-    parts += [ref[...].reshape(NODES, ELEMENTS) for ref in others]
-    return jnp.concatenate(parts, 0)
-
-
-def mass_tendency(table, h, u, v, tide, area_depth, weighted_area, spin):
-    p = high_low_high(h - tide)
-    slopes = dot(table[: 2 * NODES, : 3 * NODES], jnp.concatenate(p, 0))
+    fields = fields_ref[...].reshape(3 * NODES, ELEMENTS)
+    others = [ref[...].reshape(NODES, ELEMENTS) for ref in others]
+    return jnp.concatenate([fields[:NODES] - others[-1], fields[NODES:]] + others, 0)
+
+
+def mass_tendency(table, p, u, v, area_depth, weighted_area, spin):
+    slopes = dot(table[: 2 * NODES, : 3 * NODES], jnp.concatenate(high_low_high(p), 0))
     flux = high_low_high(area_depth * u) + high_low_high(area_depth * v)
     spread = dot(table[2 * NODES : 3 * NODES], jnp.concatenate(flux, 0))
     return [
@@ -217,11 +210,11 @@
     ]
 
 
-def edge_values(table_ref, weight_ref, h, u, v, area, depth, spin, tide):
+def edge_values(table_ref, weight_ref, p, u, v, area, depth, spin):
     root = jnp.sqrt(area)
     mass = jnp.concatenate([weight_ref[...]] * (area.shape[1] // LANES), 1) * area
     table = table_ref[...].astype(bf16)
-    return mass_tendency(table, h, u, v, tide, root * depth, root, mass * spin) + [mass]
+    return mass_tendency(table, p, u, v, root * depth, root, mass * spin) + [mass]
 
 
 def row_edges(sums):
@@ -230,19 +223,73 @@
 
 def beside(left, right):
     return jnp.concatenate([left, right], 1)
+
+
+def one_of_four(parts, index):
+    out = parts[0]
+    for k in range(1, 4):
+        out = jnp.where(index == k, parts[k], out)
+    return out
+
+
+def folded(tide, kept, late, step):
+    half = NODES // 2
+    back = pltpu.roll(tide[half:], LANES - step, 1)
+    onward = pltpu.roll(tide[half:], step, 1)
+    return jnp.where(kept, tide[:half], jnp.where(late, back, onward))
+
+
+def unfolded(rows, late, step):
+    back = pltpu.roll(rows, LANES - step, 1)
+    onward = pltpu.roll(rows, step, 1)
+    return jnp.concatenate([rows, jnp.where(late, onward, back)], 0)
+
+
+def strip_rows(parts, late, shift, rims):
+    lane = lax.broadcasted_iota(i32, (1, LANES), 1)
+    index = (lane >> shift) & 3
+    kept = jnp.where(late, index // 2, 1 - index // 2) != 0
+    tide = folded(parts[6], kept, late, 2 << shift)
+    rim = one_of_four(rims, index)
+    return jnp.concatenate(parts[:6] + [tide, rim, jnp.zeros_like(rim)], 0)
+
+
+def placed_rows(whole, late, shift):
+    half = NODES // 2
+    tide = unfolded(whole[MOVED : MOVED + half], late, 2 << shift)
+    rim = whole[MOVED + half : MOVED + half + NP]
+    return jnp.concatenate([whole[:MOVED], tide] + spread_out(rim, late, shift), 0)
+
+
+def spread_out(rim, late, shift):
+    parts = []
+    for k in range(4):
+        first = pltpu.roll(rim, (LANES - (k << shift)) % LANES, 1) if k else rim
+        last = pltpu.roll(rim, (3 - k) << shift, 1) if k < 3 else rim
+        parts.append(jnp.where(late, first, last))
+    return parts
 
 
 def with_row_rim(whole, sums, top):
     north, south = row_edges(sums)
     rim = jnp.where(top, pltpu.roll(north, RING, 1), pltpu.roll(south, LANES - RING, 1))
-    return jnp.concatenate([whole, rim], 0)
+    parts = [rim[k * NP : (k + 1) * NP] for k in range(4)]
+    lane = lax.broadcasted_iota(i32, (1, LANES), 1)
+    spots = []
+    for k, part in enumerate(parts):
+        first = pltpu.roll(part, k * RING, 1) if k else part
+        last = pltpu.roll(part, (LANES - (3 - k) * RING) % LANES, 1) if k < 3 else part
+        spots.append(jnp.where(top, first, last))
+    rim = one_of_four(spots, (lane >> 2) & 3)
+    return jnp.concatenate([whole[: MOVED + NODES // 2 + NP], rim], 0)
 
 
 def corner_of(whole, start, top):
     lane = lax.broadcasted_iota(i32, (1, LANES), 1)
     base = LANES - start - jnp.where(top != 0, 48, 0)
+    whole = jnp.concatenate([whole, jnp.zeros((8 * CORNER_ROWS - whole.shape[0], LANES), f32)], 0)
     out = None
-    for k in range(RIM_ROWS // CORNER_ROWS):
+    for k in range(8):
         part = whole[k * CORNER_ROWS : (k + 1) * CORNER_ROWS]
         part = pltpu.roll(part, (base + 16 * k) & (LANES - 1), 1)
         out = part if k == 0 else jnp.where(lane >= 16 * k, part, out)
@@ -332,15 +379,19 @@
         return parts
 
     strip, ring = in_frame(both[:, :LANES]), in_frame(both[:, LANES : 2 * LANES])
-    rows = both[:, 3 * LANES :]
-    rows = [rows[k * NODES : (k + 1) * NODES] for k in range(ARRAYS)]
+    rows, behind = (
+        [part[k * NODES : (k + 1) * NODES] for k in range(ARRAYS)]
+        for part in (both[:, 2 * LANES : 3 * LANES], both[:, 3 * LANES :])
+    )
     edges = edge_values(
-        table_ref, weight_ref, *(jnp.concatenate(parts, 1) for parts in zip(strip, ring, rows))
+        table_ref,
+        weight_ref,
+        *(jnp.concatenate(parts, 1) for parts in zip(strip[:6], ring[:6], behind[:6])),
     )
     east = jnp.where(second, east1, east0) != 0
     ends = [part[:, LANES : 2 * LANES] for part in edges]
     ends = [jnp.where(east, part[NODES - NP :], part[:NP]) for part in ends]
-    whole = jnp.concatenate(strip + ends, 0)
+    whole = strip_rows(strip, east, 0, ends)
     out0_ref[...], out1_ref[...] = packed(whole)
     sums[0] = jnp.concatenate([part[:, :LANES] for part in edges], 0)
     top0, top1 = odd ^ flip0, odd ^ flip1
@@ -348,16 +399,17 @@
     far0_ref[...] = corner_of(whole, 0, top0)
     far1_ref[...] = corner_of(whole, 64, top1)
     sums[0] = jnp.concatenate([part[:, 2 * LANES :] for part in edges], 0)
-    rim = jnp.where(goes_up(lane), *row_edges(sums))
-    rows = jnp.concatenate([both[:, 2 * LANES : 3 * LANES], rim], 0)
-    pair_ref[...], next_ref[...] = packed(rows)
+    up = goes_up(lane)
+    rim = jnp.where(up, *row_edges(sums))
+    rim = [rim[k * NP : (k + 1) * NP] for k in range(4)]
+    pair_ref[...], next_ref[...] = packed(strip_rows(rows, up, 4, rim))
 
 
 def corners_kernel(in1_ref, in0_ref, pair_ref, table_ref, weight_ref, *refs):
     out_ref, sums = refs[-2:]
     top = 1 - (lax.axis_index("blk") & 1)
     whole = unpacked(in0_ref[...], in1_ref[...])
-    parts = [whole[k * NODES : (k + 1) * NODES] for k in range(ARRAYS)]
+    parts = [whole[k * NODES : (k + 1) * NODES] for k in range(6)]
     sums[0] = jnp.concatenate(edge_values(table_ref, weight_ref, *parts), 0)
     whole = with_row_rim(whole, sums, jnp.broadcast_to(top != 0, (1, LANES)))
     out_ref[:HALF_ROWS] = pair_ref[...]
@@ -375,7 +427,9 @@
     block_cols, seam_ref, in0_ref, in1_ref, own_ref, lanes_ref, low_ref, centre_ref, high_ref
 ):
     east0, flip0, east1, flip1 = seam_flags(seam_ref, block_cols)
-    whole = unpacked(in0_ref[...], in1_ref[...])
+    second = lax.broadcasted_iota(i32, (1, LANES), 1) >= 64
+    late = jnp.where(second, east1, east0) == 0
+    whole = placed_rows(unpacked(in0_ref[...], in1_ref[...]), late, 0)
     side = lanes_ref[16:24]
     first_at = jnp.where(side == 2, 64 * (1 - east0), 64 * east0)
     place = jnp.where(side == 0, -1, lanes_ref[8:16] + first_at)
@@ -396,21 +450,29 @@
 
     lane = lax.broadcasted_iota(i32, (1, LANES), 1)
     pair = pair_ref[...]
-    strips = unpacked(pair[:HALF_ROWS], next_ref[...])
+    late = jnp.where(lane < 64, odd, 1 - odd) != 0
+    strips = placed_rows(unpacked(pair[:HALF_ROWS], next_ref[...]), late, 4)
     strips = jnp.concatenate(
         [strips[:ROWS], jnp.zeros((EDGE_ROWS, LANES), f32), strips[ROWS:]], 0
     )
     near = pair[HALF_ROWS:]
     sources = (near[:CORNER_ROWS], near[CORNER_ROWS:], far0_ref[...], far1_ref[...])
     corners = []
-    for k in range(RIM_ROWS // CORNER_ROWS):
+    for k in range(8):
         rows = None
         for n, source in enumerate(sources):
             shift = 16 * (n - k) % LANES
             part = pltpu.roll(source, shift, 1) if shift else source
             rows = part if n == 0 else jnp.where(lane >= 16 * n, part, rows)
         corners.append(rows)
-    around = jnp.concatenate([strips, jnp.concatenate(corners, 0)], 1)
+    corners = jnp.concatenate(corners, 0)
+    rim = MOVED + NODES // 2 + NP
+    late = jnp.where((lane & 16) != 0, east1, east0) == 0
+    below = jnp.where((lane & 32) != 0, 1 - odd, odd) != 0
+    corners = jnp.concatenate(
+        [placed_rows(corners, late, 0)] + spread_out(corners[rim : rim + NP], below, 2), 0
+    )
+    around = jnp.concatenate([strips, corners], 1)
     kind = outer_ref[8:16]
     sender = jnp.where(outer_ref[16:24] != 0, odd, 1 - odd)
     strip_at = jnp.where(kind == 3, 16 * (1 - east0), 16 * east0)
@@ -484,7 +546,7 @@
         return [part * per_mass for part in edge_sum(parts, rims, rows)]
 
     def tendency(s):
-        return mass_tendency(table, *s, tide, area_depth, root, mass_spin)
+        return mass_tendency(table, *s, area_depth, root, mass_spin)
 
     def laplace(s):
         return [
@@ -498,6 +560,7 @@
     two = [0.75 * s + 0.25 * (o + time_step * c) for s, o, c in zip(start, one, change)]
     change = average(tendency(two))
     three = [s / 3.0 + 2.0 / 3.0 * (o + time_step * c) for s, o, c in zip(start, two, change)]
+    three[0] = three[0] + tide
     biharmonic = average(laplace(average(laplace(three))))
     own = ext_ref[3:4, LANES : LANES + MID] != 0
     stepped = [

time: 24.3 us -> 24.1 us (level)
  Pallas kernels: 9.42 us -> 9.1 us
    pallas_call x5, Pallas kernels: 9.42 us -> 9.1 us  [call(): pl.pallas_call(kernel, out_shape=[jax.ShapeDtypeStruct(*out) for out in o...]
where the time goes in v9:
time: 24.1 us; the launch traced here: 23.8 us
  starting transfers between devices  9.67 us (40%)
  Pallas kernels  9.1 us (38%)
  waiting for transfers between devices  4.88 us (20%)
    pallas_call x5, Pallas kernels, call(): pl.pallas_call(kernel, out_shape=[jax.ShapeDtypeStruct(*out) for out in o...  9.1 us
    ppermute x4, starting transfers between devices, eastward(): lax.ppermute(value, both, [(rank(*a), rank(*b)) for a, b in pairs.items()])  8.6 us
    ppermute x4, waiting for transfers between devices, eastward(): lax.ppermute(value, both, [(rank(*a), rank(*b)) for a, b in pairs.items()])  4.87 us
    ppermute x2, starting transfers between devices, swapped(): lax.ppermute(value, both, [(rank(f, x, y), rank(f, x, partner(y))) for f,...  1.06 us
  transfers between devices with their start and end apart: 6, of which 1 were waited for; matrix products, arithmetic and copies ran while one was open for 0% of the time, Pallas kernels for 7%

profile of v9, /device:TPU:0, one launch (start us, length us, event | category | flops | bytes accessed | tf_op | source)
XLA Modules:
  0.0 23.8 jit_solution(12913508762000294559)
XLA Ops:
  0.0 2.4 %strips.1 = (f32[216,128]{1,0:T(8,128)S(1)}, f32[56,128]{1,0:T(8,128)S(1)}, f32[216,128]{1,0:T(8,128)S(1)}, f32[56,128]{1,0:T(8,128)S(1)}, f32[216,128]{1,0:T(8,...) custom-call(s32[2,256]{1,0:T(2,128)} %seam_ref.3, s32[1,256]{1,0:T(1,128)} %slot_ref.1, ...), custom_call_target="tpu_custom_call" | custom-call | flops 100000000 | bytes 2097152 | tf_op jit(solution)/shard_map/strips/pallas_call | solution.py:589
  2.4 0.0 copy-start
  2.4 6.4 %collective-permute-start = (f32[216,128]{1,0:T(8,128)S(1)}, f32[216,128]{1,0:T(8,128)S(1)}, u32[]{:S(2)}, u32[]{:S(2)}) collective-permute-start(f32[216,128]{1,0:T(8,128)S(1)} %get-tuple-element.17), channel_id=1, source_target_pairs={{0,31},{1,30},{2,29},{3,28},{4,27},{5,26},{6,25},{7,24},{8,23},{9,... | collective-permute-start | bytes 331784 | tf_op jit(solution)/shard_map/ppermute | solution.py:657
  8.9 0.5 %collective-permute-start.1 = (f32[216,128]{1,0:T(8,128)S(1)}, f32[216,128]{1,0:T(8,128)S(1)}, u32[]{:S(2)}, u32[]{:S(2)}) collective-permute-start(f32[216,128]{1,0:T(8,128)S(1)} %get-tuple-element.18), channel_id=1, source_target_pairs={{0,16},{1,17},{2,18},{3,19},{4,20},{5,21},{6,22},{7,23},{8,24},{9,... | collective-permute-start | bytes 331784 | tf_op jit(solution)/shard_map/ppermute | solution.py:657
  9.4 0.7 %collective-permute-start.4 = (f32[216,128]{1,0:T(8,128)S(1)}, f32[216,128]{1,0:T(8,128)S(1)}, u32[]{:S(2)}, u32[]{:S(2)}) collective-permute-start(f32[216,128]{1,0:T(8,128)S(1)} %get-tuple-element.24), channel_id=1, source_target_pairs={{0,0},{1,2},{2,1},{3,4},{4,3},{5,6},{6,5},{7,8},{8,7},{9,10},{10,9... | collective-permute-start | bytes 331784 | tf_op jit(solution)/shard_map/ppermute | solution.py:642
  10.1 1.2 %collective-permute-start.2 = (f32[56,128]{1,0:T(8,128)S(1)}, f32[56,128]{1,0:T(8,128)S(1)}, u32[]{:S(2)}, u32[]{:S(2)}) collective-permute-start(f32[56,128]{1,0:T(8,128)S(1)} %get-tuple-element.22), channel_id=1, source_target_pairs={{0,31},{1,29},{2,30},{3,27},{4,28},{5,25},{6,26},{7,23},{8,24},{9,... | collective-permute-start | bytes 86024 | tf_op jit(solution)/shard_map/ppermute | solution.py:657
  11.2 0.5 %collective-permute-start.3 = (f32[56,128]{1,0:T(8,128)S(1)}, f32[56,128]{1,0:T(8,128)S(1)}, u32[]{:S(2)}, u32[]{:S(2)}) collective-permute-start(f32[56,128]{1,0:T(8,128)S(1)} %get-tuple-element.23), channel_id=1, source_target_pairs={{0,16},{1,18},{2,17},{3,20},{4,19},{5,22},{6,21},{7,24},{8,23},{9,... | collective-permute-start | bytes 86024 | tf_op jit(solution)/shard_map/ppermute | solution.py:657
  11.7 0.0 copy-done.2
  11.7 0.0 copy-done.6
  11.7 0.6 %own.1 = (f32[448,384]{1,0:T(8,128)S(1)}, bf16[256,384]{1,0:T(8,128)(2,1)S(1)}) custom-call(f32[448,256]{1,0:T(8,128)S(1)} %get-tuple-element.20.stored_ref, s32[1,256]{1,0:T(1,128)S(1)} %copy-done.6, s32[24,384]{1,0:T(8,128)S(1)} %copy-done.2), custom_call_target="tpu_custom_call" | custom-call | flops 100000000 | bytes 2097152 | tf_op jit(solution)/shard_map/own/pallas_call | solution.py:589
  12.3 4.9 %collective-permute-done.2.refs_1_.far1_ref = f32[56,128]{1,0:T(8,128)S(1)} collective-permute-done((f32[56,128]{1,0:T(8,128)S(1)}, f32[56,128]{1,0:T(8,128)S(1)}, u32[]{:S(2)}, u32[]{:S(2)}) %collective-permute-start.2) | collective-permute-done | bytes 28704 | tf_op jit(solution)/shard_map/ppermute | solution.py:657
  17.2 0.0 collective-permute-done.3.refs_2_.far0_ref
  17.2 0.0 collective-permute-done.in1_ref
  17.2 0.0 collective-permute-done.1.in0_ref
  17.2 0.0 collective-permute-done.4.refs_3_.next_ref
  17.2 0.0 copy-done
  17.2 0.0 copy-done.1
  17.2 0.0 copy-start.5
  17.2 0.5 %corners.1 = f32[328,128]{1,0:T(8,128)S(1)} custom-call(f32[216,128]{1,0:T(8,128)S(1)} %collective-permute-done.in1_ref, f32[216,128]{1,0:T(8,128)S(1)} %collective-permute-done.1.in0_ref, f32[216,128]{1,0:T(8,128)S(1)} %get-tuple-element.19.pair_ref, f32[256,384]{1,0:T(8,128)S(1)} %copy-done, f32[64,128]{1,0:T(8,128)S(1)} %copy-done.1, ...), custom_call_target="tpu_custom_call" | custom-call | flops 100000000 | bytes 2097152 | tf_op jit(solution)/shard_map/corners/pallas_call | solution.py:589
  17.7 0.4 %collective-permute-start.5 = (f32[328,128]{1,0:T(8,128)S(1)}, f32[328,128]{1,0:T(8,128)S(1)}, u32[]{:S(2)}, u32[]{:S(2)}) collective-permute-start(f32[328,128]{1,0:T(8,128)S(1)} %corners.1), channel_id=1, source_target_pairs={{0,1},{1,0},{2,3},{3,2},{4,5},{5,4},{6,7},{7,6},{8,9},{9,8},{10,11... | collective-permute-start | bytes 503816 | tf_op jit(solution)/shard_map/ppermute | solution.py:642
  18.1 0.0 copy-done.5
  18.1 1.0 %middle.1 = (f32[480,128]{1,0:T(8,128)S(1)}, f32[480,128]{1,0:T(8,128)S(1)}, f32[480,128]{1,0:T(8,128)S(1)}) custom-call(s32[2,256]{1,0:T(2,128)S(1)} %copy-done.5, f32[216,128]{1,0:T(8,128)S(1)} %collective-permute-done.1.in0_ref, f32[216,128]{1,0:T(8,128)S(1)} %collective-permute-done.in1_ref, f32[448,384]{1,0:T(8,128)S(1)} %get-tuple-element.25.own_ref, ...), custom_call_target="tpu_custom_call" | custom-call | flops 100000000 | bytes 2097152 | tf_op jit(solution)/shard_map/middle/pallas_call | solution.py:589
  19.1 0.0 collective-permute-done.5.pair_ref
  19.1 4.6 %steps.1 = f32[3,8,8,256]{3,2,1,0:T(8,128)} custom-call(s32[2,256]{1,0:T(2,128)S(1)} %copy-done.5, f32[328,128]{1,0:T(8,128)S(1)} %collective-permute-done.5.pair_ref, f32[216,128]{1,0:T(8,128)S(1)} %collective-permute-done.4.refs_3_.next_ref, f32[56,128]{1,0:T(8,128)S(1)} %collective-permute-done.3.refs_2_.far0_ref, ...), custom_call_target="tpu_custom_call" | custom-call | flops 100000000 | bytes 2097152 | tf_op jit(solution)/shard_map/steps/pallas_call | solution.py:589
  (7 shorter events, 0.0 us)
Async XLA Ops:
  0.0 11.7 %copy-start.2 = (s32[24,384]{1,0:T(8,128)S(1)}, s32[24,384]{1,0:T(8,128)}, u32[]{:S(2)}) copy-start(s32[24,384]{1,0:T(8,128)} %constant.12.clone.lanes_ref) | copy-start | bytes 110596
  0.0 11.7 %copy-start.6 = (s32[1,256]{1,0:T(1,128)S(1)}, s32[1,256]{1,0:T(1,128)}, u32[]{:S(2)}) copy-start(s32[1,256]{1,0:T(1,128)} %slot_ref.1) | copy-start | bytes 3076
  2.4 14.8 %copy-start = (f32[256,384]{1,0:T(8,128)S(1)}, f32[256,384]{1,0:T(8,128)}, u32[]{:S(2)}) copy-start(f32[256,384]{1,0:T(8,128)} %constant.10.clone.refs_7_.table_ref) | copy-start | bytes 1179652
  2.4 14.7 %collective-permute-start = (f32[216,128]{1,0:T(8,128)S(1)}, f32[216,128]{1,0:T(8,128)S(1)}, u32[]{:S(2)}, u32[]{:S(2)}) collective-permute-start(f32[216,128]{1,0:T(8,128)S(1)} %get-tuple-element.17), channel_id=1, source_target_pairs={{0,31},{1,30},{2,29},{3,28},{4,27},{5,26},{6,25},{7,24},{8,23},{9,... | collective-permute-start | bytes 331784 | tf_op jit(solution)/shard_map/ppermute | solution.py:657
  8.9 8.3 %collective-permute-start.1 = (f32[216,128]{1,0:T(8,128)S(1)}, f32[216,128]{1,0:T(8,128)S(1)}, u32[]{:S(2)}, u32[]{:S(2)}) collective-permute-start(f32[216,128]{1,0:T(8,128)S(1)} %get-tuple-element.18), channel_id=1, source_target_pairs={{0,16},{1,17},{2,18},{3,19},{4,20},{5,21},{6,22},{7,23},{8,24},{9,... | collective-permute-start | bytes 331784 | tf_op jit(solution)/shard_map/ppermute | solution.py:657
  9.4 7.8 %collective-permute-start.4 = (f32[216,128]{1,0:T(8,128)S(1)}, f32[216,128]{1,0:T(8,128)S(1)}, u32[]{:S(2)}, u32[]{:S(2)}) collective-permute-start(f32[216,128]{1,0:T(8,128)S(1)} %get-tuple-element.24), channel_id=1, source_target_pairs={{0,0},{1,2},{2,1},{3,4},{4,3},{5,6},{6,5},{7,8},{8,7},{9,10},{10,9... | collective-permute-start | bytes 331784 | tf_op jit(solution)/shard_map/ppermute | solution.py:642
  10.1 7.1 %collective-permute-start.2 = (f32[56,128]{1,0:T(8,128)S(1)}, f32[56,128]{1,0:T(8,128)S(1)}, u32[]{:S(2)}, u32[]{:S(2)}) collective-permute-start(f32[56,128]{1,0:T(8,128)S(1)} %get-tuple-element.22), channel_id=1, source_target_pairs={{0,31},{1,29},{2,30},{3,27},{4,28},{5,25},{6,26},{7,23},{8,24},{9,... | collective-permute-start | bytes 86024 | tf_op jit(solution)/shard_map/ppermute | solution.py:657
  11.2 5.9 %collective-permute-start.3 = (f32[56,128]{1,0:T(8,128)S(1)}, f32[56,128]{1,0:T(8,128)S(1)}, u32[]{:S(2)}, u32[]{:S(2)}) collective-permute-start(f32[56,128]{1,0:T(8,128)S(1)} %get-tuple-element.23), channel_id=1, source_target_pairs={{0,16},{1,18},{2,17},{3,20},{4,19},{5,22},{6,21},{7,24},{8,23},{9,... | collective-permute-start | bytes 86024 | tf_op jit(solution)/shard_map/ppermute | solution.py:657
  11.7 5.5 %copy-start.1 = (f32[64,128]{1,0:T(8,128)S(1)}, f32[64,128]{1,0:T(8,128)}, u32[]{:S(2)}) copy-start(f32[64,128]{1,0:T(8,128)} %constant.11.clone.refs_8_.weight_ref) | copy-start | bytes 98308
  17.2 0.9 %copy-start.5 = (s32[2,256]{1,0:T(2,128)S(1)}, s32[2,256]{1,0:T(2,128)}, u32[]{:S(2)}) copy-start(s32[2,256]{1,0:T(2,128)} %seam_ref.3) | copy-start | bytes 6148
  17.7 1.4 %collective-permute-start.5 = (f32[328,128]{1,0:T(8,128)S(1)}, f32[328,128]{1,0:T(8,128)S(1)}, u32[]{:S(2)}, u32[]{:S(2)}) collective-permute-start(f32[328,128]{1,0:T(8,128)S(1)} %corners.1), channel_id=1, source_target_pairs={{0,1},{1,0},{2,3},{3,2},{4,5},{5,4},{6,7},{7,6},{8,9},{9,8},{10,11... | collective-permute-start | bytes 503816 | tf_op jit(solution)/shard_map/ppermute | solution.py:642
  18.1 1.0 %copy-start.3 = (s32[24,256]{1,0:T(8,128)S(1)}, s32[24,256]{1,0:T(8,128)}, u32[]{:S(2)}) copy-start(s32[24,256]{1,0:T(8,128)} %constant.14.clone.outer_ref) | copy-start | bytes 73732
  18.1 1.0 %copy-start.4 = (s32[8,640]{1,0:T(8,128)S(1)}, s32[8,640]{1,0:T(8,128)}, u32[]{:S(2)}) copy-start(s32[8,640]{1,0:T(8,128)} %constant.13.clone.ext_ref) | copy-start | bytes 61444

commit v10 on v9

--- a/solution.py
+++ b/solution.py
@@ -639,9 +639,11 @@
         return other if 0 <= other < BY else y
 
     def swapped(value, partner):
-        return lax.ppermute(
-            value, both, [(rank(f, x, y), rank(f, x, partner(y))) for f, x, y in places]
-        )
+        pairs = [
+            (rank(f, x, y), rank(f if partner(y) != y else 1 - f, x, partner(y)))
+            for f, x, y in places
+        ]
+        return lax.ppermute(value, both, pairs)
 
     def across(value0, value1, partner):
         last = block_cols - 1

time: 24.1 us -> 24.6 us (1.021)
  waiting for transfers between devices: 4.88 us -> 5.25 us
    ppermute x2, starting transfers between devices: 1.06 us -> 1.53 us  [swapped(): return lax.ppermute(value, both, pairs)]
    ppermute x4, starting transfers between devices: 8.6 us -> 8.32 us  [eastward(): lax.ppermute(value, both, [(rank(*a), rank(*b)) for a, b in pairs.items()])]
  transfers between devices with their start and end apart: 6 -> 6, of which waited for: 1 -> 3; matrix products, arithmetic and copies ran while one was open for 0% -> 0% of each run, Pallas kernels for 7% -> 6%
where the time goes in v10:
time: 24.6 us; the launch traced here: 24.4 us
  starting transfers between devices  9.85 us (40%)
  Pallas kernels  9.08 us (37%)
  waiting for transfers between devices  5.25 us (21%)
    pallas_call x5, Pallas kernels, call(): pl.pallas_call(kernel, out_shape=[jax.ShapeDtypeStruct(*out) for out in o...  9.08 us
    ppermute x4, starting transfers between devices, eastward(): lax.ppermute(value, both, [(rank(*a), rank(*b)) for a, b in pairs.items()])  8.32 us
    ppermute x4, waiting for transfers between devices, eastward(): lax.ppermute(value, both, [(rank(*a), rank(*b)) for a, b in pairs.items()])  5.02 us
    ppermute x2, starting transfers between devices, swapped(): return lax.ppermute(value, both, pairs)  1.53 us
  transfers between devices with their start and end apart: 6, of which 3 were waited for; matrix products, arithmetic and copies ran while one was open for 0% of the time, Pallas kernels for 6%

profile of v10, /device:TPU:0, one launch (start us, length us, event | category | flops | bytes accessed | tf_op | source)
XLA Modules:
  0.0 24.4 jit_solution(6277559298540082671)
XLA Ops:
  0.0 2.4 %strips.1 = (f32[216,128]{1,0:T(8,128)S(1)}, f32[56,128]{1,0:T(8,128)S(1)}, f32[216,128]{1,0:T(8,128)S(1)}, f32[56,128]{1,0:T(8,128)S(1)}, f32[216,128]{1,0:T(8,...) custom-call(s32[2,256]{1,0:T(2,128)} %seam_ref.3, s32[1,256]{1,0:T(1,128)} %slot_ref.1, ...), custom_call_target="tpu_custom_call" | custom-call | flops 100000000 | bytes 2097152 | tf_op jit(solution)/shard_map/strips/pallas_call | solution.py:589
  2.4 0.0 copy-start
  2.4 6.4 %collective-permute-start = (f32[216,128]{1,0:T(8,128)S(1)}, f32[216,128]{1,0:T(8,128)S(1)}, u32[]{:S(2)}, u32[]{:S(2)}) collective-permute-start(f32[216,128]{1,0:T(8,128)S(1)} %get-tuple-element.17), channel_id=1, source_target_pairs={{0,31},{1,30},{2,29},{3,28},{4,27},{5,26},{6,25},{7,24},{8,23},{9,... | collective-permute-start | bytes 331784 | tf_op jit(solution)/shard_map/ppermute | solution.py:659
  8.9 0.5 %collective-permute-start.1 = (f32[216,128]{1,0:T(8,128)S(1)}, f32[216,128]{1,0:T(8,128)S(1)}, u32[]{:S(2)}, u32[]{:S(2)}) collective-permute-start(f32[216,128]{1,0:T(8,128)S(1)} %get-tuple-element.18), channel_id=1, source_target_pairs={{0,16},{1,17},{2,18},{3,19},{4,20},{5,21},{6,22},{7,23},{8,24},{9,... | collective-permute-start | bytes 331784 | tf_op jit(solution)/shard_map/ppermute | solution.py:659
  9.4 1.5 %collective-permute-start.4 = (f32[216,128]{1,0:T(8,128)S(1)}, f32[216,128]{1,0:T(8,128)S(1)}, u32[]{:S(2)}, u32[]{:S(2)}) collective-permute-start(f32[216,128]{1,0:T(8,128)S(1)} %get-tuple-element.24), channel_id=1, source_target_pairs={{0,16},{1,2},{2,1},{3,4},{4,3},{5,6},{6,5},{7,8},{8,7},{9,10},{10,... | collective-permute-start | bytes 331784 | tf_op jit(solution)/shard_map/ppermute | solution.py:646
  10.9 0.0 collective-permute-start.2
  10.9 1.3 %collective-permute-start.3 = (f32[56,128]{1,0:T(8,128)S(1)}, f32[56,128]{1,0:T(8,128)S(1)}, u32[]{:S(2)}, u32[]{:S(2)}) collective-permute-start(f32[56,128]{1,0:T(8,128)S(1)} %get-tuple-element.23), channel_id=1, source_target_pairs={{0,16},{1,18},{2,17},{3,20},{4,19},{5,22},{6,21},{7,24},{8,23},{9,... | collective-permute-start | bytes 86024 | tf_op jit(solution)/shard_map/ppermute | solution.py:659
  12.2 0.0 copy-done.2
  12.2 0.0 copy-done.6
  12.3 0.6 %own.1 = (f32[448,384]{1,0:T(8,128)S(1)}, bf16[256,384]{1,0:T(8,128)(2,1)S(1)}) custom-call(f32[448,256]{1,0:T(8,128)S(1)} %get-tuple-element.20.stored_ref, s32[1,256]{1,0:T(1,128)S(1)} %copy-done.6, s32[24,384]{1,0:T(8,128)S(1)} %copy-done.2), custom_call_target="tpu_custom_call" | custom-call | flops 100000000 | bytes 2097152 | tf_op jit(solution)/shard_map/own/pallas_call | solution.py:589
  12.8 5.0 %collective-permute-done.2.refs_1_.far1_ref = f32[56,128]{1,0:T(8,128)S(1)} collective-permute-done((f32[56,128]{1,0:T(8,128)S(1)}, f32[56,128]{1,0:T(8,128)S(1)}, u32[]{:S(2)}, u32[]{:S(2)}) %collective-permute-start.2) | collective-permute-done | bytes 28704 | tf_op jit(solution)/shard_map/ppermute | solution.py:659
  17.8 0.1 collective-permute-done.3.refs_2_.far0_ref
  17.8 0.0 collective-permute-done.in1_ref
  17.8 0.0 collective-permute-done.1.in0_ref
  17.9 0.0 collective-permute-done.4.refs_3_.next_ref
  17.9 0.0 copy-done
  17.9 0.0 copy-done.1
  17.9 0.0 copy-start.5
  17.9 0.5 %corners.1 = f32[328,128]{1,0:T(8,128)S(1)} custom-call(f32[216,128]{1,0:T(8,128)S(1)} %collective-permute-done.in1_ref, f32[216,128]{1,0:T(8,128)S(1)} %collective-permute-done.1.in0_ref, f32[216,128]{1,0:T(8,128)S(1)} %get-tuple-element.19.pair_ref, f32[256,384]{1,0:T(8,128)S(1)} %copy-done, f32[64,128]{1,0:T(8,128)S(1)} %copy-done.1, ...), custom_call_target="tpu_custom_call" | custom-call | flops 100000000 | bytes 2097152 | tf_op jit(solution)/shard_map/corners/pallas_call | solution.py:589
  18.4 0.0 collective-permute-start.5
  18.4 0.1 copy-done.5
  18.6 1.0 %middle.1 = (f32[480,128]{1,0:T(8,128)S(1)}, f32[480,128]{1,0:T(8,128)S(1)}, f32[480,128]{1,0:T(8,128)S(1)}) custom-call(s32[2,256]{1,0:T(2,128)S(1)} %copy-done.5, f32[216,128]{1,0:T(8,128)S(1)} %collective-permute-done.1.in0_ref, f32[216,128]{1,0:T(8,128)S(1)} %collective-permute-done.in1_ref, f32[448,384]{1,0:T(8,128)S(1)} %get-tuple-element.25.own_ref, ...), custom_call_target="tpu_custom_call" | custom-call | flops 100000000 | bytes 2097152 | tf_op jit(solution)/shard_map/middle/pallas_call | solution.py:589
  19.6 0.2 collective-permute-done.5.pair_ref
  19.8 4.6 %steps.1 = f32[3,8,8,256]{3,2,1,0:T(8,128)} custom-call(s32[2,256]{1,0:T(2,128)S(1)} %copy-done.5, f32[328,128]{1,0:T(8,128)S(1)} %collective-permute-done.5.pair_ref, f32[216,128]{1,0:T(8,128)S(1)} %collective-permute-done.4.refs_3_.next_ref, f32[56,128]{1,0:T(8,128)S(1)} %collective-permute-done.3.refs_2_.far0_ref, ...), custom_call_target="tpu_custom_call" | custom-call | flops 100000000 | bytes 2097152 | tf_op jit(solution)/shard_map/steps/pallas_call | solution.py:589
  (7 shorter events, 0.0 us)
Async XLA Ops:
  0.0 12.2 %copy-start.2 = (s32[24,384]{1,0:T(8,128)S(1)}, s32[24,384]{1,0:T(8,128)}, u32[]{:S(2)}) copy-start(s32[24,384]{1,0:T(8,128)} %constant.12.clone.lanes_ref) | copy-start | bytes 110596
  0.0 12.2 %copy-start.6 = (s32[1,256]{1,0:T(1,128)S(1)}, s32[1,256]{1,0:T(1,128)}, u32[]{:S(2)}) copy-start(s32[1,256]{1,0:T(1,128)} %slot_ref.1) | copy-start | bytes 3076
  2.4 15.4 %copy-start = (f32[256,384]{1,0:T(8,128)S(1)}, f32[256,384]{1,0:T(8,128)}, u32[]{:S(2)}) copy-start(f32[256,384]{1,0:T(8,128)} %constant.10.clone.refs_7_.table_ref) | copy-start | bytes 1179652
  2.4 15.4 %collective-permute-start = (f32[216,128]{1,0:T(8,128)S(1)}, f32[216,128]{1,0:T(8,128)S(1)}, u32[]{:S(2)}, u32[]{:S(2)}) collective-permute-start(f32[216,128]{1,0:T(8,128)S(1)} %get-tuple-element.17), channel_id=1, source_target_pairs={{0,31},{1,30},{2,29},{3,28},{4,27},{5,26},{6,25},{7,24},{8,23},{9,... | collective-permute-start | bytes 331784 | tf_op jit(solution)/shard_map/ppermute | solution.py:659
  8.9 9.0 %collective-permute-start.1 = (f32[216,128]{1,0:T(8,128)S(1)}, f32[216,128]{1,0:T(8,128)S(1)}, u32[]{:S(2)}, u32[]{:S(2)}) collective-permute-start(f32[216,128]{1,0:T(8,128)S(1)} %get-tuple-element.18), channel_id=1, source_target_pairs={{0,16},{1,17},{2,18},{3,19},{4,20},{5,21},{6,22},{7,23},{8,24},{9,... | collective-permute-start | bytes 331784 | tf_op jit(solution)/shard_map/ppermute | solution.py:659
  9.4 8.4 %collective-permute-start.4 = (f32[216,128]{1,0:T(8,128)S(1)}, f32[216,128]{1,0:T(8,128)S(1)}, u32[]{:S(2)}, u32[]{:S(2)}) collective-permute-start(f32[216,128]{1,0:T(8,128)S(1)} %get-tuple-element.24), channel_id=1, source_target_pairs={{0,16},{1,2},{2,1},{3,4},{4,3},{5,6},{6,5},{7,8},{8,7},{9,10},{10,... | collective-permute-start | bytes 331784 | tf_op jit(solution)/shard_map/ppermute | solution.py:646
  10.9 6.9 %collective-permute-start.2 = (f32[56,128]{1,0:T(8,128)S(1)}, f32[56,128]{1,0:T(8,128)S(1)}, u32[]{:S(2)}, u32[]{:S(2)}) collective-permute-start(f32[56,128]{1,0:T(8,128)S(1)} %get-tuple-element.22), channel_id=1, source_target_pairs={{0,31},{1,29},{2,30},{3,27},{4,28},{5,25},{6,26},{7,23},{8,24},{9,... | collective-permute-start | bytes 86024 | tf_op jit(solution)/shard_map/ppermute | solution.py:659
  10.9 6.9 %collective-permute-start.3 = (f32[56,128]{1,0:T(8,128)S(1)}, f32[56,128]{1,0:T(8,128)S(1)}, u32[]{:S(2)}, u32[]{:S(2)}) collective-permute-start(f32[56,128]{1,0:T(8,128)S(1)} %get-tuple-element.23), channel_id=1, source_target_pairs={{0,16},{1,18},{2,17},{3,20},{4,19},{5,22},{6,21},{7,24},{8,23},{9,... | collective-permute-start | bytes 86024 | tf_op jit(solution)/shard_map/ppermute | solution.py:659
  12.3 5.6 %copy-start.1 = (f32[64,128]{1,0:T(8,128)S(1)}, f32[64,128]{1,0:T(8,128)}, u32[]{:S(2)}) copy-start(f32[64,128]{1,0:T(8,128)} %constant.11.clone.refs_8_.weight_ref) | copy-start | bytes 98308
  17.9 0.7 %copy-start.5 = (s32[2,256]{1,0:T(2,128)S(1)}, s32[2,256]{1,0:T(2,128)}, u32[]{:S(2)}) copy-start(s32[2,256]{1,0:T(2,128)} %seam_ref.3) | copy-start | bytes 6148
  18.4 1.4 %collective-permute-start.5 = (f32[328,128]{1,0:T(8,128)S(1)}, f32[328,128]{1,0:T(8,128)S(1)}, u32[]{:S(2)}, u32[]{:S(2)}) collective-permute-start(f32[328,128]{1,0:T(8,128)S(1)} %corners.1), channel_id=1, source_target_pairs={{0,1},{1,0},{2,3},{3,2},{4,5},{5,4},{6,7},{7,6},{8,9},{9,8},{10,11... | collective-permute-start | bytes 503816 | tf_op jit(solution)/shard_map/ppermute | solution.py:646
  18.6 1.2 %copy-start.3 = (s32[24,256]{1,0:T(8,128)S(1)}, s32[24,256]{1,0:T(8,128)}, u32[]{:S(2)}) copy-start(s32[24,256]{1,0:T(8,128)} %constant.14.clone.outer_ref) | copy-start | bytes 73732
  18.6 1.2 %copy-start.4 = (s32[8,640]{1,0:T(8,128)S(1)}, s32[8,640]{1,0:T(8,128)}, u32[]{:S(2)}) copy-start(s32[8,640]{1,0:T(8,128)} %constant.13.clone.ext_ref) | copy-start | bytes 61444

commit v11 on v10

--- a/solution.py
+++ b/solution.py
@@ -153,14 +153,10 @@
     return jnp.dot(a, b, preferred_element_type=f32)
 
 
-def dot_other(a, b):
-    return lax.dot_general(a, b, (((1,), (1,)), ((), ())), preferred_element_type=f32)
-
-
-def picked(values, one_hot, product=dot):
+def picked(values, one_hot):
     high = values.astype(bf16)
     low = (values - high.astype(f32)).astype(bf16)
-    return product(high, one_hot) + product(low, one_hot)
+    return dot(high, one_hot) + dot(low, one_hot)
 
 
 def as_one_hot(row_of_lane, depth):
@@ -420,7 +416,7 @@
 def own_kernel(stored_ref, slot_ref, lanes_ref, own_ref, hot_ref):
     one_hot = by_slot(slot_ref, lanes_ref[0:8])
     own_ref[...] = picked(stored_ref[...], one_hot)
-    hot_ref[...] = one_hot
+    hot_ref[...] = one_hot.astype(f32).T.astype(bf16)
 
 
 def middle_kernel(
@@ -479,74 +475,89 @@
     place = outer_ref[0:8] + jnp.where(kind == 1, 64 * sender, 32 * sender + strip_at)
     outer = picked(around, as_one_hot(jnp.where(kind == 0, -1, place), 2 * LANES))
     tiles = (outer[:, :LANES], low_ref, centre_ref, high_ref, outer[:, LANES:])
-
-    def rows_of(start, count):
-        return jnp.concatenate([ref[start : start + count] for ref in tiles], 1)
-
+    count = len(tiles)
     table = table_ref[...].astype(bf16)
-    weight = jnp.concatenate([weight_ref[...]] * len(tiles), 1)
-    at_rim = ext_ref[0:1] != 0
-    top_row = jnp.where(block_y == BY - 1, ext_ref[1:2], 0) != 0
-    bottom_row = jnp.where(block_y == 0, ext_ref[2:3], 0) != 0
-
-    first_row = ext_ref[4:5] != 0
-    last_row = ext_ref[5:6] != 0
-
-    def edge_sum(parts, rims=None, rows=None):
-        count = len(parts) * NP
+    weight = weight_ref[...]
+    masks = [ext_ref[:, k * LANES : (k + 1) * LANES] for k in range(count)]
+    at_rim = [mask[0:1] != 0 for mask in masks]
+    closed_above = [jnp.where(block_y == BY - 1, mask[1:2], 0) != 0 for mask in masks]
+    closed_below = [jnp.where(block_y == 0, mask[2:3], 0) != 0 for mask in masks]
+    first_row = masks[0][4:5] != 0
+    last_row = masks[-1][5:6] != 0
+
+    def shifted(parts, by):
+        turned = [pltpu.roll(part, -by % LANES, 1) for part in parts]
+        if by > 0:
+            return [
+                jnp.where(lane >= LANES - by, turned[min(k + 1, count - 1)], turned[k])
+                for k in range(count)
+            ]
+        return [jnp.where(lane < -by, turned[max(k - 1, 0)], turned[k]) for k in range(count)]
+
+    def edge_sum(components, rims=None, rows=None):
+        for c in range(components):
+            west_at = slice(c * NODES, c * NODES + NP)
+            east_at = slice((c + 1) * NODES - NP, (c + 1) * NODES)
+            west = [sums[k, west_at] for k in range(count)]
+            east = [sums[k, east_at] for k in range(count)]
+            at_east, at_west = shifted(west, 1), shifted(east, -1)
+            for k in range(count):
+                if rims is not None:
+                    at_east[k] = jnp.where(at_rim[k], rims[k][c], at_east[k])
+                    at_west[k] = jnp.where(at_rim[k], rims[k][c], at_west[k])
+                sums[k, west_at] = west[k] + at_west[k]
+                sums[k, east_at] = east[k] + at_east[k]
+        south_at = pl.ds(0, components * NP, stride=NP)
+        north_at = pl.ds(NP - 1, components * NP, stride=NP)
+        south = [sums[k, south_at] for k in range(count)]
+        north = [sums[k, north_at] for k in range(count)]
+        at_north, at_south = shifted(south, PITCH), shifted(north, -PITCH)
+        for k in range(count):
+            at_north[k] = jnp.where(closed_above[k], 0.0, at_north[k])
+            at_south[k] = jnp.where(closed_below[k], 0.0, at_south[k])
+        if rows is not None:
+            at_south[0] = jnp.where(first_row, rows[0], at_south[0])
+            at_north[-1] = jnp.where(last_row, rows[1], at_north[-1])
+        for k in range(count):
+            sums[k, south_at] = south[k] + at_south[k]
+            sums[k, north_at] = north[k] + at_north[k]
+
+    def part_of(k, n):
+        return tiles[k][n * NODES : (n + 1) * NODES]
+
+    node = lax.broadcasted_iota(i32, (1, NP, 1), 1)
+    rows = []
+    for tile in (tiles[0], tiles[-1]):
+        rim = tile[ALL_ROWS:]
+        east = pltpu.roll(rim, LANES - 1, 1).reshape(4, NP, LANES)
+        west = pltpu.roll(rim, 1, 1).reshape(4, NP, LANES)
+        rim = (
+            rim.reshape(4, NP, LANES)
+            + jnp.where(node == NP - 1, pltpu.roll(east, NP - 1, 1), 0.0)
+            + jnp.where(node == 0, pltpu.roll(west, 1, 1), 0.0)
+        )
+        rows.append(rim.reshape(EDGE_ROWS, LANES))
+    rims = [
+        [tile[ROWS + c * NP : ROWS + (c + 1) * NP] for c in range(4)] for tile in tiles
+    ]
+
+    start, fixed = [], []
+    for k in range(count):
+        area = part_of(k, 3)
+        root = jnp.sqrt(area)
+        mass = weight * area
+        start.append([part_of(k, c) for c in range(3)])
+        fixed.append((root * part_of(k, 4), root, mass * part_of(k, 5)))
+        sums[k, :NODES] = mass
+    edge_sum(1, [rim[3:] for rim in rims], [rim[3 * NP :] for rim in rows])
+    per_mass = [1.0 / sums[k, :NODES] for k in range(count)]
+
+    def put(k, parts):
         for c, part in enumerate(parts):
-            west, east = part[:NP], part[NODES - NP :]
-            at_east = pltpu.roll(west, EXT - 1, 1)
-            at_west = pltpu.roll(east, 1, 1)
-            if rims is not None:
-                at_east = jnp.where(at_rim, rims[c], at_east)
-                at_west = jnp.where(at_rim, rims[c], at_west)
-            part = jnp.concatenate([west + at_west, part[NP : NODES - NP], east + at_east], 0)
-            for k in range(len(tiles)):
-                sums[k, c * NODES : (c + 1) * NODES] = part[:, k * LANES : (k + 1) * LANES]
-        south_at, north_at = pl.ds(0, count, stride=NP), pl.ds(NP - 1, count, stride=NP)
-        south = jnp.concatenate([sums[k, south_at] for k in range(len(tiles))], 1)
-        north = jnp.concatenate([sums[k, north_at] for k in range(len(tiles))], 1)
-        at_north = jnp.where(top_row, 0.0, pltpu.roll(south, EXT - PITCH, 1))
-        at_south = jnp.where(bottom_row, 0.0, pltpu.roll(north, PITCH, 1))
-        if rows is not None:
-            at_north = jnp.where(last_row, rows, at_north)
-            at_south = jnp.where(first_row, rows, at_south)
-        to_north, to_south = north + at_north, south + at_south
-        for k in range(len(tiles)):
-            sums[k, south_at] = to_south[:, k * LANES : (k + 1) * LANES]
-            sums[k, north_at] = to_north[:, k * LANES : (k + 1) * LANES]
-        return [
-            jnp.concatenate(
-                [sums[k, c * NODES : (c + 1) * NODES] for k in range(len(tiles))], 1
-            )
-            for c in range(len(parts))
-        ]
-
-    start = [rows_of(c * NODES, NODES) for c in range(3)]
-    area, depth, spin, tide = [rows_of(c * NODES, NODES) for c in range(3, ARRAYS)]
-    root = jnp.sqrt(area)
-    mass = weight * area
-    mass_spin = mass * spin
-    area_depth = root * depth
-    rims = [rows_of(ROWS + c * NP, NP) for c in range(4)]
-    blank = jnp.zeros((EDGE_ROWS, MID), f32)
-    rows = jnp.concatenate([tiles[0][ALL_ROWS:], blank, tiles[-1][ALL_ROWS:]], 1)
-    node = lax.broadcasted_iota(i32, (1, NP, 1), 1)
-    east = pltpu.roll(rows, EXT - 1, 1).reshape(4, NP, EXT)
-    west = pltpu.roll(rows, 1, 1).reshape(4, NP, EXT)
-    rows = (
-        rows.reshape(4, NP, EXT)
-        + jnp.where(node == NP - 1, pltpu.roll(east, NP - 1, 1), 0.0)
-        + jnp.where(node == 0, pltpu.roll(west, 1, 1), 0.0)
-    ).reshape(EDGE_ROWS, EXT)
-    per_mass = 1.0 / edge_sum([mass], rims[3:], rows[3 * NP :])[0]
-
-    def average(parts, rims=None, rows=None):
-        return [part * per_mass for part in edge_sum(parts, rims, rows)]
-
-    def tendency(s):
-        return mass_tendency(table, *s, area_depth, root, mass_spin)
+            sums[k, c * NODES : (c + 1) * NODES] = part
+
+    def average(k):
+        return [sums[k, c * NODES : (c + 1) * NODES] * per_mass[k] for c in range(3)]
 
     def laplace(s):
         return [
@@ -554,24 +565,42 @@
             for part in s
         ]
 
-    change = average(tendency(start), rims[:3], rows[: 3 * NP])
-    one = [s + time_step * c for s, c in zip(start, change)]
-    change = average(tendency(one))
-    two = [0.75 * s + 0.25 * (o + time_step * c) for s, o, c in zip(start, one, change)]
-    change = average(tendency(two))
-    three = [s / 3.0 + 2.0 / 3.0 * (o + time_step * c) for s, o, c in zip(start, two, change)]
-    three[0] = three[0] + tide
-    biharmonic = average(laplace(average(laplace(three))))
-    own = ext_ref[3:4, LANES : LANES + MID] != 0
-    stepped = [
-        jnp.where(
-            own,
-            (s - time_step * hyper_coeff * b)[:, LANES : LANES + MID],
-            0.0,
+    for k in range(count):
+        put(k, mass_tendency(table, *start[k], *fixed[k]))
+    edge_sum(3, rims, [rim[: 3 * NP] for rim in rows])
+    one = []
+    for k in range(count):
+        one.append([s + time_step * c for s, c in zip(start[k], average(k))])
+        put(k, mass_tendency(table, *one[k], *fixed[k]))
+    edge_sum(3)
+    two = []
+    for k in range(count):
+        two.append(
+            [
+                0.75 * s + 0.25 * (o + time_step * c)
+                for s, o, c in zip(start[k], one[k], average(k))
+            ]
         )
-        for s, b in zip(three, biharmonic)
-    ]
-    stored = picked(jnp.concatenate(stepped, 0), hot_ref[...], dot_other)
+        put(k, mass_tendency(table, *two[k], *fixed[k]))
+    edge_sum(3)
+    three = []
+    for k in range(count):
+        now = [
+            s / 3.0 + 2.0 / 3.0 * (o + time_step * c)
+            for s, o, c in zip(start[k], two[k], average(k))
+        ]
+        now[0] = now[0] + part_of(k, 6)
+        three.append(now)
+        put(k, laplace(now))
+    edge_sum(3)
+    for k in range(count):
+        put(k, laplace(average(k)))
+    edge_sum(3)
+    stepped = []
+    for k in range(1, count - 1):
+        now = [s - time_step * hyper_coeff * b for s, b in zip(three[k], average(k))]
+        stepped.append(jnp.where(masks[k][3:4] != 0, jnp.concatenate(now, 0), 0.0))
+    stored = picked(jnp.concatenate(stepped, 1), hot_ref[...])
     out_ref[...] = stored.reshape(out_ref.shape)
 
 
@@ -647,12 +676,18 @@
 
     def across(value0, value1, partner):
         last = block_cols - 1
+
+        def aligned(y):
+            return partner is same or partner(y) != y
+
         straight = {
             (f, x, y): (f, x + 1, partner(y)) if x < last else (1 - f, 0, partner(y))
             for f, x, y in places
         }
         turned = {
-            (f, last, y): (1 - f, 0, BY - 1 - partner(y)) for f in range(2) for y in range(BY)
+            (f, last, y): (1 - f, 0, BY - 1 - partner(y) if aligned(y) else y)
+            for f in range(2)
+            for y in range(BY)
         }
 
         def eastward(value, pairs):
@@ -685,7 +720,7 @@
     own, hot = call(
         own_kernel,
         [(vmem, x) for x in (stored, slot_of, lanes)],
-        [((ROWS, MID), f32), ((ELEMENTS, MID), bf16)],
+        [((ROWS, MID), f32), ((MID, ELEMENTS), bf16)],
         10**8,
         name="own",
     )

time: 24.6 us -> 25 us (1.016)
  starting transfers between devices: 9.85 us -> 10.5 us
  waiting for transfers between devices: 5.25 us -> 4.89 us
    ppermute x4, starting transfers between devices: 8.32 us -> 9 us  [eastward(): lax.ppermute(value, both, [(rank(*a), rank(*b)) for a, b in pairs.items()])]
    ppermute x4, waiting for transfers between devices: 5.02 us -> 4.66 us  [eastward(): lax.ppermute(value, both, [(rank(*a), rank(*b)) for a, b in pairs.items()])]
where the time goes in v11:
time: 25 us; the launch traced here: 24.9 us
  starting transfers between devices  10.5 us (42%)
  Pallas kernels  9.23 us (37%)
  waiting for transfers between devices  4.89 us (20%)
    pallas_call x5, Pallas kernels, call(): pl.pallas_call(kernel, out_shape=[jax.ShapeDtypeStruct(*out) for out in o...  9.23 us
    ppermute x4, starting transfers between devices, eastward(): lax.ppermute(value, both, [(rank(*a), rank(*b)) for a, b in pairs.items()])  9 us
    ppermute x4, waiting for transfers between devices, eastward(): lax.ppermute(value, both, [(rank(*a), rank(*b)) for a, b in pairs.items()])  4.66 us
    ppermute x2, starting transfers between devices, swapped(): return lax.ppermute(value, both, pairs)  1.53 us
  transfers between devices with their start and end apart: 6, of which 3 were waited for; matrix products, arithmetic and copies ran while one was open for 0% of the time, Pallas kernels for 6%

profile of v11, /device:TPU:0, one launch (start us, length us, event | category | flops | bytes accessed | tf_op | source)
XLA Modules:
  0.0 24.9 jit_solution(12414989677959128851)
XLA Ops:
  0.0 2.4 %strips.1 = (f32[216,128]{1,0:T(8,128)S(1)}, f32[56,128]{1,0:T(8,128)S(1)}, f32[216,128]{1,0:T(8,128)S(1)}, f32[56,128]{1,0:T(8,128)S(1)}, f32[216,128]{1,0:T(8,...) custom-call(s32[2,256]{1,0:T(2,128)} %seam_ref.3, s32[1,256]{1,0:T(1,128)} %slot_ref.1, ...), custom_call_target="tpu_custom_call" | custom-call | flops 100000000 | bytes 2097152 | tf_op jit(solution)/shard_map/strips/pallas_call | solution.py:618
  2.4 0.0 copy-start
  2.4 6.4 %collective-permute-start = (f32[216,128]{1,0:T(8,128)S(1)}, f32[216,128]{1,0:T(8,128)S(1)}, u32[]{:S(2)}, u32[]{:S(2)}) collective-permute-start(f32[216,128]{1,0:T(8,128)S(1)} %get-tuple-element.17), channel_id=1, source_target_pairs={{0,31},{1,30},{2,29},{3,28},{4,27},{5,26},{6,25},{7,24},{8,23},{9,... | collective-permute-start | bytes 331784 | tf_op jit(solution)/shard_map/ppermute | solution.py:694
  8.9 0.5 %collective-permute-start.1 = (f32[216,128]{1,0:T(8,128)S(1)}, f32[216,128]{1,0:T(8,128)S(1)}, u32[]{:S(2)}, u32[]{:S(2)}) collective-permute-start(f32[216,128]{1,0:T(8,128)S(1)} %get-tuple-element.18), channel_id=1, source_target_pairs={{0,16},{1,17},{2,18},{3,19},{4,20},{5,21},{6,22},{7,23},{8,24},{9,... | collective-permute-start | bytes 331784 | tf_op jit(solution)/shard_map/ppermute | solution.py:694
  9.4 1.5 %collective-permute-start.4 = (f32[216,128]{1,0:T(8,128)S(1)}, f32[216,128]{1,0:T(8,128)S(1)}, u32[]{:S(2)}, u32[]{:S(2)}) collective-permute-start(f32[216,128]{1,0:T(8,128)S(1)} %get-tuple-element.24), channel_id=1, source_target_pairs={{0,16},{1,2},{2,1},{3,4},{4,3},{5,6},{6,5},{7,8},{8,7},{9,10},{10,... | collective-permute-start | bytes 331784 | tf_op jit(solution)/shard_map/ppermute | solution.py:675
  10.9 0.5 %collective-permute-start.2 = (f32[56,128]{1,0:T(8,128)S(1)}, f32[56,128]{1,0:T(8,128)S(1)}, u32[]{:S(2)}, u32[]{:S(2)}) collective-permute-start(f32[56,128]{1,0:T(8,128)S(1)} %get-tuple-element.22), channel_id=1, source_target_pairs={{0,16},{1,29},{2,30},{3,27},{4,28},{5,25},{6,26},{7,23},{8,24},{9,... | collective-permute-start | bytes 86024 | tf_op jit(solution)/shard_map/ppermute | solution.py:694
  11.4 1.5 %collective-permute-start.3 = (f32[56,128]{1,0:T(8,128)S(1)}, f32[56,128]{1,0:T(8,128)S(1)}, u32[]{:S(2)}, u32[]{:S(2)}) collective-permute-start(f32[56,128]{1,0:T(8,128)S(1)} %get-tuple-element.23), channel_id=1, source_target_pairs={{0,16},{1,18},{2,17},{3,20},{4,19},{5,22},{6,21},{7,24},{8,23},{9,... | collective-permute-start | bytes 86024 | tf_op jit(solution)/shard_map/ppermute | solution.py:694
  12.9 0.0 copy-done.2
  12.9 0.0 copy-done.6
  12.9 0.6 %own.1 = (f32[448,384]{1,0:T(8,128)S(1)}, bf16[384,256]{1,0:T(8,128)(2,1)S(1)}) custom-call(f32[448,256]{1,0:T(8,128)S(1)} %get-tuple-element.20.stored_ref, s32[1,256]{1,0:T(1,128)S(1)} %copy-done.6, s32[24,384]{1,0:T(8,128)S(1)} %copy-done.2), custom_call_target="tpu_custom_call" | custom-call | flops 100000000 | bytes 2097152 | tf_op jit(solution)/shard_map/own/pallas_call | solution.py:618
  13.5 4.3 %collective-permute-done.2.refs_1_.far1_ref = f32[56,128]{1,0:T(8,128)S(1)} collective-permute-done((f32[56,128]{1,0:T(8,128)S(1)}, f32[56,128]{1,0:T(8,128)S(1)}, u32[]{:S(2)}, u32[]{:S(2)}) %collective-permute-start.2) | collective-permute-done | bytes 28704 | tf_op jit(solution)/shard_map/ppermute | solution.py:694
  17.8 0.3 %collective-permute-done.3.refs_2_.far0_ref = f32[56,128]{1,0:T(8,128)S(1)} collective-permute-done((f32[56,128]{1,0:T(8,128)S(1)}, f32[56,128]{1,0:T(8,128)S(1)}, u32[]{:S(2)}, u32[]{:S(2)}) %collective-permute-start.3) | collective-permute-done | bytes 28704 | tf_op jit(solution)/shard_map/ppermute | solution.py:694
  18.2 0.0 collective-permute-done.in1_ref
  18.2 0.0 collective-permute-done.1.in0_ref
  18.2 0.0 collective-permute-done.4.refs_3_.next_ref
  18.2 0.0 copy-done
  18.2 0.0 copy-done.1
  18.2 0.0 copy-start.5
  18.2 0.5 %corners.1 = f32[328,128]{1,0:T(8,128)S(1)} custom-call(f32[216,128]{1,0:T(8,128)S(1)} %collective-permute-done.in1_ref, f32[216,128]{1,0:T(8,128)S(1)} %collective-permute-done.1.in0_ref, f32[216,128]{1,0:T(8,128)S(1)} %get-tuple-element.19.pair_ref, f32[256,384]{1,0:T(8,128)S(1)} %copy-done, f32[64,128]{1,0:T(8,128)S(1)} %copy-done.1, ...), custom_call_target="tpu_custom_call" | custom-call | flops 100000000 | bytes 2097152 | tf_op jit(solution)/shard_map/corners/pallas_call | solution.py:618
  18.7 0.0 collective-permute-start.5
  18.7 0.1 copy-done.5
  18.9 1.0 %middle.1 = (f32[480,128]{1,0:T(8,128)S(1)}, f32[480,128]{1,0:T(8,128)S(1)}, f32[480,128]{1,0:T(8,128)S(1)}) custom-call(s32[2,256]{1,0:T(2,128)S(1)} %copy-done.5, f32[216,128]{1,0:T(8,128)S(1)} %collective-permute-done.1.in0_ref, f32[216,128]{1,0:T(8,128)S(1)} %collective-permute-done.in1_ref, f32[448,384]{1,0:T(8,128)S(1)} %get-tuple-element.25.own_ref, ...), custom_call_target="tpu_custom_call" | custom-call | flops 100000000 | bytes 2097152 | tf_op jit(solution)/shard_map/middle/pallas_call | solution.py:618
  19.9 0.2 collective-permute-done.5.pair_ref
  20.1 4.8 %steps.1 = f32[3,8,8,256]{3,2,1,0:T(8,128)} custom-call(s32[2,256]{1,0:T(2,128)S(1)} %copy-done.5, f32[328,128]{1,0:T(8,128)S(1)} %collective-permute-done.5.pair_ref, f32[216,128]{1,0:T(8,128)S(1)} %collective-permute-done.4.refs_3_.next_ref, f32[56,128]{1,0:T(8,128)S(1)} %collective-permute-done.3.refs_2_.far0_ref, ...), custom_call_target="tpu_custom_call" | custom-call | flops 100000000 | bytes 2097152 | tf_op jit(solution)/shard_map/steps/pallas_call | solution.py:618
  (7 shorter events, 0.0 us)
Async XLA Ops:
  0.0 12.9 %copy-start.2 = (s32[24,384]{1,0:T(8,128)S(1)}, s32[24,384]{1,0:T(8,128)}, u32[]{:S(2)}) copy-start(s32[24,384]{1,0:T(8,128)} %constant.12.clone.lanes_ref) | copy-start | bytes 110596
  0.0 12.9 %copy-start.6 = (s32[1,256]{1,0:T(1,128)S(1)}, s32[1,256]{1,0:T(1,128)}, u32[]{:S(2)}) copy-start(s32[1,256]{1,0:T(1,128)} %slot_ref.1) | copy-start | bytes 3076
  2.4 15.7 %copy-start = (f32[256,384]{1,0:T(8,128)S(1)}, f32[256,384]{1,0:T(8,128)}, u32[]{:S(2)}) copy-start(f32[256,384]{1,0:T(8,128)} %constant.10.clone.refs_7_.table_ref) | copy-start | bytes 1179652
  2.4 15.7 %collective-permute-start = (f32[216,128]{1,0:T(8,128)S(1)}, f32[216,128]{1,0:T(8,128)S(1)}, u32[]{:S(2)}, u32[]{:S(2)}) collective-permute-start(f32[216,128]{1,0:T(8,128)S(1)} %get-tuple-element.17), channel_id=1, source_target_pairs={{0,31},{1,30},{2,29},{3,28},{4,27},{5,26},{6,25},{7,24},{8,23},{9,... | collective-permute-start | bytes 331784 | tf_op jit(solution)/shard_map/ppermute | solution.py:694
  8.9 9.3 %collective-permute-start.1 = (f32[216,128]{1,0:T(8,128)S(1)}, f32[216,128]{1,0:T(8,128)S(1)}, u32[]{:S(2)}, u32[]{:S(2)}) collective-permute-start(f32[216,128]{1,0:T(8,128)S(1)} %get-tuple-element.18), channel_id=1, source_target_pairs={{0,16},{1,17},{2,18},{3,19},{4,20},{5,21},{6,22},{7,23},{8,24},{9,... | collective-permute-start | bytes 331784 | tf_op jit(solution)/shard_map/ppermute | solution.py:694
  9.4 8.8 %collective-permute-start.4 = (f32[216,128]{1,0:T(8,128)S(1)}, f32[216,128]{1,0:T(8,128)S(1)}, u32[]{:S(2)}, u32[]{:S(2)}) collective-permute-start(f32[216,128]{1,0:T(8,128)S(1)} %get-tuple-element.24), channel_id=1, source_target_pairs={{0,16},{1,2},{2,1},{3,4},{4,3},{5,6},{6,5},{7,8},{8,7},{9,10},{10,... | collective-permute-start | bytes 331784 | tf_op jit(solution)/shard_map/ppermute | solution.py:675
  10.9 6.9 %collective-permute-start.2 = (f32[56,128]{1,0:T(8,128)S(1)}, f32[56,128]{1,0:T(8,128)S(1)}, u32[]{:S(2)}, u32[]{:S(2)}) collective-permute-start(f32[56,128]{1,0:T(8,128)S(1)} %get-tuple-element.22), channel_id=1, source_target_pairs={{0,16},{1,29},{2,30},{3,27},{4,28},{5,25},{6,26},{7,23},{8,24},{9,... | collective-permute-start | bytes 86024 | tf_op jit(solution)/shard_map/ppermute | solution.py:694
  11.4 6.7 %collective-permute-start.3 = (f32[56,128]{1,0:T(8,128)S(1)}, f32[56,128]{1,0:T(8,128)S(1)}, u32[]{:S(2)}, u32[]{:S(2)}) collective-permute-start(f32[56,128]{1,0:T(8,128)S(1)} %get-tuple-element.23), channel_id=1, source_target_pairs={{0,16},{1,18},{2,17},{3,20},{4,19},{5,22},{6,21},{7,24},{8,23},{9,... | collective-permute-start | bytes 86024 | tf_op jit(solution)/shard_map/ppermute | solution.py:694
  12.9 5.2 %copy-start.1 = (f32[64,128]{1,0:T(8,128)S(1)}, f32[64,128]{1,0:T(8,128)}, u32[]{:S(2)}) copy-start(f32[64,128]{1,0:T(8,128)} %constant.11.clone.refs_8_.weight_ref) | copy-start | bytes 98308
  18.2 0.7 %copy-start.5 = (s32[2,256]{1,0:T(2,128)S(1)}, s32[2,256]{1,0:T(2,128)}, u32[]{:S(2)}) copy-start(s32[2,256]{1,0:T(2,128)} %seam_ref.3) | copy-start | bytes 6148
  18.7 1.4 %collective-permute-start.5 = (f32[328,128]{1,0:T(8,128)S(1)}, f32[328,128]{1,0:T(8,128)S(1)}, u32[]{:S(2)}, u32[]{:S(2)}) collective-permute-start(f32[328,128]{1,0:T(8,128)S(1)} %corners.1), channel_id=1, source_target_pairs={{0,1},{1,0},{2,3},{3,2},{4,5},{5,4},{6,7},{7,6},{8,9},{9,8},{10,11... | collective-permute-start | bytes 503816 | tf_op jit(solution)/shard_map/ppermute | solution.py:675
  18.9 1.2 %copy-start.3 = (s32[24,256]{1,0:T(8,128)S(1)}, s32[24,256]{1,0:T(8,128)}, u32[]{:S(2)}) copy-start(s32[24,256]{1,0:T(8,128)} %constant.14.clone.outer_ref) | copy-start | bytes 73732
  18.9 1.2 %copy-start.4 = (s32[8,640]{1,0:T(8,128)S(1)}, s32[8,640]{1,0:T(8,128)}, u32[]{:S(2)}) copy-start(s32[8,640]{1,0:T(8,128)} %constant.13.clone.ext_ref) | copy-start | bytes 61444

commit v12 on v11

--- a/solution.py
+++ b/solution.py
@@ -103,12 +103,15 @@
     along_y = node_weight * np.kron(eye, derivative)
     second = derivative @ derivative
     both = node_weight * (np.kron(second, eye) + np.kron(eye, second))
-    table = np.zeros((4 * NODES, 6 * NODES), ml_dtypes.bfloat16)
+    table = np.zeros((5 * NODES, 4 * NODES), ml_dtypes.bfloat16)
     table[:NODES, : 3 * NODES] = in_three(along_x)
     table[NODES : 2 * NODES, : 3 * NODES] = in_three(along_y)
-    table[2 * NODES : 3 * NODES, : 3 * NODES] = in_three(along_x)
-    table[2 * NODES : 3 * NODES, 3 * NODES :] = in_three(along_y)
-    table[3 * NODES :, : 3 * NODES] = in_three(both)
+    flux = [in_three(along_x), in_three(along_y)]
+    for k, part in enumerate(flux):
+        at = 2 * k * NODES
+        table[2 * NODES : 3 * NODES, at : at + 2 * NODES] = part[:, : 2 * NODES]
+        table[3 * NODES : 4 * NODES, at : at + NODES] = part[:, 2 * NODES :]
+    table[4 * NODES :, : 3 * NODES] = in_three(both)
     spread = np.broadcast_to(node_weight, (NODES, LANES)).astype(np.float32)
     return table.astype(np.float32), np.ascontiguousarray(spread)
 
@@ -197,10 +200,10 @@
 
 def mass_tendency(table, p, u, v, area_depth, weighted_area, spin):
     slopes = dot(table[: 2 * NODES, : 3 * NODES], jnp.concatenate(high_low_high(p), 0))
-    flux = high_low_high(area_depth * u) + high_low_high(area_depth * v)
-    spread = dot(table[2 * NODES : 3 * NODES], jnp.concatenate(flux, 0))
+    flux = high_low_high(area_depth * u)[:2] + high_low_high(area_depth * v)[:2]
+    spread = dot(table[2 * NODES : 4 * NODES], jnp.concatenate(flux, 0))
     return [
-        -spread,
+        -(spread[:NODES] + spread[NODES:]),
         spin * v - weighted_area * slopes[:NODES],
         -spin * u - weighted_area * slopes[NODES:],
     ]
@@ -419,9 +422,8 @@
     hot_ref[...] = one_hot.astype(f32).T.astype(bf16)
 
 
-def middle_kernel(
-    block_cols, seam_ref, in0_ref, in1_ref, own_ref, lanes_ref, low_ref, centre_ref, high_ref
-):
+def middle_kernel(block_cols, seam_ref, in0_ref, in1_ref, own_ref, lanes_ref, *refs):
+    low_ref, centre_ref, high_ref = refs[-3:]
     east0, flip0, east1, flip1 = seam_flags(seam_ref, block_cols)
     second = lax.broadcasted_iota(i32, (1, LANES), 1) >= 64
     late = jnp.where(second, east1, east0) == 0
@@ -480,50 +482,49 @@
     weight = weight_ref[...]
     masks = [ext_ref[:, k * LANES : (k + 1) * LANES] for k in range(count)]
     at_rim = [mask[0:1] != 0 for mask in masks]
-    closed_above = [jnp.where(block_y == BY - 1, mask[1:2], 0) != 0 for mask in masks]
-    closed_below = [jnp.where(block_y == 0, mask[2:3], 0) != 0 for mask in masks]
+    closed_above = jnp.where(block_y == BY - 1, masks[-2][1:2], 0) != 0
+    closed_below = jnp.where(block_y == 0, masks[1][2:3], 0) != 0
     first_row = masks[0][4:5] != 0
     last_row = masks[-1][5:6] != 0
 
-    def shifted(parts, by):
+    def shifted(parts, by, ring):
         turned = [pltpu.roll(part, -by % LANES, 1) for part in parts]
-        if by > 0:
-            return [
-                jnp.where(lane >= LANES - by, turned[min(k + 1, count - 1)], turned[k])
-                for k in range(count)
-            ]
-        return [jnp.where(lane < -by, turned[max(k - 1, 0)], turned[k]) for k in range(count)]
-
-    def edge_sum(components, rims=None, rows=None):
+        size = len(parts)
+        step = 1 if by > 0 else -1
+        others = [(k + step) % size if ring else min(max(k + step, 0), size - 1) for k in range(size)]
+        from_other = lane >= LANES - by if by > 0 else lane < -by
+        return [jnp.where(from_other, turned[others[k]], turned[k]) for k in range(size)]
+
+    def edge_sum(components, slots, rims=None, rows=None):
+        ring = len(slots) < count
         for c in range(components):
             west_at = slice(c * NODES, c * NODES + NP)
             east_at = slice((c + 1) * NODES - NP, (c + 1) * NODES)
-            west = [sums[k, west_at] for k in range(count)]
-            east = [sums[k, east_at] for k in range(count)]
-            at_east, at_west = shifted(west, 1), shifted(east, -1)
-            for k in range(count):
+            west = [sums[k, west_at] for k in slots]
+            east = [sums[k, east_at] for k in slots]
+            at_east, at_west = shifted(west, 1, ring), shifted(east, -1, ring)
+            for n, k in enumerate(slots):
                 if rims is not None:
-                    at_east[k] = jnp.where(at_rim[k], rims[k][c], at_east[k])
-                    at_west[k] = jnp.where(at_rim[k], rims[k][c], at_west[k])
-                sums[k, west_at] = west[k] + at_west[k]
-                sums[k, east_at] = east[k] + at_east[k]
+                    at_east[n] = jnp.where(at_rim[k], rims[k][c], at_east[n])
+                    at_west[n] = jnp.where(at_rim[k], rims[k][c], at_west[n])
+                sums[k, west_at] = west[n] + at_west[n]
+                sums[k, east_at] = east[n] + at_east[n]
         south_at = pl.ds(0, components * NP, stride=NP)
         north_at = pl.ds(NP - 1, components * NP, stride=NP)
-        south = [sums[k, south_at] for k in range(count)]
-        north = [sums[k, north_at] for k in range(count)]
-        at_north, at_south = shifted(south, PITCH), shifted(north, -PITCH)
-        for k in range(count):
-            at_north[k] = jnp.where(closed_above[k], 0.0, at_north[k])
-            at_south[k] = jnp.where(closed_below[k], 0.0, at_south[k])
+        south = [sums[k, south_at] for k in slots]
+        north = [sums[k, north_at] for k in slots]
+        at_north, at_south = shifted(south, PITCH, ring), shifted(north, -PITCH, ring)
+        for n, k in enumerate(slots):
+            if k == count - 2:
+                at_north[n] = jnp.where(closed_above, 0.0, at_north[n])
+            if k == 1:
+                at_south[n] = jnp.where(closed_below, 0.0, at_south[n])
         if rows is not None:
             at_south[0] = jnp.where(first_row, rows[0], at_south[0])
             at_north[-1] = jnp.where(last_row, rows[1], at_north[-1])
-        for k in range(count):
-            sums[k, south_at] = south[k] + at_south[k]
-            sums[k, north_at] = north[k] + at_north[k]
-
-    def part_of(k, n):
-        return tiles[k][n * NODES : (n + 1) * NODES]
+        for n, k in enumerate(slots):
+            sums[k, south_at] = south[n] + at_south[n]
+            sums[k, north_at] = north[n] + at_north[n]
 
     node = lax.broadcasted_iota(i32, (1, NP, 1), 1)
     rows = []
@@ -541,66 +542,100 @@
         [tile[ROWS + c * NP : ROWS + (c + 1) * NP] for c in range(4)] for tile in tiles
     ]
 
-    start, fixed = [], []
-    for k in range(count):
-        area = part_of(k, 3)
-        root = jnp.sqrt(area)
-        mass = weight * area
-        start.append([part_of(k, c) for c in range(3)])
-        fixed.append((root * part_of(k, 4), root, mass * part_of(k, 5)))
-        sums[k, :NODES] = mass
-    edge_sum(1, [rim[3:] for rim in rims], [rim[3 * NP :] for rim in rows])
-    per_mass = [1.0 / sums[k, :NODES] for k in range(count)]
-
-    def put(k, parts):
+    every = tuple(range(count))
+    groups = (every[0:2], every[2:4], every[4:])
+
+    def part_of(group, n):
+        return jnp.concatenate([tiles[k][n * NODES : (n + 1) * NODES] for k in group], 1)
+
+    def put(group, parts):
         for c, part in enumerate(parts):
-            sums[k, c * NODES : (c + 1) * NODES] = part
-
-    def average(k):
-        return [sums[k, c * NODES : (c + 1) * NODES] * per_mass[k] for c in range(3)]
+            for n, k in enumerate(group):
+                sums[k, c * NODES : (c + 1) * NODES] = part[:, n * LANES : (n + 1) * LANES]
+
+    def summed(group, c):
+        return jnp.concatenate([sums[k, c * NODES : (c + 1) * NODES] for k in group], 1)
+
+    def average(group, per_mass):
+        return [summed(group, c) * per_mass for c in range(3)]
 
     def laplace(s):
         return [
-            dot(table[3 * NODES :, : 3 * NODES], jnp.concatenate(high_low_high(part), 0))
+            dot(table[4 * NODES :, : 3 * NODES], jnp.concatenate(high_low_high(part), 0))
             for part in s
         ]
 
-    for k in range(count):
-        put(k, mass_tendency(table, *start[k], *fixed[k]))
-    edge_sum(3, rims, [rim[: 3 * NP] for rim in rows])
+    start, fixed = [], []
+    for group in groups:
+        area = part_of(group, 3)
+        root = jnp.sqrt(area)
+        mass = jnp.concatenate([weight] * len(group), 1) * area
+        start.append([part_of(group, c) for c in range(3)])
+        fixed.append((root * part_of(group, 4), root, mass * part_of(group, 5)))
+        put(group, [mass])
+    edge_sum(1, every, [rim[3:] for rim in rims], [rim[3 * NP :] for rim in rows])
+    per_mass = [1.0 / summed(group, 0) for group in groups]
+
+    for n, group in enumerate(groups):
+        put(group, mass_tendency(table, *start[n], *fixed[n]))
+    edge_sum(3, every, rims, [rim[: 3 * NP] for rim in rows])
     one = []
-    for k in range(count):
-        one.append([s + time_step * c for s, c in zip(start[k], average(k))])
-        put(k, mass_tendency(table, *one[k], *fixed[k]))
-    edge_sum(3)
+    for n, group in enumerate(groups):
+        change = average(group, per_mass[n])
+        one.append([s + time_step * c for s, c in zip(start[n], change)])
+        put(group, mass_tendency(table, *one[n], *fixed[n]))
+    edge_sum(3, every)
     two = []
-    for k in range(count):
+    for n, group in enumerate(groups):
+        change = average(group, per_mass[n])
         two.append(
-            [
-                0.75 * s + 0.25 * (o + time_step * c)
-                for s, o, c in zip(start[k], one[k], average(k))
-            ]
+            [0.75 * s + 0.25 * (o + time_step * c) for s, o, c in zip(start[n], one[n], change)]
         )
-        put(k, mass_tendency(table, *two[k], *fixed[k]))
-    edge_sum(3)
+        put(group, mass_tendency(table, *two[n], *fixed[n]))
+    edge_sum(3, every)
+
+    def regrouped(per_group):
+        (outer_low, high_above) = per_group[0], per_group[1]
+        below, low = outer_low[:, :LANES], outer_low[:, LANES:]
+        centre, high = high_above[:, :LANES], high_above[:, LANES:]
+        near = jnp.where(lane < LANES // 2, per_group[2], below)
+        return [beside(low, centre), beside(high, near)]
+
+    def of_groups(values):
+        return [list(parts) for parts in zip(*(regrouped(part) for part in zip(*values)))]
+
+    for c in range(3):
+        rows_at = slice(c * NODES, (c + 1) * NODES)
+        sums[count - 1, rows_at] = jnp.where(
+            lane < LANES // 2, sums[count - 1, rows_at], sums[0, rows_at]
+        )
+    slots = every[1:]
+    groups = (slots[0:2], slots[2:4])
+    start, two = of_groups(start), of_groups(two)
+    tide = regrouped([part_of(every[0:2], 6), part_of(every[2:4], 6), part_of(every[4:], 6)])
+    per_mass = regrouped(per_mass)
     three = []
-    for k in range(count):
+    for n, group in enumerate(groups):
+        change = average(group, per_mass[n])
         now = [
             s / 3.0 + 2.0 / 3.0 * (o + time_step * c)
-            for s, o, c in zip(start[k], two[k], average(k))
+            for s, o, c in zip(start[n], two[n], change)
         ]
-        now[0] = now[0] + part_of(k, 6)
+        now[0] = now[0] + tide[n]
         three.append(now)
-        put(k, laplace(now))
-    edge_sum(3)
-    for k in range(count):
-        put(k, laplace(average(k)))
-    edge_sum(3)
+        put(group, laplace(now))
+    edge_sum(3, slots)
+    for n, group in enumerate(groups):
+        put(group, laplace(average(group, per_mass[n])))
+    edge_sum(3, slots)
     stepped = []
-    for k in range(1, count - 1):
-        now = [s - time_step * hyper_coeff * b for s, b in zip(three[k], average(k))]
-        stepped.append(jnp.where(masks[k][3:4] != 0, jnp.concatenate(now, 0), 0.0))
-    stored = picked(jnp.concatenate(stepped, 1), hot_ref[...])
+    for n, group in enumerate(groups):
+        change = average(group, per_mass[n])
+        now = [s - time_step * hyper_coeff * b for s, b in zip(three[n], change)]
+        stepped.append(jnp.concatenate(now, 0))
+    stepped = jnp.concatenate(stepped, 1)[:, :MID]
+    own = ext_ref[3:4, LANES : LANES + MID] != 0
+    stored = picked(jnp.where(own, stepped, 0.0), hot_ref[...])
     out_ref[...] = stored.reshape(out_ref.shape)
 
 
@@ -726,7 +761,7 @@
     )
     (to_pair,) = call(
         corners_kernel,
-        [(vmem, x) for x in (halo1, halo0, to_pair, table, weight, hot, far1, far0, from_next)],
+        [(vmem, x) for x in (halo1, halo0, to_pair, table, weight, hot)],
         [((HALF_ROWS + 2 * CORNER_ROWS, LANES), f32)],
         10**8,
         scratch=scratch,
@@ -736,9 +771,9 @@
     tile = ((ALL_ROWS, LANES), f32)
     low, centre, high = call(
         functools.partial(middle_kernel, block_cols),
-        [(smem, seam_rows)] + [(vmem, x) for x in (halo0, halo1, own, lanes)],
+        [(smem, seam_rows)] + [(vmem, x) for x in (halo0, halo1, own, lanes, far1, far0, from_next)],
         [tile, tile, tile],
-        10**8,
+        10**11,
         name="middle",
     )
     (stepped,) = call(

time: 25 us -> 23.3 us (0.932)
  waiting for transfers between devices: 4.89 us -> 3.73 us
  Pallas kernels: 9.23 us -> 8.74 us
    ppermute x4, waiting for transfers between devices: 4.66 us -> 3.73 us  [eastward(): lax.ppermute(value, both, [(rank(*a), rank(*b)) for a, b in pairs.items()])]
    pallas_call x5, Pallas kernels: 9.23 us -> 8.74 us  [call(): pl.pallas_call(kernel, out_shape=[jax.ShapeDtypeStruct(*out) for out in o...]
  transfers between devices with their start and end apart: 6 -> 6, of which waited for: 3 -> 3; matrix products, arithmetic and copies ran while one was open for 0% -> 0% of each run, Pallas kernels for 6% -> 9%
where the time goes in v12:
time: 23.3 us; the launch traced here: 23.2 us
  starting transfers between devices  10.6 us (45%)
  Pallas kernels  8.74 us (38%)
  waiting for transfers between devices  3.73 us (16%)
    ppermute x4, starting transfers between devices, eastward(): lax.ppermute(value, both, [(rank(*a), rank(*b)) for a, b in pairs.items()])  9 us
    pallas_call x5, Pallas kernels, call(): pl.pallas_call(kernel, out_shape=[jax.ShapeDtypeStruct(*out) for out in o...  8.74 us
    ppermute x4, waiting for transfers between devices, eastward(): lax.ppermute(value, both, [(rank(*a), rank(*b)) for a, b in pairs.items()])  3.73 us
    ppermute x2, starting transfers between devices, swapped(): return lax.ppermute(value, both, pairs)  1.59 us
  transfers between devices with their start and end apart: 6, of which 3 were waited for; matrix products, arithmetic and copies ran while one was open for 0% of the time, Pallas kernels for 9%

profile of v12, /device:TPU:0, one launch (start us, length us, event | category | flops | bytes accessed | tf_op | source)
XLA Modules:
  0.0 23.2 jit_solution(9847958874491642023)
XLA Ops:
  0.0 2.4 %strips.1 = (f32[216,128]{1,0:T(8,128)S(1)}, f32[56,128]{1,0:T(8,128)S(1)}, f32[216,128]{1,0:T(8,128)S(1)}, f32[56,128]{1,0:T(8,128)S(1)}, f32[216,128]{1,0:T(8,...) custom-call(s32[2,256]{1,0:T(2,128)} %seam_ref.3, s32[1,256]{1,0:T(1,128)} %slot_ref.1, ...), custom_call_target="tpu_custom_call" | custom-call | flops 100000000 | bytes 2097152 | tf_op jit(solution)/shard_map/strips/pallas_call | solution.py:653
  2.4 0.0 copy-start
  2.4 6.4 %collective-permute-start = (f32[216,128]{1,0:T(8,128)S(1)}, f32[216,128]{1,0:T(8,128)S(1)}, u32[]{:S(2)}, u32[]{:S(2)}) collective-permute-start(f32[216,128]{1,0:T(8,128)S(1)} %get-tuple-element.17), channel_id=1, source_target_pairs={{0,31},{1,30},{2,29},{3,28},{4,27},{5,26},{6,25},{7,24},{8,23},{9,... | collective-permute-start | bytes 331784 | tf_op jit(solution)/shard_map/ppermute | solution.py:729
  8.8 0.5 %collective-permute-start.1 = (f32[216,128]{1,0:T(8,128)S(1)}, f32[216,128]{1,0:T(8,128)S(1)}, u32[]{:S(2)}, u32[]{:S(2)}) collective-permute-start(f32[216,128]{1,0:T(8,128)S(1)} %get-tuple-element.18), channel_id=1, source_target_pairs={{0,16},{1,17},{2,18},{3,19},{4,20},{5,21},{6,22},{7,23},{8,24},{9,... | collective-permute-start | bytes 331784 | tf_op jit(solution)/shard_map/ppermute | solution.py:729
  9.4 1.5 %collective-permute-start.3 = (f32[216,128]{1,0:T(8,128)S(1)}, f32[216,128]{1,0:T(8,128)S(1)}, u32[]{:S(2)}, u32[]{:S(2)}) collective-permute-start(f32[216,128]{1,0:T(8,128)S(1)} %get-tuple-element.22), channel_id=1, source_target_pairs={{0,16},{1,2},{2,1},{3,4},{4,3},{5,6},{6,5},{7,8},{8,7},{9,10},{10,... | collective-permute-start | bytes 331784 | tf_op jit(solution)/shard_map/ppermute | solution.py:710
  10.9 0.5 %collective-permute-start.4 = (f32[56,128]{1,0:T(8,128)S(1)}, f32[56,128]{1,0:T(8,128)S(1)}, u32[]{:S(2)}, u32[]{:S(2)}) collective-permute-start(f32[56,128]{1,0:T(8,128)S(1)} %get-tuple-element.23), channel_id=1, source_target_pairs={{0,16},{1,18},{2,17},{3,20},{4,19},{5,22},{6,21},{7,24},{8,23},{9,... | collective-permute-start | bytes 86024 | tf_op jit(solution)/shard_map/ppermute | solution.py:729
  11.4 1.5 %collective-permute-start.5 = (f32[56,128]{1,0:T(8,128)S(1)}, f32[56,128]{1,0:T(8,128)S(1)}, u32[]{:S(2)}, u32[]{:S(2)}) collective-permute-start(f32[56,128]{1,0:T(8,128)S(1)} %get-tuple-element.24), channel_id=1, source_target_pairs={{0,16},{1,29},{2,30},{3,27},{4,28},{5,25},{6,26},{7,23},{8,24},{9,... | collective-permute-start | bytes 86024 | tf_op jit(solution)/shard_map/ppermute | solution.py:729
  12.9 0.0 copy-done.2
  12.9 0.0 copy-done.6
  12.9 0.6 %own.1 = (f32[448,384]{1,0:T(8,128)S(1)}, bf16[384,256]{1,0:T(8,128)(2,1)S(1)}) custom-call(f32[448,256]{1,0:T(8,128)S(1)} %get-tuple-element.20.stored_ref, s32[1,256]{1,0:T(1,128)S(1)} %copy-done.6, s32[24,384]{1,0:T(8,128)S(1)} %copy-done.2), custom_call_target="tpu_custom_call" | custom-call | flops 100000000 | bytes 2097152 | tf_op jit(solution)/shard_map/own/pallas_call | solution.py:653
  13.5 0.0 collective-permute-done.in1_ref
  13.5 2.2 %collective-permute-done.1.in0_ref = f32[216,128]{1,0:T(8,128)S(1)} collective-permute-done((f32[216,128]{1,0:T(8,128)S(1)}, f32[216,128]{1,0:T(8,128)S(1)}, u32[]{:S(2)}, u32[]{:S(2)}) %collective-permute-start.1) | collective-permute-done | bytes 110624 | tf_op jit(solution)/shard_map/ppermute | solution.py:729
  15.7 0.0 copy-done
  15.7 0.0 copy-done.1
  15.7 0.5 %corners.1 = f32[328,128]{1,0:T(8,128)S(1)} custom-call(f32[216,128]{1,0:T(8,128)S(1)} %collective-permute-done.in1_ref, f32[216,128]{1,0:T(8,128)S(1)} %collective-permute-done.1.in0_ref, f32[216,128]{1,0:T(8,128)S(1)} %get-tuple-element.19.pair_ref, f32[320,256]{1,0:T(8,128)S(1)} %copy-done, f32[64,128]{1,0:T(8,128)S(1)} %copy-done.1, ...), custom_call_target="tpu_custom_call" | custom-call | flops 100000000 | bytes 2097152 | tf_op jit(solution)/shard_map/corners/pallas_call | solution.py:653
  16.2 0.1 collective-permute-start.2
  16.3 1.2 %collective-permute-done.4.refs_1_.far0_ref = f32[56,128]{1,0:T(8,128)S(1)} collective-permute-done((f32[56,128]{1,0:T(8,128)S(1)}, f32[56,128]{1,0:T(8,128)S(1)}, u32[]{:S(2)}, u32[]{:S(2)}) %collective-permute-start.4) | collective-permute-done | bytes 28704 | tf_op jit(solution)/shard_map/ppermute | solution.py:729
  17.5 0.3 %collective-permute-done.5.refs_0_.far1_ref = f32[56,128]{1,0:T(8,128)S(1)} collective-permute-done((f32[56,128]{1,0:T(8,128)S(1)}, f32[56,128]{1,0:T(8,128)S(1)}, u32[]{:S(2)}, u32[]{:S(2)}) %collective-permute-start.5) | collective-permute-done | bytes 28704 | tf_op jit(solution)/shard_map/ppermute | solution.py:729
  17.8 0.0 collective-permute-done.3.refs_2_.next_ref
  17.8 0.0 copy-done.5
  17.8 0.0 copy-start.4
  17.9 1.0 %middle.1 = (f32[480,128]{1,0:T(8,128)S(1)}, f32[480,128]{1,0:T(8,128)S(1)}, f32[480,128]{1,0:T(8,128)S(1)}) custom-call(s32[2,256]{1,0:T(2,128)S(1)} %copy-done.5, f32[216,128]{1,0:T(8,128)S(1)} %collective-permute-done.1.in0_ref, f32[216,128]{1,0:T(8,128)S(1)} %collective-permute-done.in1_ref, f32[448,384]{1,0:T(8,128)S(1)} %get-tuple-element.25.own_ref, ...), custom_call_target="tpu_custom_call" | custom-call | flops 99999997952 | bytes 2097152 | tf_op jit(solution)/shard_map/middle/pallas_call | solution.py:653
  18.9 0.0 collective-permute-done.2.pair_ref
  18.9 4.3 %steps.1 = f32[3,8,8,256]{3,2,1,0:T(8,128)} custom-call(s32[2,256]{1,0:T(2,128)S(1)} %copy-done.5, f32[328,128]{1,0:T(8,128)S(1)} %collective-permute-done.2.pair_ref, f32[216,128]{1,0:T(8,128)S(1)} %collective-permute-done.3.refs_2_.next_ref, f32[56,128]{1,0:T(8,128)S(1)} %collective-permute-done.4.refs_1_.far0_ref, ...), custom_call_target="tpu_custom_call" | custom-call | flops 100000000 | bytes 2097152 | tf_op jit(solution)/shard_map/steps/pallas_call | solution.py:653
  (7 shorter events, 0.0 us)
Async XLA Ops:
  0.0 12.9 %copy-start.2 = (s32[24,384]{1,0:T(8,128)S(1)}, s32[24,384]{1,0:T(8,128)}, u32[]{:S(2)}) copy-start(s32[24,384]{1,0:T(8,128)} %constant.12.clone.lanes_ref) | copy-start | bytes 110596
  0.0 12.9 %copy-start.6 = (s32[1,256]{1,0:T(1,128)S(1)}, s32[1,256]{1,0:T(1,128)}, u32[]{:S(2)}) copy-start(s32[1,256]{1,0:T(1,128)} %slot_ref.1) | copy-start | bytes 3076
  2.4 13.3 %copy-start = (f32[320,256]{1,0:T(8,128)S(1)}, f32[320,256]{1,0:T(8,128)}, u32[]{:S(2)}) copy-start(f32[320,256]{1,0:T(8,128)} %constant.10.clone.refs_7_.table_ref) | copy-start | bytes 983044
  2.4 11.1 %collective-permute-start = (f32[216,128]{1,0:T(8,128)S(1)}, f32[216,128]{1,0:T(8,128)S(1)}, u32[]{:S(2)}, u32[]{:S(2)}) collective-permute-start(f32[216,128]{1,0:T(8,128)S(1)} %get-tuple-element.17), channel_id=1, source_target_pairs={{0,31},{1,30},{2,29},{3,28},{4,27},{5,26},{6,25},{7,24},{8,23},{9,... | collective-permute-start | bytes 331784 | tf_op jit(solution)/shard_map/ppermute | solution.py:729
  8.8 6.9 %collective-permute-start.1 = (f32[216,128]{1,0:T(8,128)S(1)}, f32[216,128]{1,0:T(8,128)S(1)}, u32[]{:S(2)}, u32[]{:S(2)}) collective-permute-start(f32[216,128]{1,0:T(8,128)S(1)} %get-tuple-element.18), channel_id=1, source_target_pairs={{0,16},{1,17},{2,18},{3,19},{4,20},{5,21},{6,22},{7,23},{8,24},{9,... | collective-permute-start | bytes 331784 | tf_op jit(solution)/shard_map/ppermute | solution.py:729
  9.4 8.4 %collective-permute-start.3 = (f32[216,128]{1,0:T(8,128)S(1)}, f32[216,128]{1,0:T(8,128)S(1)}, u32[]{:S(2)}, u32[]{:S(2)}) collective-permute-start(f32[216,128]{1,0:T(8,128)S(1)} %get-tuple-element.22), channel_id=1, source_target_pairs={{0,16},{1,2},{2,1},{3,4},{4,3},{5,6},{6,5},{7,8},{8,7},{9,10},{10,... | collective-permute-start | bytes 331784 | tf_op jit(solution)/shard_map/ppermute | solution.py:710
  10.9 6.6 %collective-permute-start.4 = (f32[56,128]{1,0:T(8,128)S(1)}, f32[56,128]{1,0:T(8,128)S(1)}, u32[]{:S(2)}, u32[]{:S(2)}) collective-permute-start(f32[56,128]{1,0:T(8,128)S(1)} %get-tuple-element.23), channel_id=1, source_target_pairs={{0,16},{1,18},{2,17},{3,20},{4,19},{5,22},{6,21},{7,24},{8,23},{9,... | collective-permute-start | bytes 86024 | tf_op jit(solution)/shard_map/ppermute | solution.py:729
  11.4 6.4 %collective-permute-start.5 = (f32[56,128]{1,0:T(8,128)S(1)}, f32[56,128]{1,0:T(8,128)S(1)}, u32[]{:S(2)}, u32[]{:S(2)}) collective-permute-start(f32[56,128]{1,0:T(8,128)S(1)} %get-tuple-element.24), channel_id=1, source_target_pairs={{0,16},{1,29},{2,30},{3,27},{4,28},{5,25},{6,26},{7,23},{8,24},{9,... | collective-permute-start | bytes 86024 | tf_op jit(solution)/shard_map/ppermute | solution.py:729
  12.9 2.8 %copy-start.1 = (f32[64,128]{1,0:T(8,128)S(1)}, f32[64,128]{1,0:T(8,128)}, u32[]{:S(2)}) copy-start(f32[64,128]{1,0:T(8,128)} %constant.11.clone.refs_8_.weight_ref) | copy-start | bytes 98308
  15.7 2.1 %copy-start.5 = (s32[2,256]{1,0:T(2,128)S(1)}, s32[2,256]{1,0:T(2,128)}, u32[]{:S(2)}) copy-start(s32[2,256]{1,0:T(2,128)} %seam_ref.3) | copy-start | bytes 6148
  16.2 2.6 %collective-permute-start.2 = (f32[328,128]{1,0:T(8,128)S(1)}, f32[328,128]{1,0:T(8,128)S(1)}, u32[]{:S(2)}, u32[]{:S(2)}) collective-permute-start(f32[328,128]{1,0:T(8,128)S(1)} %corners.1), channel_id=1, source_target_pairs={{0,1},{1,0},{2,3},{3,2},{4,5},{5,4},{6,7},{7,6},{8,9},{9,8},{10,11... | collective-permute-start | bytes 503816 | tf_op jit(solution)/shard_map/ppermute | solution.py:710
  17.8 1.1 %copy-start.3 = (s32[24,256]{1,0:T(8,128)S(1)}, s32[24,256]{1,0:T(8,128)}, u32[]{:S(2)}) copy-start(s32[24,256]{1,0:T(8,128)} %constant.14.clone.outer_ref) | copy-start | bytes 73732
  17.8 1.1 %copy-start.4 = (s32[8,640]{1,0:T(8,128)S(1)}, s32[8,640]{1,0:T(8,128)}, u32[]{:S(2)}) copy-start(s32[8,640]{1,0:T(8,128)} %constant.13.clone.ext_ref) | copy-start | bytes 61444

commit v13 on v12

--- a/solution.py
+++ b/solution.py
@@ -181,17 +181,6 @@
     return jnp.where(index == chosen[0:1], 1.0, 0.0).astype(bf16)
 
 
-def brought(sources, buffers, sems):
-    copies = [
-        pltpu.make_async_copy(source, buffer, sems.at[k])
-        for k, (source, buffer) in enumerate(zip(sources, buffers))
-    ]
-    for copy in copies:
-        copy.start()
-    for copy in copies:
-        copy.wait()
-
-
 def stored_rows(fields_ref, others):
     fields = fields_ref[...].reshape(3 * NODES, ELEMENTS)
     others = [ref[...].reshape(NODES, ELEMENTS) for ref in others]
@@ -331,12 +320,18 @@
 
 
 def strips_kernel(block_cols, *refs):
-    sources = refs[:9]
-    out1_ref, far1_ref, out0_ref, far0_ref, next_ref, pair_ref, stored_ref = refs[9:16]
-    buffers, sems, sums = refs[16:25], refs[25], refs[26]
-    brought(sources, buffers, sems)
+    sources, (out1_ref, out0_ref, stored_ref) = refs[:9], refs[9:12]
+    buffers, sems = refs[12:21], refs[21]
+    copies = [
+        pltpu.make_async_copy(source, buffer, sems.at[k])
+        for k, (source, buffer) in enumerate(zip(sources, buffers))
+    ]
+    for copy in copies:
+        copy.start()
     seam_ref, slot_ref, fields_ref, area_ref, depth_ref, spin_ref, tide_ref = buffers[:7]
     table_ref, weight_ref = buffers[7:]
+    for copy in copies[:2]:
+        copy.wait()
     east0, flip0, east1, flip1 = seam_flags(seam_ref, block_cols)
     lane = lax.broadcasted_iota(i32, (8, 2 * LANES), 1)
     second = (lane & 64) != 0
@@ -346,18 +341,10 @@
     east = jnp.where(second, east1, east0) != 0
     col = jnp.where(east, GX - RING, 0) + (place & 3)
     col = jnp.where(lane >= LANES, jnp.where(east, GX - RING - 1, RING), col)
-    cells = col * GY + row
-    odd = lax.axis_index("blk") & 1
-
-    def goes_up(lane):
-        return jnp.where((lane & 64) != 0, odd, 1 - odd) != 0
-
-    up = goes_up(lane)
-    row = jnp.where(up, GY - RING, 0) + ((lane & 63) >> 4)
-    row = jnp.where(lane >= LANES, jnp.where(up, GY - RING - 1, RING), row)
-    one_hot = by_slot(slot_ref, beside(cells, (lane & 15) * GY + row))
+    one_hot = by_slot(slot_ref, col * GY + row)
+    for copy in copies[2:7]:
+        copy.wait()
     stored = stored_rows(fields_ref, (area_ref, depth_ref, spin_ref, tide_ref))
-    stored_ref[...] = stored
     both = picked(stored, one_hot)
 
     lane = lax.broadcasted_iota(i32, (1, LANES), 1)
@@ -377,27 +364,45 @@
         parts[5] = parts[5] * sign
         return parts
 
-    strip, ring = in_frame(both[:, :LANES]), in_frame(both[:, LANES : 2 * LANES])
+    strip, ring = in_frame(both[:, :LANES]), in_frame(both[:, LANES:])
+    for copy in copies[7:]:
+        copy.wait()
+    edges = edge_values(table_ref, weight_ref, *ring[:6])
+    east = jnp.where(second, east1, east0) != 0
+    ends = [jnp.where(east, part[NODES - NP :], part[:NP]) for part in edges]
+    out0_ref[...], out1_ref[...] = packed(strip_rows(strip, east, 0, ends))
+    stored_ref[...] = stored
+
+
+def rows_kernel(
+    block_cols, seam_ref, stored_ref, strip1_ref, strip0_ref, slot_ref, table_ref, weight_ref,
+    next_ref, far0_ref, far1_ref, pair_ref, sums,
+):
+    east0, flip0, east1, flip1 = seam_flags(seam_ref, block_cols)
+    odd = lax.axis_index("blk") & 1
+
+    def goes_up(lane):
+        return jnp.where((lane & 64) != 0, odd, 1 - odd) != 0
+
+    lane = lax.broadcasted_iota(i32, (8, 2 * LANES), 1)
+    up = goes_up(lane)
+    row = jnp.where(up, GY - RING, 0) + ((lane & 63) >> 4)
+    row = jnp.where(lane >= LANES, jnp.where(up, GY - RING - 1, RING), row)
+    both = picked(stored_ref[...], by_slot(slot_ref, (lane & 15) * GY + row))
     rows, behind = (
         [part[k * NODES : (k + 1) * NODES] for k in range(ARRAYS)]
-        for part in (both[:, 2 * LANES : 3 * LANES], both[:, 3 * LANES :])
-    )
-    edges = edge_values(
-        table_ref,
-        weight_ref,
-        *(jnp.concatenate(parts, 1) for parts in zip(strip[:6], ring[:6], behind[:6])),
-    )
-    east = jnp.where(second, east1, east0) != 0
-    ends = [part[:, LANES : 2 * LANES] for part in edges]
-    ends = [jnp.where(east, part[NODES - NP :], part[:NP]) for part in ends]
-    whole = strip_rows(strip, east, 0, ends)
-    out0_ref[...], out1_ref[...] = packed(whole)
+        for part in (both[:, :LANES], both[:, LANES:])
+    )
+    whole = unpacked(strip0_ref[...], strip1_ref[...])
+    strip = [whole[k * NODES : (k + 1) * NODES] for k in range(6)]
+    edges = edge_values(table_ref, weight_ref, *map(beside, strip, behind[:6]))
     sums[0] = jnp.concatenate([part[:, :LANES] for part in edges], 0)
+    lane = lax.broadcasted_iota(i32, (1, LANES), 1)
     top0, top1 = odd ^ flip0, odd ^ flip1
-    whole = with_row_rim(whole, sums, jnp.where(second, top1, top0) != 0)
+    whole = with_row_rim(whole, sums, jnp.where(lane >= 64, top1, top0) != 0)
     far0_ref[...] = corner_of(whole, 0, top0)
     far1_ref[...] = corner_of(whole, 64, top1)
-    sums[0] = jnp.concatenate([part[:, 2 * LANES :] for part in edges], 0)
+    sums[0] = jnp.concatenate([part[:, LANES:] for part in edges], 0)
     up = goes_up(lane)
     rim = jnp.where(up, *row_edges(sums))
     rim = [rim[k * NP : (k + 1) * NP] for k in range(4)]
@@ -422,8 +427,9 @@
     hot_ref[...] = one_hot.astype(f32).T.astype(bf16)
 
 
-def middle_kernel(block_cols, seam_ref, in0_ref, in1_ref, own_ref, lanes_ref, *refs):
-    low_ref, centre_ref, high_ref = refs[-3:]
+def middle_kernel(
+    block_cols, seam_ref, in0_ref, in1_ref, own_ref, lanes_ref, low_ref, centre_ref, high_ref
+):
     east0, flip0, east1, flip1 = seam_flags(seam_ref, block_cols)
     second = lax.broadcasted_iota(i32, (1, LANES), 1) >= 64
     late = jnp.where(second, east1, east0) == 0
@@ -438,8 +444,14 @@
         ref[ROWS:] = placed[ROWS:, part]
 
 
+def far_kernel(far1_ref, far0_ref, *refs):
+    out_ref = refs[-1]
+    out_ref[:CORNER_ROWS] = far0_ref[...]
+    out_ref[CORNER_ROWS:] = far1_ref[...]
+
+
 def steps_kernel(
-    block_cols, seam_ref, pair_ref, next_ref, far0_ref, far1_ref, low_ref, centre_ref,
+    block_cols, seam_ref, pair_ref, next_ref, far_ref, low_ref, centre_ref,
     high_ref, hot_ref, table_ref, weight_ref, ext_ref, outer_ref, out_ref, sums,
 ):
     east0, flip0, east1, flip1 = seam_flags(seam_ref, block_cols)
@@ -454,7 +466,8 @@
         [strips[:ROWS], jnp.zeros((EDGE_ROWS, LANES), f32), strips[ROWS:]], 0
     )
     near = pair[HALF_ROWS:]
-    sources = (near[:CORNER_ROWS], near[CORNER_ROWS:], far0_ref[...], far1_ref[...])
+    far = far_ref[...]
+    sources = (near[:CORNER_ROWS], near[CORNER_ROWS:], far[:CORNER_ROWS], far[CORNER_ROWS:])
     corners = []
     for k in range(8):
         rows = None
@@ -677,13 +690,22 @@
     needed = (seam_rows, slot_of, *held, table, weight)
     corner = ((CORNER_ROWS, LANES), f32)
     scratch = [pltpu.VMEM((1, 4 * NODES, LANES), f32)]
-    strip1, far1, strip0, far0, to_next, to_pair, stored = call(
+    strip1, strip0, stored = call(
         functools.partial(strips_kernel, block_cols),
         [(hbm, x) for x in needed],
-        [strip, corner, strip, corner, strip, strip, ((ROWS, ELEMENTS), f32)],
+        [strip, strip, ((ROWS, ELEMENTS), f32)],
         10**8,
-        scratch=room(needed, [pltpu.SMEM] + [pltpu.VMEM] * (len(needed) - 1)) + scratch,
+        scratch=room(needed, [pltpu.SMEM] + [pltpu.VMEM] * (len(needed) - 1)),
         name="strips",
+    )
+    to_next, far0, far1, to_pair = call(
+        functools.partial(rows_kernel, block_cols),
+        [(smem, seam_rows)]
+        + [(vmem, x) for x in (stored, strip1, strip0, slot_of, table, weight)],
+        [strip, corner, corner, strip],
+        10**8,
+        scratch=scratch,
+        name="rows",
     )
     span = block_cols * BY
     both = ("face", "blk")
@@ -771,10 +793,17 @@
     tile = ((ALL_ROWS, LANES), f32)
     low, centre, high = call(
         functools.partial(middle_kernel, block_cols),
-        [(smem, seam_rows)] + [(vmem, x) for x in (halo0, halo1, own, lanes, far1, far0, from_next)],
+        [(smem, seam_rows)] + [(vmem, x) for x in (halo0, halo1, own, lanes)],
         [tile, tile, tile],
+        10**8,
+        name="middle",
+    )
+    (far,) = call(
+        far_kernel,
+        [(vmem, x) for x in (far1, far0, from_next, low)],
+        [((2 * CORNER_ROWS, LANES), f32)],
         10**11,
-        name="middle",
+        name="far",
     )
     (stepped,) = call(
         functools.partial(steps_kernel, block_cols),
@@ -782,7 +811,7 @@
         + [
             (vmem, x)
             for x in (
-                from_pair, from_next, far0, far1, low, centre, high,
+                from_pair, from_next, far, low, centre, high,
                 hot, table, weight, ext, outer,
             )
         ],

time: 23.3 us -> 22.8 us (0.979)
  waiting for transfers between devices: 3.73 us -> 1.49 us
  Pallas kernels: 8.74 us -> 9.59 us
  local copies, waits for them, and re-layouts: 0.03 us -> 0.87 us
    ppermute x4, waiting for transfers between devices: 3.73 us -> 1.48 us  [eastward(): lax.ppermute(value, both, [(rank(*a), rank(*b)) for a, b in pairs.items()])]
    pallas_call x5 -> x7, Pallas kernels: 8.74 us -> 9.59 us  [call(): pl.pallas_call(kernel, out_shape=[jax.ShapeDtypeStruct(*out) for out in o...]
    unnamed x14, local copies, waits for them, and re-layouts: 0.03 us -> 0.87 us
  transfers between devices with their start and end apart: 6 -> 6, of which waited for: 3 -> 3; matrix products, arithmetic and copies ran while one was open for 0% -> 0% of each run, Pallas kernels for 9% -> 16%
where the time goes in v13:
time: 22.8 us; the launch traced here: 22.6 us
  starting transfers between devices  10.5 us (46%)
  Pallas kernels  9.59 us (42%)
  waiting for transfers between devices  1.49 us (7%)
  local copies, waits for them, and re-layouts  0.87 us (4%)
    pallas_call x7, Pallas kernels, call(): pl.pallas_call(kernel, out_shape=[jax.ShapeDtypeStruct(*out) for out in o...  9.59 us
    ppermute x4, starting transfers between devices, eastward(): lax.ppermute(value, both, [(rank(*a), rank(*b)) for a, b in pairs.items()])  9 us
    ppermute x2, starting transfers between devices, swapped(): return lax.ppermute(value, both, pairs)  1.55 us
    ppermute x4, waiting for transfers between devices, eastward(): lax.ppermute(value, both, [(rank(*a), rank(*b)) for a, b in pairs.items()])  1.48 us
    unnamed x14, local copies, waits for them, and re-layouts  0.87 us
  transfers between devices with their start and end apart: 6, of which 3 were waited for; matrix products, arithmetic and copies ran while one was open for 0% of the time, Pallas kernels for 16%

profile of v13, /device:TPU:0, one launch (start us, length us, event | category | flops | bytes accessed | tf_op | source)
XLA Modules:
  0.0 22.6 jit_solution(7433799701228027101)
XLA Ops:
  0.0 1.8 %strips.1 = (f32[216,128]{1,0:T(8,128)S(1)}, f32[216,128]{1,0:T(8,128)S(1)}, f32[448,256]{1,0:T(8,128)S(1)}) custom-call(s32[2,256]{1,0:T(2,128)} %seam_ref.5, s32[1,256]{1,0:T(1,128)} %slot_ref.3, f32[3,8,8,256]{3,2,1,0:T(8,128)} %refs_2_.1, f32[8,8,256]{2,1,0:T(8,128)} %refs_3_.1, f32[8,8,256]{2,1,0:T(8,128)} %refs_4_.1, f32[8,8,256]{2,1,0:T(8,128)} %refs_5_.1, ...), custom_call_target="tpu_custom_call" | custom-call | flops 100000000 | bytes 2097152 | tf_op jit(solution)/shard_map/strips/pallas_call | solution.py:666
  1.8 0.0 copy-start.3
  1.8 6.4 %collective-permute-start = (f32[216,128]{1,0:T(8,128)S(1)}, f32[216,128]{1,0:T(8,128)S(1)}, u32[]{:S(2)}, u32[]{:S(2)}) collective-permute-start(f32[216,128]{1,0:T(8,128)S(1)} %get-tuple-element.17.strip1_ref), channel_id=1, source_target_pairs={{0,31},{1,30},{2,29},{3,28},{4,27},{5,26},{6,25},{7,24},{8,23},{9,... | collective-permute-start | bytes 331784 | tf_op jit(solution)/shard_map/ppermute | solution.py:751
  8.3 0.5 %collective-permute-start.1 = (f32[216,128]{1,0:T(8,128)S(1)}, f32[216,128]{1,0:T(8,128)S(1)}, u32[]{:S(2)}, u32[]{:S(2)}) collective-permute-start(f32[216,128]{1,0:T(8,128)S(1)} %get-tuple-element.18.strip0_ref), channel_id=1, source_target_pairs={{0,16},{1,17},{2,18},{3,19},{4,20},{5,21},{6,22},{7,23},{8,24},{9,... | collective-permute-start | bytes 331784 | tf_op jit(solution)/shard_map/ppermute | solution.py:751
  8.8 0.0 copy-done
  8.8 0.0 copy-done.1
  8.8 0.1 copy-done.6
  9.0 1.4 %rows.1 = (f32[216,128]{1,0:T(8,128)S(1)}, f32[56,128]{1,0:T(8,128)S(1)}, f32[56,128]{1,0:T(8,128)S(1)}, f32[216,128]{1,0:T(8,128)S(1)}) custom-call(s32[2,256]{1,0:T(2,128)S(1)} %copy-done.3, f32[448,256]{1,0:T(8,128)S(1)} %get-tuple-element.19.stored_ref, f32[216,128]{1,0:T(8,128)S(1)} %get-tuple-element.17.strip1_ref, ...), custom_call_target="tpu_custom_call" | custom-call | flops 100000000 | bytes 2097152 | tf_op jit(solution)/shard_map/rows/pallas_call | solution.py:666
  10.4 1.4 %collective-permute-start.3 = (f32[216,128]{1,0:T(8,128)S(1)}, f32[216,128]{1,0:T(8,128)S(1)}, u32[]{:S(2)}, u32[]{:S(2)}) collective-permute-start(f32[216,128]{1,0:T(8,128)S(1)} %get-tuple-element.22), channel_id=1, source_target_pairs={{0,16},{1,2},{2,1},{3,4},{4,3},{5,6},{6,5},{7,8},{8,7},{9,10},{10,... | collective-permute-start | bytes 331784 | tf_op jit(solution)/shard_map/ppermute | solution.py:732
  11.8 0.6 %collective-permute-start.4 = (f32[56,128]{1,0:T(8,128)S(1)}, f32[56,128]{1,0:T(8,128)S(1)}, u32[]{:S(2)}, u32[]{:S(2)}) collective-permute-start(f32[56,128]{1,0:T(8,128)S(1)} %get-tuple-element.23), channel_id=1, source_target_pairs={{0,16},{1,29},{2,30},{3,27},{4,28},{5,25},{6,26},{7,23},{8,24},{9,... | collective-permute-start | bytes 86024 | tf_op jit(solution)/shard_map/ppermute | solution.py:751
  12.5 1.4 %collective-permute-start.5 = (f32[56,128]{1,0:T(8,128)S(1)}, f32[56,128]{1,0:T(8,128)S(1)}, u32[]{:S(2)}, u32[]{:S(2)}) collective-permute-start(f32[56,128]{1,0:T(8,128)S(1)} %get-tuple-element.24), channel_id=1, source_target_pairs={{0,16},{1,18},{2,17},{3,20},{4,19},{5,22},{6,21},{7,24},{8,23},{9,... | collective-permute-start | bytes 86024 | tf_op jit(solution)/shard_map/ppermute | solution.py:751
  13.8 0.6 %own.1 = (f32[448,384]{1,0:T(8,128)S(1)}, bf16[384,256]{1,0:T(8,128)(2,1)S(1)}) custom-call(f32[448,256]{1,0:T(8,128)S(1)} %get-tuple-element.19.stored_ref, s32[1,256]{1,0:T(1,128)S(1)} %copy-done.6, s32[24,384]{1,0:T(8,128)S(1)} %copy-done.2), custom_call_target="tpu_custom_call" | custom-call | flops 100000000 | bytes 2097152 | tf_op jit(solution)/shard_map/own/pallas_call | solution.py:666
  14.4 0.0 collective-permute-done.in1_ref
  14.4 0.4 %collective-permute-done.1.in0_ref = f32[216,128]{1,0:T(8,128)S(1)} collective-permute-done((f32[216,128]{1,0:T(8,128)S(1)}, f32[216,128]{1,0:T(8,128)S(1)}, u32[]{:S(2)}, u32[]{:S(2)}) %collective-permute-start.1) | collective-permute-done | bytes 110624 | tf_op jit(solution)/shard_map/ppermute | solution.py:751
  14.8 0.5 %corners.1 = f32[328,128]{1,0:T(8,128)S(1)} custom-call(f32[216,128]{1,0:T(8,128)S(1)} %collective-permute-done.in1_ref, f32[216,128]{1,0:T(8,128)S(1)} %collective-permute-done.1.in0_ref, f32[216,128]{1,0:T(8,128)S(1)} %get-tuple-element.20.pair_ref, f32[320,256]{1,0:T(8,128)S(1)} %copy-done, f32[64,128]{1,0:T(8,128)S(1)} %copy-done.1, ...), custom_call_target="tpu_custom_call" | custom-call | flops 100000000 | bytes 2097152 | tf_op jit(solution)/shard_map/corners/pallas_call | solution.py:666
  15.3 0.1 collective-permute-start.2
  15.5 1.0 %middle.1 = (f32[480,128]{1,0:T(8,128)S(1)}, f32[480,128]{1,0:T(8,128)S(1)}, f32[480,128]{1,0:T(8,128)S(1)}) custom-call(s32[2,256]{1,0:T(2,128)S(1)} %copy-done.3, f32[216,128]{1,0:T(8,128)S(1)} %collective-permute-done.1.in0_ref, f32[216,128]{1,0:T(8,128)S(1)} %collective-permute-done.in1_ref, f32[448,384]{1,0:T(8,128)S(1)} %get-tuple-element.25.own_ref, ...), custom_call_target="tpu_custom_call" | custom-call | flops 100000000 | bytes 2097152 | tf_op jit(solution)/shard_map/middle/pallas_call | solution.py:666
  16.5 0.8 %collective-permute-done.4.far1_ref = f32[56,128]{1,0:T(8,128)S(1)} collective-permute-done((f32[56,128]{1,0:T(8,128)S(1)}, f32[56,128]{1,0:T(8,128)S(1)}, u32[]{:S(2)}, u32[]{:S(2)}) %collective-permute-start.4) | collective-permute-done | bytes 28704 | tf_op jit(solution)/shard_map/ppermute | solution.py:751
  17.2 0.3 %collective-permute-done.5.far0_ref = f32[56,128]{1,0:T(8,128)S(1)} collective-permute-done((f32[56,128]{1,0:T(8,128)S(1)}, f32[56,128]{1,0:T(8,128)S(1)}, u32[]{:S(2)}, u32[]{:S(2)}) %collective-permute-start.5) | collective-permute-done | bytes 28704 | tf_op jit(solution)/shard_map/ppermute | solution.py:751
  17.6 0.0 collective-permute-done.3.refs_0_.next_ref
  17.6 0.0 collective-permute-done.2.pair_ref
  17.6 0.7 %copy-done.4 = s32[24,256]{1,0:T(8,128)S(1)} copy-done((s32[24,256]{1,0:T(8,128)S(1)}, s32[24,256]{1,0:T(8,128)}, u32[]{:S(2)}) %copy-start.4) | copy-done | bytes 24600
  18.3 0.0 copy-done.5
  18.3 4.3 %steps.1 = f32[3,8,8,256]{3,2,1,0:T(8,128)} custom-call(s32[2,256]{1,0:T(2,128)S(1)} %copy-done.3, f32[328,128]{1,0:T(8,128)S(1)} %collective-permute-done.2.pair_ref, f32[216,128]{1,0:T(8,128)S(1)} %collective-permute-done.3.refs_0_.next_ref, f32[112,128]{1,0:T(8,128)S(1)} %far.1.far_ref, f32[480,128]{1,0:T(8,128)S(1)} %get-tuple-element.26.refs_1_.low_ref, ...), custom_call_target="tpu_custom_call" | custom-call | flops 100000000 | bytes 2097152 | tf_op jit(solution)/shard_map/steps/pallas_call | solution.py:666
  (9 shorter events, 0.0 us)
Async XLA Ops:
  0.0 8.8 %copy-start = (f32[320,256]{1,0:T(8,128)S(1)}, f32[320,256]{1,0:T(8,128)}, u32[]{:S(2)}) copy-start(f32[320,256]{1,0:T(8,128)} %constant.10.clone.refs_7_.table_ref) | copy-start | bytes 983044
  0.0 8.8 %copy-start.1 = (f32[64,128]{1,0:T(8,128)S(1)}, f32[64,128]{1,0:T(8,128)}, u32[]{:S(2)}) copy-start(f32[64,128]{1,0:T(8,128)} %constant.11.clone.refs_8_.weight_ref) | copy-start | bytes 98308
  1.8 7.0 %copy-start.3 = (s32[2,256]{1,0:T(2,128)S(1)}, s32[2,256]{1,0:T(2,128)}, u32[]{:S(2)}) copy-start(s32[2,256]{1,0:T(2,128)} %seam_ref.5) | copy-start | bytes 6148
  1.8 12.6 %collective-permute-start = (f32[216,128]{1,0:T(8,128)S(1)}, f32[216,128]{1,0:T(8,128)S(1)}, u32[]{:S(2)}, u32[]{:S(2)}) collective-permute-start(f32[216,128]{1,0:T(8,128)S(1)} %get-tuple-element.17.strip1_ref), channel_id=1, source_target_pairs={{0,31},{1,30},{2,29},{3,28},{4,27},{5,26},{6,25},{7,24},{8,23},{9,... | collective-permute-start | bytes 331784 | tf_op jit(solution)/shard_map/ppermute | solution.py:751
  8.3 0.7 %copy-start.6 = (s32[1,256]{1,0:T(1,128)S(1)}, s32[1,256]{1,0:T(1,128)}, u32[]{:S(2)}) copy-start(s32[1,256]{1,0:T(1,128)} %slot_ref.3) | copy-start | bytes 3076
  8.3 6.6 %collective-permute-start.1 = (f32[216,128]{1,0:T(8,128)S(1)}, f32[216,128]{1,0:T(8,128)S(1)}, u32[]{:S(2)}, u32[]{:S(2)}) collective-permute-start(f32[216,128]{1,0:T(8,128)S(1)} %get-tuple-element.18.strip0_ref), channel_id=1, source_target_pairs={{0,16},{1,17},{2,18},{3,19},{4,20},{5,21},{6,22},{7,23},{8,24},{9,... | collective-permute-start | bytes 331784 | tf_op jit(solution)/shard_map/ppermute | solution.py:751
  9.0 4.9 %copy-start.2 = (s32[24,384]{1,0:T(8,128)S(1)}, s32[24,384]{1,0:T(8,128)}, u32[]{:S(2)}) copy-start(s32[24,384]{1,0:T(8,128)} %constant.12.clone.lanes_ref) | copy-start | bytes 110596
  10.4 7.2 %collective-permute-start.3 = (f32[216,128]{1,0:T(8,128)S(1)}, f32[216,128]{1,0:T(8,128)S(1)}, u32[]{:S(2)}, u32[]{:S(2)}) collective-permute-start(f32[216,128]{1,0:T(8,128)S(1)} %get-tuple-element.22), channel_id=1, source_target_pairs={{0,16},{1,2},{2,1},{3,4},{4,3},{5,6},{6,5},{7,8},{8,7},{9,10},{10,... | collective-permute-start | bytes 331784 | tf_op jit(solution)/shard_map/ppermute | solution.py:732
  11.8 5.4 %collective-permute-start.4 = (f32[56,128]{1,0:T(8,128)S(1)}, f32[56,128]{1,0:T(8,128)S(1)}, u32[]{:S(2)}, u32[]{:S(2)}) collective-permute-start(f32[56,128]{1,0:T(8,128)S(1)} %get-tuple-element.23), channel_id=1, source_target_pairs={{0,16},{1,29},{2,30},{3,27},{4,28},{5,25},{6,26},{7,23},{8,24},{9,... | collective-permute-start | bytes 86024 | tf_op jit(solution)/shard_map/ppermute | solution.py:751
  12.5 5.1 %collective-permute-start.5 = (f32[56,128]{1,0:T(8,128)S(1)}, f32[56,128]{1,0:T(8,128)S(1)}, u32[]{:S(2)}, u32[]{:S(2)}) collective-permute-start(f32[56,128]{1,0:T(8,128)S(1)} %get-tuple-element.24), channel_id=1, source_target_pairs={{0,16},{1,18},{2,17},{3,20},{4,19},{5,22},{6,21},{7,24},{8,23},{9,... | collective-permute-start | bytes 86024 | tf_op jit(solution)/shard_map/ppermute | solution.py:751
  15.3 2.2 %collective-permute-start.2 = (f32[328,128]{1,0:T(8,128)S(1)}, f32[328,128]{1,0:T(8,128)S(1)}, u32[]{:S(2)}, u32[]{:S(2)}) collective-permute-start(f32[328,128]{1,0:T(8,128)S(1)} %corners.1), channel_id=1, source_target_pairs={{0,1},{1,0},{2,3},{3,2},{4,5},{5,4},{6,7},{7,6},{8,9},{9,8},{10,11... | collective-permute-start | bytes 503816 | tf_op jit(solution)/shard_map/ppermute | solution.py:732
  17.6 0.7 %copy-start.4 = (s32[24,256]{1,0:T(8,128)S(1)}, s32[24,256]{1,0:T(8,128)}, u32[]{:S(2)}) copy-start(s32[24,256]{1,0:T(8,128)} %constant.14.clone.outer_ref) | copy-start | bytes 73732
  17.6 0.7 %copy-start.5 = (s32[8,640]{1,0:T(8,128)S(1)}, s32[8,640]{1,0:T(8,128)}, u32[]{:S(2)}) copy-start(s32[8,640]{1,0:T(8,128)} %constant.13.clone.ext_ref) | copy-start | bytes 61444

commit v14 on v13

--- a/solution.py
+++ b/solution.py
@@ -149,7 +149,11 @@
                 outer[0:8, place] = LANES + step * RING + (x + RING if x < 0 else x - GX)
                 outer[8:16, place] = 2 if x < 0 else 3
             outer[16:24, place] = y > 0
-    return table, ext, outer
+    whole = np.zeros((56, EXT), np.int32)
+    whole[0:24, :MID] = table
+    whole[24:32] = ext
+    whole[32:56, : 2 * LANES] = outer
+    return whole
 
 
 def dot(a, b):
@@ -422,26 +426,49 @@
 
 
 def own_kernel(stored_ref, slot_ref, lanes_ref, own_ref, hot_ref):
-    one_hot = by_slot(slot_ref, lanes_ref[0:8])
+    one_hot = by_slot(slot_ref, lanes_ref[0:8, :MID])
     own_ref[...] = picked(stored_ref[...], one_hot)
     hot_ref[...] = one_hot.astype(f32).T.astype(bf16)
 
 
+def first_sums(table, weight, parts, rims, at_rim):
+    p, u, v, area, depth, spin, tide = parts
+    size = area.shape[1]
+    root = jnp.sqrt(area)
+    mass = jnp.concatenate([weight] * (size // LANES), 1) * area
+    used = [p, u, v, root * depth, root, mass * spin, tide]
+    for part, rim in zip(mass_tendency(table, p, u, v, *used[3:6]) + [mass], rims):
+        west, east = part[:NP], part[NODES - NP :]
+        at_east = jnp.where(at_rim, rim, pltpu.roll(west, size - 1, 1))
+        at_west = jnp.where(at_rim, rim, pltpu.roll(east, 1, 1))
+        used.append(
+            jnp.concatenate([west + at_west, part[NP : NODES - NP], east + at_east], 0)
+        )
+    return used
+
+
 def middle_kernel(
-    block_cols, seam_ref, in0_ref, in1_ref, own_ref, lanes_ref, low_ref, centre_ref, high_ref
+    block_cols, seam_ref, in0_ref, in1_ref, own_ref, lanes_ref, table_ref, weight_ref,
+    low_ref, centre_ref, high_ref,
 ):
     east0, flip0, east1, flip1 = seam_flags(seam_ref, block_cols)
     second = lax.broadcasted_iota(i32, (1, LANES), 1) >= 64
     late = jnp.where(second, east1, east0) == 0
     whole = placed_rows(unpacked(in0_ref[...], in1_ref[...]), late, 0)
-    side = lanes_ref[16:24]
+    side = lanes_ref[16:24, :MID]
     first_at = jnp.where(side == 2, 64 * (1 - east0), 64 * east0)
-    place = jnp.where(side == 0, -1, lanes_ref[8:16] + first_at)
+    place = jnp.where(side == 0, -1, lanes_ref[8:16, :MID] + first_at)
     placed = picked(whole, as_one_hot(place, LANES))
+    parts = [
+        placed[k * NODES : (k + 1) * NODES] + own_ref[k * NODES : (k + 1) * NODES]
+        for k in range(ARRAYS)
+    ]
+    rims = [placed[ROWS + c * NP : ROWS + (c + 1) * NP] for c in range(4)]
+    at_rim = lanes_ref[24:25, LANES : LANES + MID] != 0
+    used = first_sums(table_ref[...].astype(bf16), weight_ref[...], parts, rims, at_rim)
     for k, ref in enumerate((low_ref, centre_ref, high_ref)):
-        part = slice(k * LANES, (k + 1) * LANES)
-        ref[:ROWS] = placed[:ROWS, part] + own_ref[:, part]
-        ref[ROWS:] = placed[ROWS:, part]
+        for n, part in enumerate(used):
+            ref[n * NODES : (n + 1) * NODES] = part[:, k * LANES : (k + 1) * LANES]
 
 
 def far_kernel(far1_ref, far0_ref, *refs):
@@ -452,7 +479,7 @@
 
 def steps_kernel(
     block_cols, seam_ref, pair_ref, next_ref, far_ref, low_ref, centre_ref,
-    high_ref, hot_ref, table_ref, weight_ref, ext_ref, outer_ref, out_ref, sums,
+    high_ref, hot_ref, table_ref, weight_ref, lanes_ref, out_ref, sums, leaving, sems,
 ):
     east0, flip0, east1, flip1 = seam_flags(seam_ref, block_cols)
     odd = lax.axis_index("blk") & 1
@@ -484,21 +511,27 @@
         [placed_rows(corners, late, 0)] + spread_out(corners[rim : rim + NP], below, 2), 0
     )
     around = jnp.concatenate([strips, corners], 1)
-    kind = outer_ref[8:16]
-    sender = jnp.where(outer_ref[16:24] != 0, odd, 1 - odd)
+    kind = lanes_ref[40:48, : 2 * LANES]
+    sender = jnp.where(lanes_ref[48:56, : 2 * LANES] != 0, odd, 1 - odd)
     strip_at = jnp.where(kind == 3, 16 * (1 - east0), 16 * east0)
-    place = outer_ref[0:8] + jnp.where(kind == 1, 64 * sender, 32 * sender + strip_at)
+    place = lanes_ref[32:40, : 2 * LANES]
+    place = place + jnp.where(kind == 1, 64 * sender, 32 * sender + strip_at)
     outer = picked(around, as_one_hot(jnp.where(kind == 0, -1, place), 2 * LANES))
-    tiles = (outer[:, :LANES], low_ref, centre_ref, high_ref, outer[:, LANES:])
+    table = table_ref[...].astype(bf16)
+    tiles = (None, low_ref, centre_ref, high_ref, None)
     count = len(tiles)
-    table = table_ref[...].astype(bf16)
-    weight = weight_ref[...]
-    masks = [ext_ref[:, k * LANES : (k + 1) * LANES] for k in range(count)]
-    at_rim = [mask[0:1] != 0 for mask in masks]
+    masks = [lanes_ref[24:32, k * LANES : (k + 1) * LANES] for k in range(count)]
     closed_above = jnp.where(block_y == BY - 1, masks[-2][1:2], 0) != 0
     closed_below = jnp.where(block_y == 0, masks[1][2:3], 0) != 0
     first_row = masks[0][4:5] != 0
     last_row = masks[-1][5:6] != 0
+    outer_used = first_sums(
+        table,
+        weight_ref[...],
+        [outer[k * NODES : (k + 1) * NODES] for k in range(ARRAYS)],
+        [outer[ROWS + c * NP : ROWS + (c + 1) * NP] for c in range(4)],
+        beside(masks[0][0:1], masks[-1][0:1]) != 0,
+    )
 
     def shifted(parts, by, ring):
         turned = [pltpu.roll(part, -by % LANES, 1) for part in parts]
@@ -508,7 +541,7 @@
         from_other = lane >= LANES - by if by > 0 else lane < -by
         return [jnp.where(from_other, turned[others[k]], turned[k]) for k in range(size)]
 
-    def edge_sum(components, slots, rims=None, rows=None):
+    def edge_x(components, slots):
         ring = len(slots) < count
         for c in range(components):
             west_at = slice(c * NODES, c * NODES + NP)
@@ -517,11 +550,11 @@
             east = [sums[k, east_at] for k in slots]
             at_east, at_west = shifted(west, 1, ring), shifted(east, -1, ring)
             for n, k in enumerate(slots):
-                if rims is not None:
-                    at_east[n] = jnp.where(at_rim[k], rims[k][c], at_east[n])
-                    at_west[n] = jnp.where(at_rim[k], rims[k][c], at_west[n])
                 sums[k, west_at] = west[n] + at_west[n]
                 sums[k, east_at] = east[n] + at_east[n]
+
+    def edge_y(components, slots, rows=None):
+        ring = len(slots) < count
         south_at = pl.ds(0, components * NP, stride=NP)
         north_at = pl.ds(NP - 1, components * NP, stride=NP)
         south = [sums[k, south_at] for k in slots]
@@ -539,10 +572,13 @@
             sums[k, south_at] = south[n] + at_south[n]
             sums[k, north_at] = north[n] + at_north[n]
 
+    def edge_sum(slots):
+        edge_x(3, slots)
+        edge_y(3, slots)
+
     node = lax.broadcasted_iota(i32, (1, NP, 1), 1)
     rows = []
-    for tile in (tiles[0], tiles[-1]):
-        rim = tile[ALL_ROWS:]
+    for rim in (outer[ALL_ROWS:, :LANES], outer[ALL_ROWS:, LANES:]):
         east = pltpu.roll(rim, LANES - 1, 1).reshape(4, NP, LANES)
         west = pltpu.roll(rim, 1, 1).reshape(4, NP, LANES)
         rim = (
@@ -551,15 +587,17 @@
             + jnp.where(node == 0, pltpu.roll(west, 1, 1), 0.0)
         )
         rows.append(rim.reshape(EDGE_ROWS, LANES))
-    rims = [
-        [tile[ROWS + c * NP : ROWS + (c + 1) * NP] for c in range(4)] for tile in tiles
-    ]
 
     every = tuple(range(count))
     groups = (every[0:2], every[2:4], every[4:])
 
+    def tile_part(k, n):
+        if tiles[k] is None:
+            return outer_used[n][:, :LANES] if k == 0 else outer_used[n][:, LANES:]
+        return tiles[k][n * NODES : (n + 1) * NODES]
+
     def part_of(group, n):
-        return jnp.concatenate([tiles[k][n * NODES : (n + 1) * NODES] for k in group], 1)
+        return jnp.concatenate([tile_part(k, n) for k in group], 1)
 
     def put(group, parts):
         for c, part in enumerate(parts):
@@ -578,26 +616,18 @@
             for part in s
         ]
 
-    start, fixed = [], []
-    for group in groups:
-        area = part_of(group, 3)
-        root = jnp.sqrt(area)
-        mass = jnp.concatenate([weight] * len(group), 1) * area
-        start.append([part_of(group, c) for c in range(3)])
-        fixed.append((root * part_of(group, 4), root, mass * part_of(group, 5)))
-        put(group, [mass])
-    edge_sum(1, every, [rim[3:] for rim in rims], [rim[3 * NP :] for rim in rows])
-    per_mass = [1.0 / summed(group, 0) for group in groups]
-
-    for n, group in enumerate(groups):
-        put(group, mass_tendency(table, *start[n], *fixed[n]))
-    edge_sum(3, every, rims, [rim[: 3 * NP] for rim in rows])
+    start = [[part_of(group, n) for n in range(3)] for group in groups]
+    fixed = [[part_of(group, n) for n in range(3, 6)] for group in groups]
+    for k in every:
+        put((k,), [tile_part(k, n) for n in range(7, 11)])
+    edge_y(4, every, rows)
+    per_mass = [1.0 / summed(group, 3) for group in groups]
     one = []
     for n, group in enumerate(groups):
         change = average(group, per_mass[n])
         one.append([s + time_step * c for s, c in zip(start[n], change)])
         put(group, mass_tendency(table, *one[n], *fixed[n]))
-    edge_sum(3, every)
+    edge_sum(every)
     two = []
     for n, group in enumerate(groups):
         change = average(group, per_mass[n])
@@ -605,7 +635,7 @@
             [0.75 * s + 0.25 * (o + time_step * c) for s, o, c in zip(start[n], one[n], change)]
         )
         put(group, mass_tendency(table, *two[n], *fixed[n]))
-    edge_sum(3, every)
+    edge_sum(every)
 
     def regrouped(per_group):
         (outer_low, high_above) = per_group[0], per_group[1]
@@ -637,37 +667,41 @@
         now[0] = now[0] + tide[n]
         three.append(now)
         put(group, laplace(now))
-    edge_sum(3, slots)
+    edge_sum(slots)
     for n, group in enumerate(groups):
         put(group, laplace(average(group, per_mass[n])))
-    edge_sum(3, slots)
-    stepped = []
-    for n, group in enumerate(groups):
-        change = average(group, per_mass[n])
-        now = [s - time_step * hyper_coeff * b for s, b in zip(three[n], change)]
-        stepped.append(jnp.concatenate(now, 0))
-    stepped = jnp.concatenate(stepped, 1)[:, :MID]
-    own = ext_ref[3:4, LANES : LANES + MID] != 0
-    stored = picked(jnp.where(own, stepped, 0.0), hot_ref[...])
-    out_ref[...] = stored.reshape(out_ref.shape)
+    edge_sum(slots)
+    own = lanes_ref[27:28, LANES : LANES + MID] != 0
+    hot = hot_ref[...]
+    change = [average(group, per_mass[n]) for n, group in enumerate(groups)]
+    copies = []
+    for c in range(3):
+        now = [s[c] - time_step * hyper_coeff * b[c] for s, b in zip(three, change)]
+        stepped = jnp.concatenate(now, 1)[:, :MID]
+        stored = picked(jnp.where(own, stepped, 0.0), hot)
+        leaving[c] = stored.reshape(leaving.shape[1:])
+        copies.append(pltpu.make_async_copy(leaving.at[c], out_ref.at[c], sems.at[c]))
+        copies[c].start()
+    for copy in copies:
+        copy.wait()
 
 
 def on_device(fields, jacobian, water_depth, coriolis, tide_height, slot_of, seam_rows):
     block_cols = lax.axis_size("blk") // BY
     table, weight = operator_table()
-    table, weight, lanes, ext, outer = map(jnp.asarray, (table, weight, *lane_tables()))
+    table, weight, lanes = map(jnp.asarray, (table, weight, lane_tables()))
     vmem = pl.BlockSpec(memory_space=pltpu.VMEM)
     smem = pl.BlockSpec(memory_space=pltpu.SMEM)
     hbm = pl.BlockSpec(memory_space=pltpu.HBM)
     params = pltpu.CompilerParams(vmem_limit_bytes=48 * 2**20)
     held = (fields, jacobian, water_depth, coriolis, tide_height)
 
-    def call(kernel, ins, outs, cost, scratch=(), name=None):
+    def call(kernel, ins, outs, cost, scratch=(), name=None, out_specs=None):
         return pl.pallas_call(
             kernel,
             out_shape=[jax.ShapeDtypeStruct(*out) for out in outs],
             in_specs=[spec for spec, value in ins],
-            out_specs=[vmem] * len(outs),
+            out_specs=out_specs or [vmem] * len(outs),
             scratch_shapes=list(scratch),
             compiler_params=params,
             cost_estimate=pl.CostEstimate(
@@ -790,10 +824,10 @@
         name="corners",
     )
     from_pair = swapped(to_pair, in_pair)
-    tile = ((ALL_ROWS, LANES), f32)
+    tile = ((11 * NODES, LANES), f32)
     low, centre, high = call(
         functools.partial(middle_kernel, block_cols),
-        [(smem, seam_rows)] + [(vmem, x) for x in (halo0, halo1, own, lanes)],
+        [(smem, seam_rows)] + [(vmem, x) for x in (halo0, halo1, own, lanes, table, weight)],
         [tile, tile, tile],
         10**8,
         name="middle",
@@ -812,12 +846,17 @@
             (vmem, x)
             for x in (
                 from_pair, from_next, far, low, centre, high,
-                hot, table, weight, ext, outer,
+                hot, table, weight, lanes,
             )
         ],
         [(fields.shape, f32)],
         10**8,
-        scratch=[pltpu.VMEM((EXT // LANES, 3 * NODES, LANES), f32)],
+        scratch=[
+            pltpu.VMEM((EXT // LANES, 4 * NODES, LANES), f32),
+            pltpu.VMEM(fields.shape, f32),
+            pltpu.SemaphoreType.DMA((3,)),
+        ],
+        out_specs=[hbm],
         name="steps",
     )
     return stepped

time: 22.8 us -> 22 us (0.965)
  local copies, waits for them, and re-layouts: 0.87 us -> 0.15 us
  Pallas kernels: 9.59 us -> 9.97 us
  waiting for transfers between devices: 1.49 us -> 1.14 us
    unnamed x14 -> x10, local copies, waits for them, and re-layouts: 0.87 us -> 0.15 us
    pallas_call x7, Pallas kernels: 9.59 us -> 9.97 us  [call(): pl.pallas_call(kernel, out_shape=[jax.ShapeDtypeStruct(*out) for out in o...]
    ppermute x4, waiting for transfers between devices: 1.48 us -> 1.13 us  [eastward(): lax.ppermute(value, both, [(rank(*a), rank(*b)) for a, b in pairs.items()])]
  transfers between devices with their start and end apart: 6 -> 6, of which waited for: 3 -> 3; matrix products, arithmetic and copies ran while one was open for 0% -> 0% of each run, Pallas kernels for 16% -> 18%
where the time goes in v14:
time: 22 us; the launch traced here: 21.9 us
  starting transfers between devices  10.5 us (48%)
  Pallas kernels  9.97 us (45%)
  waiting for transfers between devices  1.14 us (5%)
    pallas_call x7, Pallas kernels, call(): pl.pallas_call(kernel, out_shape=[jax.ShapeDtypeStruct(*out) for out in o...  9.97 us
    ppermute x4, starting transfers between devices, eastward(): lax.ppermute(value, both, [(rank(*a), rank(*b)) for a, b in pairs.items()])  9 us
    ppermute x2, starting transfers between devices, swapped(): return lax.ppermute(value, both, pairs)  1.55 us
    ppermute x4, waiting for transfers between devices, eastward(): lax.ppermute(value, both, [(rank(*a), rank(*b)) for a, b in pairs.items()])  1.13 us
  transfers between devices with their start and end apart: 6, of which 3 were waited for; matrix products, arithmetic and copies ran while one was open for 0% of the time, Pallas kernels for 18%

profile of v14, /device:TPU:0, one launch (start us, length us, event | category | flops | bytes accessed | tf_op | source)
XLA Modules:
  0.0 21.9 jit_solution(8125143096017697786)
XLA Ops:
  0.0 1.8 %strips.1 = (f32[216,128]{1,0:T(8,128)S(1)}, f32[216,128]{1,0:T(8,128)S(1)}, f32[448,256]{1,0:T(8,128)S(1)}) custom-call(s32[2,256]{1,0:T(2,128)} %seam_ref.5, s32[1,256]{1,0:T(1,128)} %slot_ref.3, f32[3,8,8,256]{3,2,1,0:T(8,128)} %refs_2_.1, f32[8,8,256]{2,1,0:T(8,128)} %refs_3_.1, f32[8,8,256]{2,1,0:T(8,128)} %refs_4_.1, f32[8,8,256]{2,1,0:T(8,128)} %refs_5_.1, ...), custom_call_target="tpu_custom_call" | custom-call | flops 100000000 | bytes 2097152 | tf_op jit(solution)/shard_map/strips/pallas_call | solution.py:700
  1.8 0.0 copy-start.3
  1.8 6.4 %collective-permute-start = (f32[216,128]{1,0:T(8,128)S(1)}, f32[216,128]{1,0:T(8,128)S(1)}, u32[]{:S(2)}, u32[]{:S(2)}) collective-permute-start(f32[216,128]{1,0:T(8,128)S(1)} %get-tuple-element.17.strip1_ref), channel_id=1, source_target_pairs={{0,31},{1,30},{2,29},{3,28},{4,27},{5,26},{6,25},{7,24},{8,23},{9,... | collective-permute-start | bytes 331784 | tf_op jit(solution)/shard_map/ppermute | solution.py:785
  8.3 0.5 %collective-permute-start.1 = (f32[216,128]{1,0:T(8,128)S(1)}, f32[216,128]{1,0:T(8,128)S(1)}, u32[]{:S(2)}, u32[]{:S(2)}) collective-permute-start(f32[216,128]{1,0:T(8,128)S(1)} %get-tuple-element.18.strip0_ref), channel_id=1, source_target_pairs={{0,16},{1,17},{2,18},{3,19},{4,20},{5,21},{6,22},{7,23},{8,24},{9,... | collective-permute-start | bytes 331784 | tf_op jit(solution)/shard_map/ppermute | solution.py:785
  8.8 0.0 copy-done
  8.8 0.0 copy-done.2
  8.8 0.0 copy-done.3
  8.8 0.1 copy-done.4
  9.0 1.4 %rows.1 = (f32[216,128]{1,0:T(8,128)S(1)}, f32[56,128]{1,0:T(8,128)S(1)}, f32[56,128]{1,0:T(8,128)S(1)}, f32[216,128]{1,0:T(8,128)S(1)}) custom-call(s32[2,256]{1,0:T(2,128)S(1)} %copy-done.3, f32[448,256]{1,0:T(8,128)S(1)} %get-tuple-element.19.stored_ref, f32[216,128]{1,0:T(8,128)S(1)} %get-tuple-element.17.strip1_ref, ...), custom_call_target="tpu_custom_call" | custom-call | flops 100000000 | bytes 2097152 | tf_op jit(solution)/shard_map/rows/pallas_call | solution.py:700
  10.4 1.4 %collective-permute-start.3 = (f32[216,128]{1,0:T(8,128)S(1)}, f32[216,128]{1,0:T(8,128)S(1)}, u32[]{:S(2)}, u32[]{:S(2)}) collective-permute-start(f32[216,128]{1,0:T(8,128)S(1)} %get-tuple-element.22), channel_id=1, source_target_pairs={{0,16},{1,2},{2,1},{3,4},{4,3},{5,6},{6,5},{7,8},{8,7},{9,10},{10,... | collective-permute-start | bytes 331784 | tf_op jit(solution)/shard_map/ppermute | solution.py:766
  11.8 0.6 %collective-permute-start.4 = (f32[56,128]{1,0:T(8,128)S(1)}, f32[56,128]{1,0:T(8,128)S(1)}, u32[]{:S(2)}, u32[]{:S(2)}) collective-permute-start(f32[56,128]{1,0:T(8,128)S(1)} %get-tuple-element.23), channel_id=1, source_target_pairs={{0,16},{1,29},{2,30},{3,27},{4,28},{5,25},{6,26},{7,23},{8,24},{9,... | collective-permute-start | bytes 86024 | tf_op jit(solution)/shard_map/ppermute | solution.py:785
  12.5 1.4 %collective-permute-start.5 = (f32[56,128]{1,0:T(8,128)S(1)}, f32[56,128]{1,0:T(8,128)S(1)}, u32[]{:S(2)}, u32[]{:S(2)}) collective-permute-start(f32[56,128]{1,0:T(8,128)S(1)} %get-tuple-element.24), channel_id=1, source_target_pairs={{0,16},{1,18},{2,17},{3,20},{4,19},{5,22},{6,21},{7,24},{8,23},{9,... | collective-permute-start | bytes 86024 | tf_op jit(solution)/shard_map/ppermute | solution.py:785
  13.8 0.0 copy-done.1
  13.8 0.6 %own.1 = (f32[448,384]{1,0:T(8,128)S(1)}, bf16[384,256]{1,0:T(8,128)(2,1)S(1)}) custom-call(f32[448,256]{1,0:T(8,128)S(1)} %get-tuple-element.19.stored_ref, s32[1,256]{1,0:T(1,128)S(1)} %copy-done.4, s32[56,640]{1,0:T(8,128)S(1)} %copy-done.1), custom_call_target="tpu_custom_call" | custom-call | flops 100000000 | bytes 2097152 | tf_op jit(solution)/shard_map/own/pallas_call | solution.py:700
  14.4 0.0 collective-permute-done.in1_ref
  14.4 0.4 %collective-permute-done.1.in0_ref = f32[216,128]{1,0:T(8,128)S(1)} collective-permute-done((f32[216,128]{1,0:T(8,128)S(1)}, f32[216,128]{1,0:T(8,128)S(1)}, u32[]{:S(2)}, u32[]{:S(2)}) %collective-permute-start.1) | collective-permute-done | bytes 110624 | tf_op jit(solution)/shard_map/ppermute | solution.py:785
  14.8 0.5 %corners.1 = f32[328,128]{1,0:T(8,128)S(1)} custom-call(f32[216,128]{1,0:T(8,128)S(1)} %collective-permute-done.in1_ref, f32[216,128]{1,0:T(8,128)S(1)} %collective-permute-done.1.in0_ref, f32[216,128]{1,0:T(8,128)S(1)} %get-tuple-element.20.pair_ref, f32[320,256]{1,0:T(8,128)S(1)} %copy-done, f32[64,128]{1,0:T(8,128)S(1)} %copy-done.2, ...), custom_call_target="tpu_custom_call" | custom-call | flops 100000000 | bytes 2097152 | tf_op jit(solution)/shard_map/corners/pallas_call | solution.py:700
  15.3 0.1 collective-permute-start.2
  15.5 1.4 %middle.1 = (f32[704,128]{1,0:T(8,128)S(1)}, f32[704,128]{1,0:T(8,128)S(1)}, f32[704,128]{1,0:T(8,128)S(1)}) custom-call(s32[2,256]{1,0:T(2,128)S(1)} %copy-done.3, f32[216,128]{1,0:T(8,128)S(1)} %collective-permute-done.1.in0_ref, f32[216,128]{1,0:T(8,128)S(1)} %collective-permute-done.in1_ref, f32[448,384]{1,0:T(8,128)S(1)} %get-tuple-element.25.own_ref, ...), custom_call_target="tpu_custom_call" | custom-call | flops 100000000 | bytes 2097152 | tf_op jit(solution)/shard_map/middle/pallas_call | solution.py:700
  16.8 0.4 %collective-permute-done.4.far1_ref = f32[56,128]{1,0:T(8,128)S(1)} collective-permute-done((f32[56,128]{1,0:T(8,128)S(1)}, f32[56,128]{1,0:T(8,128)S(1)}, u32[]{:S(2)}, u32[]{:S(2)}) %collective-permute-start.4) | collective-permute-done | bytes 28704 | tf_op jit(solution)/shard_map/ppermute | solution.py:785
  17.2 0.3 %collective-permute-done.5.far0_ref = f32[56,128]{1,0:T(8,128)S(1)} collective-permute-done((f32[56,128]{1,0:T(8,128)S(1)}, f32[56,128]{1,0:T(8,128)S(1)}, u32[]{:S(2)}, u32[]{:S(2)}) %collective-permute-start.5) | collective-permute-done | bytes 28704 | tf_op jit(solution)/shard_map/ppermute | solution.py:785
  17.6 0.0 collective-permute-done.3.refs_0_.next_ref
  17.6 0.0 collective-permute-done.2.pair_ref
  17.6 4.3 %steps.1 = f32[3,8,8,256]{3,2,1,0:T(8,128)} custom-call(s32[2,256]{1,0:T(2,128)S(1)} %copy-done.3, f32[328,128]{1,0:T(8,128)S(1)} %collective-permute-done.2.pair_ref, f32[216,128]{1,0:T(8,128)S(1)} %collective-permute-done.3.refs_0_.next_ref, f32[112,128]{1,0:T(8,128)S(1)} %far.1.far_ref, f32[704,128]{1,0:T(8,128)S(1)} %get-tuple-element.26.refs_1_.low_ref, ...), custom_call_target="tpu_custom_call" | custom-call | flops 100000000 | bytes 2097152 | tf_op jit(solution)/shard_map/steps/pallas_call | solution.py:700
  (5 shorter events, 0.0 us)
Async XLA Ops:
  0.0 8.8 %copy-start = (f32[320,256]{1,0:T(8,128)S(1)}, f32[320,256]{1,0:T(8,128)}, u32[]{:S(2)}) copy-start(f32[320,256]{1,0:T(8,128)} %constant.6.clone.refs_7_.table_ref) | copy-start | bytes 983044
  0.0 8.8 %copy-start.2 = (f32[64,128]{1,0:T(8,128)S(1)}, f32[64,128]{1,0:T(8,128)}, u32[]{:S(2)}) copy-start(f32[64,128]{1,0:T(8,128)} %constant.7.clone.refs_8_.weight_ref) | copy-start | bytes 98308
  1.8 7.0 %copy-start.3 = (s32[2,256]{1,0:T(2,128)S(1)}, s32[2,256]{1,0:T(2,128)}, u32[]{:S(2)}) copy-start(s32[2,256]{1,0:T(2,128)} %seam_ref.5) | copy-start | bytes 6148
  1.8 12.6 %collective-permute-start = (f32[216,128]{1,0:T(8,128)S(1)}, f32[216,128]{1,0:T(8,128)S(1)}, u32[]{:S(2)}, u32[]{:S(2)}) collective-permute-start(f32[216,128]{1,0:T(8,128)S(1)} %get-tuple-element.17.strip1_ref), channel_id=1, source_target_pairs={{0,31},{1,30},{2,29},{3,28},{4,27},{5,26},{6,25},{7,24},{8,23},{9,... | collective-permute-start | bytes 331784 | tf_op jit(solution)/shard_map/ppermute | solution.py:785
  8.3 0.7 %copy-start.4 = (s32[1,256]{1,0:T(1,128)S(1)}, s32[1,256]{1,0:T(1,128)}, u32[]{:S(2)}) copy-start(s32[1,256]{1,0:T(1,128)} %slot_ref.3) | copy-start | bytes 3076
  8.3 6.6 %collective-permute-start.1 = (f32[216,128]{1,0:T(8,128)S(1)}, f32[216,128]{1,0:T(8,128)S(1)}, u32[]{:S(2)}, u32[]{:S(2)}) collective-permute-start(f32[216,128]{1,0:T(8,128)S(1)} %get-tuple-element.18.strip0_ref), channel_id=1, source_target_pairs={{0,16},{1,17},{2,18},{3,19},{4,20},{5,21},{6,22},{7,23},{8,24},{9,... | collective-permute-start | bytes 331784 | tf_op jit(solution)/shard_map/ppermute | solution.py:785
  9.0 4.9 %copy-start.1 = (s32[56,640]{1,0:T(8,128)S(1)}, s32[56,640]{1,0:T(8,128)}, u32[]{:S(2)}) copy-start(s32[56,640]{1,0:T(8,128)} %constant.8.clone.lanes_ref) | copy-start | bytes 430084
  10.4 7.2 %collective-permute-start.3 = (f32[216,128]{1,0:T(8,128)S(1)}, f32[216,128]{1,0:T(8,128)S(1)}, u32[]{:S(2)}, u32[]{:S(2)}) collective-permute-start(f32[216,128]{1,0:T(8,128)S(1)} %get-tuple-element.22), channel_id=1, source_target_pairs={{0,16},{1,2},{2,1},{3,4},{4,3},{5,6},{6,5},{7,8},{8,7},{9,10},{10,... | collective-permute-start | bytes 331784 | tf_op jit(solution)/shard_map/ppermute | solution.py:766
  11.8 5.4 %collective-permute-start.4 = (f32[56,128]{1,0:T(8,128)S(1)}, f32[56,128]{1,0:T(8,128)S(1)}, u32[]{:S(2)}, u32[]{:S(2)}) collective-permute-start(f32[56,128]{1,0:T(8,128)S(1)} %get-tuple-element.23), channel_id=1, source_target_pairs={{0,16},{1,29},{2,30},{3,27},{4,28},{5,25},{6,26},{7,23},{8,24},{9,... | collective-permute-start | bytes 86024 | tf_op jit(solution)/shard_map/ppermute | solution.py:785
  12.5 5.1 %collective-permute-start.5 = (f32[56,128]{1,0:T(8,128)S(1)}, f32[56,128]{1,0:T(8,128)S(1)}, u32[]{:S(2)}, u32[]{:S(2)}) collective-permute-start(f32[56,128]{1,0:T(8,128)S(1)} %get-tuple-element.24), channel_id=1, source_target_pairs={{0,16},{1,18},{2,17},{3,20},{4,19},{5,22},{6,21},{7,24},{8,23},{9,... | collective-permute-start | bytes 86024 | tf_op jit(solution)/shard_map/ppermute | solution.py:785
  15.3 2.2 %collective-permute-start.2 = (f32[328,128]{1,0:T(8,128)S(1)}, f32[328,128]{1,0:T(8,128)S(1)}, u32[]{:S(2)}, u32[]{:S(2)}) collective-permute-start(f32[328,128]{1,0:T(8,128)S(1)} %corners.1), channel_id=1, source_target_pairs={{0,1},{1,0},{2,3},{3,2},{4,5},{5,4},{6,7},{7,6},{8,9},{9,8},{10,11... | collective-permute-start | bytes 503816 | tf_op jit(solution)/shard_map/ppermute | solution.py:766

commit v15 on v14

--- a/solution.py
+++ b/solution.py
@@ -163,7 +163,8 @@
 def picked(values, one_hot):
     high = values.astype(bf16)
     low = (values - high.astype(f32)).astype(bf16)
-    return dot(high, one_hot) + dot(low, one_hot)
+    both = dot(jnp.concatenate([high, low], 0), one_hot)
+    return both[: values.shape[0]] + both[values.shape[0] :]
 
 
 def as_one_hot(row_of_lane, depth):
@@ -479,7 +480,7 @@
 
 def steps_kernel(
     block_cols, seam_ref, pair_ref, next_ref, far_ref, low_ref, centre_ref,
-    high_ref, hot_ref, table_ref, weight_ref, lanes_ref, out_ref, sums, leaving, sems,
+    high_ref, hot_ref, table_ref, weight_ref, lanes_ref, out_ref, sums,
 ):
     east0, flip0, east1, flip1 = seam_flags(seam_ref, block_cols)
     odd = lax.axis_index("blk") & 1
@@ -541,17 +542,23 @@
         from_other = lane >= LANES - by if by > 0 else lane < -by
         return [jnp.where(from_other, turned[others[k]], turned[k]) for k in range(size)]
 
-    def edge_x(components, slots):
+    def put_x_sums(groups, components):
+        slots = [k for group in groups for k in group]
         ring = len(slots) < count
-        for c in range(components):
-            west_at = slice(c * NODES, c * NODES + NP)
-            east_at = slice((c + 1) * NODES - NP, (c + 1) * NODES)
-            west = [sums[k, west_at] for k in slots]
-            east = [sums[k, east_at] for k in slots]
+        per_tile = [
+            [part[:, n * LANES : (n + 1) * LANES] for part in parts]
+            for group, parts in zip(groups, components)
+            for n in range(len(group))
+        ]
+        for c in range(3):
+            parts = [tile[c] for tile in per_tile]
+            west = [part[:NP] for part in parts]
+            east = [part[NODES - NP :] for part in parts]
             at_east, at_west = shifted(west, 1, ring), shifted(east, -1, ring)
             for n, k in enumerate(slots):
-                sums[k, west_at] = west[n] + at_west[n]
-                sums[k, east_at] = east[n] + at_east[n]
+                sums[k, c * NODES : c * NODES + NP] = west[n] + at_west[n]
+                sums[k, c * NODES + NP : (c + 1) * NODES - NP] = parts[n][NP : NODES - NP]
+                sums[k, (c + 1) * NODES - NP : (c + 1) * NODES] = east[n] + at_east[n]
 
     def edge_y(components, slots, rows=None):
         ring = len(slots) < count
@@ -572,10 +579,6 @@
             sums[k, south_at] = south[n] + at_south[n]
             sums[k, north_at] = north[n] + at_north[n]
 
-    def edge_sum(slots):
-        edge_x(3, slots)
-        edge_y(3, slots)
-
     node = lax.broadcasted_iota(i32, (1, NP, 1), 1)
     rows = []
     for rim in (outer[ALL_ROWS:, :LANES], outer[ALL_ROWS:, LANES:]):
@@ -599,11 +602,6 @@
     def part_of(group, n):
         return jnp.concatenate([tile_part(k, n) for k in group], 1)
 
-    def put(group, parts):
-        for c, part in enumerate(parts):
-            for n, k in enumerate(group):
-                sums[k, c * NODES : (c + 1) * NODES] = part[:, n * LANES : (n + 1) * LANES]
-
     def summed(group, c):
         return jnp.concatenate([sums[k, c * NODES : (c + 1) * NODES] for k in group], 1)
 
@@ -619,23 +617,24 @@
     start = [[part_of(group, n) for n in range(3)] for group in groups]
     fixed = [[part_of(group, n) for n in range(3, 6)] for group in groups]
     for k in every:
-        put((k,), [tile_part(k, n) for n in range(7, 11)])
+        for c in range(4):
+            sums[k, c * NODES : (c + 1) * NODES] = tile_part(k, 7 + c)
     edge_y(4, every, rows)
     per_mass = [1.0 / summed(group, 3) for group in groups]
     one = []
     for n, group in enumerate(groups):
         change = average(group, per_mass[n])
         one.append([s + time_step * c for s, c in zip(start[n], change)])
-        put(group, mass_tendency(table, *one[n], *fixed[n]))
-    edge_sum(every)
+    put_x_sums(groups, [mass_tendency(table, *s, *f) for s, f in zip(one, fixed)])
+    edge_y(3, every)
     two = []
     for n, group in enumerate(groups):
         change = average(group, per_mass[n])
         two.append(
             [0.75 * s + 0.25 * (o + time_step * c) for s, o, c in zip(start[n], one[n], change)]
         )
-        put(group, mass_tendency(table, *two[n], *fixed[n]))
-    edge_sum(every)
+    put_x_sums(groups, [mass_tendency(table, *s, *f) for s, f in zip(two, fixed)])
+    edge_y(3, every)
 
     def regrouped(per_group):
         (outer_low, high_above) = per_group[0], per_group[1]
@@ -666,24 +665,20 @@
         ]
         now[0] = now[0] + tide[n]
         three.append(now)
-        put(group, laplace(now))
-    edge_sum(slots)
+    put_x_sums(groups, [laplace(s) for s in three])
+    edge_y(3, slots)
+    change = [average(group, per_mass[n]) for n, group in enumerate(groups)]
+    put_x_sums(groups, [laplace(s) for s in change])
+    edge_y(3, slots)
+    stepped = []
     for n, group in enumerate(groups):
-        put(group, laplace(average(group, per_mass[n])))
-    edge_sum(slots)
+        change = average(group, per_mass[n])
+        now = [s - time_step * hyper_coeff * b for s, b in zip(three[n], change)]
+        stepped.append(jnp.concatenate(now, 0))
+    stepped = jnp.concatenate(stepped, 1)[:, :MID]
     own = lanes_ref[27:28, LANES : LANES + MID] != 0
-    hot = hot_ref[...]
-    change = [average(group, per_mass[n]) for n, group in enumerate(groups)]
-    copies = []
-    for c in range(3):
-        now = [s[c] - time_step * hyper_coeff * b[c] for s, b in zip(three, change)]
-        stepped = jnp.concatenate(now, 1)[:, :MID]
-        stored = picked(jnp.where(own, stepped, 0.0), hot)
-        leaving[c] = stored.reshape(leaving.shape[1:])
-        copies.append(pltpu.make_async_copy(leaving.at[c], out_ref.at[c], sems.at[c]))
-        copies[c].start()
-    for copy in copies:
-        copy.wait()
+    stored = picked(jnp.where(own, stepped, 0.0), hot_ref[...])
+    out_ref[...] = stored.reshape(out_ref.shape)
 
 
 def on_device(fields, jacobian, water_depth, coriolis, tide_height, slot_of, seam_rows):
@@ -696,12 +691,12 @@
     params = pltpu.CompilerParams(vmem_limit_bytes=48 * 2**20)
     held = (fields, jacobian, water_depth, coriolis, tide_height)
 
-    def call(kernel, ins, outs, cost, scratch=(), name=None, out_specs=None):
+    def call(kernel, ins, outs, cost, scratch=(), name=None):
         return pl.pallas_call(
             kernel,
             out_shape=[jax.ShapeDtypeStruct(*out) for out in outs],
             in_specs=[spec for spec, value in ins],
-            out_specs=out_specs or [vmem] * len(outs),
+            out_specs=[vmem] * len(outs),
             scratch_shapes=list(scratch),
             compiler_params=params,
             cost_estimate=pl.CostEstimate(
@@ -851,12 +846,7 @@
         ],
         [(fields.shape, f32)],
         10**8,
-        scratch=[
-            pltpu.VMEM((EXT // LANES, 4 * NODES, LANES), f32),
-            pltpu.VMEM(fields.shape, f32),
-            pltpu.SemaphoreType.DMA((3,)),
-        ],
-        out_specs=[hbm],
+        scratch=[pltpu.VMEM((EXT // LANES, 4 * NODES, LANES), f32)],
         name="steps",
     )
     return stepped

time: 22 us -> 21.9 us (level)
  no operation moved by 1% of the time
where the time goes in v15:
time: 21.9 us; the launch traced here: 21.7 us
  starting transfers between devices  10.5 us (48%)
  Pallas kernels  9.81 us (45%)
  waiting for transfers between devices  1.17 us (5%)
    pallas_call x7, Pallas kernels, call(): pl.pallas_call(kernel, out_shape=[jax.ShapeDtypeStruct(*out) for out in o...  9.81 us
    ppermute x4, starting transfers between devices, eastward(): lax.ppermute(value, both, [(rank(*a), rank(*b)) for a, b in pairs.items()])  9 us
    ppermute x2, starting transfers between devices, swapped(): return lax.ppermute(value, both, pairs)  1.54 us
    ppermute x4, waiting for transfers between devices, eastward(): lax.ppermute(value, both, [(rank(*a), rank(*b)) for a, b in pairs.items()])  1.17 us
  transfers between devices with their start and end apart: 6, of which 3 were waited for; matrix products, arithmetic and copies ran while one was open for 0% of the time, Pallas kernels for 18%

profile of v15, /device:TPU:0, one launch (start us, length us, event | category | flops | bytes accessed | tf_op | source)
XLA Modules:
  0.0 21.7 jit_solution(16152860424054099106)
XLA Ops:
  0.0 1.8 %strips.1 = (f32[216,128]{1,0:T(8,128)S(1)}, f32[216,128]{1,0:T(8,128)S(1)}, f32[448,256]{1,0:T(8,128)S(1)}) custom-call(s32[2,256]{1,0:T(2,128)} %seam_ref.5, s32[1,256]{1,0:T(1,128)} %slot_ref.3, f32[3,8,8,256]{3,2,1,0:T(8,128)} %refs_2_.1, f32[8,8,256]{2,1,0:T(8,128)} %refs_3_.1, f32[8,8,256]{2,1,0:T(8,128)} %refs_4_.1, f32[8,8,256]{2,1,0:T(8,128)} %refs_5_.1, ...), custom_call_target="tpu_custom_call" | custom-call | flops 100000000 | bytes 2097152 | tf_op jit(solution)/shard_map/strips/pallas_call | solution.py:695
  1.8 0.0 copy-start.3
  1.8 6.4 %collective-permute-start = (f32[216,128]{1,0:T(8,128)S(1)}, f32[216,128]{1,0:T(8,128)S(1)}, u32[]{:S(2)}, u32[]{:S(2)}) collective-permute-start(f32[216,128]{1,0:T(8,128)S(1)} %get-tuple-element.17.strip1_ref), channel_id=1, source_target_pairs={{0,31},{1,30},{2,29},{3,28},{4,27},{5,26},{6,25},{7,24},{8,23},{9,... | collective-permute-start | bytes 331784 | tf_op jit(solution)/shard_map/ppermute | solution.py:780
  8.3 0.5 %collective-permute-start.1 = (f32[216,128]{1,0:T(8,128)S(1)}, f32[216,128]{1,0:T(8,128)S(1)}, u32[]{:S(2)}, u32[]{:S(2)}) collective-permute-start(f32[216,128]{1,0:T(8,128)S(1)} %get-tuple-element.18.strip0_ref), channel_id=1, source_target_pairs={{0,16},{1,17},{2,18},{3,19},{4,20},{5,21},{6,22},{7,23},{8,24},{9,... | collective-permute-start | bytes 331784 | tf_op jit(solution)/shard_map/ppermute | solution.py:780
  8.8 0.0 copy-done
  8.8 0.0 copy-done.2
  8.8 0.0 copy-done.3
  8.8 0.1 copy-done.4
  8.9 1.4 %rows.1 = (f32[216,128]{1,0:T(8,128)S(1)}, f32[56,128]{1,0:T(8,128)S(1)}, f32[56,128]{1,0:T(8,128)S(1)}, f32[216,128]{1,0:T(8,128)S(1)}) custom-call(s32[2,256]{1,0:T(2,128)S(1)} %copy-done.3, f32[448,256]{1,0:T(8,128)S(1)} %get-tuple-element.19.stored_ref, f32[216,128]{1,0:T(8,128)S(1)} %get-tuple-element.17.strip1_ref, ...), custom_call_target="tpu_custom_call" | custom-call | flops 100000000 | bytes 2097152 | tf_op jit(solution)/shard_map/rows/pallas_call | solution.py:695
  10.4 1.4 %collective-permute-start.3 = (f32[216,128]{1,0:T(8,128)S(1)}, f32[216,128]{1,0:T(8,128)S(1)}, u32[]{:S(2)}, u32[]{:S(2)}) collective-permute-start(f32[216,128]{1,0:T(8,128)S(1)} %get-tuple-element.22), channel_id=1, source_target_pairs={{0,16},{1,2},{2,1},{3,4},{4,3},{5,6},{6,5},{7,8},{8,7},{9,10},{10,... | collective-permute-start | bytes 331784 | tf_op jit(solution)/shard_map/ppermute | solution.py:761
  11.8 0.7 %collective-permute-start.4 = (f32[56,128]{1,0:T(8,128)S(1)}, f32[56,128]{1,0:T(8,128)S(1)}, u32[]{:S(2)}, u32[]{:S(2)}) collective-permute-start(f32[56,128]{1,0:T(8,128)S(1)} %get-tuple-element.23), channel_id=1, source_target_pairs={{0,16},{1,29},{2,30},{3,27},{4,28},{5,25},{6,26},{7,23},{8,24},{9,... | collective-permute-start | bytes 86024 | tf_op jit(solution)/shard_map/ppermute | solution.py:780
  12.5 1.4 %collective-permute-start.5 = (f32[56,128]{1,0:T(8,128)S(1)}, f32[56,128]{1,0:T(8,128)S(1)}, u32[]{:S(2)}, u32[]{:S(2)}) collective-permute-start(f32[56,128]{1,0:T(8,128)S(1)} %get-tuple-element.24), channel_id=1, source_target_pairs={{0,16},{1,18},{2,17},{3,20},{4,19},{5,22},{6,21},{7,24},{8,23},{9,... | collective-permute-start | bytes 86024 | tf_op jit(solution)/shard_map/ppermute | solution.py:780
  13.8 0.0 copy-done.1
  13.8 0.6 %own.1 = (f32[448,384]{1,0:T(8,128)S(1)}, bf16[384,256]{1,0:T(8,128)(2,1)S(1)}) custom-call(f32[448,256]{1,0:T(8,128)S(1)} %get-tuple-element.19.stored_ref, s32[1,256]{1,0:T(1,128)S(1)} %copy-done.4, s32[56,640]{1,0:T(8,128)S(1)} %copy-done.1), custom_call_target="tpu_custom_call" | custom-call | flops 100000000 | bytes 2097152 | tf_op jit(solution)/shard_map/own/pallas_call | solution.py:695
  14.4 0.0 collective-permute-done.in1_ref
  14.4 0.4 %collective-permute-done.1.in0_ref = f32[216,128]{1,0:T(8,128)S(1)} collective-permute-done((f32[216,128]{1,0:T(8,128)S(1)}, f32[216,128]{1,0:T(8,128)S(1)}, u32[]{:S(2)}, u32[]{:S(2)}) %collective-permute-start.1) | collective-permute-done | bytes 110624 | tf_op jit(solution)/shard_map/ppermute | solution.py:780
  14.8 0.5 %corners.1 = f32[328,128]{1,0:T(8,128)S(1)} custom-call(f32[216,128]{1,0:T(8,128)S(1)} %collective-permute-done.in1_ref, f32[216,128]{1,0:T(8,128)S(1)} %collective-permute-done.1.in0_ref, f32[216,128]{1,0:T(8,128)S(1)} %get-tuple-element.20.pair_ref, f32[320,256]{1,0:T(8,128)S(1)} %copy-done, f32[64,128]{1,0:T(8,128)S(1)} %copy-done.2, ...), custom_call_target="tpu_custom_call" | custom-call | flops 100000000 | bytes 2097152 | tf_op jit(solution)/shard_map/corners/pallas_call | solution.py:695
  15.3 0.1 collective-permute-start.2
  15.5 1.4 %middle.1 = (f32[704,128]{1,0:T(8,128)S(1)}, f32[704,128]{1,0:T(8,128)S(1)}, f32[704,128]{1,0:T(8,128)S(1)}) custom-call(s32[2,256]{1,0:T(2,128)S(1)} %copy-done.3, f32[216,128]{1,0:T(8,128)S(1)} %collective-permute-done.1.in0_ref, f32[216,128]{1,0:T(8,128)S(1)} %collective-permute-done.in1_ref, f32[448,384]{1,0:T(8,128)S(1)} %get-tuple-element.25.own_ref, ...), custom_call_target="tpu_custom_call" | custom-call | flops 100000000 | bytes 2097152 | tf_op jit(solution)/shard_map/middle/pallas_call | solution.py:695
  16.8 0.4 %collective-permute-done.4.far1_ref = f32[56,128]{1,0:T(8,128)S(1)} collective-permute-done((f32[56,128]{1,0:T(8,128)S(1)}, f32[56,128]{1,0:T(8,128)S(1)}, u32[]{:S(2)}, u32[]{:S(2)}) %collective-permute-start.4) | collective-permute-done | bytes 28704 | tf_op jit(solution)/shard_map/ppermute | solution.py:780
  17.2 0.3 %collective-permute-done.5.far0_ref = f32[56,128]{1,0:T(8,128)S(1)} collective-permute-done((f32[56,128]{1,0:T(8,128)S(1)}, f32[56,128]{1,0:T(8,128)S(1)}, u32[]{:S(2)}, u32[]{:S(2)}) %collective-permute-start.5) | collective-permute-done | bytes 28704 | tf_op jit(solution)/shard_map/ppermute | solution.py:780
  17.5 0.0 collective-permute-done.3.refs_0_.next_ref
  17.6 0.0 collective-permute-done.2.pair_ref
  17.6 4.2 %steps.1 = f32[3,8,8,256]{3,2,1,0:T(8,128)} custom-call(s32[2,256]{1,0:T(2,128)S(1)} %copy-done.3, f32[328,128]{1,0:T(8,128)S(1)} %collective-permute-done.2.pair_ref, f32[216,128]{1,0:T(8,128)S(1)} %collective-permute-done.3.refs_0_.next_ref, f32[112,128]{1,0:T(8,128)S(1)} %far.1.far_ref, f32[704,128]{1,0:T(8,128)S(1)} %get-tuple-element.26.refs_1_.low_ref, ...), custom_call_target="tpu_custom_call" | custom-call | flops 100000000 | bytes 2097152 | tf_op jit(solution)/shard_map/steps/pallas_call | solution.py:695
  (5 shorter events, 0.0 us)
Async XLA Ops:
  0.0 8.8 %copy-start = (f32[320,256]{1,0:T(8,128)S(1)}, f32[320,256]{1,0:T(8,128)}, u32[]{:S(2)}) copy-start(f32[320,256]{1,0:T(8,128)} %constant.6.clone.refs_7_.table_ref) | copy-start | bytes 983044
  0.0 8.8 %copy-start.2 = (f32[64,128]{1,0:T(8,128)S(1)}, f32[64,128]{1,0:T(8,128)}, u32[]{:S(2)}) copy-start(f32[64,128]{1,0:T(8,128)} %constant.7.clone.refs_8_.weight_ref) | copy-start | bytes 98308
  1.8 7.0 %copy-start.3 = (s32[2,256]{1,0:T(2,128)S(1)}, s32[2,256]{1,0:T(2,128)}, u32[]{:S(2)}) copy-start(s32[2,256]{1,0:T(2,128)} %seam_ref.5) | copy-start | bytes 6148
  1.8 12.6 %collective-permute-start = (f32[216,128]{1,0:T(8,128)S(1)}, f32[216,128]{1,0:T(8,128)S(1)}, u32[]{:S(2)}, u32[]{:S(2)}) collective-permute-start(f32[216,128]{1,0:T(8,128)S(1)} %get-tuple-element.17.strip1_ref), channel_id=1, source_target_pairs={{0,31},{1,30},{2,29},{3,28},{4,27},{5,26},{6,25},{7,24},{8,23},{9,... | collective-permute-start | bytes 331784 | tf_op jit(solution)/shard_map/ppermute | solution.py:780
  8.3 0.7 %copy-start.4 = (s32[1,256]{1,0:T(1,128)S(1)}, s32[1,256]{1,0:T(1,128)}, u32[]{:S(2)}) copy-start(s32[1,256]{1,0:T(1,128)} %slot_ref.3) | copy-start | bytes 3076
  8.3 6.6 %collective-permute-start.1 = (f32[216,128]{1,0:T(8,128)S(1)}, f32[216,128]{1,0:T(8,128)S(1)}, u32[]{:S(2)}, u32[]{:S(2)}) collective-permute-start(f32[216,128]{1,0:T(8,128)S(1)} %get-tuple-element.18.strip0_ref), channel_id=1, source_target_pairs={{0,16},{1,17},{2,18},{3,19},{4,20},{5,21},{6,22},{7,23},{8,24},{9,... | collective-permute-start | bytes 331784 | tf_op jit(solution)/shard_map/ppermute | solution.py:780
  8.9 4.9 %copy-start.1 = (s32[56,640]{1,0:T(8,128)S(1)}, s32[56,640]{1,0:T(8,128)}, u32[]{:S(2)}) copy-start(s32[56,640]{1,0:T(8,128)} %constant.8.clone.lanes_ref) | copy-start | bytes 430084
  10.4 7.2 %collective-permute-start.3 = (f32[216,128]{1,0:T(8,128)S(1)}, f32[216,128]{1,0:T(8,128)S(1)}, u32[]{:S(2)}, u32[]{:S(2)}) collective-permute-start(f32[216,128]{1,0:T(8,128)S(1)} %get-tuple-element.22), channel_id=1, source_target_pairs={{0,16},{1,2},{2,1},{3,4},{4,3},{5,6},{6,5},{7,8},{8,7},{9,10},{10,... | collective-permute-start | bytes 331784 | tf_op jit(solution)/shard_map/ppermute | solution.py:761
  11.8 5.4 %collective-permute-start.4 = (f32[56,128]{1,0:T(8,128)S(1)}, f32[56,128]{1,0:T(8,128)S(1)}, u32[]{:S(2)}, u32[]{:S(2)}) collective-permute-start(f32[56,128]{1,0:T(8,128)S(1)} %get-tuple-element.23), channel_id=1, source_target_pairs={{0,16},{1,29},{2,30},{3,27},{4,28},{5,25},{6,26},{7,23},{8,24},{9,... | collective-permute-start | bytes 86024 | tf_op jit(solution)/shard_map/ppermute | solution.py:780
  12.5 5.1 %collective-permute-start.5 = (f32[56,128]{1,0:T(8,128)S(1)}, f32[56,128]{1,0:T(8,128)S(1)}, u32[]{:S(2)}, u32[]{:S(2)}) collective-permute-start(f32[56,128]{1,0:T(8,128)S(1)} %get-tuple-element.24), channel_id=1, source_target_pairs={{0,16},{1,18},{2,17},{3,20},{4,19},{5,22},{6,21},{7,24},{8,23},{9,... | collective-permute-start | bytes 86024 | tf_op jit(solution)/shard_map/ppermute | solution.py:780
  15.3 2.2 %collective-permute-start.2 = (f32[328,128]{1,0:T(8,128)S(1)}, f32[328,128]{1,0:T(8,128)S(1)}, u32[]{:S(2)}, u32[]{:S(2)}) collective-permute-start(f32[328,128]{1,0:T(8,128)S(1)} %corners.1), channel_id=1, source_target_pairs={{0,1},{1,0},{2,3},{3,2},{4,5},{5,4},{6,7},{7,6},{8,9},{9,8},{10,11... | collective-permute-start | bytes 503816 | tf_op jit(solution)/shard_map/ppermute | solution.py:761

commit v16 on v15

--- a/solution.py
+++ b/solution.py
@@ -472,6 +472,10 @@
             ref[n * NODES : (n + 1) * NODES] = part[:, k * LANES : (k + 1) * LANES]
 
 
+def next_kernel(next_ref, _, out_ref):
+    out_ref[...] = next_ref[...]
+
+
 def far_kernel(far1_ref, far0_ref, *refs):
     out_ref = refs[-1]
     out_ref[:CORNER_ROWS] = far0_ref[...]
@@ -829,10 +833,17 @@
     )
     (far,) = call(
         far_kernel,
-        [(vmem, x) for x in (far1, far0, from_next, low)],
+        [(vmem, x) for x in (far1, far0, low)],
         [((2 * CORNER_ROWS, LANES), f32)],
         10**11,
         name="far",
+    )
+    (from_next,) = call(
+        next_kernel,
+        [(vmem, x) for x in (from_next, far)],
+        [strip],
+        10**10,
+        name="next",
     )
     (stepped,) = call(
         functools.partial(steps_kernel, block_cols),

time: 21.9 us -> 21.9 us (level)
    ppermute x4, waiting for transfers between devices: 1.17 us -> 0.45 us  [eastward(): lax.ppermute(value, both, [(rank(*a), rank(*b)) for a, b in pairs.items()])]
    ppermute x2, waiting for transfers between devices: 0.01 us -> 0.71 us  [swapped(): return lax.ppermute(value, both, pairs)]
    pallas_call x7 -> x8, Pallas kernels: 9.81 us -> 9.82 us  [call(): pl.pallas_call(kernel, out_shape=[jax.ShapeDtypeStruct(*out) for out in o...]
  transfers between devices with their start and end apart: 6 -> 6, of which waited for: 3 -> 2; matrix products, arithmetic and copies ran while one was open for 0% -> 0% of each run, Pallas kernels for 18% -> 18%
where the time goes in v16:
time: 21.9 us; the launch traced here: 21.7 us
  starting transfers between devices  10.5 us (48%)
  Pallas kernels  9.82 us (45%)
  waiting for transfers between devices  1.16 us (5%)
    pallas_call x8, Pallas kernels, call(): pl.pallas_call(kernel, out_shape=[jax.ShapeDtypeStruct(*out) for out in o...  9.82 us
    ppermute x4, starting transfers between devices, eastward(): lax.ppermute(value, both, [(rank(*a), rank(*b)) for a, b in pairs.items()])  9.04 us
    ppermute x2, starting transfers between devices, swapped(): return lax.ppermute(value, both, pairs)  1.48 us
    ppermute x2, waiting for transfers between devices, swapped(): return lax.ppermute(value, both, pairs)  0.71 us
    ppermute x4, waiting for transfers between devices, eastward(): lax.ppermute(value, both, [(rank(*a), rank(*b)) for a, b in pairs.items()])  0.45 us
  transfers between devices with their start and end apart: 6, of which 2 were waited for; matrix products, arithmetic and copies ran while one was open for 0% of the time, Pallas kernels for 18%

profile of v16, /device:TPU:0, one launch (start us, length us, event | category | flops | bytes accessed | tf_op | source)
XLA Modules:
  0.0 21.7 jit_solution(389923386953026981)
XLA Ops:
  0.0 1.8 %strips.1 = (f32[216,128]{1,0:T(8,128)S(1)}, f32[216,128]{1,0:T(8,128)S(1)}, f32[448,256]{1,0:T(8,128)S(1)}) custom-call(s32[2,256]{1,0:T(2,128)} %seam_ref.5, s32[1,256]{1,0:T(1,128)} %slot_ref.3, f32[3,8,8,256]{3,2,1,0:T(8,128)} %refs_2_.1, f32[8,8,256]{2,1,0:T(8,128)} %refs_3_.1, f32[8,8,256]{2,1,0:T(8,128)} %refs_4_.1, f32[8,8,256]{2,1,0:T(8,128)} %refs_5_.1, ...), custom_call_target="tpu_custom_call" | custom-call | flops 100000000 | bytes 2097152 | tf_op jit(solution)/shard_map/strips/pallas_call | solution.py:699
  1.8 0.0 copy-start.3
  1.8 6.4 %collective-permute-start = (f32[216,128]{1,0:T(8,128)S(1)}, f32[216,128]{1,0:T(8,128)S(1)}, u32[]{:S(2)}, u32[]{:S(2)}) collective-permute-start(f32[216,128]{1,0:T(8,128)S(1)} %get-tuple-element.17.strip1_ref), channel_id=1, source_target_pairs={{0,31},{1,30},{2,29},{3,28},{4,27},{5,26},{6,25},{7,24},{8,23},{9,... | collective-permute-start | bytes 331784 | tf_op jit(solution)/shard_map/ppermute | solution.py:784
  8.3 0.5 %collective-permute-start.1 = (f32[216,128]{1,0:T(8,128)S(1)}, f32[216,128]{1,0:T(8,128)S(1)}, u32[]{:S(2)}, u32[]{:S(2)}) collective-permute-start(f32[216,128]{1,0:T(8,128)S(1)} %get-tuple-element.18.strip0_ref), channel_id=1, source_target_pairs={{0,16},{1,17},{2,18},{3,19},{4,20},{5,21},{6,22},{7,23},{8,24},{9,... | collective-permute-start | bytes 331784 | tf_op jit(solution)/shard_map/ppermute | solution.py:784
  8.8 0.0 copy-done
  8.8 0.0 copy-done.2
  8.8 0.0 copy-done.3
  8.8 0.1 copy-done.4
  8.9 1.4 %rows.1 = (f32[216,128]{1,0:T(8,128)S(1)}, f32[56,128]{1,0:T(8,128)S(1)}, f32[56,128]{1,0:T(8,128)S(1)}, f32[216,128]{1,0:T(8,128)S(1)}) custom-call(s32[2,256]{1,0:T(2,128)S(1)} %copy-done.3, f32[448,256]{1,0:T(8,128)S(1)} %get-tuple-element.19.stored_ref, f32[216,128]{1,0:T(8,128)S(1)} %get-tuple-element.17.strip1_ref, ...), custom_call_target="tpu_custom_call" | custom-call | flops 100000000 | bytes 2097152 | tf_op jit(solution)/shard_map/rows/pallas_call | solution.py:699
  10.4 1.4 %collective-permute-start.4 = (f32[56,128]{1,0:T(8,128)S(1)}, f32[56,128]{1,0:T(8,128)S(1)}, u32[]{:S(2)}, u32[]{:S(2)}) collective-permute-start(f32[56,128]{1,0:T(8,128)S(1)} %get-tuple-element.23), channel_id=1, source_target_pairs={{0,16},{1,29},{2,30},{3,27},{4,28},{5,25},{6,26},{7,23},{8,24},{9,... | collective-permute-start | bytes 86024 | tf_op jit(solution)/shard_map/ppermute | solution.py:784
  11.8 0.7 %collective-permute-start.5 = (f32[56,128]{1,0:T(8,128)S(1)}, f32[56,128]{1,0:T(8,128)S(1)}, u32[]{:S(2)}, u32[]{:S(2)}) collective-permute-start(f32[56,128]{1,0:T(8,128)S(1)} %get-tuple-element.24), channel_id=1, source_target_pairs={{0,16},{1,18},{2,17},{3,20},{4,19},{5,22},{6,21},{7,24},{8,23},{9,... | collective-permute-start | bytes 86024 | tf_op jit(solution)/shard_map/ppermute | solution.py:784
  12.5 1.4 %collective-permute-start.3 = (f32[216,128]{1,0:T(8,128)S(1)}, f32[216,128]{1,0:T(8,128)S(1)}, u32[]{:S(2)}, u32[]{:S(2)}) collective-permute-start(f32[216,128]{1,0:T(8,128)S(1)} %get-tuple-element.22), channel_id=1, source_target_pairs={{0,16},{1,2},{2,1},{3,4},{4,3},{5,6},{6,5},{7,8},{8,7},{9,10},{10,... | collective-permute-start | bytes 331784 | tf_op jit(solution)/shard_map/ppermute | solution.py:765
  13.8 0.0 copy-done.1
  13.8 0.6 %own.1 = (f32[448,384]{1,0:T(8,128)S(1)}, bf16[384,256]{1,0:T(8,128)(2,1)S(1)}) custom-call(f32[448,256]{1,0:T(8,128)S(1)} %get-tuple-element.19.stored_ref, s32[1,256]{1,0:T(1,128)S(1)} %copy-done.4, s32[56,640]{1,0:T(8,128)S(1)} %copy-done.1), custom_call_target="tpu_custom_call" | custom-call | flops 100000000 | bytes 2097152 | tf_op jit(solution)/shard_map/own/pallas_call | solution.py:699
  14.4 0.0 collective-permute-done.in1_ref
  14.4 0.4 %collective-permute-done.1.in0_ref = f32[216,128]{1,0:T(8,128)S(1)} collective-permute-done((f32[216,128]{1,0:T(8,128)S(1)}, f32[216,128]{1,0:T(8,128)S(1)}, u32[]{:S(2)}, u32[]{:S(2)}) %collective-permute-start.1) | collective-permute-done | bytes 110624 | tf_op jit(solution)/shard_map/ppermute | solution.py:784
  14.9 0.5 %corners.1 = f32[328,128]{1,0:T(8,128)S(1)} custom-call(f32[216,128]{1,0:T(8,128)S(1)} %collective-permute-done.in1_ref, f32[216,128]{1,0:T(8,128)S(1)} %collective-permute-done.1.in0_ref, f32[216,128]{1,0:T(8,128)S(1)} %get-tuple-element.20.pair_ref, f32[320,256]{1,0:T(8,128)S(1)} %copy-done, f32[64,128]{1,0:T(8,128)S(1)} %copy-done.2, ...), custom_call_target="tpu_custom_call" | custom-call | flops 100000000 | bytes 2097152 | tf_op jit(solution)/shard_map/corners/pallas_call | solution.py:699
  15.3 0.1 collective-permute-start.2
  15.5 1.4 %middle.1 = (f32[704,128]{1,0:T(8,128)S(1)}, f32[704,128]{1,0:T(8,128)S(1)}, f32[704,128]{1,0:T(8,128)S(1)}) custom-call(s32[2,256]{1,0:T(2,128)S(1)} %copy-done.3, f32[216,128]{1,0:T(8,128)S(1)} %collective-permute-done.1.in0_ref, f32[216,128]{1,0:T(8,128)S(1)} %collective-permute-done.in1_ref, f32[448,384]{1,0:T(8,128)S(1)} %get-tuple-element.25.own_ref, ...), custom_call_target="tpu_custom_call" | custom-call | flops 100000000 | bytes 2097152 | tf_op jit(solution)/shard_map/middle/pallas_call | solution.py:699
  16.8 0.0 collective-permute-done.4.far1_ref
  16.8 0.0 collective-permute-done.5.far0_ref
  16.8 0.7 %collective-permute-done.3.next_ref = f32[216,128]{1,0:T(8,128)S(1)} collective-permute-done((f32[216,128]{1,0:T(8,128)S(1)}, f32[216,128]{1,0:T(8,128)S(1)}, u32[]{:S(2)}, u32[]{:S(2)}) %collective-permute-start.3) | collective-permute-done | bytes 110624 | tf_op jit(solution)/shard_map/ppermute | solution.py:765
  17.6 0.0 collective-permute-done.2.pair_ref
  17.6 4.2 %steps.1 = f32[3,8,8,256]{3,2,1,0:T(8,128)} custom-call(s32[2,256]{1,0:T(2,128)S(1)} %copy-done.3, f32[328,128]{1,0:T(8,128)S(1)} %collective-permute-done.2.pair_ref, f32[216,128]{1,0:T(8,128)S(1)} %next.1.next_ref, f32[112,128]{1,0:T(8,128)S(1)} %far.1._.far_ref, f32[704,128]{1,0:T(8,128)S(1)} %get-tuple-element.26.refs_0_.low_ref, ...), custom_call_target="tpu_custom_call" | custom-call | flops 100000000 | bytes 2097152 | tf_op jit(solution)/shard_map/steps/pallas_call | solution.py:699
  (6 shorter events, 0.0 us)
Async XLA Ops:
  0.0 8.8 %copy-start = (f32[320,256]{1,0:T(8,128)S(1)}, f32[320,256]{1,0:T(8,128)}, u32[]{:S(2)}) copy-start(f32[320,256]{1,0:T(8,128)} %constant.6.clone.refs_7_.table_ref) | copy-start | bytes 983044
  0.0 8.8 %copy-start.2 = (f32[64,128]{1,0:T(8,128)S(1)}, f32[64,128]{1,0:T(8,128)}, u32[]{:S(2)}) copy-start(f32[64,128]{1,0:T(8,128)} %constant.7.clone.refs_8_.weight_ref) | copy-start | bytes 98308
  1.8 7.0 %copy-start.3 = (s32[2,256]{1,0:T(2,128)S(1)}, s32[2,256]{1,0:T(2,128)}, u32[]{:S(2)}) copy-start(s32[2,256]{1,0:T(2,128)} %seam_ref.5) | copy-start | bytes 6148
  1.8 12.6 %collective-permute-start = (f32[216,128]{1,0:T(8,128)S(1)}, f32[216,128]{1,0:T(8,128)S(1)}, u32[]{:S(2)}, u32[]{:S(2)}) collective-permute-start(f32[216,128]{1,0:T(8,128)S(1)} %get-tuple-element.17.strip1_ref), channel_id=1, source_target_pairs={{0,31},{1,30},{2,29},{3,28},{4,27},{5,26},{6,25},{7,24},{8,23},{9,... | collective-permute-start | bytes 331784 | tf_op jit(solution)/shard_map/ppermute | solution.py:784
  8.3 0.7 %copy-start.4 = (s32[1,256]{1,0:T(1,128)S(1)}, s32[1,256]{1,0:T(1,128)}, u32[]{:S(2)}) copy-start(s32[1,256]{1,0:T(1,128)} %slot_ref.3) | copy-start | bytes 3076
  8.3 6.6 %collective-permute-start.1 = (f32[216,128]{1,0:T(8,128)S(1)}, f32[216,128]{1,0:T(8,128)S(1)}, u32[]{:S(2)}, u32[]{:S(2)}) collective-permute-start(f32[216,128]{1,0:T(8,128)S(1)} %get-tuple-element.18.strip0_ref), channel_id=1, source_target_pairs={{0,16},{1,17},{2,18},{3,19},{4,20},{5,21},{6,22},{7,23},{8,24},{9,... | collective-permute-start | bytes 331784 | tf_op jit(solution)/shard_map/ppermute | solution.py:784
  8.9 4.9 %copy-start.1 = (s32[56,640]{1,0:T(8,128)S(1)}, s32[56,640]{1,0:T(8,128)}, u32[]{:S(2)}) copy-start(s32[56,640]{1,0:T(8,128)} %constant.8.clone.lanes_ref) | copy-start | bytes 430084
  10.4 6.4 %collective-permute-start.4 = (f32[56,128]{1,0:T(8,128)S(1)}, f32[56,128]{1,0:T(8,128)S(1)}, u32[]{:S(2)}, u32[]{:S(2)}) collective-permute-start(f32[56,128]{1,0:T(8,128)S(1)} %get-tuple-element.23), channel_id=1, source_target_pairs={{0,16},{1,29},{2,30},{3,27},{4,28},{5,25},{6,26},{7,23},{8,24},{9,... | collective-permute-start | bytes 86024 | tf_op jit(solution)/shard_map/ppermute | solution.py:784
  11.8 5.0 %collective-permute-start.5 = (f32[56,128]{1,0:T(8,128)S(1)}, f32[56,128]{1,0:T(8,128)S(1)}, u32[]{:S(2)}, u32[]{:S(2)}) collective-permute-start(f32[56,128]{1,0:T(8,128)S(1)} %get-tuple-element.24), channel_id=1, source_target_pairs={{0,16},{1,18},{2,17},{3,20},{4,19},{5,22},{6,21},{7,24},{8,23},{9,... | collective-permute-start | bytes 86024 | tf_op jit(solution)/shard_map/ppermute | solution.py:784
  12.5 5.1 %collective-permute-start.3 = (f32[216,128]{1,0:T(8,128)S(1)}, f32[216,128]{1,0:T(8,128)S(1)}, u32[]{:S(2)}, u32[]{:S(2)}) collective-permute-start(f32[216,128]{1,0:T(8,128)S(1)} %get-tuple-element.22), channel_id=1, source_target_pairs={{0,16},{1,2},{2,1},{3,4},{4,3},{5,6},{6,5},{7,8},{8,7},{9,10},{10,... | collective-permute-start | bytes 331784 | tf_op jit(solution)/shard_map/ppermute | solution.py:765
  15.3 2.2 %collective-permute-start.2 = (f32[328,128]{1,0:T(8,128)S(1)}, f32[328,128]{1,0:T(8,128)S(1)}, u32[]{:S(2)}, u32[]{:S(2)}) collective-permute-start(f32[328,128]{1,0:T(8,128)S(1)} %corners.1), channel_id=1, source_target_pairs={{0,1},{1,0},{2,3},{3,2},{4,5},{5,4},{6,7},{7,6},{8,9},{9,8},{10,11... | collective-permute-start | bytes 503816 | tf_op jit(solution)/shard_map/ppermute | solution.py:765

commit v17 on v15

--- a/solution.py
+++ b/solution.py
@@ -179,11 +179,16 @@
 
 
 def by_slot(slot_ref, cell_of_lane):
-    slots = jnp.broadcast_to(slot_ref[...], (8, ELEMENTS)).astype(f32).astype(bf16)
-    chosen = dot(slots, as_one_hot(cell_of_lane, ELEMENTS))
-    chosen = jnp.where(cell_of_lane >= 0, chosen, -1.0)
-    index = lax.broadcasted_iota(i32, (ELEMENTS, cell_of_lane.shape[1]), 0).astype(f32)
-    return jnp.where(index == chosen[0:1], 1.0, 0.0).astype(bf16)
+    size = cell_of_lane.shape[1]
+    halves = [
+        jnp.broadcast_to(slot_ref[:, k * LANES : (k + 1) * LANES], (8, LANES)) for k in range(2)
+    ]
+    chosen = []
+    for k in range(size // LANES):
+        cell = cell_of_lane[:, k * LANES : (k + 1) * LANES]
+        low, high = (jnp.take_along_axis(half, cell & (LANES - 1), axis=1) for half in halves)
+        chosen.append(jnp.where(cell < 0, -1, jnp.where(cell < LANES, low, high)))
+    return as_one_hot(jnp.concatenate(chosen, 1), ELEMENTS)
 
 
 def stored_rows(fields_ref, others):
@@ -358,24 +363,32 @@
     sign = jnp.where(flip, -1.0, 1.0)
     node = lax.broadcasted_iota(i32, (1, NP, 1), 1)
 
-    def in_frame(values):
+    def turned(values):
         shaped = values.reshape(-1, NP, LANES)
-        turned = pltpu.roll(shaped, 4, 1)
-        turned = jnp.where((node & 2) == 0, pltpu.roll(turned, 6, 1), pltpu.roll(turned, 2, 1))
-        turned = jnp.where((node & 1) == 0, pltpu.roll(turned, 7, 1), pltpu.roll(turned, 1, 1))
-        values = jnp.where(flip[None], turned, shaped).reshape(values.shape)
-        parts = [values[k * NODES : (k + 1) * NODES] for k in range(ARRAYS)]
-        parts[2] = parts[2] * sign
-        parts[5] = parts[5] * sign
-        return parts
-
-    strip, ring = in_frame(both[:, :LANES]), in_frame(both[:, LANES:])
+        shaped = pltpu.roll(shaped, 4, 1)
+        shaped = jnp.where((node & 2) == 0, pltpu.roll(shaped, 6, 1), pltpu.roll(shaped, 2, 1))
+        shaped = jnp.where((node & 1) == 0, pltpu.roll(shaped, 7, 1), pltpu.roll(shaped, 1, 1))
+        return shaped.reshape(values.shape)
+
+    strip, ring = (
+        [part[k * NODES : (k + 1) * NODES] for k in range(ARRAYS)]
+        for part in (both[:, :LANES], both[:, LANES:])
+    )
     for copy in copies[7:]:
         copy.wait()
     edges = edge_values(table_ref, weight_ref, *ring[:6])
     east = jnp.where(second, east1, east0) != 0
     ends = [jnp.where(east, part[NODES - NP :], part[:NP]) for part in edges]
-    out0_ref[...], out1_ref[...] = packed(strip_rows(strip, east, 0, ends))
+    ends[2] = ends[2] * sign
+    strip[2] = strip[2] * sign
+    strip[5] = strip[5] * sign
+    for ref, part, flip in zip(
+        (out0_ref, out1_ref), packed(strip_rows(strip, east, 0, ends)), (flip0, flip1)
+    ):
+        if isinstance(flip, int):
+            ref[...] = turned(part) if flip else part
+        else:
+            ref[...] = jnp.where(flip != 0, turned(part), part)
     stored_ref[...] = stored
 
 

time: 21.9 us -> 21.9 us (level)
  transfers between devices with their start and end apart: 6 -> 6, of which waited for: 3 -> 3; matrix products, arithmetic and copies ran while one was open for 0% -> 0% of each run, Pallas kernels for 18% -> 17%
where the time goes in v17:
time: 21.9 us; the launch traced here: 21.7 us
  starting transfers between devices  10.5 us (48%)
  Pallas kernels  9.67 us (44%)
  waiting for transfers between devices  1.28 us (6%)
    pallas_call x7, Pallas kernels, call(): pl.pallas_call(kernel, out_shape=[jax.ShapeDtypeStruct(*out) for out in o...  9.67 us
    ppermute x4, starting transfers between devices, eastward(): lax.ppermute(value, both, [(rank(*a), rank(*b)) for a, b in pairs.items()])  8.99 us
    ppermute x2, starting transfers between devices, swapped(): return lax.ppermute(value, both, pairs)  1.54 us
    ppermute x4, waiting for transfers between devices, eastward(): lax.ppermute(value, both, [(rank(*a), rank(*b)) for a, b in pairs.items()])  1.28 us
  transfers between devices with their start and end apart: 6, of which 3 were waited for; matrix products, arithmetic and copies ran while one was open for 0% of the time, Pallas kernels for 17%

profile of v17, /device:TPU:0, one launch (start us, length us, event | category | flops | bytes accessed | tf_op | source)
XLA Modules:
  0.0 21.7 jit_solution(1407867103356429215)
XLA Ops:
  0.0 1.8 %strips.1 = (f32[216,128]{1,0:T(8,128)S(1)}, f32[216,128]{1,0:T(8,128)S(1)}, f32[448,256]{1,0:T(8,128)S(1)}) custom-call(s32[2,256]{1,0:T(2,128)} %seam_ref.5, s32[1,256]{1,0:T(1,128)} %slot_ref.3, f32[3,8,8,256]{3,2,1,0:T(8,128)} %refs_2_.1, f32[8,8,256]{2,1,0:T(8,128)} %refs_3_.1, f32[8,8,256]{2,1,0:T(8,128)} %refs_4_.1, f32[8,8,256]{2,1,0:T(8,128)} %refs_5_.1, ...), custom_call_target="tpu_custom_call" | custom-call | flops 100000000 | bytes 2097152 | tf_op jit(solution)/shard_map/strips/pallas_call | solution.py:708
  1.8 0.0 copy-start.3
  1.8 6.4 %collective-permute-start = (f32[216,128]{1,0:T(8,128)S(1)}, f32[216,128]{1,0:T(8,128)S(1)}, u32[]{:S(2)}, u32[]{:S(2)}) collective-permute-start(f32[216,128]{1,0:T(8,128)S(1)} %get-tuple-element.17.strip1_ref), channel_id=1, source_target_pairs={{0,31},{1,30},{2,29},{3,28},{4,27},{5,26},{6,25},{7,24},{8,23},{9,... | collective-permute-start | bytes 331784 | tf_op jit(solution)/shard_map/ppermute | solution.py:793
  8.2 0.5 %collective-permute-start.1 = (f32[216,128]{1,0:T(8,128)S(1)}, f32[216,128]{1,0:T(8,128)S(1)}, u32[]{:S(2)}, u32[]{:S(2)}) collective-permute-start(f32[216,128]{1,0:T(8,128)S(1)} %get-tuple-element.18.strip0_ref), channel_id=1, source_target_pairs={{0,16},{1,17},{2,18},{3,19},{4,20},{5,21},{6,22},{7,23},{8,24},{9,... | collective-permute-start | bytes 331784 | tf_op jit(solution)/shard_map/ppermute | solution.py:793
  8.8 0.0 copy-done
  8.8 0.0 copy-done.2
  8.8 0.0 copy-done.3
  8.8 0.1 copy-done.4
  8.9 1.4 %rows.1 = (f32[216,128]{1,0:T(8,128)S(1)}, f32[56,128]{1,0:T(8,128)S(1)}, f32[56,128]{1,0:T(8,128)S(1)}, f32[216,128]{1,0:T(8,128)S(1)}) custom-call(s32[2,256]{1,0:T(2,128)S(1)} %copy-done.3, f32[448,256]{1,0:T(8,128)S(1)} %get-tuple-element.19.stored_ref, f32[216,128]{1,0:T(8,128)S(1)} %get-tuple-element.17.strip1_ref, ...), custom_call_target="tpu_custom_call" | custom-call | flops 100000000 | bytes 2097152 | tf_op jit(solution)/shard_map/rows/pallas_call | solution.py:708
  10.3 1.4 %collective-permute-start.3 = (f32[216,128]{1,0:T(8,128)S(1)}, f32[216,128]{1,0:T(8,128)S(1)}, u32[]{:S(2)}, u32[]{:S(2)}) collective-permute-start(f32[216,128]{1,0:T(8,128)S(1)} %get-tuple-element.22), channel_id=1, source_target_pairs={{0,16},{1,2},{2,1},{3,4},{4,3},{5,6},{6,5},{7,8},{8,7},{9,10},{10,... | collective-permute-start | bytes 331784 | tf_op jit(solution)/shard_map/ppermute | solution.py:774
  11.7 0.6 %collective-permute-start.4 = (f32[56,128]{1,0:T(8,128)S(1)}, f32[56,128]{1,0:T(8,128)S(1)}, u32[]{:S(2)}, u32[]{:S(2)}) collective-permute-start(f32[56,128]{1,0:T(8,128)S(1)} %get-tuple-element.23), channel_id=1, source_target_pairs={{0,16},{1,29},{2,30},{3,27},{4,28},{5,25},{6,26},{7,23},{8,24},{9,... | collective-permute-start | bytes 86024 | tf_op jit(solution)/shard_map/ppermute | solution.py:793
  12.4 1.4 %collective-permute-start.5 = (f32[56,128]{1,0:T(8,128)S(1)}, f32[56,128]{1,0:T(8,128)S(1)}, u32[]{:S(2)}, u32[]{:S(2)}) collective-permute-start(f32[56,128]{1,0:T(8,128)S(1)} %get-tuple-element.24), channel_id=1, source_target_pairs={{0,16},{1,18},{2,17},{3,20},{4,19},{5,22},{6,21},{7,24},{8,23},{9,... | collective-permute-start | bytes 86024 | tf_op jit(solution)/shard_map/ppermute | solution.py:793
  13.8 0.0 copy-done.1
  13.8 0.5 %own.1 = (f32[448,384]{1,0:T(8,128)S(1)}, bf16[384,256]{1,0:T(8,128)(2,1)S(1)}) custom-call(f32[448,256]{1,0:T(8,128)S(1)} %get-tuple-element.19.stored_ref, s32[1,256]{1,0:T(1,128)S(1)} %copy-done.4, s32[56,640]{1,0:T(8,128)S(1)} %copy-done.1), custom_call_target="tpu_custom_call" | custom-call | flops 100000000 | bytes 2097152 | tf_op jit(solution)/shard_map/own/pallas_call | solution.py:708
  14.3 0.0 collective-permute-done.in1_ref
  14.3 0.5 %collective-permute-done.1.in0_ref = f32[216,128]{1,0:T(8,128)S(1)} collective-permute-done((f32[216,128]{1,0:T(8,128)S(1)}, f32[216,128]{1,0:T(8,128)S(1)}, u32[]{:S(2)}, u32[]{:S(2)}) %collective-permute-start.1) | collective-permute-done | bytes 110624 | tf_op jit(solution)/shard_map/ppermute | solution.py:793
  14.8 0.5 %corners.1 = f32[328,128]{1,0:T(8,128)S(1)} custom-call(f32[216,128]{1,0:T(8,128)S(1)} %collective-permute-done.in1_ref, f32[216,128]{1,0:T(8,128)S(1)} %collective-permute-done.1.in0_ref, f32[216,128]{1,0:T(8,128)S(1)} %get-tuple-element.20.pair_ref, f32[320,256]{1,0:T(8,128)S(1)} %copy-done, f32[64,128]{1,0:T(8,128)S(1)} %copy-done.2, ...), custom_call_target="tpu_custom_call" | custom-call | flops 100000000 | bytes 2097152 | tf_op jit(solution)/shard_map/corners/pallas_call | solution.py:708
  15.3 0.1 collective-permute-start.2
  15.4 1.4 %middle.1 = (f32[704,128]{1,0:T(8,128)S(1)}, f32[704,128]{1,0:T(8,128)S(1)}, f32[704,128]{1,0:T(8,128)S(1)}) custom-call(s32[2,256]{1,0:T(2,128)S(1)} %copy-done.3, f32[216,128]{1,0:T(8,128)S(1)} %collective-permute-done.1.in0_ref, f32[216,128]{1,0:T(8,128)S(1)} %collective-permute-done.in1_ref, f32[448,384]{1,0:T(8,128)S(1)} %get-tuple-element.25.own_ref, ...), custom_call_target="tpu_custom_call" | custom-call | flops 100000000 | bytes 2097152 | tf_op jit(solution)/shard_map/middle/pallas_call | solution.py:708
  16.8 0.4 %collective-permute-done.4.far1_ref = f32[56,128]{1,0:T(8,128)S(1)} collective-permute-done((f32[56,128]{1,0:T(8,128)S(1)}, f32[56,128]{1,0:T(8,128)S(1)}, u32[]{:S(2)}, u32[]{:S(2)}) %collective-permute-start.4) | collective-permute-done | bytes 28704 | tf_op jit(solution)/shard_map/ppermute | solution.py:793
  17.2 0.3 %collective-permute-done.5.far0_ref = f32[56,128]{1,0:T(8,128)S(1)} collective-permute-done((f32[56,128]{1,0:T(8,128)S(1)}, f32[56,128]{1,0:T(8,128)S(1)}, u32[]{:S(2)}, u32[]{:S(2)}) %collective-permute-start.5) | collective-permute-done | bytes 28704 | tf_op jit(solution)/shard_map/ppermute | solution.py:793
  17.5 0.0 collective-permute-done.3.refs_0_.next_ref
  17.5 0.0 collective-permute-done.2.pair_ref
  17.5 4.2 %steps.1 = f32[3,8,8,256]{3,2,1,0:T(8,128)} custom-call(s32[2,256]{1,0:T(2,128)S(1)} %copy-done.3, f32[328,128]{1,0:T(8,128)S(1)} %collective-permute-done.2.pair_ref, f32[216,128]{1,0:T(8,128)S(1)} %collective-permute-done.3.refs_0_.next_ref, f32[112,128]{1,0:T(8,128)S(1)} %far.1.far_ref, f32[704,128]{1,0:T(8,128)S(1)} %get-tuple-element.26.refs_1_.low_ref, ...), custom_call_target="tpu_custom_call" | custom-call | flops 100000000 | bytes 2097152 | tf_op jit(solution)/shard_map/steps/pallas_call | solution.py:708
  (5 shorter events, 0.0 us)
Async XLA Ops:
  0.0 8.8 %copy-start = (f32[320,256]{1,0:T(8,128)S(1)}, f32[320,256]{1,0:T(8,128)}, u32[]{:S(2)}) copy-start(f32[320,256]{1,0:T(8,128)} %constant.6.clone.refs_7_.table_ref) | copy-start | bytes 983044
  0.0 8.8 %copy-start.2 = (f32[64,128]{1,0:T(8,128)S(1)}, f32[64,128]{1,0:T(8,128)}, u32[]{:S(2)}) copy-start(f32[64,128]{1,0:T(8,128)} %constant.7.clone.refs_8_.weight_ref) | copy-start | bytes 98308
  1.8 7.0 %copy-start.3 = (s32[2,256]{1,0:T(2,128)S(1)}, s32[2,256]{1,0:T(2,128)}, u32[]{:S(2)}) copy-start(s32[2,256]{1,0:T(2,128)} %seam_ref.5) | copy-start | bytes 6148
  1.8 12.5 %collective-permute-start = (f32[216,128]{1,0:T(8,128)S(1)}, f32[216,128]{1,0:T(8,128)S(1)}, u32[]{:S(2)}, u32[]{:S(2)}) collective-permute-start(f32[216,128]{1,0:T(8,128)S(1)} %get-tuple-element.17.strip1_ref), channel_id=1, source_target_pairs={{0,31},{1,30},{2,29},{3,28},{4,27},{5,26},{6,25},{7,24},{8,23},{9,... | collective-permute-start | bytes 331784 | tf_op jit(solution)/shard_map/ppermute | solution.py:793
  8.2 0.7 %copy-start.4 = (s32[1,256]{1,0:T(1,128)S(1)}, s32[1,256]{1,0:T(1,128)}, u32[]{:S(2)}) copy-start(s32[1,256]{1,0:T(1,128)} %slot_ref.3) | copy-start | bytes 3076
  8.2 6.6 %collective-permute-start.1 = (f32[216,128]{1,0:T(8,128)S(1)}, f32[216,128]{1,0:T(8,128)S(1)}, u32[]{:S(2)}, u32[]{:S(2)}) collective-permute-start(f32[216,128]{1,0:T(8,128)S(1)} %get-tuple-element.18.strip0_ref), channel_id=1, source_target_pairs={{0,16},{1,17},{2,18},{3,19},{4,20},{5,21},{6,22},{7,23},{8,24},{9,... | collective-permute-start | bytes 331784 | tf_op jit(solution)/shard_map/ppermute | solution.py:793
  8.9 4.8 %copy-start.1 = (s32[56,640]{1,0:T(8,128)S(1)}, s32[56,640]{1,0:T(8,128)}, u32[]{:S(2)}) copy-start(s32[56,640]{1,0:T(8,128)} %constant.8.clone.lanes_ref) | copy-start | bytes 430084
  10.3 7.2 %collective-permute-start.3 = (f32[216,128]{1,0:T(8,128)S(1)}, f32[216,128]{1,0:T(8,128)S(1)}, u32[]{:S(2)}, u32[]{:S(2)}) collective-permute-start(f32[216,128]{1,0:T(8,128)S(1)} %get-tuple-element.22), channel_id=1, source_target_pairs={{0,16},{1,2},{2,1},{3,4},{4,3},{5,6},{6,5},{7,8},{8,7},{9,10},{10,... | collective-permute-start | bytes 331784 | tf_op jit(solution)/shard_map/ppermute | solution.py:774
  11.7 5.5 %collective-permute-start.4 = (f32[56,128]{1,0:T(8,128)S(1)}, f32[56,128]{1,0:T(8,128)S(1)}, u32[]{:S(2)}, u32[]{:S(2)}) collective-permute-start(f32[56,128]{1,0:T(8,128)S(1)} %get-tuple-element.23), channel_id=1, source_target_pairs={{0,16},{1,29},{2,30},{3,27},{4,28},{5,25},{6,26},{7,23},{8,24},{9,... | collective-permute-start | bytes 86024 | tf_op jit(solution)/shard_map/ppermute | solution.py:793
  12.4 5.1 %collective-permute-start.5 = (f32[56,128]{1,0:T(8,128)S(1)}, f32[56,128]{1,0:T(8,128)S(1)}, u32[]{:S(2)}, u32[]{:S(2)}) collective-permute-start(f32[56,128]{1,0:T(8,128)S(1)} %get-tuple-element.24), channel_id=1, source_target_pairs={{0,16},{1,18},{2,17},{3,20},{4,19},{5,22},{6,21},{7,24},{8,23},{9,... | collective-permute-start | bytes 86024 | tf_op jit(solution)/shard_map/ppermute | solution.py:793
  15.3 2.2 %collective-permute-start.2 = (f32[328,128]{1,0:T(8,128)S(1)}, f32[328,128]{1,0:T(8,128)S(1)}, u32[]{:S(2)}, u32[]{:S(2)}) collective-permute-start(f32[328,128]{1,0:T(8,128)S(1)} %corners.1), channel_id=1, source_target_pairs={{0,1},{1,0},{2,3},{3,2},{4,5},{5,4},{6,7},{7,6},{8,9},{9,8},{10,11... | collective-permute-start | bytes 503816 | tf_op jit(solution)/shard_map/ppermute | solution.py:774

commit v18 on v17

--- a/solution.py
+++ b/solution.py
@@ -427,7 +427,7 @@
     pair_ref[...], next_ref[...] = packed(strip_rows(rows, up, 4, rim))
 
 
-def corners_kernel(in1_ref, in0_ref, pair_ref, table_ref, weight_ref, *refs):
+def corners_kernel(in0_ref, in1_ref, pair_ref, table_ref, weight_ref, *refs):
     out_ref, sums = refs[-2:]
     top = 1 - (lax.axis_index("blk") & 1)
     whole = unpacked(in0_ref[...], in1_ref[...])
@@ -825,7 +825,7 @@
     )
     (to_pair,) = call(
         corners_kernel,
-        [(vmem, x) for x in (halo1, halo0, to_pair, table, weight, hot)],
+        [(vmem, x) for x in (halo0, halo1, to_pair, table, weight, hot)],
         [((HALF_ROWS + 2 * CORNER_ROWS, LANES), f32)],
         10**8,
         scratch=scratch,

time: 21.9 us -> 20.8 us (0.950)
  the two profiles are of different devices: /device:TPU:0 before, /device:TPU:9 now
where the time goes in v18:
time: 20.8 us; the launch traced here: 20.7 us
  Pallas kernels  9.67 us (46%)
  starting transfers between devices  8.71 us (42%)
  waiting for transfers between devices  2.19 us (11%)
    pallas_call x7, Pallas kernels, call(): pl.pallas_call(kernel, out_shape=[jax.ShapeDtypeStruct(*out) for out in o...  9.67 us
    ppermute x4, starting transfers between devices, eastward(): lax.ppermute(value, both, [(rank(*a), rank(*b)) for a, b in pairs.items()])  7.43 us
    ppermute x4, waiting for transfers between devices, eastward(): lax.ppermute(value, both, [(rank(*a), rank(*b)) for a, b in pairs.items()])  2.19 us
    ppermute x2, starting transfers between devices, swapped(): return lax.ppermute(value, both, pairs)  1.29 us
  transfers between devices with their start and end apart: 6, of which 1 were waited for; matrix products, arithmetic and copies ran while one was open for 0% of the time, Pallas kernels for 18%

profile of v18, /device:TPU:9, one launch (start us, length us, event | category | flops | bytes accessed | tf_op | source)
XLA Modules:
  0.0 20.7 jit_solution(4267597747916873825)
XLA Ops:
  0.0 1.8 %strips.1 = (f32[216,128]{1,0:T(8,128)S(1)}, f32[216,128]{1,0:T(8,128)S(1)}, f32[448,256]{1,0:T(8,128)S(1)}) custom-call(s32[2,256]{1,0:T(2,128)} %seam_ref.5, s32[1,256]{1,0:T(1,128)} %slot_ref.3, f32[3,8,8,256]{3,2,1,0:T(8,128)} %refs_2_.1, f32[8,8,256]{2,1,0:T(8,128)} %refs_3_.1, f32[8,8,256]{2,1,0:T(8,128)} %refs_4_.1, f32[8,8,256]{2,1,0:T(8,128)} %refs_5_.1, ...), custom_call_target="tpu_custom_call" | custom-call | flops 100000000 | bytes 2097152 | tf_op jit(solution)/shard_map/strips/pallas_call | solution.py:708
  1.8 0.0 copy-start.3
  1.8 1.3 %collective-permute-start = (f32[216,128]{1,0:T(8,128)S(1)}, f32[216,128]{1,0:T(8,128)S(1)}, u32[]{:S(2)}, u32[]{:S(2)}) collective-permute-start(f32[216,128]{1,0:T(8,128)S(1)} %get-tuple-element.17.strip0_ref), channel_id=1, source_target_pairs={{0,16},{1,17},{2,18},{3,19},{4,20},{5,21},{6,22},{7,23},{8,24},{9,... | collective-permute-start | bytes 331784 | tf_op jit(solution)/shard_map/ppermute | solution.py:793
  3.1 3.1 %collective-permute-start.1 = (f32[216,128]{1,0:T(8,128)S(1)}, f32[216,128]{1,0:T(8,128)S(1)}, u32[]{:S(2)}, u32[]{:S(2)}) collective-permute-start(f32[216,128]{1,0:T(8,128)S(1)} %get-tuple-element.18.strip1_ref), channel_id=1, source_target_pairs={{0,31},{1,30},{2,29},{3,28},{4,27},{5,26},{6,25},{7,24},{8,23},{9,... | collective-permute-start | bytes 331784 | tf_op jit(solution)/shard_map/ppermute | solution.py:793
  6.1 0.0 copy-done
  6.1 0.0 copy-done.2
  6.2 0.0 copy-done.3
  6.2 0.0 copy-done.4
  6.2 0.0 copy-start.1
  6.2 1.4 %rows.1 = (f32[216,128]{1,0:T(8,128)S(1)}, f32[56,128]{1,0:T(8,128)S(1)}, f32[56,128]{1,0:T(8,128)S(1)}, f32[216,128]{1,0:T(8,128)S(1)}) custom-call(s32[2,256]{1,0:T(2,128)S(1)} %copy-done.3, f32[448,256]{1,0:T(8,128)S(1)} %get-tuple-element.19.stored_ref, f32[216,128]{1,0:T(8,128)S(1)} %get-tuple-element.18.strip1_ref, ...), custom_call_target="tpu_custom_call" | custom-call | flops 100000000 | bytes 2097152 | tf_op jit(solution)/shard_map/rows/pallas_call | solution.py:708
  7.6 0.0 collective-permute-start.3
  7.6 1.2 %collective-permute-start.4 = (f32[56,128]{1,0:T(8,128)S(1)}, f32[56,128]{1,0:T(8,128)S(1)}, u32[]{:S(2)}, u32[]{:S(2)}) collective-permute-start(f32[56,128]{1,0:T(8,128)S(1)} %get-tuple-element.23), channel_id=1, source_target_pairs={{0,16},{1,29},{2,30},{3,27},{4,28},{5,25},{6,26},{7,23},{8,24},{9,... | collective-permute-start | bytes 86024 | tf_op jit(solution)/shard_map/ppermute | solution.py:793
  8.8 1.9 %collective-permute-start.5 = (f32[56,128]{1,0:T(8,128)S(1)}, f32[56,128]{1,0:T(8,128)S(1)}, u32[]{:S(2)}, u32[]{:S(2)}) collective-permute-start(f32[56,128]{1,0:T(8,128)S(1)} %get-tuple-element.24), channel_id=1, source_target_pairs={{0,16},{1,18},{2,17},{3,20},{4,19},{5,22},{6,21},{7,24},{8,23},{9,... | collective-permute-start | bytes 86024 | tf_op jit(solution)/shard_map/ppermute | solution.py:793
  10.7 0.5 %own.1 = (f32[448,384]{1,0:T(8,128)S(1)}, bf16[384,256]{1,0:T(8,128)(2,1)S(1)}) custom-call(f32[448,256]{1,0:T(8,128)S(1)} %get-tuple-element.19.stored_ref, s32[1,256]{1,0:T(1,128)S(1)} %copy-done.4, s32[56,640]{1,0:T(8,128)S(1)} %copy-done.1), custom_call_target="tpu_custom_call" | custom-call | flops 100000000 | bytes 2097152 | tf_op jit(solution)/shard_map/own/pallas_call | solution.py:708
  11.2 0.0 collective-permute-done.in0_ref
  11.2 2.2 %collective-permute-done.1.in1_ref = f32[216,128]{1,0:T(8,128)S(1)} collective-permute-done((f32[216,128]{1,0:T(8,128)S(1)}, f32[216,128]{1,0:T(8,128)S(1)}, u32[]{:S(2)}, u32[]{:S(2)}) %collective-permute-start.1) | collective-permute-done | bytes 110624 | tf_op jit(solution)/shard_map/ppermute | solution.py:793
  13.4 0.5 %corners.1 = f32[328,128]{1,0:T(8,128)S(1)} custom-call(f32[216,128]{1,0:T(8,128)S(1)} %collective-permute-done.in0_ref, f32[216,128]{1,0:T(8,128)S(1)} %collective-permute-done.1.in1_ref, f32[216,128]{1,0:T(8,128)S(1)} %get-tuple-element.20.pair_ref, f32[320,256]{1,0:T(8,128)S(1)} %copy-done, f32[64,128]{1,0:T(8,128)S(1)} %copy-done.2, ...), custom_call_target="tpu_custom_call" | custom-call | flops 100000000 | bytes 2097152 | tf_op jit(solution)/shard_map/corners/pallas_call | solution.py:708
  13.9 1.2 %collective-permute-start.2 = (f32[328,128]{1,0:T(8,128)S(1)}, f32[328,128]{1,0:T(8,128)S(1)}, u32[]{:S(2)}, u32[]{:S(2)}) collective-permute-start(f32[328,128]{1,0:T(8,128)S(1)} %corners.1), channel_id=1, source_target_pairs={{0,1},{1,0},{2,3},{3,2},{4,5},{5,4},{6,7},{7,6},{8,9},{9,8},{10,11... | collective-permute-start | bytes 503816 | tf_op jit(solution)/shard_map/ppermute | solution.py:774
  15.1 1.4 %middle.1 = (f32[704,128]{1,0:T(8,128)S(1)}, f32[704,128]{1,0:T(8,128)S(1)}, f32[704,128]{1,0:T(8,128)S(1)}) custom-call(s32[2,256]{1,0:T(2,128)S(1)} %copy-done.3, f32[216,128]{1,0:T(8,128)S(1)} %collective-permute-done.in0_ref, f32[216,128]{1,0:T(8,128)S(1)} %collective-permute-done.1.in1_ref, f32[448,384]{1,0:T(8,128)S(1)} %get-tuple-element.25.own_ref, ...), custom_call_target="tpu_custom_call" | custom-call | flops 100000000 | bytes 2097152 | tf_op jit(solution)/shard_map/middle/pallas_call | solution.py:708
  16.5 0.0 collective-permute-done.4.far1_ref
  16.5 0.0 collective-permute-done.5.far0_ref
  16.5 0.0 collective-permute-done.3.refs_0_.next_ref
  16.5 0.0 collective-permute-done.2.pair_ref
  16.5 4.2 %steps.1 = f32[3,8,8,256]{3,2,1,0:T(8,128)} custom-call(s32[2,256]{1,0:T(2,128)S(1)} %copy-done.3, f32[328,128]{1,0:T(8,128)S(1)} %collective-permute-done.2.pair_ref, f32[216,128]{1,0:T(8,128)S(1)} %collective-permute-done.3.refs_0_.next_ref, f32[112,128]{1,0:T(8,128)S(1)} %far.1.far_ref, f32[704,128]{1,0:T(8,128)S(1)} %get-tuple-element.26.refs_1_.low_ref, ...), custom_call_target="tpu_custom_call" | custom-call | flops 100000000 | bytes 2097152 | tf_op jit(solution)/shard_map/steps/pallas_call | solution.py:708
  (5 shorter events, 0.0 us)
Async XLA Ops:
  0.0 6.1 %copy-start = (f32[320,256]{1,0:T(8,128)S(1)}, f32[320,256]{1,0:T(8,128)}, u32[]{:S(2)}) copy-start(f32[320,256]{1,0:T(8,128)} %constant.6.clone.refs_7_.table_ref) | copy-start | bytes 983044
  0.0 6.1 %copy-start.2 = (f32[64,128]{1,0:T(8,128)S(1)}, f32[64,128]{1,0:T(8,128)}, u32[]{:S(2)}) copy-start(f32[64,128]{1,0:T(8,128)} %constant.7.clone.refs_8_.weight_ref) | copy-start | bytes 98308
  1.8 4.4 %copy-start.3 = (s32[2,256]{1,0:T(2,128)S(1)}, s32[2,256]{1,0:T(2,128)}, u32[]{:S(2)}) copy-start(s32[2,256]{1,0:T(2,128)} %seam_ref.5) | copy-start | bytes 6148
  1.8 9.4 %collective-permute-start = (f32[216,128]{1,0:T(8,128)S(1)}, f32[216,128]{1,0:T(8,128)S(1)}, u32[]{:S(2)}, u32[]{:S(2)}) collective-permute-start(f32[216,128]{1,0:T(8,128)S(1)} %get-tuple-element.17.strip0_ref), channel_id=1, source_target_pairs={{0,16},{1,17},{2,18},{3,19},{4,20},{5,21},{6,22},{7,23},{8,24},{9,... | collective-permute-start | bytes 331784 | tf_op jit(solution)/shard_map/ppermute | solution.py:793
  3.1 3.1 %copy-start.4 = (s32[1,256]{1,0:T(1,128)S(1)}, s32[1,256]{1,0:T(1,128)}, u32[]{:S(2)}) copy-start(s32[1,256]{1,0:T(1,128)} %slot_ref.3) | copy-start | bytes 3076
  3.1 10.3 %collective-permute-start.1 = (f32[216,128]{1,0:T(8,128)S(1)}, f32[216,128]{1,0:T(8,128)S(1)}, u32[]{:S(2)}, u32[]{:S(2)}) collective-permute-start(f32[216,128]{1,0:T(8,128)S(1)} %get-tuple-element.18.strip1_ref), channel_id=1, source_target_pairs={{0,31},{1,30},{2,29},{3,28},{4,27},{5,26},{6,25},{7,24},{8,23},{9,... | collective-permute-start | bytes 331784 | tf_op jit(solution)/shard_map/ppermute | solution.py:793
  6.2 4.5 %copy-start.1 = (s32[56,640]{1,0:T(8,128)S(1)}, s32[56,640]{1,0:T(8,128)}, u32[]{:S(2)}) copy-start(s32[56,640]{1,0:T(8,128)} %constant.8.clone.lanes_ref) | copy-start | bytes 430084
  7.6 8.9 %collective-permute-start.3 = (f32[216,128]{1,0:T(8,128)S(1)}, f32[216,128]{1,0:T(8,128)S(1)}, u32[]{:S(2)}, u32[]{:S(2)}) collective-permute-start(f32[216,128]{1,0:T(8,128)S(1)} %get-tuple-element.22), channel_id=1, source_target_pairs={{0,16},{1,2},{2,1},{3,4},{4,3},{5,6},{6,5},{7,8},{8,7},{9,10},{10,... | collective-permute-start | bytes 331784 | tf_op jit(solution)/shard_map/ppermute | solution.py:774
  7.6 8.9 %collective-permute-start.4 = (f32[56,128]{1,0:T(8,128)S(1)}, f32[56,128]{1,0:T(8,128)S(1)}, u32[]{:S(2)}, u32[]{:S(2)}) collective-permute-start(f32[56,128]{1,0:T(8,128)S(1)} %get-tuple-element.23), channel_id=1, source_target_pairs={{0,16},{1,29},{2,30},{3,27},{4,28},{5,25},{6,26},{7,23},{8,24},{9,... | collective-permute-start | bytes 86024 | tf_op jit(solution)/shard_map/ppermute | solution.py:793
  8.8 7.7 %collective-permute-start.5 = (f32[56,128]{1,0:T(8,128)S(1)}, f32[56,128]{1,0:T(8,128)S(1)}, u32[]{:S(2)}, u32[]{:S(2)}) collective-permute-start(f32[56,128]{1,0:T(8,128)S(1)} %get-tuple-element.24), channel_id=1, source_target_pairs={{0,16},{1,18},{2,17},{3,20},{4,19},{5,22},{6,21},{7,24},{8,23},{9,... | collective-permute-start | bytes 86024 | tf_op jit(solution)/shard_map/ppermute | solution.py:793
  13.9 2.6 %collective-permute-start.2 = (f32[328,128]{1,0:T(8,128)S(1)}, f32[328,128]{1,0:T(8,128)S(1)}, u32[]{:S(2)}, u32[]{:S(2)}) collective-permute-start(f32[328,128]{1,0:T(8,128)S(1)} %corners.1), channel_id=1, source_target_pairs={{0,1},{1,0},{2,3},{3,2},{4,5},{5,4},{6,7},{7,6},{8,9},{9,8},{10,11... | collective-permute-start | bytes 503816 | tf_op jit(solution)/shard_map/ppermute | solution.py:774

commit v19 on v18

--- a/solution.py
+++ b/solution.py
@@ -127,32 +127,36 @@
             table[8:16, lane] = row * RING + (col if x < 0 else x - GX)
         table[16:24, lane] = 0 if own else (1 if x < 0 else 2)
     ext = np.zeros((8, EXT), np.int32)
-    outer = np.zeros((24, 2 * LANES), np.int32)
+    outer = np.zeros((32, 2 * LANES), np.int32)
     for lane in range(EXT):
         row, col = divmod(lane - LEAD, PITCH)
         y = row - RING
         x = col - RING
-        inside = 0 <= row < GY + 2 * RING
         ext[0, lane] = x in (-RING, GX + RING - 1)
         ext[1, lane] = y == GY - 1
         ext[2, lane] = y == 0
         ext[3, lane] = 0 <= y < GY and 0 <= x < GX
         ext[4, lane] = y == -RING
         ext[5, lane] = y == GY + RING - 1
-        if inside and not 0 <= y < GY:
-            place = lane if y < 0 else lane - LANES - MID + LANES
+        if -RING - 1 <= y < 0 or GY <= y <= GY + RING:
+            place = lane if y < 0 else lane - MID
             step = y + RING if y < 0 else y - GY
+            near = step + 1 if y < 0 else step
+            far = 0 <= step < RING
             if 0 <= x < GX:
-                outer[0:8, place] = step * GX + x
+                outer[0:8, place] = near * GX + x
                 outer[8:16, place] = 1
+                outer[24:32, place] = LANES + step * GX + x if far else -1
             else:
-                outer[0:8, place] = LANES + step * RING + (x + RING if x < 0 else x - GX)
+                across = x + RING if x < 0 else x - GX
+                outer[0:8, place] = (RING + 1) * GX + near * RING + across
                 outer[8:16, place] = 2 if x < 0 else 3
+                outer[24:32, place] = LANES + RING * GX + step * RING + across if far else -1
             outer[16:24, place] = y > 0
-    whole = np.zeros((56, EXT), np.int32)
+    whole = np.zeros((64, EXT), np.int32)
     whole[0:24, :MID] = table
     whole[24:32] = ext
-    whole[32:56, : 2 * LANES] = outer
+    whole[32:64, : 2 * LANES] = outer
     return whole
 
 
@@ -398,22 +402,17 @@
 ):
     east0, flip0, east1, flip1 = seam_flags(seam_ref, block_cols)
     odd = lax.axis_index("blk") & 1
-
-    def goes_up(lane):
-        return jnp.where((lane & 64) != 0, odd, 1 - odd) != 0
-
     lane = lax.broadcasted_iota(i32, (8, 2 * LANES), 1)
-    up = goes_up(lane)
-    row = jnp.where(up, GY - RING, 0) + ((lane & 63) >> 4)
-    row = jnp.where(lane >= LANES, jnp.where(up, GY - RING - 1, RING), row)
+    row = jnp.where(odd != 0, GY - RING, 0) + ((lane & 63) >> 4)
+    row = jnp.where((lane & 64) != 0, jnp.where(odd != 0, GY - RING - 1, RING), row)
+    five = jnp.where(odd != 0, 0, GY - RING - 1) + jnp.minimum((lane & (LANES - 1)) >> 4, RING)
+    row = jnp.where(lane >= LANES, five, row)
     both = picked(stored_ref[...], by_slot(slot_ref, (lane & 15) * GY + row))
-    rows, behind = (
-        [part[k * NODES : (k + 1) * NODES] for k in range(ARRAYS)]
-        for part in (both[:, :LANES], both[:, LANES:])
-    )
+    pair_ref[...] = both[:, LANES:]
+    rows = [both[k * NODES : (k + 1) * NODES, :LANES] for k in range(ARRAYS)]
     whole = unpacked(strip0_ref[...], strip1_ref[...])
     strip = [whole[k * NODES : (k + 1) * NODES] for k in range(6)]
-    edges = edge_values(table_ref, weight_ref, *map(beside, strip, behind[:6]))
+    edges = edge_values(table_ref, weight_ref, *map(beside, strip, rows[:6]))
     sums[0] = jnp.concatenate([part[:, :LANES] for part in edges], 0)
     lane = lax.broadcasted_iota(i32, (1, LANES), 1)
     top0, top1 = odd ^ flip0, odd ^ flip1
@@ -421,22 +420,24 @@
     far0_ref[...] = corner_of(whole, 0, top0)
     far1_ref[...] = corner_of(whole, 64, top1)
     sums[0] = jnp.concatenate([part[:, LANES:] for part in edges], 0)
-    up = goes_up(lane)
-    rim = jnp.where(up, *row_edges(sums))
+    up = jnp.broadcast_to(odd != 0, (1, LANES))
+    rim = pltpu.roll(jnp.where(up, *row_edges(sums)), 64, 1)
     rim = [rim[k * NP : (k + 1) * NP] for k in range(4)]
-    pair_ref[...], next_ref[...] = packed(strip_rows(rows, up, 4, rim))
-
-
-def corners_kernel(in0_ref, in1_ref, pair_ref, table_ref, weight_ref, *refs):
-    out_ref, sums = refs[-2:]
+    whole = strip_rows(rows, up, 4, rim)
+    top, bottom = whole[:HALF_ROWS], whole[HALF_ROWS:]
+    next_ref[...] = jnp.where(lane >= 64, pltpu.roll(bottom, 64, 1), top)
+
+
+def corners_kernel(block_cols, seam_ref, in0_ref, in1_ref, pair_ref, _, out_ref):
+    east0, flip0, east1, flip1 = seam_flags(seam_ref, block_cols)
     top = 1 - (lax.axis_index("blk") & 1)
-    whole = unpacked(in0_ref[...], in1_ref[...])
-    parts = [whole[k * NODES : (k + 1) * NODES] for k in range(6)]
-    sums[0] = jnp.concatenate(edge_values(table_ref, weight_ref, *parts), 0)
-    whole = with_row_rim(whole, sums, jnp.broadcast_to(top != 0, (1, LANES)))
-    out_ref[:HALF_ROWS] = pair_ref[...]
-    out_ref[HALF_ROWS : HALF_ROWS + CORNER_ROWS] = corner_of(whole, 0, top)
-    out_ref[HALF_ROWS + CORNER_ROWS :] = corner_of(whole, 64, top)
+    lane = lax.broadcasted_iota(i32, (1, LANES), 1)
+    late = jnp.where(lane >= 64, east1, east0) == 0
+    whole = placed_rows(unpacked(in0_ref[...], in1_ref[...]), late, 0)
+    pair = jnp.concatenate([pair_ref[...], jnp.zeros((EDGE_ROWS, LANES), f32)], 0)
+    first = pltpu.roll(whole, jnp.where(top != 0, 36, 80), 1)
+    other = pltpu.roll(whole, jnp.where(top != 0, LANES - 8, 36), 1)
+    out_ref[...] = jnp.where(lane < 80, pair, jnp.where(lane < 100, first, other))
 
 
 def own_kernel(stored_ref, slot_ref, lanes_ref, own_ref, hot_ref):
@@ -500,36 +501,35 @@
     block_y = lax.rem(lax.axis_index("blk"), BY)
 
     lane = lax.broadcasted_iota(i32, (1, LANES), 1)
-    pair = pair_ref[...]
-    late = jnp.where(lane < 64, odd, 1 - odd) != 0
-    strips = placed_rows(unpacked(pair[:HALF_ROWS], next_ref[...]), late, 4)
-    strips = jnp.concatenate(
-        [strips[:ROWS], jnp.zeros((EDGE_ROWS, LANES), f32), strips[ROWS:]], 0
-    )
-    near = pair[HALF_ROWS:]
+    strip = jnp.concatenate([next_ref[...], pltpu.roll(next_ref[...], 64, 1)], 0)
+    strip = placed_rows(strip, jnp.broadcast_to(odd == 0, (1, LANES)), 4)
+    strip = jnp.concatenate(
+        [strip[:ROWS], jnp.zeros((EDGE_ROWS, LANES), f32), strip[ROWS:]], 0
+    )
     far = far_ref[...]
-    sources = (near[:CORNER_ROWS], near[CORNER_ROWS:], far[:CORNER_ROWS], far[CORNER_ROWS:])
     corners = []
     for k in range(8):
-        rows = None
-        for n, source in enumerate(sources):
-            shift = 16 * (n - k) % LANES
-            part = pltpu.roll(source, shift, 1) if shift else source
-            rows = part if n == 0 else jnp.where(lane >= 16 * n, part, rows)
-        corners.append(rows)
+        first = pltpu.roll(far[:CORNER_ROWS], (64 - 16 * k) % LANES, 1)
+        other = pltpu.roll(far[CORNER_ROWS:], (80 - 16 * k) % LANES, 1)
+        corners.append(jnp.where((lane & 16) == 0, first, other))
     corners = jnp.concatenate(corners, 0)
     rim = MOVED + NODES // 2 + NP
     late = jnp.where((lane & 16) != 0, east1, east0) == 0
-    below = jnp.where((lane & 32) != 0, 1 - odd, odd) != 0
+    below = jnp.broadcast_to(odd == 0, (1, LANES))
     corners = jnp.concatenate(
         [placed_rows(corners, late, 0)] + spread_out(corners[rim : rim + NP], below, 2), 0
     )
-    around = jnp.concatenate([strips, corners], 1)
-    kind = lanes_ref[40:48, : 2 * LANES]
-    sender = jnp.where(lanes_ref[48:56, : 2 * LANES] != 0, odd, 1 - odd)
-    strip_at = jnp.where(kind == 3, 16 * (1 - east0), 16 * east0)
-    place = lanes_ref[32:40, : 2 * LANES]
-    place = place + jnp.where(kind == 1, 64 * sender, 32 * sender + strip_at)
+    pair = jnp.concatenate([pair_ref[...], jnp.zeros((EDGE_ROWS, LANES), f32)], 0)
+    around = beside(pair, jnp.where(lane < 64, strip, corners))
+    outer_at = [lanes_ref[32 + 8 * k : 40 + 8 * k, : 2 * LANES] for k in range(4)]
+    kind = outer_at[1]
+    from_pair = jnp.where(outer_at[2] != 0, 1 - odd, odd) != 0
+    strip_at = jnp.where(kind == 3, 1 - east0, jnp.where(kind == 2, east0, 0))
+    place = jnp.where(
+        from_pair,
+        outer_at[0] + (RING + 1) * RING * strip_at,
+        jnp.where(outer_at[3] < 0, -1, outer_at[3] + RING * RING * strip_at),
+    )
     outer = picked(around, as_one_hot(jnp.where(kind == 0, -1, place), 2 * LANES))
     table = table_ref[...].astype(bf16)
     tiles = (None, low_ref, centre_ref, high_ref, None)
@@ -537,8 +537,8 @@
     masks = [lanes_ref[24:32, k * LANES : (k + 1) * LANES] for k in range(count)]
     closed_above = jnp.where(block_y == BY - 1, masks[-2][1:2], 0) != 0
     closed_below = jnp.where(block_y == 0, masks[1][2:3], 0) != 0
-    first_row = masks[0][4:5] != 0
-    last_row = masks[-1][5:6] != 0
+    first_row = jnp.where(odd == 0, masks[0][4:5], 0) != 0
+    last_row = jnp.where(odd != 0, masks[-1][5:6], 0) != 0
     outer_used = first_sums(
         table,
         weight_ref[...],
@@ -744,7 +744,7 @@
         functools.partial(rows_kernel, block_cols),
         [(smem, seam_rows)]
         + [(vmem, x) for x in (stored, strip1, strip0, slot_of, table, weight)],
-        [strip, corner, corner, strip],
+        [strip, corner, corner, ((ROWS, LANES), f32)],
         10**8,
         scratch=scratch,
         name="rows",
@@ -824,11 +824,10 @@
         name="own",
     )
     (to_pair,) = call(
-        corners_kernel,
-        [(vmem, x) for x in (halo0, halo1, to_pair, table, weight, hot)],
-        [((HALF_ROWS + 2 * CORNER_ROWS, LANES), f32)],
+        functools.partial(corners_kernel, block_cols),
+        [(smem, seam_rows)] + [(vmem, x) for x in (halo0, halo1, to_pair, hot)],
+        [((ALL_ROWS, LANES), f32)],
         10**8,
-        scratch=scratch,
         name="corners",
     )
     from_pair = swapped(to_pair, in_pair)

time: 20.8 us -> 21.1 us (1.014)
  the two profiles are of different devices: /device:TPU:9 before, /device:TPU:0 now
where the time goes in v19:
time: 21.1 us; the launch traced here: 20.7 us
  starting transfers between devices  10.6 us (50%)
  Pallas kernels  9.96 us (47%)
    pallas_call x7, Pallas kernels, call(): pl.pallas_call(kernel, out_shape=[jax.ShapeDtypeStruct(*out) for out in o...  9.96 us
    ppermute x4, starting transfers between devices, eastward(): lax.ppermute(value, both, [(rank(*a), rank(*b)) for a, b in pairs.items()])  8.71 us
    ppermute x2, starting transfers between devices, swapped(): return lax.ppermute(value, both, pairs)  1.9 us
  transfers between devices with their start and end apart: 6, of which 0 were waited for; matrix products, arithmetic and copies ran while one was open for 0% of the time, Pallas kernels for 20%

profile of v19, /device:TPU:0, one launch (start us, length us, event | category | flops | bytes accessed | tf_op | source)
XLA Modules:
  0.0 20.7 jit_solution(13605512304535411839)
XLA Ops:
  0.0 1.8 %strips.1 = (f32[216,128]{1,0:T(8,128)S(1)}, f32[216,128]{1,0:T(8,128)S(1)}, f32[448,256]{1,0:T(8,128)S(1)}) custom-call(s32[2,256]{1,0:T(2,128)} %seam_ref.7, s32[1,256]{1,0:T(1,128)} %slot_ref.3, f32[3,8,8,256]{3,2,1,0:T(8,128)} %refs_2_.1, f32[8,8,256]{2,1,0:T(8,128)} %refs_3_.1, f32[8,8,256]{2,1,0:T(8,128)} %refs_4_.1, f32[8,8,256]{2,1,0:T(8,128)} %refs_5_.1, ...), custom_call_target="tpu_custom_call" | custom-call | flops 100000000 | bytes 2097152 | tf_op jit(solution)/shard_map/strips/pallas_call | solution.py:708
  1.8 0.0 copy-start.3
  1.8 3.0 %collective-permute-start = (f32[216,128]{1,0:T(8,128)S(1)}, f32[216,128]{1,0:T(8,128)S(1)}, u32[]{:S(2)}, u32[]{:S(2)}) collective-permute-start(f32[216,128]{1,0:T(8,128)S(1)} %get-tuple-element.17.strip0_ref), channel_id=1, source_target_pairs={{0,16},{1,17},{2,18},{3,19},{4,20},{5,21},{6,22},{7,23},{8,24},{9,... | collective-permute-start | bytes 331784 | tf_op jit(solution)/shard_map/ppermute | solution.py:793
  4.8 3.7 %collective-permute-start.1 = (f32[216,128]{1,0:T(8,128)S(1)}, f32[216,128]{1,0:T(8,128)S(1)}, u32[]{:S(2)}, u32[]{:S(2)}) collective-permute-start(f32[216,128]{1,0:T(8,128)S(1)} %get-tuple-element.18.strip1_ref), channel_id=1, source_target_pairs={{0,31},{1,30},{2,29},{3,28},{4,27},{5,26},{6,25},{7,24},{8,23},{9,... | collective-permute-start | bytes 331784 | tf_op jit(solution)/shard_map/ppermute | solution.py:793
  8.5 0.0 copy-done
  8.5 0.0 copy-done.2
  8.5 0.0 copy-done.3
  8.5 0.0 copy-start.1
  8.5 1.4 %rows.1 = (f32[216,128]{1,0:T(8,128)S(1)}, f32[56,128]{1,0:T(8,128)S(1)}, f32[56,128]{1,0:T(8,128)S(1)}, f32[448,128]{1,0:T(8,128)S(1)}) custom-call(s32[2,256]{1,0:T(2,128)S(1)} %copy-done.3, f32[448,256]{1,0:T(8,128)S(1)} %get-tuple-element.19.stored_ref, f32[216,128]{1,0:T(8,128)S(1)} %get-tuple-element.18.strip1_ref, ...), custom_call_target="tpu_custom_call" | custom-call | flops 100000000 | bytes 2097152 | tf_op jit(solution)/shard_map/rows/pallas_call | solution.py:708
  9.9 1.5 %collective-permute-start.3 = (f32[216,128]{1,0:T(8,128)S(1)}, f32[216,128]{1,0:T(8,128)S(1)}, u32[]{:S(2)}, u32[]{:S(2)}) collective-permute-start(f32[216,128]{1,0:T(8,128)S(1)} %get-tuple-element.22), channel_id=1, source_target_pairs={{0,16},{1,2},{2,1},{3,4},{4,3},{5,6},{6,5},{7,8},{8,7},{9,10},{10,... | collective-permute-start | bytes 331784 | tf_op jit(solution)/shard_map/ppermute | solution.py:774
  11.5 0.5 %collective-permute-start.4 = (f32[56,128]{1,0:T(8,128)S(1)}, f32[56,128]{1,0:T(8,128)S(1)}, u32[]{:S(2)}, u32[]{:S(2)}) collective-permute-start(f32[56,128]{1,0:T(8,128)S(1)} %get-tuple-element.23), channel_id=1, source_target_pairs={{0,16},{1,29},{2,30},{3,27},{4,28},{5,25},{6,26},{7,23},{8,24},{9,... | collective-permute-start | bytes 86024 | tf_op jit(solution)/shard_map/ppermute | solution.py:793
  12.0 1.5 %collective-permute-start.5 = (f32[56,128]{1,0:T(8,128)S(1)}, f32[56,128]{1,0:T(8,128)S(1)}, u32[]{:S(2)}, u32[]{:S(2)}) collective-permute-start(f32[56,128]{1,0:T(8,128)S(1)} %get-tuple-element.24), channel_id=1, source_target_pairs={{0,16},{1,18},{2,17},{3,20},{4,19},{5,22},{6,21},{7,24},{8,23},{9,... | collective-permute-start | bytes 86024 | tf_op jit(solution)/shard_map/ppermute | solution.py:793
  13.5 0.0 copy-done.1
  13.5 0.5 %own.1 = (f32[448,384]{1,0:T(8,128)S(1)}, bf16[384,256]{1,0:T(8,128)(2,1)S(1)}) custom-call(f32[448,256]{1,0:T(8,128)S(1)} %get-tuple-element.19.stored_ref, s32[1,256]{1,0:T(1,128)S(1)} %copy-done.4, s32[64,640]{1,0:T(8,128)S(1)} %copy-done.1), custom_call_target="tpu_custom_call" | custom-call | flops 100000000 | bytes 2097152 | tf_op jit(solution)/shard_map/own/pallas_call | solution.py:708
  14.0 0.0 collective-permute-done.in0_ref
  14.0 0.0 collective-permute-done.1.in1_ref
  14.0 0.9 %corners.1 = f32[480,128]{1,0:T(8,128)S(1)} custom-call(s32[2,256]{1,0:T(2,128)S(1)} %copy-done.3, f32[216,128]{1,0:T(8,128)S(1)} %collective-permute-done.in0_ref, f32[216,128]{1,0:T(8,128)S(1)} %collective-permute-done.1.in1_ref, f32[448,128]{1,0:T(8,128)S(1)} %get-tuple-element.20.pair_ref, bf16[384,256]{1,0:T(8,128)(2,1)S(1)} %get-tuple-element.21._.hot_ref), custom_call_target="tpu_custom_call" | custom-call | flops 100000000 | bytes 2097152 | tf_op jit(solution)/shard_map/corners/pallas_call | solution.py:708
  14.9 0.4 %collective-permute-start.2 = (f32[480,128]{1,0:T(8,128)S(1)}, f32[480,128]{1,0:T(8,128)S(1)}, u32[]{:S(2)}, u32[]{:S(2)}) collective-permute-start(f32[480,128]{1,0:T(8,128)S(1)} %corners.1), channel_id=1, source_target_pairs={{0,1},{1,0},{2,3},{3,2},{4,5},{5,4},{6,7},{7,6},{8,9},{9,8},{10,11... | collective-permute-start | bytes 737288 | tf_op jit(solution)/shard_map/ppermute | solution.py:774
  15.3 1.3 %middle.1 = (f32[704,128]{1,0:T(8,128)S(1)}, f32[704,128]{1,0:T(8,128)S(1)}, f32[704,128]{1,0:T(8,128)S(1)}) custom-call(s32[2,256]{1,0:T(2,128)S(1)} %copy-done.3, f32[216,128]{1,0:T(8,128)S(1)} %collective-permute-done.in0_ref, f32[216,128]{1,0:T(8,128)S(1)} %collective-permute-done.1.in1_ref, f32[448,384]{1,0:T(8,128)S(1)} %get-tuple-element.25.own_ref, ...), custom_call_target="tpu_custom_call" | custom-call | flops 100000000 | bytes 2097152 | tf_op jit(solution)/shard_map/middle/pallas_call | solution.py:708
  16.6 0.0 collective-permute-done.4.far1_ref
  16.6 0.0 collective-permute-done.5.far0_ref
  16.7 0.0 collective-permute-done.3.refs_0_.next_ref
  16.7 0.0 collective-permute-done.2.pair_ref
  16.7 4.0 %steps.1 = f32[3,8,8,256]{3,2,1,0:T(8,128)} custom-call(s32[2,256]{1,0:T(2,128)S(1)} %copy-done.3, f32[480,128]{1,0:T(8,128)S(1)} %collective-permute-done.2.pair_ref, f32[216,128]{1,0:T(8,128)S(1)} %collective-permute-done.3.refs_0_.next_ref, f32[112,128]{1,0:T(8,128)S(1)} %far.1.far_ref, f32[704,128]{1,0:T(8,128)S(1)} %get-tuple-element.26.refs_1_.low_ref, ...), custom_call_target="tpu_custom_call" | custom-call | flops 100000000 | bytes 2097152 | tf_op jit(solution)/shard_map/steps/pallas_call | solution.py:708
  (5 shorter events, 0.0 us)
Async XLA Ops:
  0.0 8.5 %copy-start = (f32[320,256]{1,0:T(8,128)S(1)}, f32[320,256]{1,0:T(8,128)}, u32[]{:S(2)}) copy-start(f32[320,256]{1,0:T(8,128)} %constant.6.clone.refs_7_.table_ref) | copy-start | bytes 983044
  0.0 8.5 %copy-start.2 = (f32[64,128]{1,0:T(8,128)S(1)}, f32[64,128]{1,0:T(8,128)}, u32[]{:S(2)}) copy-start(f32[64,128]{1,0:T(8,128)} %constant.7.clone.refs_8_.weight_ref) | copy-start | bytes 98308
  1.8 6.7 %copy-start.3 = (s32[2,256]{1,0:T(2,128)S(1)}, s32[2,256]{1,0:T(2,128)}, u32[]{:S(2)}) copy-start(s32[2,256]{1,0:T(2,128)} %seam_ref.7) | copy-start | bytes 6148
  1.8 12.2 %collective-permute-start = (f32[216,128]{1,0:T(8,128)S(1)}, f32[216,128]{1,0:T(8,128)S(1)}, u32[]{:S(2)}, u32[]{:S(2)}) collective-permute-start(f32[216,128]{1,0:T(8,128)S(1)} %get-tuple-element.17.strip0_ref), channel_id=1, source_target_pairs={{0,16},{1,17},{2,18},{3,19},{4,20},{5,21},{6,22},{7,23},{8,24},{9,... | collective-permute-start | bytes 331784 | tf_op jit(solution)/shard_map/ppermute | solution.py:793
  4.8 3.7 %copy-start.4 = (s32[1,256]{1,0:T(1,128)S(1)}, s32[1,256]{1,0:T(1,128)}, u32[]{:S(2)}) copy-start(s32[1,256]{1,0:T(1,128)} %slot_ref.3) | copy-start | bytes 3076
  4.8 9.2 %collective-permute-start.1 = (f32[216,128]{1,0:T(8,128)S(1)}, f32[216,128]{1,0:T(8,128)S(1)}, u32[]{:S(2)}, u32[]{:S(2)}) collective-permute-start(f32[216,128]{1,0:T(8,128)S(1)} %get-tuple-element.18.strip1_ref), channel_id=1, source_target_pairs={{0,31},{1,30},{2,29},{3,28},{4,27},{5,26},{6,25},{7,24},{8,23},{9,... | collective-permute-start | bytes 331784 | tf_op jit(solution)/shard_map/ppermute | solution.py:793
  8.5 5.0 %copy-start.1 = (s32[64,640]{1,0:T(8,128)S(1)}, s32[64,640]{1,0:T(8,128)}, u32[]{:S(2)}) copy-start(s32[64,640]{1,0:T(8,128)} %constant.8.clone.lanes_ref) | copy-start | bytes 491524
  9.9 6.7 %collective-permute-start.3 = (f32[216,128]{1,0:T(8,128)S(1)}, f32[216,128]{1,0:T(8,128)S(1)}, u32[]{:S(2)}, u32[]{:S(2)}) collective-permute-start(f32[216,128]{1,0:T(8,128)S(1)} %get-tuple-element.22), channel_id=1, source_target_pairs={{0,16},{1,2},{2,1},{3,4},{4,3},{5,6},{6,5},{7,8},{8,7},{9,10},{10,... | collective-permute-start | bytes 331784 | tf_op jit(solution)/shard_map/ppermute | solution.py:774
  11.5 5.2 %collective-permute-start.4 = (f32[56,128]{1,0:T(8,128)S(1)}, f32[56,128]{1,0:T(8,128)S(1)}, u32[]{:S(2)}, u32[]{:S(2)}) collective-permute-start(f32[56,128]{1,0:T(8,128)S(1)} %get-tuple-element.23), channel_id=1, source_target_pairs={{0,16},{1,29},{2,30},{3,27},{4,28},{5,25},{6,26},{7,23},{8,24},{9,... | collective-permute-start | bytes 86024 | tf_op jit(solution)/shard_map/ppermute | solution.py:793
  12.0 4.7 %collective-permute-start.5 = (f32[56,128]{1,0:T(8,128)S(1)}, f32[56,128]{1,0:T(8,128)S(1)}, u32[]{:S(2)}, u32[]{:S(2)}) collective-permute-start(f32[56,128]{1,0:T(8,128)S(1)} %get-tuple-element.24), channel_id=1, source_target_pairs={{0,16},{1,18},{2,17},{3,20},{4,19},{5,22},{6,21},{7,24},{8,23},{9,... | collective-permute-start | bytes 86024 | tf_op jit(solution)/shard_map/ppermute | solution.py:793
  14.9 1.8 %collective-permute-start.2 = (f32[480,128]{1,0:T(8,128)S(1)}, f32[480,128]{1,0:T(8,128)S(1)}, u32[]{:S(2)}, u32[]{:S(2)}) collective-permute-start(f32[480,128]{1,0:T(8,128)S(1)} %corners.1), channel_id=1, source_target_pairs={{0,1},{1,0},{2,3},{3,2},{4,5},{5,4},{6,7},{7,6},{8,9},{9,8},{10,11... | collective-permute-start | bytes 737288 | tf_op jit(solution)/shard_map/ppermute | solution.py:774

commit v20 on v19

--- a/solution.py
+++ b/solution.py
@@ -286,16 +286,47 @@
     return jnp.concatenate([whole[: MOVED + NODES // 2 + NP], rim], 0)
 
 
+def in_eight(whole):
+    whole = jnp.concatenate([whole, jnp.zeros((8 * CORNER_ROWS - whole.shape[0], LANES), f32)], 0)
+    return [whole[k * CORNER_ROWS : (k + 1) * CORNER_ROWS] for k in range(8)]
+
+
 def corner_of(whole, start, top):
     lane = lax.broadcasted_iota(i32, (1, LANES), 1)
-    base = LANES - start - jnp.where(top != 0, 48, 0)
-    whole = jnp.concatenate([whole, jnp.zeros((8 * CORNER_ROWS - whole.shape[0], LANES), f32)], 0)
     out = None
-    for k in range(8):
-        part = whole[k * CORNER_ROWS : (k + 1) * CORNER_ROWS]
-        part = pltpu.roll(part, (base + 16 * k) & (LANES - 1), 1)
+    for k, part in enumerate(in_eight(whole)):
+        last = pltpu.roll(part, (LANES - start - 48 + 16 * k) % LANES, 1)
+        first = pltpu.roll(part, (LANES - start + 16 * k) % LANES, 1)
+        part = jnp.where(top != 0, last, first)
         out = part if k == 0 else jnp.where(lane >= 16 * k, part, out)
     return out
+
+
+def both_corners(whole, odd):
+    group = lax.broadcasted_iota(i32, (1, LANES), 1) >> 4
+    other_group = (group + jnp.where(odd != 0, 7, 1)) & 7
+    first, other = None, None
+    for k, part in enumerate(in_eight(whole)):
+        part = pltpu.roll(part, (LANES + 16 * k - 48 * odd) & (LANES - 1), 1)
+        first = part if k == 0 else jnp.where(group == k, part, first)
+        other = part if k == 0 else jnp.where(other_group == k, part, other)
+    return first, other
+
+
+def arrived_corners(far, block_cols, odd):
+    lane = lax.broadcasted_iota(i32, (1, LANES), 1)
+    far0, far1 = far[:CORNER_ROWS], far[CORNER_ROWS:]
+    corners = []
+    for k in range(8):
+        if block_cols == 1:
+            part = jnp.where((lane >> 4) == k, far0, far1)
+            part = pltpu.roll(part, (LANES + 64 + 16 * (1 - odd) - 16 * k) & (LANES - 1), 1)
+        else:
+            first = pltpu.roll(far0, (64 - 16 * k) % LANES, 1)
+            other = pltpu.roll(far1, (80 - 16 * k) % LANES, 1)
+            part = jnp.where((lane & 16) == 0, first, other)
+        corners.append(part)
+    return jnp.concatenate(corners, 0), ((lane >> 4) & 1) ^ (1 - odd if block_cols == 1 else 0)
 
 
 def packed(whole):
@@ -333,9 +364,13 @@
     return 1, at_east, 0, at_west
 
 
+def flags_in(flags_ref, tiles=1):
+    return [jnp.concatenate([flags_ref[k : k + 1]] * tiles, 1) for k in range(4)]
+
+
 def strips_kernel(block_cols, *refs):
-    sources, (out1_ref, out0_ref, stored_ref) = refs[:9], refs[9:12]
-    buffers, sems = refs[12:21], refs[21]
+    sources, (out1_ref, out0_ref, stored_ref, flags_ref) = refs[:9], refs[9:13]
+    buffers, sems = refs[13:22], refs[22]
     copies = [
         pltpu.make_async_copy(source, buffer, sems.at[k])
         for k, (source, buffer) in enumerate(zip(sources, buffers))
@@ -346,7 +381,9 @@
     table_ref, weight_ref = buffers[7:]
     for copy in copies[:2]:
         copy.wait()
-    east0, flip0, east1, flip1 = seam_flags(seam_ref, block_cols)
+    east0, flip0, east1, flip1 = flags = seam_flags(seam_ref, block_cols)
+    index = lax.broadcasted_iota(i32, (8, LANES), 0)
+    flags_ref[...] = sum(jnp.where(index == k, flag, 0) for k, flag in enumerate(flags))
     lane = lax.broadcasted_iota(i32, (8, 2 * LANES), 1)
     second = (lane & 64) != 0
     place = lane & 63
@@ -397,10 +434,10 @@
 
 
 def rows_kernel(
-    block_cols, seam_ref, stored_ref, strip1_ref, strip0_ref, slot_ref, table_ref, weight_ref,
+    block_cols, flags_ref, stored_ref, strip1_ref, strip0_ref, slot_ref, table_ref, weight_ref,
     next_ref, far0_ref, far1_ref, pair_ref, sums,
 ):
-    east0, flip0, east1, flip1 = seam_flags(seam_ref, block_cols)
+    east0, flip0, east1, flip1 = flags_in(flags_ref)
     odd = lax.axis_index("blk") & 1
     lane = lax.broadcasted_iota(i32, (8, 2 * LANES), 1)
     row = jnp.where(odd != 0, GY - RING, 0) + ((lane & 63) >> 4)
@@ -417,8 +454,11 @@
     lane = lax.broadcasted_iota(i32, (1, LANES), 1)
     top0, top1 = odd ^ flip0, odd ^ flip1
     whole = with_row_rim(whole, sums, jnp.where(lane >= 64, top1, top0) != 0)
-    far0_ref[...] = corner_of(whole, 0, top0)
-    far1_ref[...] = corner_of(whole, 64, top1)
+    if block_cols == 1:
+        far0_ref[...], far1_ref[...] = both_corners(whole, odd)
+    else:
+        far0_ref[...] = corner_of(whole, 0, top0)
+        far1_ref[...] = corner_of(whole, 64, top1)
     sums[0] = jnp.concatenate([part[:, LANES:] for part in edges], 0)
     up = jnp.broadcast_to(odd != 0, (1, LANES))
     rim = pltpu.roll(jnp.where(up, *row_edges(sums)), 64, 1)
@@ -428,16 +468,21 @@
     next_ref[...] = jnp.where(lane >= 64, pltpu.roll(bottom, 64, 1), top)
 
 
-def corners_kernel(block_cols, seam_ref, in0_ref, in1_ref, pair_ref, _, out_ref):
-    east0, flip0, east1, flip1 = seam_flags(seam_ref, block_cols)
+def corners_kernel(flags_ref, in0_ref, in1_ref, pair_ref, _, out_ref):
+    east0, flip0, east1, flip1 = flags_in(flags_ref)
     top = 1 - (lax.axis_index("blk") & 1)
     lane = lax.broadcasted_iota(i32, (1, LANES), 1)
-    late = jnp.where(lane >= 64, east1, east0) == 0
-    whole = placed_rows(unpacked(in0_ref[...], in1_ref[...]), late, 0)
-    pair = jnp.concatenate([pair_ref[...], jnp.zeros((EDGE_ROWS, LANES), f32)], 0)
-    first = pltpu.roll(whole, jnp.where(top != 0, 36, 80), 1)
-    other = pltpu.roll(whole, jnp.where(top != 0, LANES - 8, 36), 1)
-    out_ref[...] = jnp.where(lane < 80, pair, jnp.where(lane < 100, first, other))
+    halves = []
+    for start in (0, 64):
+        at0 = jnp.where(top != 0, 36, 80)
+        at1 = jnp.where(top != 0, 56, 100)
+        first = pltpu.roll(in0_ref[...], (at0 - start) & (LANES - 1), 1)
+        other = pltpu.roll(in1_ref[...], (at1 - start) & (LANES - 1), 1)
+        halves.append(jnp.where(lane < 100, first, other))
+    late = jnp.where(lane < 100, east0, east1) == 0
+    whole = placed_rows(jnp.concatenate(halves, 0), late, 0)
+    out_ref[:ROWS] = jnp.where(lane < 80, pair_ref[...], whole[:ROWS])
+    out_ref[ROWS:] = whole[ROWS:]
 
 
 def own_kernel(stored_ref, slot_ref, lanes_ref, own_ref, hot_ref):
@@ -463,15 +508,16 @@
 
 
 def middle_kernel(
-    block_cols, seam_ref, in0_ref, in1_ref, own_ref, lanes_ref, table_ref, weight_ref,
+    flags_ref, in0_ref, in1_ref, own_ref, lanes_ref, table_ref, weight_ref,
     low_ref, centre_ref, high_ref,
 ):
-    east0, flip0, east1, flip1 = seam_flags(seam_ref, block_cols)
+    east0, flip0, east1, flip1 = flags_in(flags_ref)
     second = lax.broadcasted_iota(i32, (1, LANES), 1) >= 64
     late = jnp.where(second, east1, east0) == 0
     whole = placed_rows(unpacked(in0_ref[...], in1_ref[...]), late, 0)
     side = lanes_ref[16:24, :MID]
-    first_at = jnp.where(side == 2, 64 * (1 - east0), 64 * east0)
+    east = flags_in(flags_ref, MID // LANES)[0]
+    first_at = jnp.where(side == 2, 64 * (1 - east), 64 * east)
     place = jnp.where(side == 0, -1, lanes_ref[8:16, :MID] + first_at)
     placed = picked(whole, as_one_hot(place, LANES))
     parts = [
@@ -493,10 +539,10 @@
 
 
 def steps_kernel(
-    block_cols, seam_ref, pair_ref, next_ref, far_ref, low_ref, centre_ref,
+    block_cols, flags_ref, pair_ref, next_ref, far_ref, low_ref, centre_ref,
     high_ref, hot_ref, table_ref, weight_ref, lanes_ref, out_ref, sums,
 ):
-    east0, flip0, east1, flip1 = seam_flags(seam_ref, block_cols)
+    east0, flip0, east1, flip1 = flags_in(flags_ref)
     odd = lax.axis_index("blk") & 1
     block_y = lax.rem(lax.axis_index("blk"), BY)
 
@@ -506,15 +552,9 @@
     strip = jnp.concatenate(
         [strip[:ROWS], jnp.zeros((EDGE_ROWS, LANES), f32), strip[ROWS:]], 0
     )
-    far = far_ref[...]
-    corners = []
-    for k in range(8):
-        first = pltpu.roll(far[:CORNER_ROWS], (64 - 16 * k) % LANES, 1)
-        other = pltpu.roll(far[CORNER_ROWS:], (80 - 16 * k) % LANES, 1)
-        corners.append(jnp.where((lane & 16) == 0, first, other))
-    corners = jnp.concatenate(corners, 0)
+    corners, strip_of = arrived_corners(far_ref[...], block_cols, odd)
     rim = MOVED + NODES // 2 + NP
-    late = jnp.where((lane & 16) != 0, east1, east0) == 0
+    late = jnp.where(strip_of != 0, east1, east0) == 0
     below = jnp.broadcast_to(odd == 0, (1, LANES))
     corners = jnp.concatenate(
         [placed_rows(corners, late, 0)] + spread_out(corners[rim : rim + NP], below, 2), 0
@@ -524,11 +564,14 @@
     outer_at = [lanes_ref[32 + 8 * k : 40 + 8 * k, : 2 * LANES] for k in range(4)]
     kind = outer_at[1]
     from_pair = jnp.where(outer_at[2] != 0, 1 - odd, odd) != 0
-    strip_at = jnp.where(kind == 3, 1 - east0, jnp.where(kind == 2, east0, 0))
+    east = flags_in(flags_ref, 2)[0]
+    strip_at = jnp.where(kind == 3, 1 - east, east)
+    far_at = strip_at ^ (1 - odd) if block_cols == 1 else strip_at
+    strip_at, far_at = (jnp.where(kind > 1, at, 0) for at in (strip_at, far_at))
     place = jnp.where(
         from_pair,
         outer_at[0] + (RING + 1) * RING * strip_at,
-        jnp.where(outer_at[3] < 0, -1, outer_at[3] + RING * RING * strip_at),
+        jnp.where(outer_at[3] < 0, -1, outer_at[3] + RING * RING * far_at),
     )
     outer = picked(around, as_one_hot(jnp.where(kind == 0, -1, place), 2 * LANES))
     table = table_ref[...].astype(bf16)
@@ -699,7 +742,6 @@
     table, weight = operator_table()
     table, weight, lanes = map(jnp.asarray, (table, weight, lane_tables()))
     vmem = pl.BlockSpec(memory_space=pltpu.VMEM)
-    smem = pl.BlockSpec(memory_space=pltpu.SMEM)
     hbm = pl.BlockSpec(memory_space=pltpu.HBM)
     params = pltpu.CompilerParams(vmem_limit_bytes=48 * 2**20)
     held = (fields, jacobian, water_depth, coriolis, tide_height)
@@ -732,18 +774,17 @@
     needed = (seam_rows, slot_of, *held, table, weight)
     corner = ((CORNER_ROWS, LANES), f32)
     scratch = [pltpu.VMEM((1, 4 * NODES, LANES), f32)]
-    strip1, strip0, stored = call(
+    strip1, strip0, stored, flags = call(
         functools.partial(strips_kernel, block_cols),
         [(hbm, x) for x in needed],
-        [strip, strip, ((ROWS, ELEMENTS), f32)],
+        [strip, strip, ((ROWS, ELEMENTS), f32), ((8, LANES), i32)],
         10**8,
         scratch=room(needed, [pltpu.SMEM] + [pltpu.VMEM] * (len(needed) - 1)),
         name="strips",
     )
     to_next, far0, far1, to_pair = call(
         functools.partial(rows_kernel, block_cols),
-        [(smem, seam_rows)]
-        + [(vmem, x) for x in (stored, strip1, strip0, slot_of, table, weight)],
+        [(vmem, x) for x in (flags, stored, strip1, strip0, slot_of, table, weight)],
         [strip, corner, corner, ((ROWS, LANES), f32)],
         10**8,
         scratch=scratch,
@@ -824,8 +865,8 @@
         name="own",
     )
     (to_pair,) = call(
-        functools.partial(corners_kernel, block_cols),
-        [(smem, seam_rows)] + [(vmem, x) for x in (halo0, halo1, to_pair, hot)],
+        corners_kernel,
+        [(vmem, x) for x in (flags, halo0, halo1, to_pair, hot)],
         [((ALL_ROWS, LANES), f32)],
         10**8,
         name="corners",
@@ -833,8 +874,8 @@
     from_pair = swapped(to_pair, in_pair)
     tile = ((11 * NODES, LANES), f32)
     low, centre, high = call(
-        functools.partial(middle_kernel, block_cols),
-        [(smem, seam_rows)] + [(vmem, x) for x in (halo0, halo1, own, lanes, table, weight)],
+        middle_kernel,
+        [(vmem, x) for x in (flags, halo0, halo1, own, lanes, table, weight)],
         [tile, tile, tile],
         10**8,
         name="middle",
@@ -848,12 +889,10 @@
     )
     (stepped,) = call(
         functools.partial(steps_kernel, block_cols),
-        [(smem, seam_rows)]
-        + [
+        [
             (vmem, x)
             for x in (
-                from_pair, from_next, far, low, centre, high,
-                hot, table, weight, lanes,
+                flags, from_pair, from_next, far, low, centre, high, hot, table, weight, lanes
             )
         ],
         [(fields.shape, f32)],

time: 21.1 us -> 19.8 us (0.938)
  the two profiles are of different devices: /device:TPU:0 before, /device:TPU:6 now
where the time goes in v20:
time: 19.8 us; the launch traced here: 19.7 us
  starting transfers between devices  8.17 us (41%)
  Pallas kernels  7.53 us (38%)
  waiting for transfers between devices  3.25 us (16%)
  local copies, waits for them, and re-layouts  0.68 us (3%)
    pallas_call x7, Pallas kernels, call(): pl.pallas_call(kernel, out_shape=[jax.ShapeDtypeStruct(*out) for out in o...  7.53 us
    ppermute x4, starting transfers between devices, eastward(): lax.ppermute(value, both, [(rank(*a), rank(*b)) for a, b in pairs.items()])  5.15 us
    ppermute x4, waiting for transfers between devices, eastward(): lax.ppermute(value, both, [(rank(*a), rank(*b)) for a, b in pairs.items()])  3.24 us
    ppermute x2, starting transfers between devices, swapped(): return lax.ppermute(value, both, pairs)  3.02 us
    unnamed x8, local copies, waits for them, and re-layouts  0.68 us
  transfers between devices with their start and end apart: 6, of which 2 were waited for; matrix products, arithmetic and copies ran while one was open for 0% of the time, Pallas kernels for 12%

profile of v20, /device:TPU:6, one launch (start us, length us, event | category | flops | bytes accessed | tf_op | source)
XLA Modules:
  0.0 19.7 jit_solution(7820787034713782420)
XLA Ops:
  0.0 0.0 copy-start
  0.0 0.0 copy-start.2
  0.0 1.8 %strips.1 = (f32[216,128]{1,0:T(8,128)S(1)}, f32[216,128]{1,0:T(8,128)S(1)}, f32[448,256]{1,0:T(8,128)S(1)}, s32[8,128]{1,0:T(8,128)S(1)}) custom-call(s32[2,256]{1,0:T(2,128)} %refs_0_.1, s32[1,256]{1,0:T(1,128)} %slot_ref.3, f32[3,8,8,256]{3,2,1,0:T(8,128)} %refs_2_.1, f32[8,8,256]{2,1,0:T(8,128)} %refs_3_.1, f32[8,8,256]{2,1,0:T(8,128)} %refs_4_.1, ...), custom_call_target="tpu_custom_call" | custom-call | flops 100000000 | bytes 2097152 | tf_op jit(solution)/shard_map/strips/pallas_call | solution.py:750
  1.8 0.6 %collective-permute-start = (f32[216,128]{1,0:T(8,128)S(1)}, f32[216,128]{1,0:T(8,128)S(1)}, u32[]{:S(2)}, u32[]{:S(2)}) collective-permute-start(f32[216,128]{1,0:T(8,128)S(1)} %get-tuple-element.19.strip0_ref), channel_id=1, source_target_pairs={{0,16},{1,17},{2,18},{3,19},{4,20},{5,21},{6,22},{7,23},{8,24},{9,... | collective-permute-start | bytes 331784 | tf_op jit(solution)/shard_map/ppermute | solution.py:834
  2.4 3.6 %collective-permute-start.1 = (f32[216,128]{1,0:T(8,128)S(1)}, f32[216,128]{1,0:T(8,128)S(1)}, u32[]{:S(2)}, u32[]{:S(2)}) collective-permute-start(f32[216,128]{1,0:T(8,128)S(1)} %get-tuple-element.20.strip1_ref), channel_id=1, source_target_pairs={{0,31},{1,30},{2,29},{3,28},{4,27},{5,26},{6,25},{7,24},{8,23},{9,... | collective-permute-start | bytes 331784 | tf_op jit(solution)/shard_map/ppermute | solution.py:834
  6.0 0.0 copy-done
  6.0 0.0 copy-done.2
  6.0 0.7 %copy-done.3 = s32[1,256]{1,0:T(1,128)S(1)} copy-done((s32[1,256]{1,0:T(1,128)S(1)}, s32[1,256]{1,0:T(1,128)}, u32[]{:S(2)}) %copy-start.3) | copy-done | bytes 1048
  6.7 0.8 %rows.1 = (f32[216,128]{1,0:T(8,128)S(1)}, f32[56,128]{1,0:T(8,128)S(1)}, f32[56,128]{1,0:T(8,128)S(1)}, f32[448,128]{1,0:T(8,128)S(1)}) custom-call(s32[8,128]{1,0:T(8,128)S(1)} %get-tuple-element.18.flags_ref, f32[448,256]{1,0:T(8,128)S(1)} %get-tuple-element.21.stored_ref, f32[216,128]{1,0:T(8,128)S(1)} %get-tuple-element.20.strip1_ref, ...), custom_call_target="tpu_custom_call" | custom-call | flops 100000000 | bytes 2097152 | tf_op jit(solution)/shard_map/rows/pallas_call | solution.py:750
  7.5 2.1 %collective-permute-start.3 = (f32[216,128]{1,0:T(8,128)S(1)}, f32[216,128]{1,0:T(8,128)S(1)}, u32[]{:S(2)}, u32[]{:S(2)}) collective-permute-start(f32[216,128]{1,0:T(8,128)S(1)} %get-tuple-element.24), channel_id=1, source_target_pairs={{0,16},{1,2},{2,1},{3,4},{4,3},{5,6},{6,5},{7,8},{8,7},{9,10},{10,... | collective-permute-start | bytes 331784 | tf_op jit(solution)/shard_map/ppermute | solution.py:815
  9.7 0.2 collective-permute-start.4
  9.9 0.7 %collective-permute-start.5 = (f32[56,128]{1,0:T(8,128)S(1)}, f32[56,128]{1,0:T(8,128)S(1)}, u32[]{:S(2)}, u32[]{:S(2)}) collective-permute-start(f32[56,128]{1,0:T(8,128)S(1)} %get-tuple-element.26), channel_id=1, source_target_pairs={{0,16},{1,18},{2,17},{3,20},{4,19},{5,22},{6,21},{7,24},{8,23},{9,... | collective-permute-start | bytes 86024 | tf_op jit(solution)/shard_map/ppermute | solution.py:834
  10.6 0.0 copy-done.1
  10.6 0.5 %own.1 = (f32[448,384]{1,0:T(8,128)S(1)}, bf16[384,256]{1,0:T(8,128)(2,1)S(1)}) custom-call(f32[448,256]{1,0:T(8,128)S(1)} %get-tuple-element.21.stored_ref, s32[1,256]{1,0:T(1,128)S(1)} %copy-done.3, s32[64,640]{1,0:T(8,128)S(1)} %copy-done.1), custom_call_target="tpu_custom_call" | custom-call | flops 100000000 | bytes 2097152 | tf_op jit(solution)/shard_map/own/pallas_call | solution.py:750
  11.1 0.0 collective-permute-done.in0_ref
  11.1 0.1 collective-permute-done.1.in1_ref
  11.2 0.2 %corners.1 = f32[480,128]{1,0:T(8,128)S(1)} custom-call(s32[8,128]{1,0:T(8,128)S(1)} %get-tuple-element.18.flags_ref, f32[216,128]{1,0:T(8,128)S(1)} %collective-permute-done.in0_ref, f32[216,128]{1,0:T(8,128)S(1)} %collective-permute-done.1.in1_ref, f32[448,128]{1,0:T(8,128)S(1)} %get-tuple-element.22.pair_ref, bf16[384,256]{1,0:T(8,128)(2,1)S(1)} %get-tuple-element.23._.hot_ref), custom_call_target="tpu_custom_call" | custom-call | flops 100000000 | bytes 2097152 | tf_op jit(solution)/shard_map/corners/pallas_call | solution.py:750
  11.4 0.9 %collective-permute-start.2 = (f32[480,128]{1,0:T(8,128)S(1)}, f32[480,128]{1,0:T(8,128)S(1)}, u32[]{:S(2)}, u32[]{:S(2)}) collective-permute-start(f32[480,128]{1,0:T(8,128)S(1)} %corners.1), channel_id=1, source_target_pairs={{0,1},{1,0},{2,3},{3,2},{4,5},{5,4},{6,7},{7,6},{8,9},{9,8},{10,11... | collective-permute-start | bytes 737288 | tf_op jit(solution)/shard_map/ppermute | solution.py:815
  12.3 0.8 %middle.1 = (f32[704,128]{1,0:T(8,128)S(1)}, f32[704,128]{1,0:T(8,128)S(1)}, f32[704,128]{1,0:T(8,128)S(1)}) custom-call(s32[8,128]{1,0:T(8,128)S(1)} %get-tuple-element.18.flags_ref, f32[216,128]{1,0:T(8,128)S(1)} %collective-permute-done.in0_ref, f32[216,128]{1,0:T(8,128)S(1)} %collective-permute-done.1.in1_ref, f32[448,384]{1,0:T(8,128)S(1)} %get-tuple-element.27.own_ref, ...), custom_call_target="tpu_custom_call" | custom-call | flops 100000000 | bytes 2097152 | tf_op jit(solution)/shard_map/middle/pallas_call | solution.py:750
  13.1 3.1 %collective-permute-done.4.far1_ref = f32[56,128]{1,0:T(8,128)S(1)} collective-permute-done((f32[56,128]{1,0:T(8,128)S(1)}, f32[56,128]{1,0:T(8,128)S(1)}, u32[]{:S(2)}, u32[]{:S(2)}) %collective-permute-start.4) | collective-permute-done | bytes 28704 | tf_op jit(solution)/shard_map/ppermute | solution.py:834
  16.2 0.0 collective-permute-done.5.far0_ref
  16.2 0.0 collective-permute-done.3.refs_0_.next_ref
  16.2 0.0 collective-permute-done.2.pair_ref
  16.3 3.4 %steps.1 = f32[3,8,8,256]{3,2,1,0:T(8,128)} custom-call(s32[8,128]{1,0:T(8,128)S(1)} %get-tuple-element.18.flags_ref, f32[480,128]{1,0:T(8,128)S(1)} %collective-permute-done.2.pair_ref, f32[216,128]{1,0:T(8,128)S(1)} %collective-permute-done.3.refs_0_.next_ref, f32[112,128]{1,0:T(8,128)S(1)} %far.1.far_ref, ...), custom_call_target="tpu_custom_call" | custom-call | flops 100000000 | bytes 2097152 | tf_op jit(solution)/shard_map/steps/pallas_call | solution.py:750
  (3 shorter events, 0.0 us)
Async XLA Ops:
  0.0 6.0 %copy-start = (f32[320,256]{1,0:T(8,128)S(1)}, f32[320,256]{1,0:T(8,128)}, u32[]{:S(2)}) copy-start(f32[320,256]{1,0:T(8,128)} %constant.6.clone.refs_7_.table_ref) | copy-start | bytes 983044
  0.0 6.0 %copy-start.2 = (f32[64,128]{1,0:T(8,128)S(1)}, f32[64,128]{1,0:T(8,128)}, u32[]{:S(2)}) copy-start(f32[64,128]{1,0:T(8,128)} %constant.7.clone.refs_8_.weight_ref) | copy-start | bytes 98308
  1.8 9.3 %collective-permute-start = (f32[216,128]{1,0:T(8,128)S(1)}, f32[216,128]{1,0:T(8,128)S(1)}, u32[]{:S(2)}, u32[]{:S(2)}) collective-permute-start(f32[216,128]{1,0:T(8,128)S(1)} %get-tuple-element.19.strip0_ref), channel_id=1, source_target_pairs={{0,16},{1,17},{2,18},{3,19},{4,20},{5,21},{6,22},{7,23},{8,24},{9,... | collective-permute-start | bytes 331784 | tf_op jit(solution)/shard_map/ppermute | solution.py:834
  2.4 8.8 %collective-permute-start.1 = (f32[216,128]{1,0:T(8,128)S(1)}, f32[216,128]{1,0:T(8,128)S(1)}, u32[]{:S(2)}, u32[]{:S(2)}) collective-permute-start(f32[216,128]{1,0:T(8,128)S(1)} %get-tuple-element.20.strip1_ref), channel_id=1, source_target_pairs={{0,31},{1,30},{2,29},{3,28},{4,27},{5,26},{6,25},{7,24},{8,23},{9,... | collective-permute-start | bytes 331784 | tf_op jit(solution)/shard_map/ppermute | solution.py:834
  6.0 0.7 %copy-start.3 = (s32[1,256]{1,0:T(1,128)S(1)}, s32[1,256]{1,0:T(1,128)}, u32[]{:S(2)}) copy-start(s32[1,256]{1,0:T(1,128)} %slot_ref.3) | copy-start | bytes 3076
  6.7 3.9 %copy-start.1 = (s32[64,640]{1,0:T(8,128)S(1)}, s32[64,640]{1,0:T(8,128)}, u32[]{:S(2)}) copy-start(s32[64,640]{1,0:T(8,128)} %constant.8.clone.lanes_ref) | copy-start | bytes 491524
  7.5 8.7 %collective-permute-start.3 = (f32[216,128]{1,0:T(8,128)S(1)}, f32[216,128]{1,0:T(8,128)S(1)}, u32[]{:S(2)}, u32[]{:S(2)}) collective-permute-start(f32[216,128]{1,0:T(8,128)S(1)} %get-tuple-element.24), channel_id=1, source_target_pairs={{0,16},{1,2},{2,1},{3,4},{4,3},{5,6},{6,5},{7,8},{8,7},{9,10},{10,... | collective-permute-start | bytes 331784 | tf_op jit(solution)/shard_map/ppermute | solution.py:815
  9.7 6.6 %collective-permute-start.4 = (f32[56,128]{1,0:T(8,128)S(1)}, f32[56,128]{1,0:T(8,128)S(1)}, u32[]{:S(2)}, u32[]{:S(2)}) collective-permute-start(f32[56,128]{1,0:T(8,128)S(1)} %get-tuple-element.25), channel_id=1, source_target_pairs={{0,16},{1,29},{2,30},{3,27},{4,28},{5,25},{6,26},{7,23},{8,24},{9,... | collective-permute-start | bytes 86024 | tf_op jit(solution)/shard_map/ppermute | solution.py:834
  9.9 6.4 %collective-permute-start.5 = (f32[56,128]{1,0:T(8,128)S(1)}, f32[56,128]{1,0:T(8,128)S(1)}, u32[]{:S(2)}, u32[]{:S(2)}) collective-permute-start(f32[56,128]{1,0:T(8,128)S(1)} %get-tuple-element.26), channel_id=1, source_target_pairs={{0,16},{1,18},{2,17},{3,20},{4,19},{5,22},{6,21},{7,24},{8,23},{9,... | collective-permute-start | bytes 86024 | tf_op jit(solution)/shard_map/ppermute | solution.py:834
  11.4 4.8 %collective-permute-start.2 = (f32[480,128]{1,0:T(8,128)S(1)}, f32[480,128]{1,0:T(8,128)S(1)}, u32[]{:S(2)}, u32[]{:S(2)}) collective-permute-start(f32[480,128]{1,0:T(8,128)S(1)} %corners.1), channel_id=1, source_target_pairs={{0,1},{1,0},{2,3},{3,2},{4,5},{5,4},{6,7},{7,6},{8,9},{9,8},{10,11... | collective-permute-start | bytes 737288 | tf_op jit(solution)/shard_map/ppermute | solution.py:815

commit v21 on v20

--- a/solution.py
+++ b/solution.py
@@ -182,11 +182,9 @@
     return [high, low, high]
 
 
-def by_slot(slot_ref, cell_of_lane):
+def by_slot(halves, cell_of_lane):
     size = cell_of_lane.shape[1]
-    halves = [
-        jnp.broadcast_to(slot_ref[:, k * LANES : (k + 1) * LANES], (8, LANES)) for k in range(2)
-    ]
+    halves = [jnp.broadcast_to(half, (8, LANES)) for half in halves]
     chosen = []
     for k in range(size // LANES):
         cell = cell_of_lane[:, k * LANES : (k + 1) * LANES]
@@ -313,9 +311,8 @@
     return first, other
 
 
-def arrived_corners(far, block_cols, odd):
+def arrived_corners(far0, far1, block_cols, odd):
     lane = lax.broadcasted_iota(i32, (1, LANES), 1)
-    far0, far1 = far[:CORNER_ROWS], far[CORNER_ROWS:]
     corners = []
     for k in range(8):
         if block_cols == 1:
@@ -362,6 +359,10 @@
     at_east = jnp.where(block_x == block_cols - 1, east_flip, 0)
     at_west = jnp.where(block_x == 0, west_flip, 0)
     return 1, at_east, 0, at_west
+
+
+def slots_in(flags_ref):
+    return flags_ref[4:5], flags_ref[5:6]
 
 
 def flags_in(flags_ref, tiles=1):
@@ -384,6 +385,8 @@
     east0, flip0, east1, flip1 = flags = seam_flags(seam_ref, block_cols)
     index = lax.broadcasted_iota(i32, (8, LANES), 0)
     flags_ref[...] = sum(jnp.where(index == k, flag, 0) for k, flag in enumerate(flags))
+    slots = slot_ref[:, :LANES], slot_ref[:, LANES:]
+    flags_ref[4:5], flags_ref[5:6] = slots
     lane = lax.broadcasted_iota(i32, (8, 2 * LANES), 1)
     second = (lane & 64) != 0
     place = lane & 63
@@ -392,7 +395,7 @@
     east = jnp.where(second, east1, east0) != 0
     col = jnp.where(east, GX - RING, 0) + (place & 3)
     col = jnp.where(lane >= LANES, jnp.where(east, GX - RING - 1, RING), col)
-    one_hot = by_slot(slot_ref, col * GY + row)
+    one_hot = by_slot(slots, col * GY + row)
     for copy in copies[2:7]:
         copy.wait()
     stored = stored_rows(fields_ref, (area_ref, depth_ref, spin_ref, tide_ref))
@@ -434,7 +437,7 @@
 
 
 def rows_kernel(
-    block_cols, flags_ref, stored_ref, strip1_ref, strip0_ref, slot_ref, table_ref, weight_ref,
+    block_cols, flags_ref, stored_ref, strip1_ref, strip0_ref, table_ref, weight_ref,
     next_ref, far0_ref, far1_ref, pair_ref, sums,
 ):
     east0, flip0, east1, flip1 = flags_in(flags_ref)
@@ -444,7 +447,7 @@
     row = jnp.where((lane & 64) != 0, jnp.where(odd != 0, GY - RING - 1, RING), row)
     five = jnp.where(odd != 0, 0, GY - RING - 1) + jnp.minimum((lane & (LANES - 1)) >> 4, RING)
     row = jnp.where(lane >= LANES, five, row)
-    both = picked(stored_ref[...], by_slot(slot_ref, (lane & 15) * GY + row))
+    both = picked(stored_ref[...], by_slot(slots_in(flags_ref), (lane & 15) * GY + row))
     pair_ref[...] = both[:, LANES:]
     rows = [both[k * NODES : (k + 1) * NODES, :LANES] for k in range(ARRAYS)]
     whole = unpacked(strip0_ref[...], strip1_ref[...])
@@ -485,8 +488,8 @@
     out_ref[ROWS:] = whole[ROWS:]
 
 
-def own_kernel(stored_ref, slot_ref, lanes_ref, own_ref, hot_ref):
-    one_hot = by_slot(slot_ref, lanes_ref[0:8, :MID])
+def own_kernel(flags_ref, stored_ref, lanes_ref, own_ref, hot_ref):
+    one_hot = by_slot(slots_in(flags_ref), lanes_ref[0:8, :MID])
     own_ref[...] = picked(stored_ref[...], one_hot)
     hot_ref[...] = one_hot.astype(f32).T.astype(bf16)
 
@@ -532,14 +535,26 @@
             ref[n * NODES : (n + 1) * NODES] = part[:, k * LANES : (k + 1) * LANES]
 
 
-def far_kernel(far1_ref, far0_ref, *refs):
-    out_ref = refs[-1]
-    out_ref[:CORNER_ROWS] = far0_ref[...]
-    out_ref[CORNER_ROWS:] = far1_ref[...]
+def far_kernel(block_cols, flags_ref, far1_ref, far0_ref, next_ref, _, out_ref):
+    east0, flip0, east1, flip1 = flags_in(flags_ref)
+    odd = lax.axis_index("blk") & 1
+    lane = lax.broadcasted_iota(i32, (1, LANES), 1)
+    below = jnp.broadcast_to(odd == 0, (1, LANES))
+    strip = jnp.concatenate([next_ref[...], pltpu.roll(next_ref[...], 64, 1)], 0)
+    strip = placed_rows(strip, below, 4)
+    corners, strip_of = arrived_corners(far0_ref[...], far1_ref[...], block_cols, odd)
+    late = jnp.where(strip_of != 0, east1, east0) == 0
+    rim = MOVED + NODES // 2 + NP
+    rim = jnp.concatenate(spread_out(corners[rim : rim + NP], below, 2), 0)
+    corners = placed_rows(corners, late, 0)
+    own = lane < 64
+    out_ref[:ROWS] = jnp.where(own, strip[:ROWS], corners[:ROWS])
+    out_ref[ROWS:ALL_ROWS] = corners[ROWS:]
+    out_ref[ALL_ROWS:] = jnp.where(own, strip[ROWS:], rim)
 
 
 def steps_kernel(
-    block_cols, flags_ref, pair_ref, next_ref, far_ref, low_ref, centre_ref,
+    block_cols, flags_ref, pair_ref, next_ref, low_ref, centre_ref,
     high_ref, hot_ref, table_ref, weight_ref, lanes_ref, out_ref, sums,
 ):
     east0, flip0, east1, flip1 = flags_in(flags_ref)
@@ -547,20 +562,8 @@
     block_y = lax.rem(lax.axis_index("blk"), BY)
 
     lane = lax.broadcasted_iota(i32, (1, LANES), 1)
-    strip = jnp.concatenate([next_ref[...], pltpu.roll(next_ref[...], 64, 1)], 0)
-    strip = placed_rows(strip, jnp.broadcast_to(odd == 0, (1, LANES)), 4)
-    strip = jnp.concatenate(
-        [strip[:ROWS], jnp.zeros((EDGE_ROWS, LANES), f32), strip[ROWS:]], 0
-    )
-    corners, strip_of = arrived_corners(far_ref[...], block_cols, odd)
-    rim = MOVED + NODES // 2 + NP
-    late = jnp.where(strip_of != 0, east1, east0) == 0
-    below = jnp.broadcast_to(odd == 0, (1, LANES))
-    corners = jnp.concatenate(
-        [placed_rows(corners, late, 0)] + spread_out(corners[rim : rim + NP], below, 2), 0
-    )
     pair = jnp.concatenate([pair_ref[...], jnp.zeros((EDGE_ROWS, LANES), f32)], 0)
-    around = beside(pair, jnp.where(lane < 64, strip, corners))
+    around = beside(pair, next_ref[...])
     outer_at = [lanes_ref[32 + 8 * k : 40 + 8 * k, : 2 * LANES] for k in range(4)]
     kind = outer_at[1]
     from_pair = jnp.where(outer_at[2] != 0, 1 - odd, odd) != 0
@@ -784,7 +787,7 @@
     )
     to_next, far0, far1, to_pair = call(
         functools.partial(rows_kernel, block_cols),
-        [(vmem, x) for x in (flags, stored, strip1, strip0, slot_of, table, weight)],
+        [(vmem, x) for x in (flags, stored, strip1, strip0, table, weight)],
         [strip, corner, corner, ((ROWS, LANES), f32)],
         10**8,
         scratch=scratch,
@@ -859,7 +862,7 @@
     from_next = swapped(to_next, next_pair)
     own, hot = call(
         own_kernel,
-        [(vmem, x) for x in (stored, slot_of, lanes)],
+        [(vmem, x) for x in (flags, stored, lanes)],
         [((ROWS, MID), f32), ((MID, ELEMENTS), bf16)],
         10**8,
         name="own",
@@ -880,10 +883,10 @@
         10**8,
         name="middle",
     )
-    (far,) = call(
-        far_kernel,
-        [(vmem, x) for x in (far1, far0, from_next, low)],
-        [((2 * CORNER_ROWS, LANES), f32)],
+    (from_next,) = call(
+        functools.partial(far_kernel, block_cols),
+        [(vmem, x) for x in (flags, far1, far0, from_next, low)],
+        [((RIM_ROWS, LANES), f32)],
         10**11,
         name="far",
     )
@@ -892,7 +895,7 @@
         [
             (vmem, x)
             for x in (
-                flags, from_pair, from_next, far, low, centre, high, hot, table, weight, lanes
+                flags, from_pair, from_next, low, centre, high, hot, table, weight, lanes
             )
         ],
         [(fields.shape, f32)],

time: 19.8 us -> 19.5 us (0.985)
  the two profiles are of different devices: /device:TPU:6 before, /device:TPU:9 now
where the time goes in v21:
time: 19.5 us; the launch traced here: 19.4 us
  starting transfers between devices  8.78 us (45%)
  Pallas kernels  7.68 us (39%)
  waiting for transfers between devices  2.86 us (15%)
    pallas_call x7, Pallas kernels, call(): pl.pallas_call(kernel, out_shape=[jax.ShapeDtypeStruct(*out) for out in o...  7.68 us
    ppermute x4, starting transfers between devices, eastward(): lax.ppermute(value, both, [(rank(*a), rank(*b)) for a, b in pairs.items()])  7.43 us
    ppermute x4, waiting for transfers between devices, eastward(): lax.ppermute(value, both, [(rank(*a), rank(*b)) for a, b in pairs.items()])  2.76 us
    ppermute x2, starting transfers between devices, swapped(): return lax.ppermute(value, both, pairs)  1.36 us
  transfers between devices with their start and end apart: 6, of which 2 were waited for; matrix products, arithmetic and copies ran while one was open for 0% of the time, Pallas kernels for 13%

profile of v21, /device:TPU:9, one launch (start us, length us, event | category | flops | bytes accessed | tf_op | source)
XLA Modules:
  0.0 19.4 jit_solution(11730066450395420811)
XLA Ops:
  0.0 0.0 copy-start.2
  0.0 1.8 %strips.1 = (f32[216,128]{1,0:T(8,128)S(1)}, f32[216,128]{1,0:T(8,128)S(1)}, f32[448,256]{1,0:T(8,128)S(1)}, s32[8,128]{1,0:T(8,128)S(1)}) custom-call(s32[2,256]{1,0:T(2,128)} %refs_0_.1, s32[1,256]{1,0:T(1,128)} %refs_1_.1, f32[3,8,8,256]{3,2,1,0:T(8,128)} %refs_2_.1, f32[8,8,256]{2,1,0:T(8,128)} %refs_3_.1, f32[8,8,256]{2,1,0:T(8,128)} %refs_4_.1, ...), custom_call_target="tpu_custom_call" | custom-call | flops 100000000 | bytes 2097152 | tf_op jit(solution)/shard_map/strips/pallas_call | solution.py:753
  1.8 1.3 %collective-permute-start = (f32[216,128]{1,0:T(8,128)S(1)}, f32[216,128]{1,0:T(8,128)S(1)}, u32[]{:S(2)}, u32[]{:S(2)}) collective-permute-start(f32[216,128]{1,0:T(8,128)S(1)} %get-tuple-element.19.strip0_ref), channel_id=1, source_target_pairs={{0,16},{1,17},{2,18},{3,19},{4,20},{5,21},{6,22},{7,23},{8,24},{9,... | collective-permute-start | bytes 331784 | tf_op jit(solution)/shard_map/ppermute | solution.py:837
  3.1 3.1 %collective-permute-start.1 = (f32[216,128]{1,0:T(8,128)S(1)}, f32[216,128]{1,0:T(8,128)S(1)}, u32[]{:S(2)}, u32[]{:S(2)}) collective-permute-start(f32[216,128]{1,0:T(8,128)S(1)} %get-tuple-element.20.strip1_ref), channel_id=1, source_target_pairs={{0,31},{1,30},{2,29},{3,28},{4,27},{5,26},{6,25},{7,24},{8,23},{9,... | collective-permute-start | bytes 331784 | tf_op jit(solution)/shard_map/ppermute | solution.py:837
  6.1 0.0 copy-done
  6.1 0.0 copy-done.2
  6.1 0.0 copy-start.1
  6.1 0.8 %rows.1 = (f32[216,128]{1,0:T(8,128)S(1)}, f32[56,128]{1,0:T(8,128)S(1)}, f32[56,128]{1,0:T(8,128)S(1)}, f32[448,128]{1,0:T(8,128)S(1)}) custom-call(s32[8,128]{1,0:T(8,128)S(1)} %get-tuple-element.18.flags_ref, f32[448,256]{1,0:T(8,128)S(1)} %get-tuple-element.21.stored_ref, f32[216,128]{1,0:T(8,128)S(1)} %get-tuple-element.20.strip1_ref, ...), custom_call_target="tpu_custom_call" | custom-call | flops 100000000 | bytes 2097152 | tf_op jit(solution)/shard_map/rows/pallas_call | solution.py:753
  7.0 0.0 collective-permute-start.5
  7.0 1.2 %collective-permute-start.3 = (f32[56,128]{1,0:T(8,128)S(1)}, f32[56,128]{1,0:T(8,128)S(1)}, u32[]{:S(2)}, u32[]{:S(2)}) collective-permute-start(f32[56,128]{1,0:T(8,128)S(1)} %get-tuple-element.24), channel_id=1, source_target_pairs={{0,16},{1,29},{2,30},{3,27},{4,28},{5,25},{6,26},{7,23},{8,24},{9,... | collective-permute-start | bytes 86024 | tf_op jit(solution)/shard_map/ppermute | solution.py:837
  8.2 1.9 %collective-permute-start.4 = (f32[56,128]{1,0:T(8,128)S(1)}, f32[56,128]{1,0:T(8,128)S(1)}, u32[]{:S(2)}, u32[]{:S(2)}) collective-permute-start(f32[56,128]{1,0:T(8,128)S(1)} %get-tuple-element.25), channel_id=1, source_target_pairs={{0,16},{1,18},{2,17},{3,20},{4,19},{5,22},{6,21},{7,24},{8,23},{9,... | collective-permute-start | bytes 86024 | tf_op jit(solution)/shard_map/ppermute | solution.py:837
  10.1 0.0 copy-done.1
  10.1 0.5 %own.1 = (f32[448,384]{1,0:T(8,128)S(1)}, bf16[384,256]{1,0:T(8,128)(2,1)S(1)}) custom-call(s32[8,128]{1,0:T(8,128)S(1)} %get-tuple-element.18.flags_ref, f32[448,256]{1,0:T(8,128)S(1)} %get-tuple-element.21.stored_ref, s32[64,640]{1,0:T(8,128)S(1)} %copy-done.1), custom_call_target="tpu_custom_call" | custom-call | flops 100000000 | bytes 2097152 | tf_op jit(solution)/shard_map/own/pallas_call | solution.py:753
  10.6 0.0 collective-permute-done.in0_ref
  10.6 2.7 %collective-permute-done.1.in1_ref = f32[216,128]{1,0:T(8,128)S(1)} collective-permute-done((f32[216,128]{1,0:T(8,128)S(1)}, f32[216,128]{1,0:T(8,128)S(1)}, u32[]{:S(2)}, u32[]{:S(2)}) %collective-permute-start.1) | collective-permute-done | bytes 110624 | tf_op jit(solution)/shard_map/ppermute | solution.py:837
  13.4 0.2 %corners.1 = f32[480,128]{1,0:T(8,128)S(1)} custom-call(s32[8,128]{1,0:T(8,128)S(1)} %get-tuple-element.18.flags_ref, f32[216,128]{1,0:T(8,128)S(1)} %collective-permute-done.in0_ref, f32[216,128]{1,0:T(8,128)S(1)} %collective-permute-done.1.in1_ref, f32[448,128]{1,0:T(8,128)S(1)} %get-tuple-element.22.pair_ref, bf16[384,256]{1,0:T(8,128)(2,1)S(1)} %get-tuple-element.23._.hot_ref), custom_call_target="tpu_custom_call" | custom-call | flops 100000000 | bytes 2097152 | tf_op jit(solution)/shard_map/corners/pallas_call | solution.py:753
  13.6 1.3 %collective-permute-start.2 = (f32[480,128]{1,0:T(8,128)S(1)}, f32[480,128]{1,0:T(8,128)S(1)}, u32[]{:S(2)}, u32[]{:S(2)}) collective-permute-start(f32[480,128]{1,0:T(8,128)S(1)} %corners.1), channel_id=1, source_target_pairs={{0,1},{1,0},{2,3},{3,2},{4,5},{5,4},{6,7},{7,6},{8,9},{9,8},{10,11... | collective-permute-start | bytes 737288 | tf_op jit(solution)/shard_map/ppermute | solution.py:818
  14.9 0.8 %middle.1 = (f32[704,128]{1,0:T(8,128)S(1)}, f32[704,128]{1,0:T(8,128)S(1)}, f32[704,128]{1,0:T(8,128)S(1)}) custom-call(s32[8,128]{1,0:T(8,128)S(1)} %get-tuple-element.18.flags_ref, f32[216,128]{1,0:T(8,128)S(1)} %collective-permute-done.in0_ref, f32[216,128]{1,0:T(8,128)S(1)} %collective-permute-done.1.in1_ref, f32[448,384]{1,0:T(8,128)S(1)} %get-tuple-element.27.own_ref, ...), custom_call_target="tpu_custom_call" | custom-call | flops 100000000 | bytes 2097152 | tf_op jit(solution)/shard_map/middle/pallas_call | solution.py:753
  15.7 0.0 collective-permute-done.3.far1_ref
  15.7 0.0 collective-permute-done.4.far0_ref
  15.7 0.0 collective-permute-done.5.next_ref
  15.7 0.2 %far.1.next_ref = f32[512,128]{1,0:T(8,128)S(1)} custom-call(s32[8,128]{1,0:T(8,128)S(1)} %get-tuple-element.18.flags_ref, f32[56,128]{1,0:T(8,128)S(1)} %collective-permute-done.3.far1_ref, f32[56,128]{1,0:T(8,128)S(1)} %collective-permute-done.4.far0_ref, f32[216,128]{1,0:T(8,128)S(1)} %collective-permute-done.5.next_ref, ...), custom_call_target="tpu_custom_call" | custom-call | flops 99999997952 | bytes 2097152 | tf_op jit(solution)/shard_map/far/pallas_call | solution.py:753
  15.9 0.1 collective-permute-done.2.pair_ref
  16.0 3.4 %steps.1 = f32[3,8,8,256]{3,2,1,0:T(8,128)} custom-call(s32[8,128]{1,0:T(8,128)S(1)} %get-tuple-element.18.flags_ref, f32[480,128]{1,0:T(8,128)S(1)} %collective-permute-done.2.pair_ref, f32[512,128]{1,0:T(8,128)S(1)} %far.1.next_ref, f32[704,128]{1,0:T(8,128)S(1)} %get-tuple-element.28._.low_ref, f32[704,128]{1,0:T(8,128)S(1)} %get-tuple-element.29.centre_ref, ...), custom_call_target="tpu_custom_call" | custom-call | flops 100000000 | bytes 2097152 | tf_op jit(solution)/shard_map/steps/pallas_call | solution.py:753
  (1 shorter events, 0.0 us)
Async XLA Ops:
  0.0 6.1 %copy-start = (f32[320,256]{1,0:T(8,128)S(1)}, f32[320,256]{1,0:T(8,128)}, u32[]{:S(2)}) copy-start(f32[320,256]{1,0:T(8,128)} %constant.6.clone.refs_7_.table_ref) | copy-start | bytes 983044
  0.0 6.1 %copy-start.2 = (f32[64,128]{1,0:T(8,128)S(1)}, f32[64,128]{1,0:T(8,128)}, u32[]{:S(2)}) copy-start(f32[64,128]{1,0:T(8,128)} %constant.7.clone.refs_8_.weight_ref) | copy-start | bytes 98308
  1.8 8.8 %collective-permute-start = (f32[216,128]{1,0:T(8,128)S(1)}, f32[216,128]{1,0:T(8,128)S(1)}, u32[]{:S(2)}, u32[]{:S(2)}) collective-permute-start(f32[216,128]{1,0:T(8,128)S(1)} %get-tuple-element.19.strip0_ref), channel_id=1, source_target_pairs={{0,16},{1,17},{2,18},{3,19},{4,20},{5,21},{6,22},{7,23},{8,24},{9,... | collective-permute-start | bytes 331784 | tf_op jit(solution)/shard_map/ppermute | solution.py:837
  3.1 10.3 %collective-permute-start.1 = (f32[216,128]{1,0:T(8,128)S(1)}, f32[216,128]{1,0:T(8,128)S(1)}, u32[]{:S(2)}, u32[]{:S(2)}) collective-permute-start(f32[216,128]{1,0:T(8,128)S(1)} %get-tuple-element.20.strip1_ref), channel_id=1, source_target_pairs={{0,31},{1,30},{2,29},{3,28},{4,27},{5,26},{6,25},{7,24},{8,23},{9,... | collective-permute-start | bytes 331784 | tf_op jit(solution)/shard_map/ppermute | solution.py:837
  6.1 4.0 %copy-start.1 = (s32[64,640]{1,0:T(8,128)S(1)}, s32[64,640]{1,0:T(8,128)}, u32[]{:S(2)}) copy-start(s32[64,640]{1,0:T(8,128)} %constant.8.clone.lanes_ref) | copy-start | bytes 491524
  7.0 8.7 %collective-permute-start.5 = (f32[216,128]{1,0:T(8,128)S(1)}, f32[216,128]{1,0:T(8,128)S(1)}, u32[]{:S(2)}, u32[]{:S(2)}) collective-permute-start(f32[216,128]{1,0:T(8,128)S(1)} %get-tuple-element.26), channel_id=1, source_target_pairs={{0,16},{1,2},{2,1},{3,4},{4,3},{5,6},{6,5},{7,8},{8,7},{9,10},{10,... | collective-permute-start | bytes 331784 | tf_op jit(solution)/shard_map/ppermute | solution.py:818
  7.0 8.7 %collective-permute-start.3 = (f32[56,128]{1,0:T(8,128)S(1)}, f32[56,128]{1,0:T(8,128)S(1)}, u32[]{:S(2)}, u32[]{:S(2)}) collective-permute-start(f32[56,128]{1,0:T(8,128)S(1)} %get-tuple-element.24), channel_id=1, source_target_pairs={{0,16},{1,29},{2,30},{3,27},{4,28},{5,25},{6,26},{7,23},{8,24},{9,... | collective-permute-start | bytes 86024 | tf_op jit(solution)/shard_map/ppermute | solution.py:837
  8.2 7.5 %collective-permute-start.4 = (f32[56,128]{1,0:T(8,128)S(1)}, f32[56,128]{1,0:T(8,128)S(1)}, u32[]{:S(2)}, u32[]{:S(2)}) collective-permute-start(f32[56,128]{1,0:T(8,128)S(1)} %get-tuple-element.25), channel_id=1, source_target_pairs={{0,16},{1,18},{2,17},{3,20},{4,19},{5,22},{6,21},{7,24},{8,23},{9,... | collective-permute-start | bytes 86024 | tf_op jit(solution)/shard_map/ppermute | solution.py:837
  13.6 2.4 %collective-permute-start.2 = (f32[480,128]{1,0:T(8,128)S(1)}, f32[480,128]{1,0:T(8,128)S(1)}, u32[]{:S(2)}, u32[]{:S(2)}) collective-permute-start(f32[480,128]{1,0:T(8,128)S(1)} %corners.1), channel_id=1, source_target_pairs={{0,1},{1,0},{2,3},{3,2},{4,5},{5,4},{6,7},{7,6},{8,9},{9,8},{10,11... | collective-permute-start | bytes 737288 | tf_op jit(solution)/shard_map/ppermute | solution.py:818

commit v22 on v21

--- a/solution.py
+++ b/solution.py
@@ -112,8 +112,14 @@
         table[2 * NODES : 3 * NODES, at : at + 2 * NODES] = part[:, : 2 * NODES]
         table[3 * NODES : 4 * NODES, at : at + NODES] = part[:, 2 * NODES :]
     table[4 * NODES :, : 3 * NODES] = in_three(both)
+    table = table.astype(np.float32)
     spread = np.broadcast_to(node_weight, (NODES, LANES)).astype(np.float32)
-    return table.astype(np.float32), np.ascontiguousarray(spread)
+    ends = np.r_[:NP, NODES - NP : NODES]
+    edge_table = np.zeros((10 * NP, 4 * NODES), np.float32)
+    for k in range(4):
+        edge_table[2 * k * NP : 2 * (k + 1) * NP] = table[k * NODES + ends]
+    edge_table[8 * NP :, :LANES] = spread[ends]
+    return table, np.ascontiguousarray(spread), edge_table
 
 
 def lane_tables():
@@ -217,6 +223,25 @@
     return mass_tendency(table, p, u, v, root * depth, root, mass * spin) + [mass]
 
 
+def column_edges(table, weight, p, u, v, area, depth, spin):
+    def ends(part):
+        return jnp.concatenate([part[:NP], part[NODES - NP :]], 0)
+
+    root = jnp.sqrt(area)
+    area_depth = root * depth
+    root, mass = ends(root), weight * ends(area)
+    weighted_spin = mass * ends(spin)
+    slopes = dot(table[: 4 * NP, : 3 * NODES], jnp.concatenate(high_low_high(p), 0))
+    flux = high_low_high(area_depth * u)[:2] + high_low_high(area_depth * v)[:2]
+    spread = dot(table[4 * NP :], jnp.concatenate(flux, 0))
+    return [
+        -(spread[: 2 * NP] + spread[2 * NP :]),
+        weighted_spin * ends(v) - root * slopes[: 2 * NP],
+        -weighted_spin * ends(u) - root * slopes[2 * NP :],
+        mass,
+    ]
+
+
 def row_edges(sums):
     return tuple(sums[0, pl.ds(j, EDGE_ROWS, stride=NP)] for j in (NP - 1, 0))
 
@@ -370,8 +395,8 @@
 
 
 def strips_kernel(block_cols, *refs):
-    sources, (out1_ref, out0_ref, stored_ref, flags_ref) = refs[:9], refs[9:13]
-    buffers, sems = refs[13:22], refs[22]
+    sources, (out1_ref, out0_ref, stored_ref, flags_ref) = refs[:8], refs[8:12]
+    buffers, sems = refs[12:20], refs[20]
     copies = [
         pltpu.make_async_copy(source, buffer, sems.at[k])
         for k, (source, buffer) in enumerate(zip(sources, buffers))
@@ -379,7 +404,7 @@
     for copy in copies:
         copy.start()
     seam_ref, slot_ref, fields_ref, area_ref, depth_ref, spin_ref, tide_ref = buffers[:7]
-    table_ref, weight_ref = buffers[7:]
+    table_ref = buffers[7]
     for copy in copies[:2]:
         copy.wait()
     east0, flip0, east1, flip1 = flags = seam_flags(seam_ref, block_cols)
@@ -420,9 +445,10 @@
     )
     for copy in copies[7:]:
         copy.wait()
-    edges = edge_values(table_ref, weight_ref, *ring[:6])
+    table, weight = table_ref[: 8 * NP].astype(bf16), table_ref[8 * NP :, :LANES]
+    edges = column_edges(table, weight, *ring[:6])
     east = jnp.where(second, east1, east0) != 0
-    ends = [jnp.where(east, part[NODES - NP :], part[:NP]) for part in edges]
+    ends = [jnp.where(east, part[NP:], part[:NP]) for part in edges]
     ends[2] = ends[2] * sign
     strip[2] = strip[2] * sign
     strip[5] = strip[5] * sign
@@ -742,8 +768,7 @@
 
 def on_device(fields, jacobian, water_depth, coriolis, tide_height, slot_of, seam_rows):
     block_cols = lax.axis_size("blk") // BY
-    table, weight = operator_table()
-    table, weight, lanes = map(jnp.asarray, (table, weight, lane_tables()))
+    table, weight, edge_table, lanes = map(jnp.asarray, (*operator_table(), lane_tables()))
     vmem = pl.BlockSpec(memory_space=pltpu.VMEM)
     hbm = pl.BlockSpec(memory_space=pltpu.HBM)
     params = pltpu.CompilerParams(vmem_limit_bytes=48 * 2**20)
@@ -774,7 +799,7 @@
         buffers = [space(x.shape, x.dtype) for space, x in zip(spaces, values)]
         return buffers + [pltpu.SemaphoreType.DMA((len(values),))]
 
-    needed = (seam_rows, slot_of, *held, table, weight)
+    needed = (seam_rows, slot_of, *held, edge_table)
     corner = ((CORNER_ROWS, LANES), f32)
     scratch = [pltpu.VMEM((1, 4 * NODES, LANES), f32)]
     strip1, strip0, stored, flags = call(

time: 19.5 us -> 19.5 us (level)
  no operation moved by 1% of the time
where the time goes in v22:
time: 19.5 us; the launch traced here: 19.3 us
  starting transfers between devices  8.75 us (45%)
  Pallas kernels  7.61 us (39%)
  waiting for transfers between devices  2.9 us (15%)
    pallas_call x7, Pallas kernels, call(): pl.pallas_call(kernel, out_shape=[jax.ShapeDtypeStruct(*out) for out in o...  7.61 us
    ppermute x4, starting transfers between devices, eastward(): lax.ppermute(value, both, [(rank(*a), rank(*b)) for a, b in pairs.items()])  7.42 us
    ppermute x4, waiting for transfers between devices, eastward(): lax.ppermute(value, both, [(rank(*a), rank(*b)) for a, b in pairs.items()])  2.8 us
    ppermute x2, starting transfers between devices, swapped(): return lax.ppermute(value, both, pairs)  1.33 us
  transfers between devices with their start and end apart: 6, of which 2 were waited for; matrix products, arithmetic and copies ran while one was open for 0% of the time, Pallas kernels for 13%

profile of v22, /device:TPU:9, one launch (start us, length us, event | category | flops | bytes accessed | tf_op | source)
XLA Modules:
  0.0 19.3 jit_solution(1984118366590482827)
XLA Ops:
  0.0 0.0 copy-start
  0.0 0.0 copy-start.2
  0.0 1.7 %strips.1 = (f32[216,128]{1,0:T(8,128)S(1)}, f32[216,128]{1,0:T(8,128)S(1)}, f32[448,256]{1,0:T(8,128)S(1)}, s32[8,128]{1,0:T(8,128)S(1)}) custom-call(s32[2,256]{1,0:T(2,128)} %refs_0_.1, s32[1,256]{1,0:T(1,128)} %refs_1_.1, f32[3,8,8,256]{3,2,1,0:T(8,128)} %refs_2_.1, f32[8,8,256]{2,1,0:T(8,128)} %refs_3_.1, f32[8,8,256]{2,1,0:T(8,128)} %refs_4_.1, ...), custom_call_target="tpu_custom_call" | custom-call | flops 100000000 | bytes 2097152 | tf_op jit(solution)/shard_map/strips/pallas_call | solution.py:778
  1.7 1.3 %collective-permute-start = (f32[216,128]{1,0:T(8,128)S(1)}, f32[216,128]{1,0:T(8,128)S(1)}, u32[]{:S(2)}, u32[]{:S(2)}) collective-permute-start(f32[216,128]{1,0:T(8,128)S(1)} %get-tuple-element.19.strip0_ref), channel_id=1, source_target_pairs={{0,16},{1,17},{2,18},{3,19},{4,20},{5,21},{6,22},{7,23},{8,24},{9,... | collective-permute-start | bytes 331784 | tf_op jit(solution)/shard_map/ppermute | solution.py:862
  3.0 3.1 %collective-permute-start.1 = (f32[216,128]{1,0:T(8,128)S(1)}, f32[216,128]{1,0:T(8,128)S(1)}, u32[]{:S(2)}, u32[]{:S(2)}) collective-permute-start(f32[216,128]{1,0:T(8,128)S(1)} %get-tuple-element.20.strip1_ref), channel_id=1, source_target_pairs={{0,31},{1,30},{2,29},{3,28},{4,27},{5,26},{6,25},{7,24},{8,23},{9,... | collective-permute-start | bytes 331784 | tf_op jit(solution)/shard_map/ppermute | solution.py:862
  6.1 0.0 copy-done
  6.1 0.0 copy-done.2
  6.1 0.8 %rows.1 = (f32[216,128]{1,0:T(8,128)S(1)}, f32[56,128]{1,0:T(8,128)S(1)}, f32[56,128]{1,0:T(8,128)S(1)}, f32[448,128]{1,0:T(8,128)S(1)}) custom-call(s32[8,128]{1,0:T(8,128)S(1)} %get-tuple-element.18.flags_ref, f32[448,256]{1,0:T(8,128)S(1)} %get-tuple-element.21.stored_ref, f32[216,128]{1,0:T(8,128)S(1)} %get-tuple-element.20.strip1_ref, ...), custom_call_target="tpu_custom_call" | custom-call | flops 100000000 | bytes 2097152 | tf_op jit(solution)/shard_map/rows/pallas_call | solution.py:778
  6.9 0.0 collective-permute-start.5
  7.0 1.2 %collective-permute-start.3 = (f32[56,128]{1,0:T(8,128)S(1)}, f32[56,128]{1,0:T(8,128)S(1)}, u32[]{:S(2)}, u32[]{:S(2)}) collective-permute-start(f32[56,128]{1,0:T(8,128)S(1)} %get-tuple-element.24), channel_id=1, source_target_pairs={{0,16},{1,29},{2,30},{3,27},{4,28},{5,25},{6,26},{7,23},{8,24},{9,... | collective-permute-start | bytes 86024 | tf_op jit(solution)/shard_map/ppermute | solution.py:862
  8.1 1.9 %collective-permute-start.4 = (f32[56,128]{1,0:T(8,128)S(1)}, f32[56,128]{1,0:T(8,128)S(1)}, u32[]{:S(2)}, u32[]{:S(2)}) collective-permute-start(f32[56,128]{1,0:T(8,128)S(1)} %get-tuple-element.25), channel_id=1, source_target_pairs={{0,16},{1,18},{2,17},{3,20},{4,19},{5,22},{6,21},{7,24},{8,23},{9,... | collective-permute-start | bytes 86024 | tf_op jit(solution)/shard_map/ppermute | solution.py:862
  10.0 0.0 copy-done.1
  10.0 0.5 %own.1 = (f32[448,384]{1,0:T(8,128)S(1)}, bf16[384,256]{1,0:T(8,128)(2,1)S(1)}) custom-call(s32[8,128]{1,0:T(8,128)S(1)} %get-tuple-element.18.flags_ref, f32[448,256]{1,0:T(8,128)S(1)} %get-tuple-element.21.stored_ref, s32[64,640]{1,0:T(8,128)S(1)} %copy-done.1), custom_call_target="tpu_custom_call" | custom-call | flops 100000000 | bytes 2097152 | tf_op jit(solution)/shard_map/own/pallas_call | solution.py:778
  10.5 0.0 collective-permute-done.in0_ref
  10.6 2.8 %collective-permute-done.1.in1_ref = f32[216,128]{1,0:T(8,128)S(1)} collective-permute-done((f32[216,128]{1,0:T(8,128)S(1)}, f32[216,128]{1,0:T(8,128)S(1)}, u32[]{:S(2)}, u32[]{:S(2)}) %collective-permute-start.1) | collective-permute-done | bytes 110624 | tf_op jit(solution)/shard_map/ppermute | solution.py:862
  13.3 0.2 %corners.1 = f32[480,128]{1,0:T(8,128)S(1)} custom-call(s32[8,128]{1,0:T(8,128)S(1)} %get-tuple-element.18.flags_ref, f32[216,128]{1,0:T(8,128)S(1)} %collective-permute-done.in0_ref, f32[216,128]{1,0:T(8,128)S(1)} %collective-permute-done.1.in1_ref, f32[448,128]{1,0:T(8,128)S(1)} %get-tuple-element.22.pair_ref, bf16[384,256]{1,0:T(8,128)(2,1)S(1)} %get-tuple-element.23._.hot_ref), custom_call_target="tpu_custom_call" | custom-call | flops 100000000 | bytes 2097152 | tf_op jit(solution)/shard_map/corners/pallas_call | solution.py:778
  13.6 1.3 %collective-permute-start.2 = (f32[480,128]{1,0:T(8,128)S(1)}, f32[480,128]{1,0:T(8,128)S(1)}, u32[]{:S(2)}, u32[]{:S(2)}) collective-permute-start(f32[480,128]{1,0:T(8,128)S(1)} %corners.1), channel_id=1, source_target_pairs={{0,1},{1,0},{2,3},{3,2},{4,5},{5,4},{6,7},{7,6},{8,9},{9,8},{10,11... | collective-permute-start | bytes 737288 | tf_op jit(solution)/shard_map/ppermute | solution.py:843
  14.8 0.8 %middle.1 = (f32[704,128]{1,0:T(8,128)S(1)}, f32[704,128]{1,0:T(8,128)S(1)}, f32[704,128]{1,0:T(8,128)S(1)}) custom-call(s32[8,128]{1,0:T(8,128)S(1)} %get-tuple-element.18.flags_ref, f32[216,128]{1,0:T(8,128)S(1)} %collective-permute-done.in0_ref, f32[216,128]{1,0:T(8,128)S(1)} %collective-permute-done.1.in1_ref, f32[448,384]{1,0:T(8,128)S(1)} %get-tuple-element.27.own_ref, ...), custom_call_target="tpu_custom_call" | custom-call | flops 100000000 | bytes 2097152 | tf_op jit(solution)/shard_map/middle/pallas_call | solution.py:778
  15.6 0.0 collective-permute-done.3.far1_ref
  15.6 0.0 collective-permute-done.4.far0_ref
  15.6 0.0 collective-permute-done.5.next_ref
  15.7 0.2 %far.1.next_ref = f32[512,128]{1,0:T(8,128)S(1)} custom-call(s32[8,128]{1,0:T(8,128)S(1)} %get-tuple-element.18.flags_ref, f32[56,128]{1,0:T(8,128)S(1)} %collective-permute-done.3.far1_ref, f32[56,128]{1,0:T(8,128)S(1)} %collective-permute-done.4.far0_ref, f32[216,128]{1,0:T(8,128)S(1)} %collective-permute-done.5.next_ref, ...), custom_call_target="tpu_custom_call" | custom-call | flops 99999997952 | bytes 2097152 | tf_op jit(solution)/shard_map/far/pallas_call | solution.py:778
  15.9 0.1 collective-permute-done.2.pair_ref
  16.0 3.4 %steps.1 = f32[3,8,8,256]{3,2,1,0:T(8,128)} custom-call(s32[8,128]{1,0:T(8,128)S(1)} %get-tuple-element.18.flags_ref, f32[480,128]{1,0:T(8,128)S(1)} %collective-permute-done.2.pair_ref, f32[512,128]{1,0:T(8,128)S(1)} %far.1.next_ref, f32[704,128]{1,0:T(8,128)S(1)} %get-tuple-element.28._.low_ref, f32[704,128]{1,0:T(8,128)S(1)} %get-tuple-element.29.centre_ref, ...), custom_call_target="tpu_custom_call" | custom-call | flops 100000000 | bytes 2097152 | tf_op jit(solution)/shard_map/steps/pallas_call | solution.py:778
  (1 shorter events, 0.0 us)
Async XLA Ops:
  0.0 6.1 %copy-start = (f32[320,256]{1,0:T(8,128)S(1)}, f32[320,256]{1,0:T(8,128)}, u32[]{:S(2)}) copy-start(f32[320,256]{1,0:T(8,128)} %constant.8.clone.table_ref) | copy-start | bytes 983044
  0.0 6.1 %copy-start.2 = (f32[64,128]{1,0:T(8,128)S(1)}, f32[64,128]{1,0:T(8,128)}, u32[]{:S(2)}) copy-start(f32[64,128]{1,0:T(8,128)} %constant.9.clone.weight_ref) | copy-start | bytes 98308
  1.7 8.8 %collective-permute-start = (f32[216,128]{1,0:T(8,128)S(1)}, f32[216,128]{1,0:T(8,128)S(1)}, u32[]{:S(2)}, u32[]{:S(2)}) collective-permute-start(f32[216,128]{1,0:T(8,128)S(1)} %get-tuple-element.19.strip0_ref), channel_id=1, source_target_pairs={{0,16},{1,17},{2,18},{3,19},{4,20},{5,21},{6,22},{7,23},{8,24},{9,... | collective-permute-start | bytes 331784 | tf_op jit(solution)/shard_map/ppermute | solution.py:862
  3.0 10.3 %collective-permute-start.1 = (f32[216,128]{1,0:T(8,128)S(1)}, f32[216,128]{1,0:T(8,128)S(1)}, u32[]{:S(2)}, u32[]{:S(2)}) collective-permute-start(f32[216,128]{1,0:T(8,128)S(1)} %get-tuple-element.20.strip1_ref), channel_id=1, source_target_pairs={{0,31},{1,30},{2,29},{3,28},{4,27},{5,26},{6,25},{7,24},{8,23},{9,... | collective-permute-start | bytes 331784 | tf_op jit(solution)/shard_map/ppermute | solution.py:862
  6.1 4.0 %copy-start.1 = (s32[64,640]{1,0:T(8,128)S(1)}, s32[64,640]{1,0:T(8,128)}, u32[]{:S(2)}) copy-start(s32[64,640]{1,0:T(8,128)} %constant.11.clone.lanes_ref) | copy-start | bytes 491524
  6.9 8.7 %collective-permute-start.5 = (f32[216,128]{1,0:T(8,128)S(1)}, f32[216,128]{1,0:T(8,128)S(1)}, u32[]{:S(2)}, u32[]{:S(2)}) collective-permute-start(f32[216,128]{1,0:T(8,128)S(1)} %get-tuple-element.26), channel_id=1, source_target_pairs={{0,16},{1,2},{2,1},{3,4},{4,3},{5,6},{6,5},{7,8},{8,7},{9,10},{10,... | collective-permute-start | bytes 331784 | tf_op jit(solution)/shard_map/ppermute | solution.py:843
  7.0 8.7 %collective-permute-start.3 = (f32[56,128]{1,0:T(8,128)S(1)}, f32[56,128]{1,0:T(8,128)S(1)}, u32[]{:S(2)}, u32[]{:S(2)}) collective-permute-start(f32[56,128]{1,0:T(8,128)S(1)} %get-tuple-element.24), channel_id=1, source_target_pairs={{0,16},{1,29},{2,30},{3,27},{4,28},{5,25},{6,26},{7,23},{8,24},{9,... | collective-permute-start | bytes 86024 | tf_op jit(solution)/shard_map/ppermute | solution.py:862
  8.1 7.5 %collective-permute-start.4 = (f32[56,128]{1,0:T(8,128)S(1)}, f32[56,128]{1,0:T(8,128)S(1)}, u32[]{:S(2)}, u32[]{:S(2)}) collective-permute-start(f32[56,128]{1,0:T(8,128)S(1)} %get-tuple-element.25), channel_id=1, source_target_pairs={{0,16},{1,18},{2,17},{3,20},{4,19},{5,22},{6,21},{7,24},{8,23},{9,... | collective-permute-start | bytes 86024 | tf_op jit(solution)/shard_map/ppermute | solution.py:862
  13.6 2.4 %collective-permute-start.2 = (f32[480,128]{1,0:T(8,128)S(1)}, f32[480,128]{1,0:T(8,128)S(1)}, u32[]{:S(2)}, u32[]{:S(2)}) collective-permute-start(f32[480,128]{1,0:T(8,128)S(1)} %corners.1), channel_id=1, source_target_pairs={{0,1},{1,0},{2,3},{3,2},{4,5},{5,4},{6,7},{7,6},{8,9},{9,8},{10,11... | collective-permute-start | bytes 737288 | tf_op jit(solution)/shard_map/ppermute | solution.py:843

commit v23 on v22

--- a/solution.py
+++ b/solution.py
@@ -394,8 +394,19 @@
     return [jnp.concatenate([flags_ref[k : k + 1]] * tiles, 1) for k in range(4)]
 
 
+def mirrored_first(block_y):
+    return (block_y >= BY // 4) & (block_y < BY - BY // 4)
+
+
+def in_order(block_cols, first, second):
+    if block_cols > 1:
+        return first, second
+    swap = mirrored_first(lax.rem(lax.axis_index("blk"), BY))
+    return jnp.where(swap, second, first), jnp.where(swap, first, second)
+
+
 def strips_kernel(block_cols, *refs):
-    sources, (out1_ref, out0_ref, stored_ref, flags_ref) = refs[:8], refs[8:12]
+    sources, (first_ref, then_ref, stored_ref, flags_ref) = refs[:8], refs[8:12]
     buffers, sems = refs[12:20], refs[20]
     copies = [
         pltpu.make_async_copy(source, buffer, sems.at[k])
@@ -452,18 +463,18 @@
     ends[2] = ends[2] * sign
     strip[2] = strip[2] * sign
     strip[5] = strip[5] * sign
-    for ref, part, flip in zip(
-        (out0_ref, out1_ref), packed(strip_rows(strip, east, 0, ends)), (flip0, flip1)
-    ):
+    strips = []
+    for part, flip in zip(packed(strip_rows(strip, east, 0, ends)), (flip0, flip1)):
         if isinstance(flip, int):
-            ref[...] = turned(part) if flip else part
+            strips.append(turned(part) if flip else part)
         else:
-            ref[...] = jnp.where(flip != 0, turned(part), part)
+            strips.append(jnp.where(flip != 0, turned(part), part))
+    first_ref[...], then_ref[...] = in_order(block_cols, *strips)
     stored_ref[...] = stored
 
 
 def rows_kernel(
-    block_cols, flags_ref, stored_ref, strip1_ref, strip0_ref, table_ref, weight_ref,
+    block_cols, flags_ref, stored_ref, first_ref, then_ref, table_ref, weight_ref,
     next_ref, far0_ref, far1_ref, pair_ref, sums,
 ):
     east0, flip0, east1, flip1 = flags_in(flags_ref)
@@ -476,7 +487,7 @@
     both = picked(stored_ref[...], by_slot(slots_in(flags_ref), (lane & 15) * GY + row))
     pair_ref[...] = both[:, LANES:]
     rows = [both[k * NODES : (k + 1) * NODES, :LANES] for k in range(ARRAYS)]
-    whole = unpacked(strip0_ref[...], strip1_ref[...])
+    whole = unpacked(*in_order(block_cols, first_ref[...], then_ref[...]))
     strip = [whole[k * NODES : (k + 1) * NODES] for k in range(6)]
     edges = edge_values(table_ref, weight_ref, *map(beside, strip, rows[:6]))
     sums[0] = jnp.concatenate([part[:, :LANES] for part in edges], 0)
@@ -497,16 +508,17 @@
     next_ref[...] = jnp.where(lane >= 64, pltpu.roll(bottom, 64, 1), top)
 
 
-def corners_kernel(flags_ref, in0_ref, in1_ref, pair_ref, _, out_ref):
+def corners_kernel(block_cols, flags_ref, first_ref, then_ref, pair_ref, _, out_ref):
     east0, flip0, east1, flip1 = flags_in(flags_ref)
+    in0, in1 = in_order(block_cols, first_ref[...], then_ref[...])
     top = 1 - (lax.axis_index("blk") & 1)
     lane = lax.broadcasted_iota(i32, (1, LANES), 1)
     halves = []
     for start in (0, 64):
         at0 = jnp.where(top != 0, 36, 80)
         at1 = jnp.where(top != 0, 56, 100)
-        first = pltpu.roll(in0_ref[...], (at0 - start) & (LANES - 1), 1)
-        other = pltpu.roll(in1_ref[...], (at1 - start) & (LANES - 1), 1)
+        first = pltpu.roll(in0, (at0 - start) & (LANES - 1), 1)
+        other = pltpu.roll(in1, (at1 - start) & (LANES - 1), 1)
         halves.append(jnp.where(lane < 100, first, other))
     late = jnp.where(lane < 100, east0, east1) == 0
     whole = placed_rows(jnp.concatenate(halves, 0), late, 0)
@@ -537,13 +549,14 @@
 
 
 def middle_kernel(
-    flags_ref, in0_ref, in1_ref, own_ref, lanes_ref, table_ref, weight_ref,
+    block_cols, flags_ref, first_ref, then_ref, own_ref, lanes_ref, table_ref, weight_ref,
     low_ref, centre_ref, high_ref,
 ):
     east0, flip0, east1, flip1 = flags_in(flags_ref)
     second = lax.broadcasted_iota(i32, (1, LANES), 1) >= 64
     late = jnp.where(second, east1, east0) == 0
-    whole = placed_rows(unpacked(in0_ref[...], in1_ref[...]), late, 0)
+    whole = unpacked(*in_order(block_cols, first_ref[...], then_ref[...]))
+    whole = placed_rows(whole, late, 0)
     side = lanes_ref[16:24, :MID]
     east = flags_in(flags_ref, MID // LANES)[0]
     first_at = jnp.where(side == 2, 64 * (1 - east), 64 * east)
@@ -802,7 +815,7 @@
     needed = (seam_rows, slot_of, *held, edge_table)
     corner = ((CORNER_ROWS, LANES), f32)
     scratch = [pltpu.VMEM((1, 4 * NODES, LANES), f32)]
-    strip1, strip0, stored, flags = call(
+    first, then, stored, flags = call(
         functools.partial(strips_kernel, block_cols),
         [(hbm, x) for x in needed],
         [strip, strip, ((ROWS, ELEMENTS), f32), ((8, LANES), i32)],
@@ -812,7 +825,7 @@
     )
     to_next, far0, far1, to_pair = call(
         functools.partial(rows_kernel, block_cols),
-        [(vmem, x) for x in (flags, stored, strip1, strip0, table, weight)],
+        [(vmem, x) for x in (flags, stored, first, then, table, weight)],
         [strip, corner, corner, ((ROWS, LANES), f32)],
         10**8,
         scratch=scratch,
@@ -882,7 +895,17 @@
             ),
         )
 
-    halo0, halo1 = across(strip0, strip1, same)
+    if block_cols == 1:
+        halos = []
+        for value, mirrored in ((first, mirrored_first), (then, lambda y: not mirrored_first(y))):
+            pairs = [
+                (rank(f, x, y), rank(1 - f, x, BY - 1 - y if mirrored(y) else y))
+                for f, x, y in places
+            ]
+            halos.append(lax.ppermute(value, both, pairs))
+        halo0, halo1 = halos
+    else:
+        halo0, halo1 = across(first, then, same)
     far0, far1 = across(far0, far1, next_pair)
     from_next = swapped(to_next, next_pair)
     own, hot = call(
@@ -893,7 +916,7 @@
         name="own",
     )
     (to_pair,) = call(
-        corners_kernel,
+        functools.partial(corners_kernel, block_cols),
         [(vmem, x) for x in (flags, halo0, halo1, to_pair, hot)],
         [((ALL_ROWS, LANES), f32)],
         10**8,
@@ -902,7 +925,7 @@
     from_pair = swapped(to_pair, in_pair)
     tile = ((11 * NODES, LANES), f32)
     low, centre, high = call(
-        middle_kernel,
+        functools.partial(middle_kernel, block_cols),
         [(vmem, x) for x in (flags, halo0, halo1, own, lanes, table, weight)],
         [tile, tile, tile],
         10**8,

time: 19.5 us -> 19.3 us (0.990)
  the two profiles are of different devices: /device:TPU:9 before, /device:TPU:0 now
where the time goes in v23:
time: 19.3 us; the launch traced here: 19 us
  starting transfers between devices  10.5 us (54%)
  Pallas kernels  7.64 us (40%)
  waiting for transfers between devices  0.79 us (4%)
    pallas_call x7, Pallas kernels, call(): pl.pallas_call(kernel, out_shape=[jax.ShapeDtypeStruct(*out) for out in o...  7.64 us
    ppermute x2, starting transfers between devices, on_device(): halos.append(lax.ppermute(value, both, pairs))  6.69 us
    ppermute x2, starting transfers between devices, eastward(): lax.ppermute(value, both, [(rank(*a), rank(*b)) for a, b in pairs.items()])  2.03 us
    ppermute x2, starting transfers between devices, swapped(): return lax.ppermute(value, both, pairs)  1.75 us
    ppermute x2, waiting for transfers between devices, eastward(): lax.ppermute(value, both, [(rank(*a), rank(*b)) for a, b in pairs.items()])  0.62 us
  transfers between devices with their start and end apart: 6, of which 3 were waited for; matrix products, arithmetic and copies ran while one was open for 0% of the time, Pallas kernels for 14%

profile of v23, /device:TPU:0, one launch (start us, length us, event | category | flops | bytes accessed | tf_op | source)
XLA Modules:
  0.0 19.0 jit_solution(16538260011420417991)
XLA Ops:
  0.0 0.0 copy-start
  0.0 0.0 copy-start.2
  0.0 1.7 %strips.1 = (f32[216,128]{1,0:T(8,128)S(1)}, f32[216,128]{1,0:T(8,128)S(1)}, f32[448,256]{1,0:T(8,128)S(1)}, s32[8,128]{1,0:T(8,128)S(1)}) custom-call(s32[2,256]{1,0:T(2,128)} %refs_0_.1, s32[1,256]{1,0:T(1,128)} %refs_1_.1, f32[3,8,8,256]{3,2,1,0:T(8,128)} %refs_2_.1, f32[8,8,256]{2,1,0:T(8,128)} %refs_3_.1, f32[8,8,256]{2,1,0:T(8,128)} %refs_4_.1, ...), custom_call_target="tpu_custom_call" | custom-call | flops 100000000 | bytes 2097152 | tf_op jit(solution)/shard_map/strips/pallas_call | solution.py:791
  1.7 3.0 %collective-permute-start = (f32[216,128]{1,0:T(8,128)S(1)}, f32[216,128]{1,0:T(8,128)S(1)}, u32[]{:S(2)}, u32[]{:S(2)}) collective-permute-start(f32[216,128]{1,0:T(8,128)S(1)} %get-tuple-element.19.first_ref), channel_id=1, source_target_pairs={{0,16},{1,17},{2,18},{3,19},{4,27},{5,26},{6,25},{7,24},{8,23},{9,... | collective-permute-start | bytes 331784 | tf_op jit(solution)/shard_map/ppermute | solution.py:905
  4.7 3.7 %collective-permute-start.1 = (f32[216,128]{1,0:T(8,128)S(1)}, f32[216,128]{1,0:T(8,128)S(1)}, u32[]{:S(2)}, u32[]{:S(2)}) collective-permute-start(f32[216,128]{1,0:T(8,128)S(1)} %get-tuple-element.20.then_ref), channel_id=1, source_target_pairs={{0,31},{1,30},{2,29},{3,28},{4,20},{5,21},{6,22},{7,23},{8,24},{9,... | collective-permute-start | bytes 331784 | tf_op jit(solution)/shard_map/ppermute | solution.py:905
  8.4 0.0 copy-done
  8.4 0.0 copy-done.2
  8.4 0.8 %rows.1 = (f32[216,128]{1,0:T(8,128)S(1)}, f32[56,128]{1,0:T(8,128)S(1)}, f32[56,128]{1,0:T(8,128)S(1)}, f32[448,128]{1,0:T(8,128)S(1)}) custom-call(s32[8,128]{1,0:T(8,128)S(1)} %get-tuple-element.18.flags_ref, f32[448,256]{1,0:T(8,128)S(1)} %get-tuple-element.21.stored_ref, f32[216,128]{1,0:T(8,128)S(1)} %get-tuple-element.19.first_ref, ...), custom_call_target="tpu_custom_call" | custom-call | flops 100000000 | bytes 2097152 | tf_op jit(solution)/shard_map/rows/pallas_call | solution.py:791
  9.3 1.5 %collective-permute-start.5 = (f32[216,128]{1,0:T(8,128)S(1)}, f32[216,128]{1,0:T(8,128)S(1)}, u32[]{:S(2)}, u32[]{:S(2)}) collective-permute-start(f32[216,128]{1,0:T(8,128)S(1)} %get-tuple-element.26), channel_id=1, source_target_pairs={{0,16},{1,2},{2,1},{3,4},{4,3},{5,6},{6,5},{7,8},{8,7},{9,10},{10,... | collective-permute-start | bytes 331784 | tf_op jit(solution)/shard_map/ppermute | solution.py:856
  10.8 0.5 %collective-permute-start.3 = (f32[56,128]{1,0:T(8,128)S(1)}, f32[56,128]{1,0:T(8,128)S(1)}, u32[]{:S(2)}, u32[]{:S(2)}) collective-permute-start(f32[56,128]{1,0:T(8,128)S(1)} %get-tuple-element.24), channel_id=1, source_target_pairs={{0,16},{1,29},{2,30},{3,27},{4,28},{5,25},{6,26},{7,23},{8,24},{9,... | collective-permute-start | bytes 86024 | tf_op jit(solution)/shard_map/ppermute | solution.py:875
  11.3 1.5 %collective-permute-start.4 = (f32[56,128]{1,0:T(8,128)S(1)}, f32[56,128]{1,0:T(8,128)S(1)}, u32[]{:S(2)}, u32[]{:S(2)}) collective-permute-start(f32[56,128]{1,0:T(8,128)S(1)} %get-tuple-element.25), channel_id=1, source_target_pairs={{0,16},{1,18},{2,17},{3,20},{4,19},{5,22},{6,21},{7,24},{8,23},{9,... | collective-permute-start | bytes 86024 | tf_op jit(solution)/shard_map/ppermute | solution.py:875
  12.8 0.0 copy-done.1
  12.8 0.5 %own.1 = (f32[448,384]{1,0:T(8,128)S(1)}, bf16[384,256]{1,0:T(8,128)(2,1)S(1)}) custom-call(s32[8,128]{1,0:T(8,128)S(1)} %get-tuple-element.18.flags_ref, f32[448,256]{1,0:T(8,128)S(1)} %get-tuple-element.21.stored_ref, s32[64,640]{1,0:T(8,128)S(1)} %copy-done.1), custom_call_target="tpu_custom_call" | custom-call | flops 100000000 | bytes 2097152 | tf_op jit(solution)/shard_map/own/pallas_call | solution.py:791
  13.3 0.0 collective-permute-done.first_ref
  13.3 0.2 collective-permute-done.1.then_ref
  13.5 0.2 %corners.1 = f32[480,128]{1,0:T(8,128)S(1)} custom-call(s32[8,128]{1,0:T(8,128)S(1)} %get-tuple-element.18.flags_ref, f32[216,128]{1,0:T(8,128)S(1)} %collective-permute-done.first_ref, f32[216,128]{1,0:T(8,128)S(1)} %collective-permute-done.1.then_ref, f32[448,128]{1,0:T(8,128)S(1)} %get-tuple-element.22.pair_ref, ...), custom_call_target="tpu_custom_call" | custom-call | flops 100000000 | bytes 2097152 | tf_op jit(solution)/shard_map/corners/pallas_call | solution.py:791
  13.7 0.2 %collective-permute-start.2 = (f32[480,128]{1,0:T(8,128)S(1)}, f32[480,128]{1,0:T(8,128)S(1)}, u32[]{:S(2)}, u32[]{:S(2)}) collective-permute-start(f32[480,128]{1,0:T(8,128)S(1)} %corners.1), channel_id=1, source_target_pairs={{0,1},{1,0},{2,3},{3,2},{4,5},{5,4},{6,7},{7,6},{8,9},{9,8},{10,11... | collective-permute-start | bytes 737288 | tf_op jit(solution)/shard_map/ppermute | solution.py:856
  13.9 0.8 %middle.1 = (f32[704,128]{1,0:T(8,128)S(1)}, f32[704,128]{1,0:T(8,128)S(1)}, f32[704,128]{1,0:T(8,128)S(1)}) custom-call(s32[8,128]{1,0:T(8,128)S(1)} %get-tuple-element.18.flags_ref, f32[216,128]{1,0:T(8,128)S(1)} %collective-permute-done.first_ref, f32[216,128]{1,0:T(8,128)S(1)} %collective-permute-done.1.then_ref, ...), custom_call_target="tpu_custom_call" | custom-call | flops 100000000 | bytes 2097152 | tf_op jit(solution)/shard_map/middle/pallas_call | solution.py:791
  14.7 0.3 %collective-permute-done.3.far1_ref = f32[56,128]{1,0:T(8,128)S(1)} collective-permute-done((f32[56,128]{1,0:T(8,128)S(1)}, f32[56,128]{1,0:T(8,128)S(1)}, u32[]{:S(2)}, u32[]{:S(2)}) %collective-permute-start.3) | collective-permute-done | bytes 28704 | tf_op jit(solution)/shard_map/ppermute | solution.py:875
  15.1 0.3 %collective-permute-done.4.far0_ref = f32[56,128]{1,0:T(8,128)S(1)} collective-permute-done((f32[56,128]{1,0:T(8,128)S(1)}, f32[56,128]{1,0:T(8,128)S(1)}, u32[]{:S(2)}, u32[]{:S(2)}) %collective-permute-start.4) | collective-permute-done | bytes 28704 | tf_op jit(solution)/shard_map/ppermute | solution.py:875
  15.4 0.0 collective-permute-done.5.next_ref
  15.4 0.2 %far.1.next_ref = f32[512,128]{1,0:T(8,128)S(1)} custom-call(s32[8,128]{1,0:T(8,128)S(1)} %get-tuple-element.18.flags_ref, f32[56,128]{1,0:T(8,128)S(1)} %collective-permute-done.3.far1_ref, f32[56,128]{1,0:T(8,128)S(1)} %collective-permute-done.4.far0_ref, f32[216,128]{1,0:T(8,128)S(1)} %collective-permute-done.5.next_ref, ...), custom_call_target="tpu_custom_call" | custom-call | flops 99999997952 | bytes 2097152 | tf_op jit(solution)/shard_map/far/pallas_call | solution.py:791
  15.6 0.0 collective-permute-done.2.pair_ref
  15.6 3.4 %steps.1 = f32[3,8,8,256]{3,2,1,0:T(8,128)} custom-call(s32[8,128]{1,0:T(8,128)S(1)} %get-tuple-element.18.flags_ref, f32[480,128]{1,0:T(8,128)S(1)} %collective-permute-done.2.pair_ref, f32[512,128]{1,0:T(8,128)S(1)} %far.1.next_ref, f32[704,128]{1,0:T(8,128)S(1)} %get-tuple-element.28._.low_ref, f32[704,128]{1,0:T(8,128)S(1)} %get-tuple-element.29.centre_ref, ...), custom_call_target="tpu_custom_call" | custom-call | flops 100000000 | bytes 2097152 | tf_op jit(solution)/shard_map/steps/pallas_call | solution.py:791
  (1 shorter events, 0.0 us)
Async XLA Ops:
  0.0 8.4 %copy-start = (f32[320,256]{1,0:T(8,128)S(1)}, f32[320,256]{1,0:T(8,128)}, u32[]{:S(2)}) copy-start(f32[320,256]{1,0:T(8,128)} %constant.8.clone.table_ref) | copy-start | bytes 983044
  0.0 8.4 %copy-start.2 = (f32[64,128]{1,0:T(8,128)S(1)}, f32[64,128]{1,0:T(8,128)}, u32[]{:S(2)}) copy-start(f32[64,128]{1,0:T(8,128)} %constant.9.clone.weight_ref) | copy-start | bytes 98308
  1.7 11.6 %collective-permute-start = (f32[216,128]{1,0:T(8,128)S(1)}, f32[216,128]{1,0:T(8,128)S(1)}, u32[]{:S(2)}, u32[]{:S(2)}) collective-permute-start(f32[216,128]{1,0:T(8,128)S(1)} %get-tuple-element.19.first_ref), channel_id=1, source_target_pairs={{0,16},{1,17},{2,18},{3,19},{4,27},{5,26},{6,25},{7,24},{8,23},{9,... | collective-permute-start | bytes 331784 | tf_op jit(solution)/shard_map/ppermute | solution.py:905
  4.7 8.8 %collective-permute-start.1 = (f32[216,128]{1,0:T(8,128)S(1)}, f32[216,128]{1,0:T(8,128)S(1)}, u32[]{:S(2)}, u32[]{:S(2)}) collective-permute-start(f32[216,128]{1,0:T(8,128)S(1)} %get-tuple-element.20.then_ref), channel_id=1, source_target_pairs={{0,31},{1,30},{2,29},{3,28},{4,20},{5,21},{6,22},{7,23},{8,24},{9,... | collective-permute-start | bytes 331784 | tf_op jit(solution)/shard_map/ppermute | solution.py:905
  8.4 4.4 %copy-start.1 = (s32[64,640]{1,0:T(8,128)S(1)}, s32[64,640]{1,0:T(8,128)}, u32[]{:S(2)}) copy-start(s32[64,640]{1,0:T(8,128)} %constant.11.clone.lanes_ref) | copy-start | bytes 491524
  9.3 6.1 %collective-permute-start.5 = (f32[216,128]{1,0:T(8,128)S(1)}, f32[216,128]{1,0:T(8,128)S(1)}, u32[]{:S(2)}, u32[]{:S(2)}) collective-permute-start(f32[216,128]{1,0:T(8,128)S(1)} %get-tuple-element.26), channel_id=1, source_target_pairs={{0,16},{1,2},{2,1},{3,4},{4,3},{5,6},{6,5},{7,8},{8,7},{9,10},{10,... | collective-permute-start | bytes 331784 | tf_op jit(solution)/shard_map/ppermute | solution.py:856
  10.8 4.2 %collective-permute-start.3 = (f32[56,128]{1,0:T(8,128)S(1)}, f32[56,128]{1,0:T(8,128)S(1)}, u32[]{:S(2)}, u32[]{:S(2)}) collective-permute-start(f32[56,128]{1,0:T(8,128)S(1)} %get-tuple-element.24), channel_id=1, source_target_pairs={{0,16},{1,29},{2,30},{3,27},{4,28},{5,25},{6,26},{7,23},{8,24},{9,... | collective-permute-start | bytes 86024 | tf_op jit(solution)/shard_map/ppermute | solution.py:875
  11.3 4.0 %collective-permute-start.4 = (f32[56,128]{1,0:T(8,128)S(1)}, f32[56,128]{1,0:T(8,128)S(1)}, u32[]{:S(2)}, u32[]{:S(2)}) collective-permute-start(f32[56,128]{1,0:T(8,128)S(1)} %get-tuple-element.25), channel_id=1, source_target_pairs={{0,16},{1,18},{2,17},{3,20},{4,19},{5,22},{6,21},{7,24},{8,23},{9,... | collective-permute-start | bytes 86024 | tf_op jit(solution)/shard_map/ppermute | solution.py:875
  13.7 1.9 %collective-permute-start.2 = (f32[480,128]{1,0:T(8,128)S(1)}, f32[480,128]{1,0:T(8,128)S(1)}, u32[]{:S(2)}, u32[]{:S(2)}) collective-permute-start(f32[480,128]{1,0:T(8,128)S(1)} %corners.1), channel_id=1, source_target_pairs={{0,1},{1,0},{2,3},{3,2},{4,5},{5,4},{6,7},{7,6},{8,9},{9,8},{10,11... | collective-permute-start | bytes 737288 | tf_op jit(solution)/shard_map/ppermute | solution.py:856

commit v24 on v23

--- a/solution.py
+++ b/solution.py
@@ -574,22 +574,25 @@
             ref[n * NODES : (n + 1) * NODES] = part[:, k * LANES : (k + 1) * LANES]
 
 
-def far_kernel(block_cols, flags_ref, far1_ref, far0_ref, next_ref, _, out_ref):
+def far_kernel(block_cols, flags_ref, far1_ref, far0_ref, _, out_ref):
     east0, flip0, east1, flip1 = flags_in(flags_ref)
     odd = lax.axis_index("blk") & 1
-    lane = lax.broadcasted_iota(i32, (1, LANES), 1)
     below = jnp.broadcast_to(odd == 0, (1, LANES))
-    strip = jnp.concatenate([next_ref[...], pltpu.roll(next_ref[...], 64, 1)], 0)
-    strip = placed_rows(strip, below, 4)
     corners, strip_of = arrived_corners(far0_ref[...], far1_ref[...], block_cols, odd)
     late = jnp.where(strip_of != 0, east1, east0) == 0
     rim = MOVED + NODES // 2 + NP
-    rim = jnp.concatenate(spread_out(corners[rim : rim + NP], below, 2), 0)
-    corners = placed_rows(corners, late, 0)
-    own = lane < 64
-    out_ref[:ROWS] = jnp.where(own, strip[:ROWS], corners[:ROWS])
-    out_ref[ROWS:ALL_ROWS] = corners[ROWS:]
-    out_ref[ALL_ROWS:] = jnp.where(own, strip[ROWS:], rim)
+    out_ref[:ALL_ROWS] = placed_rows(corners, late, 0)
+    out_ref[ALL_ROWS:] = jnp.concatenate(spread_out(corners[rim : rim + NP], below, 2), 0)
+
+
+def next_kernel(next_ref, corners_ref, out_ref):
+    below = jnp.broadcast_to((lax.axis_index("blk") & 1) == 0, (1, LANES))
+    own = lax.broadcasted_iota(i32, (1, LANES), 1) < 64
+    strip = jnp.concatenate([next_ref[...], pltpu.roll(next_ref[...], 64, 1)], 0)
+    strip = placed_rows(strip, below, 4)
+    out_ref[:ROWS] = jnp.where(own, strip[:ROWS], corners_ref[:ROWS])
+    out_ref[ROWS:ALL_ROWS] = corners_ref[ROWS:ALL_ROWS]
+    out_ref[ALL_ROWS:] = jnp.where(own, strip[ROWS:], corners_ref[ALL_ROWS:])
 
 
 def steps_kernel(
@@ -931,12 +934,16 @@
         10**8,
         name="middle",
     )
-    (from_next,) = call(
+    outer = ((RIM_ROWS, LANES), f32)
+    (corners,) = call(
         functools.partial(far_kernel, block_cols),
-        [(vmem, x) for x in (flags, far1, far0, from_next, low)],
-        [((RIM_ROWS, LANES), f32)],
+        [(vmem, x) for x in (flags, far1, far0, low)],
+        [outer],
         10**11,
         name="far",
+    )
+    (from_next,) = call(
+        next_kernel, [(vmem, x) for x in (from_next, corners)], [outer], 10**10, name="next"
     )
     (stepped,) = call(
         functools.partial(steps_kernel, block_cols),

time: 19.3 us -> 20.1 us (1.041); the launches traced: 19 us -> 20 us
  waiting for transfers between devices: 0.79 us -> 1.82 us
    ppermute x2, waiting for transfers between devices: 0.01 us -> 1.32 us  [swapped(): return lax.ppermute(value, both, pairs)]
    ppermute x2, waiting for transfers between devices: 0.62 us -> 0.34 us  [eastward(): lax.ppermute(value, both, [(rank(*a), rank(*b)) for a, b in pairs.items()])]
    pallas_call x7 -> x8, Pallas kernels: 7.64 us -> 7.74 us  [call(): pl.pallas_call(kernel, out_shape=[jax.ShapeDtypeStruct(*out) for out in o...]
  transfers between devices with their start and end apart: 6 -> 6, of which waited for: 3 -> 3; matrix products, arithmetic and copies ran while one was open for 0% -> 0% of each run, Pallas kernels for 14% -> 13%
where the time goes in v24:
time: 20.1 us; the launch traced here: 20 us
  starting transfers between devices  10.4 us (52%)
  Pallas kernels  7.74 us (39%)
  waiting for transfers between devices  1.82 us (9%)
    pallas_call x8, Pallas kernels, call(): pl.pallas_call(kernel, out_shape=[jax.ShapeDtypeStruct(*out) for out in o...  7.74 us
    ppermute x2, starting transfers between devices, on_device(): halos.append(lax.ppermute(value, both, pairs))  6.69 us
    ppermute x2, starting transfers between devices, eastward(): lax.ppermute(value, both, [(rank(*a), rank(*b)) for a, b in pairs.items()])  2.07 us
    ppermute x2, starting transfers between devices, swapped(): return lax.ppermute(value, both, pairs)  1.6 us
    ppermute x2, waiting for transfers between devices, swapped(): return lax.ppermute(value, both, pairs)  1.32 us
  transfers between devices with their start and end apart: 6, of which 3 were waited for; matrix products, arithmetic and copies ran while one was open for 0% of the time, Pallas kernels for 13%

profile of v24, /device:TPU:0, one launch (start us, length us, event | category | flops | bytes accessed | tf_op | source)
XLA Modules:
  0.0 20.0 jit_solution(2498949944597660729)
XLA Ops:
  0.0 0.0 copy-start
  0.0 1.7 %strips.1 = (f32[216,128]{1,0:T(8,128)S(1)}, f32[216,128]{1,0:T(8,128)S(1)}, f32[448,256]{1,0:T(8,128)S(1)}, s32[8,128]{1,0:T(8,128)S(1)}) custom-call(s32[2,256]{1,0:T(2,128)} %refs_0_.1, s32[1,256]{1,0:T(1,128)} %refs_1_.1, f32[3,8,8,256]{3,2,1,0:T(8,128)} %refs_2_.1, f32[8,8,256]{2,1,0:T(8,128)} %refs_3_.1, f32[8,8,256]{2,1,0:T(8,128)} %refs_4_.1, ...), custom_call_target="tpu_custom_call" | custom-call | flops 100000000 | bytes 2097152 | tf_op jit(solution)/shard_map/strips/pallas_call | solution.py:794
  1.7 3.0 %collective-permute-start = (f32[216,128]{1,0:T(8,128)S(1)}, f32[216,128]{1,0:T(8,128)S(1)}, u32[]{:S(2)}, u32[]{:S(2)}) collective-permute-start(f32[216,128]{1,0:T(8,128)S(1)} %get-tuple-element.19.first_ref), channel_id=1, source_target_pairs={{0,16},{1,17},{2,18},{3,19},{4,27},{5,26},{6,25},{7,24},{8,23},{9,... | collective-permute-start | bytes 331784 | tf_op jit(solution)/shard_map/ppermute | solution.py:908
  4.7 3.7 %collective-permute-start.1 = (f32[216,128]{1,0:T(8,128)S(1)}, f32[216,128]{1,0:T(8,128)S(1)}, u32[]{:S(2)}, u32[]{:S(2)}) collective-permute-start(f32[216,128]{1,0:T(8,128)S(1)} %get-tuple-element.20.then_ref), channel_id=1, source_target_pairs={{0,31},{1,30},{2,29},{3,28},{4,20},{5,21},{6,22},{7,23},{8,24},{9,... | collective-permute-start | bytes 331784 | tf_op jit(solution)/shard_map/ppermute | solution.py:908
  8.4 0.0 copy-done
  8.4 0.0 copy-done.2
  8.4 0.8 %rows.1 = (f32[216,128]{1,0:T(8,128)S(1)}, f32[56,128]{1,0:T(8,128)S(1)}, f32[56,128]{1,0:T(8,128)S(1)}, f32[448,128]{1,0:T(8,128)S(1)}) custom-call(s32[8,128]{1,0:T(8,128)S(1)} %get-tuple-element.18.flags_ref, f32[448,256]{1,0:T(8,128)S(1)} %get-tuple-element.21.stored_ref, f32[216,128]{1,0:T(8,128)S(1)} %get-tuple-element.19.first_ref, ...), custom_call_target="tpu_custom_call" | custom-call | flops 100000000 | bytes 2097152 | tf_op jit(solution)/shard_map/rows/pallas_call | solution.py:794
  9.3 1.5 %collective-permute-start.4 = (f32[56,128]{1,0:T(8,128)S(1)}, f32[56,128]{1,0:T(8,128)S(1)}, u32[]{:S(2)}, u32[]{:S(2)}) collective-permute-start(f32[56,128]{1,0:T(8,128)S(1)} %get-tuple-element.25), channel_id=1, source_target_pairs={{0,16},{1,29},{2,30},{3,27},{4,28},{5,25},{6,26},{7,23},{8,24},{9,... | collective-permute-start | bytes 86024 | tf_op jit(solution)/shard_map/ppermute | solution.py:878
  10.8 0.5 %collective-permute-start.5 = (f32[56,128]{1,0:T(8,128)S(1)}, f32[56,128]{1,0:T(8,128)S(1)}, u32[]{:S(2)}, u32[]{:S(2)}) collective-permute-start(f32[56,128]{1,0:T(8,128)S(1)} %get-tuple-element.26), channel_id=1, source_target_pairs={{0,16},{1,18},{2,17},{3,20},{4,19},{5,22},{6,21},{7,24},{8,23},{9,... | collective-permute-start | bytes 86024 | tf_op jit(solution)/shard_map/ppermute | solution.py:878
  11.3 1.5 %collective-permute-start.3 = (f32[216,128]{1,0:T(8,128)S(1)}, f32[216,128]{1,0:T(8,128)S(1)}, u32[]{:S(2)}, u32[]{:S(2)}) collective-permute-start(f32[216,128]{1,0:T(8,128)S(1)} %get-tuple-element.24), channel_id=1, source_target_pairs={{0,16},{1,2},{2,1},{3,4},{4,3},{5,6},{6,5},{7,8},{8,7},{9,10},{10,... | collective-permute-start | bytes 331784 | tf_op jit(solution)/shard_map/ppermute | solution.py:859
  12.8 0.0 copy-done.1
  12.8 0.5 %own.1 = (f32[448,384]{1,0:T(8,128)S(1)}, bf16[384,256]{1,0:T(8,128)(2,1)S(1)}) custom-call(s32[8,128]{1,0:T(8,128)S(1)} %get-tuple-element.18.flags_ref, f32[448,256]{1,0:T(8,128)S(1)} %get-tuple-element.21.stored_ref, s32[64,640]{1,0:T(8,128)S(1)} %copy-done.1), custom_call_target="tpu_custom_call" | custom-call | flops 100000000 | bytes 2097152 | tf_op jit(solution)/shard_map/own/pallas_call | solution.py:794
  13.3 0.0 collective-permute-done.first_ref
  13.3 0.2 collective-permute-done.1.then_ref
  13.5 0.2 %corners.1 = f32[480,128]{1,0:T(8,128)S(1)} custom-call(s32[8,128]{1,0:T(8,128)S(1)} %get-tuple-element.18.flags_ref, f32[216,128]{1,0:T(8,128)S(1)} %collective-permute-done.first_ref, f32[216,128]{1,0:T(8,128)S(1)} %collective-permute-done.1.then_ref, f32[448,128]{1,0:T(8,128)S(1)} %get-tuple-element.22.pair_ref, ...), custom_call_target="tpu_custom_call" | custom-call | flops 100000000 | bytes 2097152 | tf_op jit(solution)/shard_map/corners/pallas_call | solution.py:794
  13.7 0.1 collective-permute-start.2
  13.8 0.8 %middle.1 = (f32[704,128]{1,0:T(8,128)S(1)}, f32[704,128]{1,0:T(8,128)S(1)}, f32[704,128]{1,0:T(8,128)S(1)}) custom-call(s32[8,128]{1,0:T(8,128)S(1)} %get-tuple-element.18.flags_ref, f32[216,128]{1,0:T(8,128)S(1)} %collective-permute-done.first_ref, f32[216,128]{1,0:T(8,128)S(1)} %collective-permute-done.1.then_ref, ...), custom_call_target="tpu_custom_call" | custom-call | flops 100000000 | bytes 2097152 | tf_op jit(solution)/shard_map/middle/pallas_call | solution.py:794
  14.6 0.0 collective-permute-done.4.far1_ref
  14.6 0.3 %collective-permute-done.5.far0_ref = f32[56,128]{1,0:T(8,128)S(1)} collective-permute-done((f32[56,128]{1,0:T(8,128)S(1)}, f32[56,128]{1,0:T(8,128)S(1)}, u32[]{:S(2)}, u32[]{:S(2)}) %collective-permute-start.5) | collective-permute-done | bytes 28704 | tf_op jit(solution)/shard_map/ppermute | solution.py:878
  15.0 0.2 far.1.corners_ref
  15.1 1.3 %collective-permute-done.3.next_ref = f32[216,128]{1,0:T(8,128)S(1)} collective-permute-done((f32[216,128]{1,0:T(8,128)S(1)}, f32[216,128]{1,0:T(8,128)S(1)}, u32[]{:S(2)}, u32[]{:S(2)}) %collective-permute-start.3) | collective-permute-done | bytes 110624 | tf_op jit(solution)/shard_map/ppermute | solution.py:859
  16.5 0.1 next.1.next_ref
  16.6 0.0 collective-permute-done.2.pair_ref
  16.6 3.4 %steps.1 = f32[3,8,8,256]{3,2,1,0:T(8,128)} custom-call(s32[8,128]{1,0:T(8,128)S(1)} %get-tuple-element.18.flags_ref, f32[480,128]{1,0:T(8,128)S(1)} %collective-permute-done.2.pair_ref, f32[512,128]{1,0:T(8,128)S(1)} %next.1.next_ref, f32[704,128]{1,0:T(8,128)S(1)} %get-tuple-element.28._.low_ref, f32[704,128]{1,0:T(8,128)S(1)} %get-tuple-element.29.centre_ref, ...), custom_call_target="tpu_custom_call" | custom-call | flops 100000000 | bytes 2097152 | tf_op jit(solution)/shard_map/steps/pallas_call | solution.py:794
  (2 shorter events, 0.0 us)
Async XLA Ops:
  0.0 8.4 %copy-start = (f32[320,256]{1,0:T(8,128)S(1)}, f32[320,256]{1,0:T(8,128)}, u32[]{:S(2)}) copy-start(f32[320,256]{1,0:T(8,128)} %constant.8.clone.table_ref) | copy-start | bytes 983044
  0.0 8.4 %copy-start.2 = (f32[64,128]{1,0:T(8,128)S(1)}, f32[64,128]{1,0:T(8,128)}, u32[]{:S(2)}) copy-start(f32[64,128]{1,0:T(8,128)} %constant.9.clone.weight_ref) | copy-start | bytes 98308
  1.7 11.6 %collective-permute-start = (f32[216,128]{1,0:T(8,128)S(1)}, f32[216,128]{1,0:T(8,128)S(1)}, u32[]{:S(2)}, u32[]{:S(2)}) collective-permute-start(f32[216,128]{1,0:T(8,128)S(1)} %get-tuple-element.19.first_ref), channel_id=1, source_target_pairs={{0,16},{1,17},{2,18},{3,19},{4,27},{5,26},{6,25},{7,24},{8,23},{9,... | collective-permute-start | bytes 331784 | tf_op jit(solution)/shard_map/ppermute | solution.py:908
  4.7 8.8 %collective-permute-start.1 = (f32[216,128]{1,0:T(8,128)S(1)}, f32[216,128]{1,0:T(8,128)S(1)}, u32[]{:S(2)}, u32[]{:S(2)}) collective-permute-start(f32[216,128]{1,0:T(8,128)S(1)} %get-tuple-element.20.then_ref), channel_id=1, source_target_pairs={{0,31},{1,30},{2,29},{3,28},{4,20},{5,21},{6,22},{7,23},{8,24},{9,... | collective-permute-start | bytes 331784 | tf_op jit(solution)/shard_map/ppermute | solution.py:908
  8.4 4.4 %copy-start.1 = (s32[64,640]{1,0:T(8,128)S(1)}, s32[64,640]{1,0:T(8,128)}, u32[]{:S(2)}) copy-start(s32[64,640]{1,0:T(8,128)} %constant.11.clone.lanes_ref) | copy-start | bytes 491524
  9.3 5.4 %collective-permute-start.4 = (f32[56,128]{1,0:T(8,128)S(1)}, f32[56,128]{1,0:T(8,128)S(1)}, u32[]{:S(2)}, u32[]{:S(2)}) collective-permute-start(f32[56,128]{1,0:T(8,128)S(1)} %get-tuple-element.25), channel_id=1, source_target_pairs={{0,16},{1,29},{2,30},{3,27},{4,28},{5,25},{6,26},{7,23},{8,24},{9,... | collective-permute-start | bytes 86024 | tf_op jit(solution)/shard_map/ppermute | solution.py:878
  10.8 4.2 %collective-permute-start.5 = (f32[56,128]{1,0:T(8,128)S(1)}, f32[56,128]{1,0:T(8,128)S(1)}, u32[]{:S(2)}, u32[]{:S(2)}) collective-permute-start(f32[56,128]{1,0:T(8,128)S(1)} %get-tuple-element.26), channel_id=1, source_target_pairs={{0,16},{1,18},{2,17},{3,20},{4,19},{5,22},{6,21},{7,24},{8,23},{9,... | collective-permute-start | bytes 86024 | tf_op jit(solution)/shard_map/ppermute | solution.py:878
  11.3 5.1 %collective-permute-start.3 = (f32[216,128]{1,0:T(8,128)S(1)}, f32[216,128]{1,0:T(8,128)S(1)}, u32[]{:S(2)}, u32[]{:S(2)}) collective-permute-start(f32[216,128]{1,0:T(8,128)S(1)} %get-tuple-element.24), channel_id=1, source_target_pairs={{0,16},{1,2},{2,1},{3,4},{4,3},{5,6},{6,5},{7,8},{8,7},{9,10},{10,... | collective-permute-start | bytes 331784 | tf_op jit(solution)/shard_map/ppermute | solution.py:859
  13.7 2.9 %collective-permute-start.2 = (f32[480,128]{1,0:T(8,128)S(1)}, f32[480,128]{1,0:T(8,128)S(1)}, u32[]{:S(2)}, u32[]{:S(2)}) collective-permute-start(f32[480,128]{1,0:T(8,128)S(1)} %corners.1), channel_id=1, source_target_pairs={{0,1},{1,0},{2,3},{3,2},{4,5},{5,4},{6,7},{7,6},{8,9},{9,8},{10,11... | collective-permute-start | bytes 737288 | tf_op jit(solution)/shard_map/ppermute | solution.py:859

commit v25 on v23

--- a/solution.py
+++ b/solution.py
@@ -408,9 +408,11 @@
 def strips_kernel(block_cols, *refs):
     sources, (first_ref, then_ref, stored_ref, flags_ref) = refs[:8], refs[8:12]
     buffers, sems = refs[12:20], refs[20]
+    pieces = list(zip(sources, buffers))
+    pieces[2:3] = [(sources[2].at[c], buffers[2].at[c]) for c in range(3)]
     copies = [
         pltpu.make_async_copy(source, buffer, sems.at[k])
-        for k, (source, buffer) in enumerate(zip(sources, buffers))
+        for k, (source, buffer) in enumerate(pieces)
     ]
     for copy in copies:
         copy.start()
@@ -432,7 +434,7 @@
     col = jnp.where(east, GX - RING, 0) + (place & 3)
     col = jnp.where(lane >= LANES, jnp.where(east, GX - RING - 1, RING), col)
     one_hot = by_slot(slots, col * GY + row)
-    for copy in copies[2:7]:
+    for copy in copies[2:9]:
         copy.wait()
     stored = stored_rows(fields_ref, (area_ref, depth_ref, spin_ref, tide_ref))
     both = picked(stored, one_hot)
@@ -454,7 +456,7 @@
         [part[k * NODES : (k + 1) * NODES] for k in range(ARRAYS)]
         for part in (both[:, :LANES], both[:, LANES:])
     )
-    for copy in copies[7:]:
+    for copy in copies[9:]:
         copy.wait()
     table, weight = table_ref[: 8 * NP].astype(bf16), table_ref[8 * NP :, :LANES]
     edges = column_edges(table, weight, *ring[:6])
@@ -594,7 +596,7 @@
 
 def steps_kernel(
     block_cols, flags_ref, pair_ref, next_ref, low_ref, centre_ref,
-    high_ref, hot_ref, table_ref, weight_ref, lanes_ref, out_ref, sums,
+    high_ref, hot_ref, table_ref, weight_ref, lanes_ref, out_ref, sums, leaving, sems,
 ):
     east0, flip0, east1, flip1 = flags_in(flags_ref)
     odd = lax.axis_index("blk") & 1
@@ -776,7 +778,13 @@
     stepped = jnp.concatenate(stepped, 1)[:, :MID]
     own = lanes_ref[27:28, LANES : LANES + MID] != 0
     stored = picked(jnp.where(own, stepped, 0.0), hot_ref[...])
-    out_ref[...] = stored.reshape(out_ref.shape)
+    copies = []
+    for c in range(3):
+        leaving[c] = stored[c * NODES : (c + 1) * NODES].reshape(leaving.shape[1:])
+        copies.append(pltpu.make_async_copy(leaving.at[c], out_ref.at[c], sems.at[c]))
+        copies[c].start()
+    for copy in copies:
+        copy.wait()
 
 
 def on_device(fields, jacobian, water_depth, coriolis, tide_height, slot_of, seam_rows):
@@ -787,12 +795,12 @@
     params = pltpu.CompilerParams(vmem_limit_bytes=48 * 2**20)
     held = (fields, jacobian, water_depth, coriolis, tide_height)
 
-    def call(kernel, ins, outs, cost, scratch=(), name=None):
+    def call(kernel, ins, outs, cost, scratch=(), name=None, out_spec=vmem):
         return pl.pallas_call(
             kernel,
             out_shape=[jax.ShapeDtypeStruct(*out) for out in outs],
             in_specs=[spec for spec, value in ins],
-            out_specs=[vmem] * len(outs),
+            out_specs=[out_spec] * len(outs),
             scratch_shapes=list(scratch),
             compiler_params=params,
             cost_estimate=pl.CostEstimate(
@@ -810,7 +818,7 @@
     def room(values, spaces=None):
         spaces = spaces or [pltpu.VMEM] * len(values)
         buffers = [space(x.shape, x.dtype) for space, x in zip(spaces, values)]
-        return buffers + [pltpu.SemaphoreType.DMA((len(values),))]
+        return buffers + [pltpu.SemaphoreType.DMA((len(values) + 2,))]
 
     needed = (seam_rows, slot_of, *held, edge_table)
     corner = ((CORNER_ROWS, LANES), f32)
@@ -948,7 +956,12 @@
         ],
         [(fields.shape, f32)],
         10**8,
-        scratch=[pltpu.VMEM((EXT // LANES, 4 * NODES, LANES), f32)],
+        scratch=[
+            pltpu.VMEM((EXT // LANES, 4 * NODES, LANES), f32),
+            pltpu.VMEM(fields.shape, f32),
+            pltpu.SemaphoreType.DMA((3,)),
+        ],
+        out_spec=hbm,
         name="steps",
     )
     return stepped

time: 19.3 us -> 19.3 us (level)
  no operation moved by 1% of the time
where the time goes in v25:
time: 19.3 us; the launch traced here: 19 us
  starting transfers between devices  10.5 us (54%)
  Pallas kernels  7.65 us (40%)
  waiting for transfers between devices  0.81 us (4%)
    pallas_call x7, Pallas kernels, call(): pl.pallas_call(kernel, out_shape=[jax.ShapeDtypeStruct(*out) for out in o...  7.65 us
    ppermute x2, starting transfers between devices, on_device(): halos.append(lax.ppermute(value, both, pairs))  6.69 us
    ppermute x2, starting transfers between devices, eastward(): lax.ppermute(value, both, [(rank(*a), rank(*b)) for a, b in pairs.items()])  2.03 us
    ppermute x2, starting transfers between devices, swapped(): return lax.ppermute(value, both, pairs)  1.74 us
    ppermute x2, waiting for transfers between devices, eastward(): lax.ppermute(value, both, [(rank(*a), rank(*b)) for a, b in pairs.items()])  0.63 us
  transfers between devices with their start and end apart: 6, of which 3 were waited for; matrix products, arithmetic and copies ran while one was open for 0% of the time, Pallas kernels for 14%

profile of v25, /device:TPU:0, one launch (start us, length us, event | category | flops | bytes accessed | tf_op | source)
XLA Modules:
  0.0 19.0 jit_solution(9796837147565704185)
XLA Ops:
  0.0 0.0 copy-start
  0.0 0.0 copy-start.2
  0.0 1.7 %strips.1 = (f32[216,128]{1,0:T(8,128)S(1)}, f32[216,128]{1,0:T(8,128)S(1)}, f32[448,256]{1,0:T(8,128)S(1)}, s32[8,128]{1,0:T(8,128)S(1)}) custom-call(s32[2,256]{1,0:T(2,128)} %refs_0_.1, s32[1,256]{1,0:T(1,128)} %refs_1_.1, f32[3,8,8,256]{3,2,1,0:T(8,128)} %refs_2_.1, f32[8,8,256]{2,1,0:T(8,128)} %refs_3_.1, f32[8,8,256]{2,1,0:T(8,128)} %refs_4_.1, ...), custom_call_target="tpu_custom_call" | custom-call | flops 100000000 | bytes 2097152 | tf_op jit(solution)/shard_map/strips/pallas_call | solution.py:799
  1.7 3.0 %collective-permute-start = (f32[216,128]{1,0:T(8,128)S(1)}, f32[216,128]{1,0:T(8,128)S(1)}, u32[]{:S(2)}, u32[]{:S(2)}) collective-permute-start(f32[216,128]{1,0:T(8,128)S(1)} %get-tuple-element.19.first_ref), channel_id=1, source_target_pairs={{0,16},{1,17},{2,18},{3,19},{4,27},{5,26},{6,25},{7,24},{8,23},{9,... | collective-permute-start | bytes 331784 | tf_op jit(solution)/shard_map/ppermute | solution.py:913
  4.7 3.7 %collective-permute-start.1 = (f32[216,128]{1,0:T(8,128)S(1)}, f32[216,128]{1,0:T(8,128)S(1)}, u32[]{:S(2)}, u32[]{:S(2)}) collective-permute-start(f32[216,128]{1,0:T(8,128)S(1)} %get-tuple-element.20.then_ref), channel_id=1, source_target_pairs={{0,31},{1,30},{2,29},{3,28},{4,20},{5,21},{6,22},{7,23},{8,24},{9,... | collective-permute-start | bytes 331784 | tf_op jit(solution)/shard_map/ppermute | solution.py:913
  8.4 0.0 copy-done
  8.4 0.0 copy-done.2
  8.4 0.9 %rows.1 = (f32[216,128]{1,0:T(8,128)S(1)}, f32[56,128]{1,0:T(8,128)S(1)}, f32[56,128]{1,0:T(8,128)S(1)}, f32[448,128]{1,0:T(8,128)S(1)}) custom-call(s32[8,128]{1,0:T(8,128)S(1)} %get-tuple-element.18.flags_ref, f32[448,256]{1,0:T(8,128)S(1)} %get-tuple-element.21.stored_ref, f32[216,128]{1,0:T(8,128)S(1)} %get-tuple-element.19.first_ref, ...), custom_call_target="tpu_custom_call" | custom-call | flops 100000000 | bytes 2097152 | tf_op jit(solution)/shard_map/rows/pallas_call | solution.py:799
  9.3 1.5 %collective-permute-start.5 = (f32[216,128]{1,0:T(8,128)S(1)}, f32[216,128]{1,0:T(8,128)S(1)}, u32[]{:S(2)}, u32[]{:S(2)}) collective-permute-start(f32[216,128]{1,0:T(8,128)S(1)} %get-tuple-element.26), channel_id=1, source_target_pairs={{0,16},{1,2},{2,1},{3,4},{4,3},{5,6},{6,5},{7,8},{8,7},{9,10},{10,... | collective-permute-start | bytes 331784 | tf_op jit(solution)/shard_map/ppermute | solution.py:864
  10.8 0.5 %collective-permute-start.3 = (f32[56,128]{1,0:T(8,128)S(1)}, f32[56,128]{1,0:T(8,128)S(1)}, u32[]{:S(2)}, u32[]{:S(2)}) collective-permute-start(f32[56,128]{1,0:T(8,128)S(1)} %get-tuple-element.24), channel_id=1, source_target_pairs={{0,16},{1,29},{2,30},{3,27},{4,28},{5,25},{6,26},{7,23},{8,24},{9,... | collective-permute-start | bytes 86024 | tf_op jit(solution)/shard_map/ppermute | solution.py:883
  11.4 1.5 %collective-permute-start.4 = (f32[56,128]{1,0:T(8,128)S(1)}, f32[56,128]{1,0:T(8,128)S(1)}, u32[]{:S(2)}, u32[]{:S(2)}) collective-permute-start(f32[56,128]{1,0:T(8,128)S(1)} %get-tuple-element.25), channel_id=1, source_target_pairs={{0,16},{1,18},{2,17},{3,20},{4,19},{5,22},{6,21},{7,24},{8,23},{9,... | collective-permute-start | bytes 86024 | tf_op jit(solution)/shard_map/ppermute | solution.py:883
  12.8 0.0 copy-done.1
  12.9 0.5 %own.1 = (f32[448,384]{1,0:T(8,128)S(1)}, bf16[384,256]{1,0:T(8,128)(2,1)S(1)}) custom-call(s32[8,128]{1,0:T(8,128)S(1)} %get-tuple-element.18.flags_ref, f32[448,256]{1,0:T(8,128)S(1)} %get-tuple-element.21.stored_ref, s32[64,640]{1,0:T(8,128)S(1)} %copy-done.1), custom_call_target="tpu_custom_call" | custom-call | flops 100000000 | bytes 2097152 | tf_op jit(solution)/shard_map/own/pallas_call | solution.py:799
  13.3 0.0 collective-permute-done.first_ref
  13.4 0.2 collective-permute-done.1.then_ref
  13.5 0.2 %corners.1 = f32[480,128]{1,0:T(8,128)S(1)} custom-call(s32[8,128]{1,0:T(8,128)S(1)} %get-tuple-element.18.flags_ref, f32[216,128]{1,0:T(8,128)S(1)} %collective-permute-done.first_ref, f32[216,128]{1,0:T(8,128)S(1)} %collective-permute-done.1.then_ref, f32[448,128]{1,0:T(8,128)S(1)} %get-tuple-element.22.pair_ref, ...), custom_call_target="tpu_custom_call" | custom-call | flops 100000000 | bytes 2097152 | tf_op jit(solution)/shard_map/corners/pallas_call | solution.py:799
  13.8 0.2 %collective-permute-start.2 = (f32[480,128]{1,0:T(8,128)S(1)}, f32[480,128]{1,0:T(8,128)S(1)}, u32[]{:S(2)}, u32[]{:S(2)}) collective-permute-start(f32[480,128]{1,0:T(8,128)S(1)} %corners.1), channel_id=1, source_target_pairs={{0,1},{1,0},{2,3},{3,2},{4,5},{5,4},{6,7},{7,6},{8,9},{9,8},{10,11... | collective-permute-start | bytes 737288 | tf_op jit(solution)/shard_map/ppermute | solution.py:864
  14.0 0.8 %middle.1 = (f32[704,128]{1,0:T(8,128)S(1)}, f32[704,128]{1,0:T(8,128)S(1)}, f32[704,128]{1,0:T(8,128)S(1)}) custom-call(s32[8,128]{1,0:T(8,128)S(1)} %get-tuple-element.18.flags_ref, f32[216,128]{1,0:T(8,128)S(1)} %collective-permute-done.first_ref, f32[216,128]{1,0:T(8,128)S(1)} %collective-permute-done.1.then_ref, ...), custom_call_target="tpu_custom_call" | custom-call | flops 100000000 | bytes 2097152 | tf_op jit(solution)/shard_map/middle/pallas_call | solution.py:799
  14.8 0.3 %collective-permute-done.3.far1_ref = f32[56,128]{1,0:T(8,128)S(1)} collective-permute-done((f32[56,128]{1,0:T(8,128)S(1)}, f32[56,128]{1,0:T(8,128)S(1)}, u32[]{:S(2)}, u32[]{:S(2)}) %collective-permute-start.3) | collective-permute-done | bytes 28704 | tf_op jit(solution)/shard_map/ppermute | solution.py:883
  15.1 0.3 %collective-permute-done.4.far0_ref = f32[56,128]{1,0:T(8,128)S(1)} collective-permute-done((f32[56,128]{1,0:T(8,128)S(1)}, f32[56,128]{1,0:T(8,128)S(1)}, u32[]{:S(2)}, u32[]{:S(2)}) %collective-permute-start.4) | collective-permute-done | bytes 28704 | tf_op jit(solution)/shard_map/ppermute | solution.py:883
  15.4 0.0 collective-permute-done.5.next_ref
  15.4 0.2 %far.1.next_ref = f32[512,128]{1,0:T(8,128)S(1)} custom-call(s32[8,128]{1,0:T(8,128)S(1)} %get-tuple-element.18.flags_ref, f32[56,128]{1,0:T(8,128)S(1)} %collective-permute-done.3.far1_ref, f32[56,128]{1,0:T(8,128)S(1)} %collective-permute-done.4.far0_ref, f32[216,128]{1,0:T(8,128)S(1)} %collective-permute-done.5.next_ref, ...), custom_call_target="tpu_custom_call" | custom-call | flops 99999997952 | bytes 2097152 | tf_op jit(solution)/shard_map/far/pallas_call | solution.py:799
  15.6 0.0 collective-permute-done.2.pair_ref
  15.6 3.4 %steps.1 = f32[3,8,8,256]{3,2,1,0:T(8,128)} custom-call(s32[8,128]{1,0:T(8,128)S(1)} %get-tuple-element.18.flags_ref, f32[480,128]{1,0:T(8,128)S(1)} %collective-permute-done.2.pair_ref, f32[512,128]{1,0:T(8,128)S(1)} %far.1.next_ref, f32[704,128]{1,0:T(8,128)S(1)} %get-tuple-element.28._.low_ref, f32[704,128]{1,0:T(8,128)S(1)} %get-tuple-element.29.centre_ref, ...), custom_call_target="tpu_custom_call" | custom-call | flops 100000000 | bytes 2097152 | tf_op jit(solution)/shard_map/steps/pallas_call | solution.py:799
  (1 shorter events, 0.0 us)
Async XLA Ops:
  0.0 8.4 %copy-start = (f32[320,256]{1,0:T(8,128)S(1)}, f32[320,256]{1,0:T(8,128)}, u32[]{:S(2)}) copy-start(f32[320,256]{1,0:T(8,128)} %constant.8.clone.table_ref) | copy-start | bytes 983044
  0.0 8.4 %copy-start.2 = (f32[64,128]{1,0:T(8,128)S(1)}, f32[64,128]{1,0:T(8,128)}, u32[]{:S(2)}) copy-start(f32[64,128]{1,0:T(8,128)} %constant.9.clone.weight_ref) | copy-start | bytes 98308
  1.7 11.6 %collective-permute-start = (f32[216,128]{1,0:T(8,128)S(1)}, f32[216,128]{1,0:T(8,128)S(1)}, u32[]{:S(2)}, u32[]{:S(2)}) collective-permute-start(f32[216,128]{1,0:T(8,128)S(1)} %get-tuple-element.19.first_ref), channel_id=1, source_target_pairs={{0,16},{1,17},{2,18},{3,19},{4,27},{5,26},{6,25},{7,24},{8,23},{9,... | collective-permute-start | bytes 331784 | tf_op jit(solution)/shard_map/ppermute | solution.py:913
  4.7 8.8 %collective-permute-start.1 = (f32[216,128]{1,0:T(8,128)S(1)}, f32[216,128]{1,0:T(8,128)S(1)}, u32[]{:S(2)}, u32[]{:S(2)}) collective-permute-start(f32[216,128]{1,0:T(8,128)S(1)} %get-tuple-element.20.then_ref), channel_id=1, source_target_pairs={{0,31},{1,30},{2,29},{3,28},{4,20},{5,21},{6,22},{7,23},{8,24},{9,... | collective-permute-start | bytes 331784 | tf_op jit(solution)/shard_map/ppermute | solution.py:913
  8.4 4.4 %copy-start.1 = (s32[64,640]{1,0:T(8,128)S(1)}, s32[64,640]{1,0:T(8,128)}, u32[]{:S(2)}) copy-start(s32[64,640]{1,0:T(8,128)} %constant.11.clone.lanes_ref) | copy-start | bytes 491524
  9.3 6.1 %collective-permute-start.5 = (f32[216,128]{1,0:T(8,128)S(1)}, f32[216,128]{1,0:T(8,128)S(1)}, u32[]{:S(2)}, u32[]{:S(2)}) collective-permute-start(f32[216,128]{1,0:T(8,128)S(1)} %get-tuple-element.26), channel_id=1, source_target_pairs={{0,16},{1,2},{2,1},{3,4},{4,3},{5,6},{6,5},{7,8},{8,7},{9,10},{10,... | collective-permute-start | bytes 331784 | tf_op jit(solution)/shard_map/ppermute | solution.py:864
  10.8 4.3 %collective-permute-start.3 = (f32[56,128]{1,0:T(8,128)S(1)}, f32[56,128]{1,0:T(8,128)S(1)}, u32[]{:S(2)}, u32[]{:S(2)}) collective-permute-start(f32[56,128]{1,0:T(8,128)S(1)} %get-tuple-element.24), channel_id=1, source_target_pairs={{0,16},{1,29},{2,30},{3,27},{4,28},{5,25},{6,26},{7,23},{8,24},{9,... | collective-permute-start | bytes 86024 | tf_op jit(solution)/shard_map/ppermute | solution.py:883
  11.4 4.0 %collective-permute-start.4 = (f32[56,128]{1,0:T(8,128)S(1)}, f32[56,128]{1,0:T(8,128)S(1)}, u32[]{:S(2)}, u32[]{:S(2)}) collective-permute-start(f32[56,128]{1,0:T(8,128)S(1)} %get-tuple-element.25), channel_id=1, source_target_pairs={{0,16},{1,18},{2,17},{3,20},{4,19},{5,22},{6,21},{7,24},{8,23},{9,... | collective-permute-start | bytes 86024 | tf_op jit(solution)/shard_map/ppermute | solution.py:883
  13.8 1.9 %collective-permute-start.2 = (f32[480,128]{1,0:T(8,128)S(1)}, f32[480,128]{1,0:T(8,128)S(1)}, u32[]{:S(2)}, u32[]{:S(2)}) collective-permute-start(f32[480,128]{1,0:T(8,128)S(1)} %corners.1), channel_id=1, source_target_pairs={{0,1},{1,0},{2,3},{3,2},{4,5},{5,4},{6,7},{7,6},{8,9},{9,8},{10,11... | collective-permute-start | bytes 737288 | tf_op jit(solution)/shard_map/ppermute | solution.py:864

commit v26 on v23

--- a/solution.py
+++ b/solution.py
@@ -395,7 +395,7 @@
 
 
 def mirrored_first(block_y):
-    return (block_y >= BY // 4) & (block_y < BY - BY // 4)
+    return (block_y >= BY // 8) & (block_y < BY - BY // 8)
 
 
 def in_order(block_cols, first, second):

time: 19.3 us -> 19.6 us (1.016)
  the two profiles are of different devices: /device:TPU:0 before, /device:TPU:1 now
where the time goes in v26:
time: 19.6 us; the launch traced here: 19.5 us
  starting transfers between devices  10.6 us (54%)
  Pallas kernels  7.65 us (39%)
  waiting for transfers between devices  1.1 us (6%)
    pallas_call x7, Pallas kernels, call(): pl.pallas_call(kernel, out_shape=[jax.ShapeDtypeStruct(*out) for out in o...  7.65 us
    ppermute x2, starting transfers between devices, on_device(): halos.append(lax.ppermute(value, both, pairs))  7.2 us
    ppermute x2, starting transfers between devices, eastward(): lax.ppermute(value, both, [(rank(*a), rank(*b)) for a, b in pairs.items()])  2.66 us
    ppermute x2, waiting for transfers between devices, eastward(): lax.ppermute(value, both, [(rank(*a), rank(*b)) for a, b in pairs.items()])  1.09 us
    ppermute x2, starting transfers between devices, swapped(): return lax.ppermute(value, both, pairs)  0.78 us
  transfers between devices with their start and end apart: 6, of which 2 were waited for; matrix products, arithmetic and copies ran while one was open for 0% of the time, Pallas kernels for 13%

profile of v26, /device:TPU:1, one launch (start us, length us, event | category | flops | bytes accessed | tf_op | source)
XLA Modules:
  0.0 19.5 jit_solution(8921542159588348658)
XLA Ops:
  0.0 0.0 copy-start
  0.0 0.0 copy-start.2
  0.0 1.7 %strips.1 = (f32[216,128]{1,0:T(8,128)S(1)}, f32[216,128]{1,0:T(8,128)S(1)}, f32[448,256]{1,0:T(8,128)S(1)}, s32[8,128]{1,0:T(8,128)S(1)}) custom-call(s32[2,256]{1,0:T(2,128)} %refs_0_.1, s32[1,256]{1,0:T(1,128)} %refs_1_.1, f32[3,8,8,256]{3,2,1,0:T(8,128)} %refs_2_.1, f32[8,8,256]{2,1,0:T(8,128)} %refs_3_.1, f32[8,8,256]{2,1,0:T(8,128)} %refs_4_.1, ...), custom_call_target="tpu_custom_call" | custom-call | flops 100000000 | bytes 2097152 | tf_op jit(solution)/shard_map/strips/pallas_call | solution.py:791
  1.7 2.1 %collective-permute-start = (f32[216,128]{1,0:T(8,128)S(1)}, f32[216,128]{1,0:T(8,128)S(1)}, u32[]{:S(2)}, u32[]{:S(2)}) collective-permute-start(f32[216,128]{1,0:T(8,128)S(1)} %get-tuple-element.19.first_ref), channel_id=1, source_target_pairs={{0,16},{1,17},{2,29},{3,28},{4,27},{5,26},{6,25},{7,24},{8,23},{9,... | collective-permute-start | bytes 331784 | tf_op jit(solution)/shard_map/ppermute | solution.py:905
  3.8 5.1 %collective-permute-start.1 = (f32[216,128]{1,0:T(8,128)S(1)}, f32[216,128]{1,0:T(8,128)S(1)}, u32[]{:S(2)}, u32[]{:S(2)}) collective-permute-start(f32[216,128]{1,0:T(8,128)S(1)} %get-tuple-element.20.then_ref), channel_id=1, source_target_pairs={{0,31},{1,30},{2,18},{3,19},{4,20},{5,21},{6,22},{7,23},{8,24},{9,... | collective-permute-start | bytes 331784 | tf_op jit(solution)/shard_map/ppermute | solution.py:905
  8.9 0.0 copy-done
  8.9 0.0 copy-done.2
  8.9 0.9 %rows.1 = (f32[216,128]{1,0:T(8,128)S(1)}, f32[56,128]{1,0:T(8,128)S(1)}, f32[56,128]{1,0:T(8,128)S(1)}, f32[448,128]{1,0:T(8,128)S(1)}) custom-call(s32[8,128]{1,0:T(8,128)S(1)} %get-tuple-element.18.flags_ref, f32[448,256]{1,0:T(8,128)S(1)} %get-tuple-element.21.stored_ref, f32[216,128]{1,0:T(8,128)S(1)} %get-tuple-element.19.first_ref, ...), custom_call_target="tpu_custom_call" | custom-call | flops 100000000 | bytes 2097152 | tf_op jit(solution)/shard_map/rows/pallas_call | solution.py:791
  9.8 0.0 collective-permute-start.5
  9.8 0.7 %collective-permute-start.3 = (f32[56,128]{1,0:T(8,128)S(1)}, f32[56,128]{1,0:T(8,128)S(1)}, u32[]{:S(2)}, u32[]{:S(2)}) collective-permute-start(f32[56,128]{1,0:T(8,128)S(1)} %get-tuple-element.24), channel_id=1, source_target_pairs={{0,16},{1,29},{2,30},{3,27},{4,28},{5,25},{6,26},{7,23},{8,24},{9,... | collective-permute-start | bytes 86024 | tf_op jit(solution)/shard_map/ppermute | solution.py:875
  10.5 2.0 %collective-permute-start.4 = (f32[56,128]{1,0:T(8,128)S(1)}, f32[56,128]{1,0:T(8,128)S(1)}, u32[]{:S(2)}, u32[]{:S(2)}) collective-permute-start(f32[56,128]{1,0:T(8,128)S(1)} %get-tuple-element.25), channel_id=1, source_target_pairs={{0,16},{1,18},{2,17},{3,20},{4,19},{5,22},{6,21},{7,24},{8,23},{9,... | collective-permute-start | bytes 86024 | tf_op jit(solution)/shard_map/ppermute | solution.py:875
  12.5 0.0 copy-done.1
  12.5 0.5 %own.1 = (f32[448,384]{1,0:T(8,128)S(1)}, bf16[384,256]{1,0:T(8,128)(2,1)S(1)}) custom-call(s32[8,128]{1,0:T(8,128)S(1)} %get-tuple-element.18.flags_ref, f32[448,256]{1,0:T(8,128)S(1)} %get-tuple-element.21.stored_ref, s32[64,640]{1,0:T(8,128)S(1)} %copy-done.1), custom_call_target="tpu_custom_call" | custom-call | flops 100000000 | bytes 2097152 | tf_op jit(solution)/shard_map/own/pallas_call | solution.py:791
  13.0 0.0 collective-permute-done.first_ref
  13.0 0.0 collective-permute-done.1.then_ref
  13.0 0.2 %corners.1 = f32[480,128]{1,0:T(8,128)S(1)} custom-call(s32[8,128]{1,0:T(8,128)S(1)} %get-tuple-element.18.flags_ref, f32[216,128]{1,0:T(8,128)S(1)} %collective-permute-done.first_ref, f32[216,128]{1,0:T(8,128)S(1)} %collective-permute-done.1.then_ref, f32[448,128]{1,0:T(8,128)S(1)} %get-tuple-element.22.pair_ref, ...), custom_call_target="tpu_custom_call" | custom-call | flops 100000000 | bytes 2097152 | tf_op jit(solution)/shard_map/corners/pallas_call | solution.py:791
  13.2 0.7 %collective-permute-start.2 = (f32[480,128]{1,0:T(8,128)S(1)}, f32[480,128]{1,0:T(8,128)S(1)}, u32[]{:S(2)}, u32[]{:S(2)}) collective-permute-start(f32[480,128]{1,0:T(8,128)S(1)} %corners.1), channel_id=1, source_target_pairs={{0,1},{1,0},{2,3},{3,2},{4,5},{5,4},{6,7},{7,6},{8,9},{9,8},{10,11... | collective-permute-start | bytes 737288 | tf_op jit(solution)/shard_map/ppermute | solution.py:856
  14.0 0.8 %middle.1 = (f32[704,128]{1,0:T(8,128)S(1)}, f32[704,128]{1,0:T(8,128)S(1)}, f32[704,128]{1,0:T(8,128)S(1)}) custom-call(s32[8,128]{1,0:T(8,128)S(1)} %get-tuple-element.18.flags_ref, f32[216,128]{1,0:T(8,128)S(1)} %collective-permute-done.first_ref, f32[216,128]{1,0:T(8,128)S(1)} %collective-permute-done.1.then_ref, ...), custom_call_target="tpu_custom_call" | custom-call | flops 100000000 | bytes 2097152 | tf_op jit(solution)/shard_map/middle/pallas_call | solution.py:791
  14.8 0.6 %collective-permute-done.3.far1_ref = f32[56,128]{1,0:T(8,128)S(1)} collective-permute-done((f32[56,128]{1,0:T(8,128)S(1)}, f32[56,128]{1,0:T(8,128)S(1)}, u32[]{:S(2)}, u32[]{:S(2)}) %collective-permute-start.3) | collective-permute-done | bytes 28704 | tf_op jit(solution)/shard_map/ppermute | solution.py:875
  15.4 0.4 %collective-permute-done.4.far0_ref = f32[56,128]{1,0:T(8,128)S(1)} collective-permute-done((f32[56,128]{1,0:T(8,128)S(1)}, f32[56,128]{1,0:T(8,128)S(1)}, u32[]{:S(2)}, u32[]{:S(2)}) %collective-permute-start.4) | collective-permute-done | bytes 28704 | tf_op jit(solution)/shard_map/ppermute | solution.py:875
  15.9 0.0 collective-permute-done.5.next_ref
  15.9 0.2 %far.1.next_ref = f32[512,128]{1,0:T(8,128)S(1)} custom-call(s32[8,128]{1,0:T(8,128)S(1)} %get-tuple-element.18.flags_ref, f32[56,128]{1,0:T(8,128)S(1)} %collective-permute-done.3.far1_ref, f32[56,128]{1,0:T(8,128)S(1)} %collective-permute-done.4.far0_ref, f32[216,128]{1,0:T(8,128)S(1)} %collective-permute-done.5.next_ref, ...), custom_call_target="tpu_custom_call" | custom-call | flops 99999997952 | bytes 2097152 | tf_op jit(solution)/shard_map/far/pallas_call | solution.py:791
  16.1 0.0 collective-permute-done.2.pair_ref
  16.1 3.4 %steps.1 = f32[3,8,8,256]{3,2,1,0:T(8,128)} custom-call(s32[8,128]{1,0:T(8,128)S(1)} %get-tuple-element.18.flags_ref, f32[480,128]{1,0:T(8,128)S(1)} %collective-permute-done.2.pair_ref, f32[512,128]{1,0:T(8,128)S(1)} %far.1.next_ref, f32[704,128]{1,0:T(8,128)S(1)} %get-tuple-element.28._.low_ref, f32[704,128]{1,0:T(8,128)S(1)} %get-tuple-element.29.centre_ref, ...), custom_call_target="tpu_custom_call" | custom-call | flops 100000000 | bytes 2097152 | tf_op jit(solution)/shard_map/steps/pallas_call | solution.py:791
  (1 shorter events, 0.0 us)
Async XLA Ops:
  0.0 8.9 %copy-start = (f32[320,256]{1,0:T(8,128)S(1)}, f32[320,256]{1,0:T(8,128)}, u32[]{:S(2)}) copy-start(f32[320,256]{1,0:T(8,128)} %constant.8.clone.table_ref) | copy-start | bytes 983044
  0.0 8.9 %copy-start.2 = (f32[64,128]{1,0:T(8,128)S(1)}, f32[64,128]{1,0:T(8,128)}, u32[]{:S(2)}) copy-start(f32[64,128]{1,0:T(8,128)} %constant.9.clone.weight_ref) | copy-start | bytes 98308
  1.7 11.3 %collective-permute-start = (f32[216,128]{1,0:T(8,128)S(1)}, f32[216,128]{1,0:T(8,128)S(1)}, u32[]{:S(2)}, u32[]{:S(2)}) collective-permute-start(f32[216,128]{1,0:T(8,128)S(1)} %get-tuple-element.19.first_ref), channel_id=1, source_target_pairs={{0,16},{1,17},{2,29},{3,28},{4,27},{5,26},{6,25},{7,24},{8,23},{9,... | collective-permute-start | bytes 331784 | tf_op jit(solution)/shard_map/ppermute | solution.py:905
  3.8 9.2 %collective-permute-start.1 = (f32[216,128]{1,0:T(8,128)S(1)}, f32[216,128]{1,0:T(8,128)S(1)}, u32[]{:S(2)}, u32[]{:S(2)}) collective-permute-start(f32[216,128]{1,0:T(8,128)S(1)} %get-tuple-element.20.then_ref), channel_id=1, source_target_pairs={{0,31},{1,30},{2,18},{3,19},{4,20},{5,21},{6,22},{7,23},{8,24},{9,... | collective-permute-start | bytes 331784 | tf_op jit(solution)/shard_map/ppermute | solution.py:905
  8.9 3.6 %copy-start.1 = (s32[64,640]{1,0:T(8,128)S(1)}, s32[64,640]{1,0:T(8,128)}, u32[]{:S(2)}) copy-start(s32[64,640]{1,0:T(8,128)} %constant.11.clone.lanes_ref) | copy-start | bytes 491524
  9.8 6.1 %collective-permute-start.5 = (f32[216,128]{1,0:T(8,128)S(1)}, f32[216,128]{1,0:T(8,128)S(1)}, u32[]{:S(2)}, u32[]{:S(2)}) collective-permute-start(f32[216,128]{1,0:T(8,128)S(1)} %get-tuple-element.26), channel_id=1, source_target_pairs={{0,16},{1,2},{2,1},{3,4},{4,3},{5,6},{6,5},{7,8},{8,7},{9,10},{10,... | collective-permute-start | bytes 331784 | tf_op jit(solution)/shard_map/ppermute | solution.py:856
  9.8 5.6 %collective-permute-start.3 = (f32[56,128]{1,0:T(8,128)S(1)}, f32[56,128]{1,0:T(8,128)S(1)}, u32[]{:S(2)}, u32[]{:S(2)}) collective-permute-start(f32[56,128]{1,0:T(8,128)S(1)} %get-tuple-element.24), channel_id=1, source_target_pairs={{0,16},{1,29},{2,30},{3,27},{4,28},{5,25},{6,26},{7,23},{8,24},{9,... | collective-permute-start | bytes 86024 | tf_op jit(solution)/shard_map/ppermute | solution.py:875
  10.5 5.4 %collective-permute-start.4 = (f32[56,128]{1,0:T(8,128)S(1)}, f32[56,128]{1,0:T(8,128)S(1)}, u32[]{:S(2)}, u32[]{:S(2)}) collective-permute-start(f32[56,128]{1,0:T(8,128)S(1)} %get-tuple-element.25), channel_id=1, source_target_pairs={{0,16},{1,18},{2,17},{3,20},{4,19},{5,22},{6,21},{7,24},{8,23},{9,... | collective-permute-start | bytes 86024 | tf_op jit(solution)/shard_map/ppermute | solution.py:875
  13.2 2.9 %collective-permute-start.2 = (f32[480,128]{1,0:T(8,128)S(1)}, f32[480,128]{1,0:T(8,128)S(1)}, u32[]{:S(2)}, u32[]{:S(2)}) collective-permute-start(f32[480,128]{1,0:T(8,128)S(1)} %corners.1), channel_id=1, source_target_pairs={{0,1},{1,0},{2,3},{3,2},{4,5},{5,4},{6,7},{7,6},{8,9},{9,8},{10,11... | collective-permute-start | bytes 737288 | tf_op jit(solution)/shard_map/ppermute | solution.py:856

commit v27 on v23

--- a/solution.py
+++ b/solution.py
@@ -574,22 +574,25 @@
             ref[n * NODES : (n + 1) * NODES] = part[:, k * LANES : (k + 1) * LANES]
 
 
-def far_kernel(block_cols, flags_ref, far1_ref, far0_ref, next_ref, _, out_ref):
+def next_kernel(next_ref, _, out_ref):
+    below = jnp.broadcast_to((lax.axis_index("blk") & 1) == 0, (1, LANES))
+    strip = jnp.concatenate([next_ref[...], pltpu.roll(next_ref[...], 64, 1)], 0)
+    out_ref[...] = placed_rows(strip, below, 4)
+
+
+def far_kernel(block_cols, flags_ref, far1_ref, far0_ref, strip_ref, out_ref):
     east0, flip0, east1, flip1 = flags_in(flags_ref)
     odd = lax.axis_index("blk") & 1
-    lane = lax.broadcasted_iota(i32, (1, LANES), 1)
+    own = lax.broadcasted_iota(i32, (1, LANES), 1) < 64
     below = jnp.broadcast_to(odd == 0, (1, LANES))
-    strip = jnp.concatenate([next_ref[...], pltpu.roll(next_ref[...], 64, 1)], 0)
-    strip = placed_rows(strip, below, 4)
     corners, strip_of = arrived_corners(far0_ref[...], far1_ref[...], block_cols, odd)
     late = jnp.where(strip_of != 0, east1, east0) == 0
     rim = MOVED + NODES // 2 + NP
     rim = jnp.concatenate(spread_out(corners[rim : rim + NP], below, 2), 0)
     corners = placed_rows(corners, late, 0)
-    own = lane < 64
-    out_ref[:ROWS] = jnp.where(own, strip[:ROWS], corners[:ROWS])
+    out_ref[:ROWS] = jnp.where(own, strip_ref[:ROWS], corners[:ROWS])
     out_ref[ROWS:ALL_ROWS] = corners[ROWS:]
-    out_ref[ALL_ROWS:] = jnp.where(own, strip[ROWS:], rim)
+    out_ref[ALL_ROWS:] = jnp.where(own, strip_ref[ROWS:], rim)
 
 
 def steps_kernel(
@@ -932,10 +935,17 @@
         name="middle",
     )
     (from_next,) = call(
+        next_kernel,
+        [(vmem, x) for x in (from_next, low)],
+        [((ALL_ROWS, LANES), f32)],
+        10**11,
+        name="next",
+    )
+    (from_next,) = call(
         functools.partial(far_kernel, block_cols),
-        [(vmem, x) for x in (flags, far1, far0, from_next, low)],
+        [(vmem, x) for x in (flags, far1, far0, from_next)],
         [((RIM_ROWS, LANES), f32)],
-        10**11,
+        10**10,
         name="far",
     )
     (stepped,) = call(

time: 19.3 us -> 19.2 us (level)
    pallas_call x7 -> x8, Pallas kernels: 7.64 us -> 7.75 us  [call(): pl.pallas_call(kernel, out_shape=[jax.ShapeDtypeStruct(*out) for out in o...]
where the time goes in v27:
time: 19.2 us; the launch traced here: 18.9 us
  starting transfers between devices  10.5 us (55%)
  Pallas kernels  7.75 us (40%)
  waiting for transfers between devices  0.62 us (3%)
    pallas_call x8, Pallas kernels, call(): pl.pallas_call(kernel, out_shape=[jax.ShapeDtypeStruct(*out) for out in o...  7.75 us
    ppermute x2, starting transfers between devices, on_device(): halos.append(lax.ppermute(value, both, pairs))  6.69 us
    ppermute x2, starting transfers between devices, eastward(): lax.ppermute(value, both, [(rank(*a), rank(*b)) for a, b in pairs.items()])  2.03 us
    ppermute x2, starting transfers between devices, swapped(): return lax.ppermute(value, both, pairs)  1.75 us
    ppermute x2, waiting for transfers between devices, eastward(): lax.ppermute(value, both, [(rank(*a), rank(*b)) for a, b in pairs.items()])  0.45 us
  transfers between devices with their start and end apart: 6, of which 3 were waited for; matrix products, arithmetic and copies ran while one was open for 0% of the time, Pallas kernels for 14%

profile of v27, /device:TPU:0, one launch (start us, length us, event | category | flops | bytes accessed | tf_op | source)
XLA Modules:
  0.0 18.9 jit_solution(16438963411938129783)
XLA Ops:
  0.0 0.0 copy-start
  0.0 1.7 %strips.1 = (f32[216,128]{1,0:T(8,128)S(1)}, f32[216,128]{1,0:T(8,128)S(1)}, f32[448,256]{1,0:T(8,128)S(1)}, s32[8,128]{1,0:T(8,128)S(1)}) custom-call(s32[2,256]{1,0:T(2,128)} %refs_0_.1, s32[1,256]{1,0:T(1,128)} %refs_1_.1, f32[3,8,8,256]{3,2,1,0:T(8,128)} %refs_2_.1, f32[8,8,256]{2,1,0:T(8,128)} %refs_3_.1, f32[8,8,256]{2,1,0:T(8,128)} %refs_4_.1, ...), custom_call_target="tpu_custom_call" | custom-call | flops 100000000 | bytes 2097152 | tf_op jit(solution)/shard_map/strips/pallas_call | solution.py:794
  1.7 3.0 %collective-permute-start = (f32[216,128]{1,0:T(8,128)S(1)}, f32[216,128]{1,0:T(8,128)S(1)}, u32[]{:S(2)}, u32[]{:S(2)}) collective-permute-start(f32[216,128]{1,0:T(8,128)S(1)} %get-tuple-element.19.first_ref), channel_id=1, source_target_pairs={{0,16},{1,17},{2,18},{3,19},{4,27},{5,26},{6,25},{7,24},{8,23},{9,... | collective-permute-start | bytes 331784 | tf_op jit(solution)/shard_map/ppermute | solution.py:908
  4.7 3.7 %collective-permute-start.1 = (f32[216,128]{1,0:T(8,128)S(1)}, f32[216,128]{1,0:T(8,128)S(1)}, u32[]{:S(2)}, u32[]{:S(2)}) collective-permute-start(f32[216,128]{1,0:T(8,128)S(1)} %get-tuple-element.20.then_ref), channel_id=1, source_target_pairs={{0,31},{1,30},{2,29},{3,28},{4,20},{5,21},{6,22},{7,23},{8,24},{9,... | collective-permute-start | bytes 331784 | tf_op jit(solution)/shard_map/ppermute | solution.py:908
  8.4 0.0 copy-done
  8.4 0.0 copy-done.2
  8.4 0.8 %rows.1 = (f32[216,128]{1,0:T(8,128)S(1)}, f32[56,128]{1,0:T(8,128)S(1)}, f32[56,128]{1,0:T(8,128)S(1)}, f32[448,128]{1,0:T(8,128)S(1)}) custom-call(s32[8,128]{1,0:T(8,128)S(1)} %get-tuple-element.18.flags_ref, f32[448,256]{1,0:T(8,128)S(1)} %get-tuple-element.21.stored_ref, f32[216,128]{1,0:T(8,128)S(1)} %get-tuple-element.19.first_ref, ...), custom_call_target="tpu_custom_call" | custom-call | flops 100000000 | bytes 2097152 | tf_op jit(solution)/shard_map/rows/pallas_call | solution.py:794
  9.3 1.5 %collective-permute-start.5 = (f32[216,128]{1,0:T(8,128)S(1)}, f32[216,128]{1,0:T(8,128)S(1)}, u32[]{:S(2)}, u32[]{:S(2)}) collective-permute-start(f32[216,128]{1,0:T(8,128)S(1)} %get-tuple-element.26), channel_id=1, source_target_pairs={{0,16},{1,2},{2,1},{3,4},{4,3},{5,6},{6,5},{7,8},{8,7},{9,10},{10,... | collective-permute-start | bytes 331784 | tf_op jit(solution)/shard_map/ppermute | solution.py:859
  10.8 0.5 %collective-permute-start.3 = (f32[56,128]{1,0:T(8,128)S(1)}, f32[56,128]{1,0:T(8,128)S(1)}, u32[]{:S(2)}, u32[]{:S(2)}) collective-permute-start(f32[56,128]{1,0:T(8,128)S(1)} %get-tuple-element.24), channel_id=1, source_target_pairs={{0,16},{1,29},{2,30},{3,27},{4,28},{5,25},{6,26},{7,23},{8,24},{9,... | collective-permute-start | bytes 86024 | tf_op jit(solution)/shard_map/ppermute | solution.py:878
  11.3 1.5 %collective-permute-start.4 = (f32[56,128]{1,0:T(8,128)S(1)}, f32[56,128]{1,0:T(8,128)S(1)}, u32[]{:S(2)}, u32[]{:S(2)}) collective-permute-start(f32[56,128]{1,0:T(8,128)S(1)} %get-tuple-element.25), channel_id=1, source_target_pairs={{0,16},{1,18},{2,17},{3,20},{4,19},{5,22},{6,21},{7,24},{8,23},{9,... | collective-permute-start | bytes 86024 | tf_op jit(solution)/shard_map/ppermute | solution.py:878
  12.8 0.0 copy-done.1
  12.8 0.5 %own.1 = (f32[448,384]{1,0:T(8,128)S(1)}, bf16[384,256]{1,0:T(8,128)(2,1)S(1)}) custom-call(s32[8,128]{1,0:T(8,128)S(1)} %get-tuple-element.18.flags_ref, f32[448,256]{1,0:T(8,128)S(1)} %get-tuple-element.21.stored_ref, s32[64,640]{1,0:T(8,128)S(1)} %copy-done.1), custom_call_target="tpu_custom_call" | custom-call | flops 100000000 | bytes 2097152 | tf_op jit(solution)/shard_map/own/pallas_call | solution.py:794
  13.3 0.0 collective-permute-done.first_ref
  13.3 0.2 collective-permute-done.1.then_ref
  13.5 0.2 %corners.1 = f32[480,128]{1,0:T(8,128)S(1)} custom-call(s32[8,128]{1,0:T(8,128)S(1)} %get-tuple-element.18.flags_ref, f32[216,128]{1,0:T(8,128)S(1)} %collective-permute-done.first_ref, f32[216,128]{1,0:T(8,128)S(1)} %collective-permute-done.1.then_ref, f32[448,128]{1,0:T(8,128)S(1)} %get-tuple-element.22.pair_ref, ...), custom_call_target="tpu_custom_call" | custom-call | flops 100000000 | bytes 2097152 | tf_op jit(solution)/shard_map/corners/pallas_call | solution.py:794
  13.7 0.2 %collective-permute-start.2 = (f32[480,128]{1,0:T(8,128)S(1)}, f32[480,128]{1,0:T(8,128)S(1)}, u32[]{:S(2)}, u32[]{:S(2)}) collective-permute-start(f32[480,128]{1,0:T(8,128)S(1)} %corners.1), channel_id=1, source_target_pairs={{0,1},{1,0},{2,3},{3,2},{4,5},{5,4},{6,7},{7,6},{8,9},{9,8},{10,11... | collective-permute-start | bytes 737288 | tf_op jit(solution)/shard_map/ppermute | solution.py:859
  13.9 0.8 %middle.1 = (f32[704,128]{1,0:T(8,128)S(1)}, f32[704,128]{1,0:T(8,128)S(1)}, f32[704,128]{1,0:T(8,128)S(1)}) custom-call(s32[8,128]{1,0:T(8,128)S(1)} %get-tuple-element.18.flags_ref, f32[216,128]{1,0:T(8,128)S(1)} %collective-permute-done.first_ref, f32[216,128]{1,0:T(8,128)S(1)} %collective-permute-done.1.then_ref, ...), custom_call_target="tpu_custom_call" | custom-call | flops 100000000 | bytes 2097152 | tf_op jit(solution)/shard_map/middle/pallas_call | solution.py:794
  14.7 0.0 collective-permute-done.5.next_ref
  14.7 0.2 next.1.strip_ref
  14.9 0.1 collective-permute-done.3.far1_ref
  15.1 0.3 %collective-permute-done.4.far0_ref = f32[56,128]{1,0:T(8,128)S(1)} collective-permute-done((f32[56,128]{1,0:T(8,128)S(1)}, f32[56,128]{1,0:T(8,128)S(1)}, u32[]{:S(2)}, u32[]{:S(2)}) %collective-permute-start.4) | collective-permute-done | bytes 28704 | tf_op jit(solution)/shard_map/ppermute | solution.py:878
  15.4 0.2 far.1.next_ref
  15.5 0.0 collective-permute-done.2.pair_ref
  15.6 3.4 %steps.1 = f32[3,8,8,256]{3,2,1,0:T(8,128)} custom-call(s32[8,128]{1,0:T(8,128)S(1)} %get-tuple-element.18.flags_ref, f32[480,128]{1,0:T(8,128)S(1)} %collective-permute-done.2.pair_ref, f32[512,128]{1,0:T(8,128)S(1)} %far.1.next_ref, f32[704,128]{1,0:T(8,128)S(1)} %get-tuple-element.28._.low_ref, f32[704,128]{1,0:T(8,128)S(1)} %get-tuple-element.29.centre_ref, ...), custom_call_target="tpu_custom_call" | custom-call | flops 100000000 | bytes 2097152 | tf_op jit(solution)/shard_map/steps/pallas_call | solution.py:794
  (2 shorter events, 0.0 us)
Async XLA Ops:
  0.0 8.4 %copy-start = (f32[320,256]{1,0:T(8,128)S(1)}, f32[320,256]{1,0:T(8,128)}, u32[]{:S(2)}) copy-start(f32[320,256]{1,0:T(8,128)} %constant.8.clone.table_ref) | copy-start | bytes 983044
  0.0 8.4 %copy-start.2 = (f32[64,128]{1,0:T(8,128)S(1)}, f32[64,128]{1,0:T(8,128)}, u32[]{:S(2)}) copy-start(f32[64,128]{1,0:T(8,128)} %constant.9.clone.weight_ref) | copy-start | bytes 98308
  1.7 11.6 %collective-permute-start = (f32[216,128]{1,0:T(8,128)S(1)}, f32[216,128]{1,0:T(8,128)S(1)}, u32[]{:S(2)}, u32[]{:S(2)}) collective-permute-start(f32[216,128]{1,0:T(8,128)S(1)} %get-tuple-element.19.first_ref), channel_id=1, source_target_pairs={{0,16},{1,17},{2,18},{3,19},{4,27},{5,26},{6,25},{7,24},{8,23},{9,... | collective-permute-start | bytes 331784 | tf_op jit(solution)/shard_map/ppermute | solution.py:908
  4.7 8.8 %collective-permute-start.1 = (f32[216,128]{1,0:T(8,128)S(1)}, f32[216,128]{1,0:T(8,128)S(1)}, u32[]{:S(2)}, u32[]{:S(2)}) collective-permute-start(f32[216,128]{1,0:T(8,128)S(1)} %get-tuple-element.20.then_ref), channel_id=1, source_target_pairs={{0,31},{1,30},{2,29},{3,28},{4,20},{5,21},{6,22},{7,23},{8,24},{9,... | collective-permute-start | bytes 331784 | tf_op jit(solution)/shard_map/ppermute | solution.py:908
  8.4 4.4 %copy-start.1 = (s32[64,640]{1,0:T(8,128)S(1)}, s32[64,640]{1,0:T(8,128)}, u32[]{:S(2)}) copy-start(s32[64,640]{1,0:T(8,128)} %constant.11.clone.lanes_ref) | copy-start | bytes 491524
  9.3 5.5 %collective-permute-start.5 = (f32[216,128]{1,0:T(8,128)S(1)}, f32[216,128]{1,0:T(8,128)S(1)}, u32[]{:S(2)}, u32[]{:S(2)}) collective-permute-start(f32[216,128]{1,0:T(8,128)S(1)} %get-tuple-element.26), channel_id=1, source_target_pairs={{0,16},{1,2},{2,1},{3,4},{4,3},{5,6},{6,5},{7,8},{8,7},{9,10},{10,... | collective-permute-start | bytes 331784 | tf_op jit(solution)/shard_map/ppermute | solution.py:859
  10.8 4.2 %collective-permute-start.3 = (f32[56,128]{1,0:T(8,128)S(1)}, f32[56,128]{1,0:T(8,128)S(1)}, u32[]{:S(2)}, u32[]{:S(2)}) collective-permute-start(f32[56,128]{1,0:T(8,128)S(1)} %get-tuple-element.24), channel_id=1, source_target_pairs={{0,16},{1,29},{2,30},{3,27},{4,28},{5,25},{6,26},{7,23},{8,24},{9,... | collective-permute-start | bytes 86024 | tf_op jit(solution)/shard_map/ppermute | solution.py:878
  11.3 4.0 %collective-permute-start.4 = (f32[56,128]{1,0:T(8,128)S(1)}, f32[56,128]{1,0:T(8,128)S(1)}, u32[]{:S(2)}, u32[]{:S(2)}) collective-permute-start(f32[56,128]{1,0:T(8,128)S(1)} %get-tuple-element.25), channel_id=1, source_target_pairs={{0,16},{1,18},{2,17},{3,20},{4,19},{5,22},{6,21},{7,24},{8,23},{9,... | collective-permute-start | bytes 86024 | tf_op jit(solution)/shard_map/ppermute | solution.py:878
  13.7 1.8 %collective-permute-start.2 = (f32[480,128]{1,0:T(8,128)S(1)}, f32[480,128]{1,0:T(8,128)S(1)}, u32[]{:S(2)}, u32[]{:S(2)}) collective-permute-start(f32[480,128]{1,0:T(8,128)S(1)} %corners.1), channel_id=1, source_target_pairs={{0,1},{1,0},{2,3},{3,2},{4,5},{5,4},{6,7},{7,6},{8,9},{9,8},{10,11... | collective-permute-start | bytes 737288 | tf_op jit(solution)/shard_map/ppermute | solution.py:859

commit v28 on v23

--- a/solution.py
+++ b/solution.py
@@ -119,7 +119,7 @@
     for k in range(4):
         edge_table[2 * k * NP : 2 * (k + 1) * NP] = table[k * NODES + ends]
     edge_table[8 * NP :, :LANES] = spread[ends]
-    return table, np.ascontiguousarray(spread), edge_table
+    return table.astype(ml_dtypes.bfloat16), np.ascontiguousarray(spread), edge_table
 
 
 def lane_tables():
@@ -219,7 +219,7 @@
 def edge_values(table_ref, weight_ref, p, u, v, area, depth, spin):
     root = jnp.sqrt(area)
     mass = jnp.concatenate([weight_ref[...]] * (area.shape[1] // LANES), 1) * area
-    table = table_ref[...].astype(bf16)
+    table = table_ref[...]
     return mass_tendency(table, p, u, v, root * depth, root, mass * spin) + [mass]
 
 
@@ -568,7 +568,7 @@
     ]
     rims = [placed[ROWS + c * NP : ROWS + (c + 1) * NP] for c in range(4)]
     at_rim = lanes_ref[24:25, LANES : LANES + MID] != 0
-    used = first_sums(table_ref[...].astype(bf16), weight_ref[...], parts, rims, at_rim)
+    used = first_sums(table_ref[...], weight_ref[...], parts, rims, at_rim)
     for k, ref in enumerate((low_ref, centre_ref, high_ref)):
         for n, part in enumerate(used):
             ref[n * NODES : (n + 1) * NODES] = part[:, k * LANES : (k + 1) * LANES]
@@ -616,7 +616,7 @@
         jnp.where(outer_at[3] < 0, -1, outer_at[3] + RING * RING * far_at),
     )
     outer = picked(around, as_one_hot(jnp.where(kind == 0, -1, place), 2 * LANES))
-    table = table_ref[...].astype(bf16)
+    table = table_ref[...]
     tiles = (None, low_ref, centre_ref, high_ref, None)
     count = len(tiles)
     masks = [lanes_ref[24:32, k * LANES : (k + 1) * LANES] for k in range(count)]

time: 19.3 us -> 19.3 us (level)
  no operation moved by 1% of the time
where the time goes in v28:
time: 19.3 us; the launch traced here: 19 us
  starting transfers between devices  10.5 us (54%)
  Pallas kernels  7.65 us (40%)
  waiting for transfers between devices  0.8 us (4%)
    pallas_call x7, Pallas kernels, call(): pl.pallas_call(kernel, out_shape=[jax.ShapeDtypeStruct(*out) for out in o...  7.65 us
    ppermute x2, starting transfers between devices, on_device(): halos.append(lax.ppermute(value, both, pairs))  6.69 us
    ppermute x2, starting transfers between devices, eastward(): lax.ppermute(value, both, [(rank(*a), rank(*b)) for a, b in pairs.items()])  2.03 us
    ppermute x2, starting transfers between devices, swapped(): return lax.ppermute(value, both, pairs)  1.74 us
    ppermute x2, waiting for transfers between devices, eastward(): lax.ppermute(value, both, [(rank(*a), rank(*b)) for a, b in pairs.items()])  0.62 us
  transfers between devices with their start and end apart: 6, of which 3 were waited for; matrix products, arithmetic and copies ran while one was open for 0% of the time, Pallas kernels for 14%

profile of v28, /device:TPU:0, one launch (start us, length us, event | category | flops | bytes accessed | tf_op | source)
XLA Modules:
  0.0 19.0 jit_solution(9158196306019181531)
XLA Ops:
  0.0 0.0 copy-start
  0.0 0.0 copy-start.2
  0.0 1.7 %strips.1 = (f32[216,128]{1,0:T(8,128)S(1)}, f32[216,128]{1,0:T(8,128)S(1)}, f32[448,256]{1,0:T(8,128)S(1)}, s32[8,128]{1,0:T(8,128)S(1)}) custom-call(s32[2,256]{1,0:T(2,128)} %refs_0_.1, s32[1,256]{1,0:T(1,128)} %refs_1_.1, f32[3,8,8,256]{3,2,1,0:T(8,128)} %refs_2_.1, f32[8,8,256]{2,1,0:T(8,128)} %refs_3_.1, f32[8,8,256]{2,1,0:T(8,128)} %refs_4_.1, ...), custom_call_target="tpu_custom_call" | custom-call | flops 100000000 | bytes 2097152 | tf_op jit(solution)/shard_map/strips/pallas_call | solution.py:791
  1.7 3.0 %collective-permute-start = (f32[216,128]{1,0:T(8,128)S(1)}, f32[216,128]{1,0:T(8,128)S(1)}, u32[]{:S(2)}, u32[]{:S(2)}) collective-permute-start(f32[216,128]{1,0:T(8,128)S(1)} %get-tuple-element.19.first_ref), channel_id=1, source_target_pairs={{0,16},{1,17},{2,18},{3,19},{4,27},{5,26},{6,25},{7,24},{8,23},{9,... | collective-permute-start | bytes 331784 | tf_op jit(solution)/shard_map/ppermute | solution.py:905
  4.7 3.7 %collective-permute-start.1 = (f32[216,128]{1,0:T(8,128)S(1)}, f32[216,128]{1,0:T(8,128)S(1)}, u32[]{:S(2)}, u32[]{:S(2)}) collective-permute-start(f32[216,128]{1,0:T(8,128)S(1)} %get-tuple-element.20.then_ref), channel_id=1, source_target_pairs={{0,31},{1,30},{2,29},{3,28},{4,20},{5,21},{6,22},{7,23},{8,24},{9,... | collective-permute-start | bytes 331784 | tf_op jit(solution)/shard_map/ppermute | solution.py:905
  8.4 0.0 copy-done
  8.4 0.0 copy-done.2
  8.4 0.9 %rows.1 = (f32[216,128]{1,0:T(8,128)S(1)}, f32[56,128]{1,0:T(8,128)S(1)}, f32[56,128]{1,0:T(8,128)S(1)}, f32[448,128]{1,0:T(8,128)S(1)}) custom-call(s32[8,128]{1,0:T(8,128)S(1)} %get-tuple-element.18.flags_ref, f32[448,256]{1,0:T(8,128)S(1)} %get-tuple-element.21.stored_ref, f32[216,128]{1,0:T(8,128)S(1)} %get-tuple-element.19.first_ref, ...), custom_call_target="tpu_custom_call" | custom-call | flops 100000000 | bytes 2097152 | tf_op jit(solution)/shard_map/rows/pallas_call | solution.py:791
  9.3 1.5 %collective-permute-start.5 = (f32[216,128]{1,0:T(8,128)S(1)}, f32[216,128]{1,0:T(8,128)S(1)}, u32[]{:S(2)}, u32[]{:S(2)}) collective-permute-start(f32[216,128]{1,0:T(8,128)S(1)} %get-tuple-element.26), channel_id=1, source_target_pairs={{0,16},{1,2},{2,1},{3,4},{4,3},{5,6},{6,5},{7,8},{8,7},{9,10},{10,... | collective-permute-start | bytes 331784 | tf_op jit(solution)/shard_map/ppermute | solution.py:856
  10.8 0.5 %collective-permute-start.3 = (f32[56,128]{1,0:T(8,128)S(1)}, f32[56,128]{1,0:T(8,128)S(1)}, u32[]{:S(2)}, u32[]{:S(2)}) collective-permute-start(f32[56,128]{1,0:T(8,128)S(1)} %get-tuple-element.24), channel_id=1, source_target_pairs={{0,16},{1,29},{2,30},{3,27},{4,28},{5,25},{6,26},{7,23},{8,24},{9,... | collective-permute-start | bytes 86024 | tf_op jit(solution)/shard_map/ppermute | solution.py:875
  11.3 1.5 %collective-permute-start.4 = (f32[56,128]{1,0:T(8,128)S(1)}, f32[56,128]{1,0:T(8,128)S(1)}, u32[]{:S(2)}, u32[]{:S(2)}) collective-permute-start(f32[56,128]{1,0:T(8,128)S(1)} %get-tuple-element.25), channel_id=1, source_target_pairs={{0,16},{1,18},{2,17},{3,20},{4,19},{5,22},{6,21},{7,24},{8,23},{9,... | collective-permute-start | bytes 86024 | tf_op jit(solution)/shard_map/ppermute | solution.py:875
  12.8 0.0 copy-done.1
  12.8 0.5 %own.1 = (f32[448,384]{1,0:T(8,128)S(1)}, bf16[384,256]{1,0:T(8,128)(2,1)S(1)}) custom-call(s32[8,128]{1,0:T(8,128)S(1)} %get-tuple-element.18.flags_ref, f32[448,256]{1,0:T(8,128)S(1)} %get-tuple-element.21.stored_ref, s32[64,640]{1,0:T(8,128)S(1)} %copy-done.1), custom_call_target="tpu_custom_call" | custom-call | flops 100000000 | bytes 2097152 | tf_op jit(solution)/shard_map/own/pallas_call | solution.py:791
  13.3 0.0 collective-permute-done.first_ref
  13.3 0.2 collective-permute-done.1.then_ref
  13.5 0.2 %corners.1 = f32[480,128]{1,0:T(8,128)S(1)} custom-call(s32[8,128]{1,0:T(8,128)S(1)} %get-tuple-element.18.flags_ref, f32[216,128]{1,0:T(8,128)S(1)} %collective-permute-done.first_ref, f32[216,128]{1,0:T(8,128)S(1)} %collective-permute-done.1.then_ref, f32[448,128]{1,0:T(8,128)S(1)} %get-tuple-element.22.pair_ref, ...), custom_call_target="tpu_custom_call" | custom-call | flops 100000000 | bytes 2097152 | tf_op jit(solution)/shard_map/corners/pallas_call | solution.py:791
  13.7 0.2 %collective-permute-start.2 = (f32[480,128]{1,0:T(8,128)S(1)}, f32[480,128]{1,0:T(8,128)S(1)}, u32[]{:S(2)}, u32[]{:S(2)}) collective-permute-start(f32[480,128]{1,0:T(8,128)S(1)} %corners.1), channel_id=1, source_target_pairs={{0,1},{1,0},{2,3},{3,2},{4,5},{5,4},{6,7},{7,6},{8,9},{9,8},{10,11... | collective-permute-start | bytes 737288 | tf_op jit(solution)/shard_map/ppermute | solution.py:856
  13.9 0.8 %middle.1 = (f32[704,128]{1,0:T(8,128)S(1)}, f32[704,128]{1,0:T(8,128)S(1)}, f32[704,128]{1,0:T(8,128)S(1)}) custom-call(s32[8,128]{1,0:T(8,128)S(1)} %get-tuple-element.18.flags_ref, f32[216,128]{1,0:T(8,128)S(1)} %collective-permute-done.first_ref, f32[216,128]{1,0:T(8,128)S(1)} %collective-permute-done.1.then_ref, ...), custom_call_target="tpu_custom_call" | custom-call | flops 100000000 | bytes 2097152 | tf_op jit(solution)/shard_map/middle/pallas_call | solution.py:791
  14.7 0.3 %collective-permute-done.3.far1_ref = f32[56,128]{1,0:T(8,128)S(1)} collective-permute-done((f32[56,128]{1,0:T(8,128)S(1)}, f32[56,128]{1,0:T(8,128)S(1)}, u32[]{:S(2)}, u32[]{:S(2)}) %collective-permute-start.3) | collective-permute-done | bytes 28704 | tf_op jit(solution)/shard_map/ppermute | solution.py:875
  15.1 0.3 %collective-permute-done.4.far0_ref = f32[56,128]{1,0:T(8,128)S(1)} collective-permute-done((f32[56,128]{1,0:T(8,128)S(1)}, f32[56,128]{1,0:T(8,128)S(1)}, u32[]{:S(2)}, u32[]{:S(2)}) %collective-permute-start.4) | collective-permute-done | bytes 28704 | tf_op jit(solution)/shard_map/ppermute | solution.py:875
  15.4 0.0 collective-permute-done.5.next_ref
  15.4 0.2 %far.1.next_ref = f32[512,128]{1,0:T(8,128)S(1)} custom-call(s32[8,128]{1,0:T(8,128)S(1)} %get-tuple-element.18.flags_ref, f32[56,128]{1,0:T(8,128)S(1)} %collective-permute-done.3.far1_ref, f32[56,128]{1,0:T(8,128)S(1)} %collective-permute-done.4.far0_ref, f32[216,128]{1,0:T(8,128)S(1)} %collective-permute-done.5.next_ref, ...), custom_call_target="tpu_custom_call" | custom-call | flops 99999997952 | bytes 2097152 | tf_op jit(solution)/shard_map/far/pallas_call | solution.py:791
  15.6 0.0 collective-permute-done.2.pair_ref
  15.6 3.4 %steps.1 = f32[3,8,8,256]{3,2,1,0:T(8,128)} custom-call(s32[8,128]{1,0:T(8,128)S(1)} %get-tuple-element.18.flags_ref, f32[480,128]{1,0:T(8,128)S(1)} %collective-permute-done.2.pair_ref, f32[512,128]{1,0:T(8,128)S(1)} %far.1.next_ref, f32[704,128]{1,0:T(8,128)S(1)} %get-tuple-element.28._.low_ref, f32[704,128]{1,0:T(8,128)S(1)} %get-tuple-element.29.centre_ref, ...), custom_call_target="tpu_custom_call" | custom-call | flops 100000000 | bytes 2097152 | tf_op jit(solution)/shard_map/steps/pallas_call | solution.py:791
  (1 shorter events, 0.0 us)
Async XLA Ops:
  0.0 8.4 %copy-start = (bf16[320,256]{1,0:T(8,128)(2,1)S(1)}, bf16[320,256]{1,0:T(8,128)(2,1)}, u32[]{:S(2)}) copy-start(bf16[320,256]{1,0:T(8,128)(2,1)} %constant.8.clone.table_ref) | copy-start | bytes 491524
  0.0 8.4 %copy-start.2 = (f32[64,128]{1,0:T(8,128)S(1)}, f32[64,128]{1,0:T(8,128)}, u32[]{:S(2)}) copy-start(f32[64,128]{1,0:T(8,128)} %constant.9.clone.weight_ref) | copy-start | bytes 98308
  1.7 11.6 %collective-permute-start = (f32[216,128]{1,0:T(8,128)S(1)}, f32[216,128]{1,0:T(8,128)S(1)}, u32[]{:S(2)}, u32[]{:S(2)}) collective-permute-start(f32[216,128]{1,0:T(8,128)S(1)} %get-tuple-element.19.first_ref), channel_id=1, source_target_pairs={{0,16},{1,17},{2,18},{3,19},{4,27},{5,26},{6,25},{7,24},{8,23},{9,... | collective-permute-start | bytes 331784 | tf_op jit(solution)/shard_map/ppermute | solution.py:905
  4.7 8.8 %collective-permute-start.1 = (f32[216,128]{1,0:T(8,128)S(1)}, f32[216,128]{1,0:T(8,128)S(1)}, u32[]{:S(2)}, u32[]{:S(2)}) collective-permute-start(f32[216,128]{1,0:T(8,128)S(1)} %get-tuple-element.20.then_ref), channel_id=1, source_target_pairs={{0,31},{1,30},{2,29},{3,28},{4,20},{5,21},{6,22},{7,23},{8,24},{9,... | collective-permute-start | bytes 331784 | tf_op jit(solution)/shard_map/ppermute | solution.py:905
  8.4 4.4 %copy-start.1 = (s32[64,640]{1,0:T(8,128)S(1)}, s32[64,640]{1,0:T(8,128)}, u32[]{:S(2)}) copy-start(s32[64,640]{1,0:T(8,128)} %constant.11.clone.lanes_ref) | copy-start | bytes 491524
  9.3 6.1 %collective-permute-start.5 = (f32[216,128]{1,0:T(8,128)S(1)}, f32[216,128]{1,0:T(8,128)S(1)}, u32[]{:S(2)}, u32[]{:S(2)}) collective-permute-start(f32[216,128]{1,0:T(8,128)S(1)} %get-tuple-element.26), channel_id=1, source_target_pairs={{0,16},{1,2},{2,1},{3,4},{4,3},{5,6},{6,5},{7,8},{8,7},{9,10},{10,... | collective-permute-start | bytes 331784 | tf_op jit(solution)/shard_map/ppermute | solution.py:856
  10.8 4.3 %collective-permute-start.3 = (f32[56,128]{1,0:T(8,128)S(1)}, f32[56,128]{1,0:T(8,128)S(1)}, u32[]{:S(2)}, u32[]{:S(2)}) collective-permute-start(f32[56,128]{1,0:T(8,128)S(1)} %get-tuple-element.24), channel_id=1, source_target_pairs={{0,16},{1,29},{2,30},{3,27},{4,28},{5,25},{6,26},{7,23},{8,24},{9,... | collective-permute-start | bytes 86024 | tf_op jit(solution)/shard_map/ppermute | solution.py:875
  11.3 4.0 %collective-permute-start.4 = (f32[56,128]{1,0:T(8,128)S(1)}, f32[56,128]{1,0:T(8,128)S(1)}, u32[]{:S(2)}, u32[]{:S(2)}) collective-permute-start(f32[56,128]{1,0:T(8,128)S(1)} %get-tuple-element.25), channel_id=1, source_target_pairs={{0,16},{1,18},{2,17},{3,20},{4,19},{5,22},{6,21},{7,24},{8,23},{9,... | collective-permute-start | bytes 86024 | tf_op jit(solution)/shard_map/ppermute | solution.py:875
  13.7 1.9 %collective-permute-start.2 = (f32[480,128]{1,0:T(8,128)S(1)}, f32[480,128]{1,0:T(8,128)S(1)}, u32[]{:S(2)}, u32[]{:S(2)}) collective-permute-start(f32[480,128]{1,0:T(8,128)S(1)} %corners.1), channel_id=1, source_target_pairs={{0,1},{1,0},{2,3},{3,2},{4,5},{5,4},{6,7},{7,6},{8,9},{9,8},{10,11... | collective-permute-start | bytes 737288 | tf_op jit(solution)/shard_map/ppermute | solution.py:856

commit v29 on v23

--- a/solution.py
+++ b/solution.py
@@ -574,7 +574,7 @@
             ref[n * NODES : (n + 1) * NODES] = part[:, k * LANES : (k + 1) * LANES]
 
 
-def far_kernel(block_cols, flags_ref, far1_ref, far0_ref, next_ref, _, out_ref):
+def far_kernel(block_cols, flags_ref, far0_ref, far1_ref, next_ref, _, out_ref):
     east0, flip0, east1, flip1 = flags_in(flags_ref)
     odd = lax.axis_index("blk") & 1
     lane = lax.broadcasted_iota(i32, (1, LANES), 1)
@@ -933,7 +933,7 @@
     )
     (from_next,) = call(
         functools.partial(far_kernel, block_cols),
-        [(vmem, x) for x in (flags, far1, far0, from_next, low)],
+        [(vmem, x) for x in (flags, far0, far1, from_next, low)],
         [((RIM_ROWS, LANES), f32)],
         10**11,
         name="far",

time: 19.3 us -> 21.6 us (1.12)
  the two profiles are of different devices: /device:TPU:0 before, /device:TPU:1 now
where the time goes in v29:
time: 21.6 us; the launch traced here: 21.5 us
  starting transfers between devices  10.5 us (49%)
  Pallas kernels  7.64 us (35%)
  waiting for transfers between devices  3.25 us (15%)
    pallas_call x7, Pallas kernels, call(): pl.pallas_call(kernel, out_shape=[jax.ShapeDtypeStruct(*out) for out in o...  7.64 us
    ppermute x2, starting transfers between devices, on_device(): halos.append(lax.ppermute(value, both, pairs))  7.2 us
    ppermute x2, waiting for transfers between devices, eastward(): lax.ppermute(value, both, [(rank(*a), rank(*b)) for a, b in pairs.items()])  3.24 us
    ppermute x2, starting transfers between devices, eastward(): lax.ppermute(value, both, [(rank(*a), rank(*b)) for a, b in pairs.items()])  2.66 us
    ppermute x2, starting transfers between devices, swapped(): return lax.ppermute(value, both, pairs)  0.67 us
  transfers between devices with their start and end apart: 6, of which 1 were waited for; matrix products, arithmetic and copies ran while one was open for 0% of the time, Pallas kernels for 12%

profile of v29, /device:TPU:1, one launch (start us, length us, event | category | flops | bytes accessed | tf_op | source)
XLA Modules:
  0.0 21.5 jit_solution(9432196340867480289)
XLA Ops:
  0.0 0.0 copy-start
  0.0 0.0 copy-start.2
  0.0 1.7 %strips.1 = (f32[216,128]{1,0:T(8,128)S(1)}, f32[216,128]{1,0:T(8,128)S(1)}, f32[448,256]{1,0:T(8,128)S(1)}, s32[8,128]{1,0:T(8,128)S(1)}) custom-call(s32[2,256]{1,0:T(2,128)} %refs_0_.1, s32[1,256]{1,0:T(1,128)} %refs_1_.1, f32[3,8,8,256]{3,2,1,0:T(8,128)} %refs_2_.1, f32[8,8,256]{2,1,0:T(8,128)} %refs_3_.1, f32[8,8,256]{2,1,0:T(8,128)} %refs_4_.1, ...), custom_call_target="tpu_custom_call" | custom-call | flops 100000000 | bytes 2097152 | tf_op jit(solution)/shard_map/strips/pallas_call | solution.py:791
  1.7 2.1 %collective-permute-start = (f32[216,128]{1,0:T(8,128)S(1)}, f32[216,128]{1,0:T(8,128)S(1)}, u32[]{:S(2)}, u32[]{:S(2)}) collective-permute-start(f32[216,128]{1,0:T(8,128)S(1)} %get-tuple-element.19.first_ref), channel_id=1, source_target_pairs={{0,16},{1,17},{2,18},{3,19},{4,27},{5,26},{6,25},{7,24},{8,23},{9,... | collective-permute-start | bytes 331784 | tf_op jit(solution)/shard_map/ppermute | solution.py:905
  3.8 5.1 %collective-permute-start.1 = (f32[216,128]{1,0:T(8,128)S(1)}, f32[216,128]{1,0:T(8,128)S(1)}, u32[]{:S(2)}, u32[]{:S(2)}) collective-permute-start(f32[216,128]{1,0:T(8,128)S(1)} %get-tuple-element.20.then_ref), channel_id=1, source_target_pairs={{0,31},{1,30},{2,29},{3,28},{4,20},{5,21},{6,22},{7,23},{8,24},{9,... | collective-permute-start | bytes 331784 | tf_op jit(solution)/shard_map/ppermute | solution.py:905
  8.9 0.0 copy-done
  8.9 0.0 copy-done.2
  8.9 0.9 %rows.1 = (f32[216,128]{1,0:T(8,128)S(1)}, f32[56,128]{1,0:T(8,128)S(1)}, f32[56,128]{1,0:T(8,128)S(1)}, f32[448,128]{1,0:T(8,128)S(1)}) custom-call(s32[8,128]{1,0:T(8,128)S(1)} %get-tuple-element.18.flags_ref, f32[448,256]{1,0:T(8,128)S(1)} %get-tuple-element.21.stored_ref, f32[216,128]{1,0:T(8,128)S(1)} %get-tuple-element.19.first_ref, ...), custom_call_target="tpu_custom_call" | custom-call | flops 100000000 | bytes 2097152 | tf_op jit(solution)/shard_map/rows/pallas_call | solution.py:791
  9.8 0.0 collective-permute-start.5
  9.8 2.7 %collective-permute-start.3 = (f32[56,128]{1,0:T(8,128)S(1)}, f32[56,128]{1,0:T(8,128)S(1)}, u32[]{:S(2)}, u32[]{:S(2)}) collective-permute-start(f32[56,128]{1,0:T(8,128)S(1)} %get-tuple-element.24), channel_id=1, source_target_pairs={{0,16},{1,18},{2,17},{3,20},{4,19},{5,22},{6,21},{7,24},{8,23},{9,... | collective-permute-start | bytes 86024 | tf_op jit(solution)/shard_map/ppermute | solution.py:875
  12.5 0.0 collective-permute-start.4
  12.5 0.0 copy-done.1
  12.5 0.5 %own.1 = (f32[448,384]{1,0:T(8,128)S(1)}, bf16[384,256]{1,0:T(8,128)(2,1)S(1)}) custom-call(s32[8,128]{1,0:T(8,128)S(1)} %get-tuple-element.18.flags_ref, f32[448,256]{1,0:T(8,128)S(1)} %get-tuple-element.21.stored_ref, s32[64,640]{1,0:T(8,128)S(1)} %copy-done.1), custom_call_target="tpu_custom_call" | custom-call | flops 100000000 | bytes 2097152 | tf_op jit(solution)/shard_map/own/pallas_call | solution.py:791
  13.0 0.0 collective-permute-done.first_ref
  13.0 0.0 collective-permute-done.1.then_ref
  13.0 0.2 %corners.1 = f32[480,128]{1,0:T(8,128)S(1)} custom-call(s32[8,128]{1,0:T(8,128)S(1)} %get-tuple-element.18.flags_ref, f32[216,128]{1,0:T(8,128)S(1)} %collective-permute-done.first_ref, f32[216,128]{1,0:T(8,128)S(1)} %collective-permute-done.1.then_ref, f32[448,128]{1,0:T(8,128)S(1)} %get-tuple-element.22.pair_ref, ...), custom_call_target="tpu_custom_call" | custom-call | flops 100000000 | bytes 2097152 | tf_op jit(solution)/shard_map/corners/pallas_call | solution.py:791
  13.2 0.6 %collective-permute-start.2 = (f32[480,128]{1,0:T(8,128)S(1)}, f32[480,128]{1,0:T(8,128)S(1)}, u32[]{:S(2)}, u32[]{:S(2)}) collective-permute-start(f32[480,128]{1,0:T(8,128)S(1)} %corners.1), channel_id=1, source_target_pairs={{0,1},{1,0},{2,3},{3,2},{4,5},{5,4},{6,7},{7,6},{8,9},{9,8},{10,11... | collective-permute-start | bytes 737288 | tf_op jit(solution)/shard_map/ppermute | solution.py:856
  13.9 0.8 %middle.1 = (f32[704,128]{1,0:T(8,128)S(1)}, f32[704,128]{1,0:T(8,128)S(1)}, f32[704,128]{1,0:T(8,128)S(1)}) custom-call(s32[8,128]{1,0:T(8,128)S(1)} %get-tuple-element.18.flags_ref, f32[216,128]{1,0:T(8,128)S(1)} %collective-permute-done.first_ref, f32[216,128]{1,0:T(8,128)S(1)} %collective-permute-done.1.then_ref, ...), custom_call_target="tpu_custom_call" | custom-call | flops 100000000 | bytes 2097152 | tf_op jit(solution)/shard_map/middle/pallas_call | solution.py:791
  14.7 0.0 collective-permute-done.3.far0_ref
  14.7 3.2 %collective-permute-done.4.far1_ref = f32[56,128]{1,0:T(8,128)S(1)} collective-permute-done((f32[56,128]{1,0:T(8,128)S(1)}, f32[56,128]{1,0:T(8,128)S(1)}, u32[]{:S(2)}, u32[]{:S(2)}) %collective-permute-start.4) | collective-permute-done | bytes 28704 | tf_op jit(solution)/shard_map/ppermute | solution.py:875
  17.9 0.0 collective-permute-done.5.next_ref
  17.9 0.2 %far.1.next_ref = f32[512,128]{1,0:T(8,128)S(1)} custom-call(s32[8,128]{1,0:T(8,128)S(1)} %get-tuple-element.18.flags_ref, f32[56,128]{1,0:T(8,128)S(1)} %collective-permute-done.3.far0_ref, f32[56,128]{1,0:T(8,128)S(1)} %collective-permute-done.4.far1_ref, f32[216,128]{1,0:T(8,128)S(1)} %collective-permute-done.5.next_ref, ...), custom_call_target="tpu_custom_call" | custom-call | flops 99999997952 | bytes 2097152 | tf_op jit(solution)/shard_map/far/pallas_call | solution.py:791
  18.1 0.0 collective-permute-done.2.pair_ref
  18.1 3.4 %steps.1 = f32[3,8,8,256]{3,2,1,0:T(8,128)} custom-call(s32[8,128]{1,0:T(8,128)S(1)} %get-tuple-element.18.flags_ref, f32[480,128]{1,0:T(8,128)S(1)} %collective-permute-done.2.pair_ref, f32[512,128]{1,0:T(8,128)S(1)} %far.1.next_ref, f32[704,128]{1,0:T(8,128)S(1)} %get-tuple-element.28._.low_ref, f32[704,128]{1,0:T(8,128)S(1)} %get-tuple-element.29.centre_ref, ...), custom_call_target="tpu_custom_call" | custom-call | flops 100000000 | bytes 2097152 | tf_op jit(solution)/shard_map/steps/pallas_call | solution.py:791
  (1 shorter events, 0.0 us)
Async XLA Ops:
  0.0 8.9 %copy-start = (f32[320,256]{1,0:T(8,128)S(1)}, f32[320,256]{1,0:T(8,128)}, u32[]{:S(2)}) copy-start(f32[320,256]{1,0:T(8,128)} %constant.8.clone.table_ref) | copy-start | bytes 983044
  0.0 8.9 %copy-start.2 = (f32[64,128]{1,0:T(8,128)S(1)}, f32[64,128]{1,0:T(8,128)}, u32[]{:S(2)}) copy-start(f32[64,128]{1,0:T(8,128)} %constant.9.clone.weight_ref) | copy-start | bytes 98308
  1.7 11.3 %collective-permute-start = (f32[216,128]{1,0:T(8,128)S(1)}, f32[216,128]{1,0:T(8,128)S(1)}, u32[]{:S(2)}, u32[]{:S(2)}) collective-permute-start(f32[216,128]{1,0:T(8,128)S(1)} %get-tuple-element.19.first_ref), channel_id=1, source_target_pairs={{0,16},{1,17},{2,18},{3,19},{4,27},{5,26},{6,25},{7,24},{8,23},{9,... | collective-permute-start | bytes 331784 | tf_op jit(solution)/shard_map/ppermute | solution.py:905
  3.8 9.2 %collective-permute-start.1 = (f32[216,128]{1,0:T(8,128)S(1)}, f32[216,128]{1,0:T(8,128)S(1)}, u32[]{:S(2)}, u32[]{:S(2)}) collective-permute-start(f32[216,128]{1,0:T(8,128)S(1)} %get-tuple-element.20.then_ref), channel_id=1, source_target_pairs={{0,31},{1,30},{2,29},{3,28},{4,20},{5,21},{6,22},{7,23},{8,24},{9,... | collective-permute-start | bytes 331784 | tf_op jit(solution)/shard_map/ppermute | solution.py:905
  8.9 3.6 %copy-start.1 = (s32[64,640]{1,0:T(8,128)S(1)}, s32[64,640]{1,0:T(8,128)}, u32[]{:S(2)}) copy-start(s32[64,640]{1,0:T(8,128)} %constant.11.clone.lanes_ref) | copy-start | bytes 491524
  9.8 8.1 %collective-permute-start.5 = (f32[216,128]{1,0:T(8,128)S(1)}, f32[216,128]{1,0:T(8,128)S(1)}, u32[]{:S(2)}, u32[]{:S(2)}) collective-permute-start(f32[216,128]{1,0:T(8,128)S(1)} %get-tuple-element.26), channel_id=1, source_target_pairs={{0,16},{1,2},{2,1},{3,4},{4,3},{5,6},{6,5},{7,8},{8,7},{9,10},{10,... | collective-permute-start | bytes 331784 | tf_op jit(solution)/shard_map/ppermute | solution.py:856
  9.8 4.8 %collective-permute-start.3 = (f32[56,128]{1,0:T(8,128)S(1)}, f32[56,128]{1,0:T(8,128)S(1)}, u32[]{:S(2)}, u32[]{:S(2)}) collective-permute-start(f32[56,128]{1,0:T(8,128)S(1)} %get-tuple-element.24), channel_id=1, source_target_pairs={{0,16},{1,18},{2,17},{3,20},{4,19},{5,22},{6,21},{7,24},{8,23},{9,... | collective-permute-start | bytes 86024 | tf_op jit(solution)/shard_map/ppermute | solution.py:875
  12.5 5.4 %collective-permute-start.4 = (f32[56,128]{1,0:T(8,128)S(1)}, f32[56,128]{1,0:T(8,128)S(1)}, u32[]{:S(2)}, u32[]{:S(2)}) collective-permute-start(f32[56,128]{1,0:T(8,128)S(1)} %get-tuple-element.25), channel_id=1, source_target_pairs={{0,16},{1,29},{2,30},{3,27},{4,28},{5,25},{6,26},{7,23},{8,24},{9,... | collective-permute-start | bytes 86024 | tf_op jit(solution)/shard_map/ppermute | solution.py:875
  13.2 4.9 %collective-permute-start.2 = (f32[480,128]{1,0:T(8,128)S(1)}, f32[480,128]{1,0:T(8,128)S(1)}, u32[]{:S(2)}, u32[]{:S(2)}) collective-permute-start(f32[480,128]{1,0:T(8,128)S(1)} %corners.1), channel_id=1, source_target_pairs={{0,1},{1,0},{2,3},{3,2},{4,5},{5,4},{6,7},{7,6},{8,9},{9,8},{10,11... | collective-permute-start | bytes 737288 | tf_op jit(solution)/shard_map/ppermute | solution.py:856

commit v30 on v26

--- a/solution.py
+++ b/solution.py
@@ -395,7 +395,7 @@
 
 
 def mirrored_first(block_y):
-    return (block_y >= BY // 8) & (block_y < BY - BY // 8)
+    return (block_y >= BY // 4 - 1) & (block_y < BY - BY // 4 + 1)
 
 
 def in_order(block_cols, first, second):

time: 19.6 us -> 19.3 us (0.985)
  the two profiles are of different devices: /device:TPU:1 before, /device:TPU:4 now
where the time goes in v30:
time: 19.3 us; the launch traced here: 19.1 us
  starting transfers between devices  9.05 us (47%)
  Pallas kernels  7.64 us (40%)
  waiting for transfers between devices  2.36 us (12%)
    pallas_call x7, Pallas kernels, call(): pl.pallas_call(kernel, out_shape=[jax.ShapeDtypeStruct(*out) for out in o...  7.64 us
    ppermute x2, starting transfers between devices, on_device(): halos.append(lax.ppermute(value, both, pairs))  4.23 us
    ppermute x2, starting transfers between devices, swapped(): return lax.ppermute(value, both, pairs)  3.59 us
    ppermute x2, waiting for transfers between devices, eastward(): lax.ppermute(value, both, [(rank(*a), rank(*b)) for a, b in pairs.items()])  1.87 us
    ppermute x2, starting transfers between devices, eastward(): lax.ppermute(value, both, [(rank(*a), rank(*b)) for a, b in pairs.items()])  1.22 us
    ppermute x2, waiting for transfers between devices, on_device(): halos.append(lax.ppermute(value, both, pairs))  0.48 us
  transfers between devices with their start and end apart: 6, of which 2 were waited for; matrix products, arithmetic and copies ran while one was open for 0% of the time, Pallas kernels for 13%

profile of v30, /device:TPU:4, one launch (start us, length us, event | category | flops | bytes accessed | tf_op | source)
XLA Modules:
  0.0 19.1 jit_solution(5207528533099492518)
XLA Ops:
  0.0 0.0 copy-start
  0.0 0.0 copy-start.2
  0.0 1.7 %strips.1 = (f32[216,128]{1,0:T(8,128)S(1)}, f32[216,128]{1,0:T(8,128)S(1)}, f32[448,256]{1,0:T(8,128)S(1)}, s32[8,128]{1,0:T(8,128)S(1)}) custom-call(s32[2,256]{1,0:T(2,128)} %refs_0_.1, s32[1,256]{1,0:T(1,128)} %refs_1_.1, f32[3,8,8,256]{3,2,1,0:T(8,128)} %refs_2_.1, f32[8,8,256]{2,1,0:T(8,128)} %refs_3_.1, f32[8,8,256]{2,1,0:T(8,128)} %refs_4_.1, ...), custom_call_target="tpu_custom_call" | custom-call | flops 100000000 | bytes 2097152 | tf_op jit(solution)/shard_map/strips/pallas_call | solution.py:791
  1.7 1.6 %collective-permute-start = (f32[216,128]{1,0:T(8,128)S(1)}, f32[216,128]{1,0:T(8,128)S(1)}, u32[]{:S(2)}, u32[]{:S(2)}) collective-permute-start(f32[216,128]{1,0:T(8,128)S(1)} %get-tuple-element.19.first_ref), channel_id=1, source_target_pairs={{0,16},{1,17},{2,18},{3,28},{4,27},{5,26},{6,25},{7,24},{8,23},{9,... | collective-permute-start | bytes 331784 | tf_op jit(solution)/shard_map/ppermute | solution.py:905
  3.3 2.7 %collective-permute-start.1 = (f32[216,128]{1,0:T(8,128)S(1)}, f32[216,128]{1,0:T(8,128)S(1)}, u32[]{:S(2)}, u32[]{:S(2)}) collective-permute-start(f32[216,128]{1,0:T(8,128)S(1)} %get-tuple-element.20.then_ref), channel_id=1, source_target_pairs={{0,31},{1,30},{2,29},{3,19},{4,20},{5,21},{6,22},{7,23},{8,24},{9,... | collective-permute-start | bytes 331784 | tf_op jit(solution)/shard_map/ppermute | solution.py:905
  6.0 0.0 copy-done
  6.0 0.0 copy-done.2
  6.0 0.9 %rows.1 = (f32[216,128]{1,0:T(8,128)S(1)}, f32[56,128]{1,0:T(8,128)S(1)}, f32[56,128]{1,0:T(8,128)S(1)}, f32[448,128]{1,0:T(8,128)S(1)}) custom-call(s32[8,128]{1,0:T(8,128)S(1)} %get-tuple-element.18.flags_ref, f32[448,256]{1,0:T(8,128)S(1)} %get-tuple-element.21.stored_ref, f32[216,128]{1,0:T(8,128)S(1)} %get-tuple-element.19.first_ref, ...), custom_call_target="tpu_custom_call" | custom-call | flops 100000000 | bytes 2097152 | tf_op jit(solution)/shard_map/rows/pallas_call | solution.py:791
  6.8 2.1 %collective-permute-start.5 = (f32[216,128]{1,0:T(8,128)S(1)}, f32[216,128]{1,0:T(8,128)S(1)}, u32[]{:S(2)}, u32[]{:S(2)}) collective-permute-start(f32[216,128]{1,0:T(8,128)S(1)} %get-tuple-element.26), channel_id=1, source_target_pairs={{0,16},{1,2},{2,1},{3,4},{4,3},{5,6},{6,5},{7,8},{8,7},{9,10},{10,... | collective-permute-start | bytes 331784 | tf_op jit(solution)/shard_map/ppermute | solution.py:856
  8.9 1.1 %collective-permute-start.3 = (f32[56,128]{1,0:T(8,128)S(1)}, f32[56,128]{1,0:T(8,128)S(1)}, u32[]{:S(2)}, u32[]{:S(2)}) collective-permute-start(f32[56,128]{1,0:T(8,128)S(1)} %get-tuple-element.24), channel_id=1, source_target_pairs={{0,16},{1,29},{2,30},{3,27},{4,28},{5,25},{6,26},{7,23},{8,24},{9,... | collective-permute-start | bytes 86024 | tf_op jit(solution)/shard_map/ppermute | solution.py:875
  10.1 0.1 collective-permute-start.4
  10.2 0.0 copy-done.1
  10.2 0.5 %own.1 = (f32[448,384]{1,0:T(8,128)S(1)}, bf16[384,256]{1,0:T(8,128)(2,1)S(1)}) custom-call(s32[8,128]{1,0:T(8,128)S(1)} %get-tuple-element.18.flags_ref, f32[448,256]{1,0:T(8,128)S(1)} %get-tuple-element.21.stored_ref, s32[64,640]{1,0:T(8,128)S(1)} %copy-done.1), custom_call_target="tpu_custom_call" | custom-call | flops 100000000 | bytes 2097152 | tf_op jit(solution)/shard_map/own/pallas_call | solution.py:791
  10.7 0.0 collective-permute-done.first_ref
  10.7 0.5 %collective-permute-done.1.then_ref = f32[216,128]{1,0:T(8,128)S(1)} collective-permute-done((f32[216,128]{1,0:T(8,128)S(1)}, f32[216,128]{1,0:T(8,128)S(1)}, u32[]{:S(2)}, u32[]{:S(2)}) %collective-permute-start.1) | collective-permute-done | bytes 110624 | tf_op jit(solution)/shard_map/ppermute | solution.py:905
  11.1 0.2 %corners.1 = f32[480,128]{1,0:T(8,128)S(1)} custom-call(s32[8,128]{1,0:T(8,128)S(1)} %get-tuple-element.18.flags_ref, f32[216,128]{1,0:T(8,128)S(1)} %collective-permute-done.first_ref, f32[216,128]{1,0:T(8,128)S(1)} %collective-permute-done.1.then_ref, f32[448,128]{1,0:T(8,128)S(1)} %get-tuple-element.22.pair_ref, ...), custom_call_target="tpu_custom_call" | custom-call | flops 100000000 | bytes 2097152 | tf_op jit(solution)/shard_map/corners/pallas_call | solution.py:791
  11.4 1.5 %collective-permute-start.2 = (f32[480,128]{1,0:T(8,128)S(1)}, f32[480,128]{1,0:T(8,128)S(1)}, u32[]{:S(2)}, u32[]{:S(2)}) collective-permute-start(f32[480,128]{1,0:T(8,128)S(1)} %corners.1), channel_id=1, source_target_pairs={{0,1},{1,0},{2,3},{3,2},{4,5},{5,4},{6,7},{7,6},{8,9},{9,8},{10,11... | collective-permute-start | bytes 737288 | tf_op jit(solution)/shard_map/ppermute | solution.py:856
  12.8 0.8 %middle.1 = (f32[704,128]{1,0:T(8,128)S(1)}, f32[704,128]{1,0:T(8,128)S(1)}, f32[704,128]{1,0:T(8,128)S(1)}) custom-call(s32[8,128]{1,0:T(8,128)S(1)} %get-tuple-element.18.flags_ref, f32[216,128]{1,0:T(8,128)S(1)} %collective-permute-done.first_ref, f32[216,128]{1,0:T(8,128)S(1)} %collective-permute-done.1.then_ref, ...), custom_call_target="tpu_custom_call" | custom-call | flops 100000000 | bytes 2097152 | tf_op jit(solution)/shard_map/middle/pallas_call | solution.py:791
  13.6 1.9 %collective-permute-done.3.far1_ref = f32[56,128]{1,0:T(8,128)S(1)} collective-permute-done((f32[56,128]{1,0:T(8,128)S(1)}, f32[56,128]{1,0:T(8,128)S(1)}, u32[]{:S(2)}, u32[]{:S(2)}) %collective-permute-start.3) | collective-permute-done | bytes 28704 | tf_op jit(solution)/shard_map/ppermute | solution.py:875
  15.5 0.0 collective-permute-done.4.far0_ref
  15.5 0.0 collective-permute-done.5.next_ref
  15.5 0.2 %far.1.next_ref = f32[512,128]{1,0:T(8,128)S(1)} custom-call(s32[8,128]{1,0:T(8,128)S(1)} %get-tuple-element.18.flags_ref, f32[56,128]{1,0:T(8,128)S(1)} %collective-permute-done.3.far1_ref, f32[56,128]{1,0:T(8,128)S(1)} %collective-permute-done.4.far0_ref, f32[216,128]{1,0:T(8,128)S(1)} %collective-permute-done.5.next_ref, ...), custom_call_target="tpu_custom_call" | custom-call | flops 99999997952 | bytes 2097152 | tf_op jit(solution)/shard_map/far/pallas_call | solution.py:791
  15.7 0.0 collective-permute-done.2.pair_ref
  15.7 3.4 %steps.1 = f32[3,8,8,256]{3,2,1,0:T(8,128)} custom-call(s32[8,128]{1,0:T(8,128)S(1)} %get-tuple-element.18.flags_ref, f32[480,128]{1,0:T(8,128)S(1)} %collective-permute-done.2.pair_ref, f32[512,128]{1,0:T(8,128)S(1)} %far.1.next_ref, f32[704,128]{1,0:T(8,128)S(1)} %get-tuple-element.28._.low_ref, f32[704,128]{1,0:T(8,128)S(1)} %get-tuple-element.29.centre_ref, ...), custom_call_target="tpu_custom_call" | custom-call | flops 100000000 | bytes 2097152 | tf_op jit(solution)/shard_map/steps/pallas_call | solution.py:791
  (1 shorter events, 0.0 us)
Async XLA Ops:
  0.0 6.0 %copy-start = (f32[320,256]{1,0:T(8,128)S(1)}, f32[320,256]{1,0:T(8,128)}, u32[]{:S(2)}) copy-start(f32[320,256]{1,0:T(8,128)} %constant.8.clone.table_ref) | copy-start | bytes 983044
  0.0 6.0 %copy-start.2 = (f32[64,128]{1,0:T(8,128)S(1)}, f32[64,128]{1,0:T(8,128)}, u32[]{:S(2)}) copy-start(f32[64,128]{1,0:T(8,128)} %constant.9.clone.weight_ref) | copy-start | bytes 98308
  1.7 8.9 %collective-permute-start = (f32[216,128]{1,0:T(8,128)S(1)}, f32[216,128]{1,0:T(8,128)S(1)}, u32[]{:S(2)}, u32[]{:S(2)}) collective-permute-start(f32[216,128]{1,0:T(8,128)S(1)} %get-tuple-element.19.first_ref), channel_id=1, source_target_pairs={{0,16},{1,17},{2,18},{3,28},{4,27},{5,26},{6,25},{7,24},{8,23},{9,... | collective-permute-start | bytes 331784 | tf_op jit(solution)/shard_map/ppermute | solution.py:905
  3.3 7.9 %collective-permute-start.1 = (f32[216,128]{1,0:T(8,128)S(1)}, f32[216,128]{1,0:T(8,128)S(1)}, u32[]{:S(2)}, u32[]{:S(2)}) collective-permute-start(f32[216,128]{1,0:T(8,128)S(1)} %get-tuple-element.20.then_ref), channel_id=1, source_target_pairs={{0,31},{1,30},{2,29},{3,19},{4,20},{5,21},{6,22},{7,23},{8,24},{9,... | collective-permute-start | bytes 331784 | tf_op jit(solution)/shard_map/ppermute | solution.py:905
  6.0 4.2 %copy-start.1 = (s32[64,640]{1,0:T(8,128)S(1)}, s32[64,640]{1,0:T(8,128)}, u32[]{:S(2)}) copy-start(s32[64,640]{1,0:T(8,128)} %constant.11.clone.lanes_ref) | copy-start | bytes 491524
  6.8 8.7 %collective-permute-start.5 = (f32[216,128]{1,0:T(8,128)S(1)}, f32[216,128]{1,0:T(8,128)S(1)}, u32[]{:S(2)}, u32[]{:S(2)}) collective-permute-start(f32[216,128]{1,0:T(8,128)S(1)} %get-tuple-element.26), channel_id=1, source_target_pairs={{0,16},{1,2},{2,1},{3,4},{4,3},{5,6},{6,5},{7,8},{8,7},{9,10},{10,... | collective-permute-start | bytes 331784 | tf_op jit(solution)/shard_map/ppermute | solution.py:856
  8.9 6.6 %collective-permute-start.3 = (f32[56,128]{1,0:T(8,128)S(1)}, f32[56,128]{1,0:T(8,128)S(1)}, u32[]{:S(2)}, u32[]{:S(2)}) collective-permute-start(f32[56,128]{1,0:T(8,128)S(1)} %get-tuple-element.24), channel_id=1, source_target_pairs={{0,16},{1,29},{2,30},{3,27},{4,28},{5,25},{6,26},{7,23},{8,24},{9,... | collective-permute-start | bytes 86024 | tf_op jit(solution)/shard_map/ppermute | solution.py:875
  10.1 5.4 %collective-permute-start.4 = (f32[56,128]{1,0:T(8,128)S(1)}, f32[56,128]{1,0:T(8,128)S(1)}, u32[]{:S(2)}, u32[]{:S(2)}) collective-permute-start(f32[56,128]{1,0:T(8,128)S(1)} %get-tuple-element.25), channel_id=1, source_target_pairs={{0,16},{1,18},{2,17},{3,20},{4,19},{5,22},{6,21},{7,24},{8,23},{9,... | collective-permute-start | bytes 86024 | tf_op jit(solution)/shard_map/ppermute | solution.py:875
  11.4 4.4 %collective-permute-start.2 = (f32[480,128]{1,0:T(8,128)S(1)}, f32[480,128]{1,0:T(8,128)S(1)}, u32[]{:S(2)}, u32[]{:S(2)}) collective-permute-start(f32[480,128]{1,0:T(8,128)S(1)} %corners.1), channel_id=1, source_target_pairs={{0,1},{1,0},{2,3},{3,2},{4,5},{5,4},{6,7},{7,6},{8,9},{9,8},{10,11... | collective-permute-start | bytes 737288 | tf_op jit(solution)/shard_map/ppermute | solution.py:856
